TPU v7x, 32 devices: a whole 2x2x4 slice. The times are simulated.
32 devices in a mesh: dp: 8 (over z, x), tp: 4 (over y, core).
Axes of the slice: x: 2, y: 2, z: 4, core: 2. Of those that a mesh axis runs over, the one named last changes fastest.
Arguments:
- layer_input: bfloat16 [8192, 2048], P(('dp', 'tp'))
- out_grad: bfloat16 [8192, 2048], P(('dp', 'tp'))
- segment_ids: int32 [8192], P('dp'), may hold values from 0 to 2, as said below
- positions: int32 [8192], P('dp'), may hold values from 0 to 1999, as said below
- w_query: float32 [2048, 2048], P('dp', 'tp'), may hold values from -0.125 to 0.125
- w_key: float32 [2048, 512], P('dp', 'tp'), may hold values from -0.125 to 0.125
- w_value: float32 [2048, 512], P('dp', 'tp'), may hold values from -0.125 to 0.125
- w_out: float32 [2048, 2048], P('tp', 'dp'), may hold values from -0.5 to 0.5
- w_gate: float32 [2048, 8192], P('dp', 'tp'), may hold values from -0.125 to 0.125
- w_up: float32 [2048, 8192], P('dp', 'tp'), may hold values from -0.125 to 0.125
- w_down: float32 [8192, 2048], P('tp', 'dp'), may hold values from -0.0625 to 0.0625
- m_query: float32 [2048, 2048], P('dp', 'tp'), may hold values from -56 to 56
- m_key: float32 [2048, 512], P('dp', 'tp'), may hold values from -112 to 112
- m_value: float32 [2048, 512], P('dp', 'tp'), may hold values from -256 to 256
- m_out: float32 [2048, 2048], P('tp', 'dp'), may hold values from -14 to 14
- m_gate: float32 [2048, 8192], P('dp', 'tp'), may hold values from -14 to 14
- m_up: float32 [2048, 8192], P('dp', 'tp'), may hold values from -16 to 16
- m_down: float32 [8192, 2048], P('tp', 'dp'), may hold values from -32 to 32
- v_query: float32 [2048, 2048], P('dp', 'tp'), may hold values from 245.76 to 3276.8
- v_key: float32 [2048, 512], P('dp', 'tp'), may hold values from 983.04 to 13107.2
- v_value: float32 [2048, 512], P('dp', 'tp'), may hold values from 6144 to 81920
- v_out: float32 [2048, 2048], P('tp', 'dp'), may hold values from 16.384 to 204.8
- v_gate: float32 [2048, 8192], P('dp', 'tp'), may hold values from 16.384 to 204.8
- v_up: float32 [2048, 8192], P('dp', 'tp'), may hold values from 24.576 to 294.912
- v_down: float32 [8192, 2048], P('tp', 'dp'), may hold values from 90.112 to 1228.8
- gain_attn: float32 [2048], replicated, may hold values from 0.5 to 1.5
- gain_ffn: float32 [2048], replicated, may hold values from 0.5 to 1.5
- m_gain_attn: float32 [2048], replicated, may hold values from -56 to 56
- m_gain_ffn: float32 [2048], replicated, may hold values from -56 to 56
- v_gain_attn: float32 [2048], replicated, may hold values from 409.6 to 6553.6
- v_gain_ffn: float32 [2048], replicated, may hold values from 245.76 to 3276.8
Outputs:
- out_value: bfloat16 [8192, 2048], P(('dp', 'tp'))
- in_grad: float32 [8192, 2048], P(('dp', 'tp'))
- grad_query: float32 [2048, 2048], P('dp', 'tp')
- grad_key: float32 [2048, 512], P('dp', 'tp')
- grad_value: float32 [2048, 512], P('dp', 'tp')
- grad_out: float32 [2048, 2048], P('tp', 'dp')
- grad_gate: float32 [2048, 8192], P('dp', 'tp')
- grad_up: float32 [2048, 8192], P('dp', 'tp')
- grad_down: float32 [8192, 2048], P('tp', 'dp')
- next_query: float32 [2048, 2048], P('dp', 'tp')
- next_key: float32 [2048, 512], P('dp', 'tp')
- next_value: float32 [2048, 512], P('dp', 'tp')
- next_out: float32 [2048, 2048], P('tp', 'dp')
- next_gate: float32 [2048, 8192], P('dp', 'tp')
- next_up: float32 [2048, 8192], P('dp', 'tp')
- next_down: float32 [8192, 2048], P('tp', 'dp')
- next_m_query: float32 [2048, 2048], P('dp', 'tp')
- next_m_key: float32 [2048, 512], P('dp', 'tp')
- next_m_value: float32 [2048, 512], P('dp', 'tp')
- next_m_out: float32 [2048, 2048], P('tp', 'dp')
- next_m_gate: float32 [2048, 8192], P('dp', 'tp')
- next_m_up: float32 [2048, 8192], P('dp', 'tp')
- next_m_down: float32 [8192, 2048], P('tp', 'dp')
- next_v_query: float32 [2048, 2048], P('dp', 'tp')
- next_v_key: float32 [2048, 512], P('dp', 'tp')
- next_v_value: float32 [2048, 512], P('dp', 'tp')
- next_v_out: float32 [2048, 2048], P('tp', 'dp')
- next_v_gate: float32 [2048, 8192], P('dp', 'tp')
- next_v_up: float32 [2048, 8192], P('dp', 'tp')
- next_v_down: float32 [8192, 2048], P('tp', 'dp')
- grad_gain_attn: float32 [2048], replicated
- grad_gain_ffn: float32 [2048], replicated
- next_gain_attn: float32 [2048], replicated
- next_gain_ffn: float32 [2048], replicated
- next_m_gain_attn: float32 [2048], replicated
- next_m_gain_ffn: float32 [2048], replicated
- next_v_gain_attn: float32 [2048], replicated
- next_v_gain_ffn: float32 [2048], replicated
Inputs may be any that keep to these rules, and one draw needn't show every extreme that they name: `segment_ids`: within each sequence of 512 consecutive tokens the ids start at 0 and rise by one at each document boundary; ids of different sequences are unrelated. Within a segment positions rise by one from token to token; every segment except the first of a sequence starts at 0.
All inputs are finite; a program needn't handle non-finite values.
Results may differ from a plain program's by a relative error of at most 0.019.
Values may be sent and summed in bfloat16 or wider, within the bound.
No kernel may reach another device: no remote copies, remote signals or barrier semaphores. Data moves between devices by JAX's collectives and lax.ppermute only.
A program may use at most 256 MiB of HBM per device.

v0:
```python
import jax
import jax.numpy as jnp
from jax import lax
from jax.sharding import PartitionSpec as P

HD = 64
LEN = 512
STEP = 5


NORM_EPS = 1e-05
ROPE_BASE = 500000.0
BETA_ONE = 0.9
BETA_TWO = 0.95
LEARN_RATE = 0.02
GAIN_RATE = 0.5
WEIGHT_DECAY = 0.1
ADAM_EPS = 1e-08


def rope_tables(positions):
    half_dim = HD // 2
    inverse_freq = ROPE_BASE ** (-2.0 * jnp.arange(half_dim, dtype=jnp.float32) / HD)
    angles = positions.astype(jnp.float32)[:, None] * inverse_freq[None, :]
    cos_half = jnp.cos(angles)
    sin_half = jnp.sin(angles)
    return (jnp.concatenate([cos_half, cos_half], 1), jnp.concatenate([sin_half, sin_half], 1))


def rotate_heads(values, cos_table, sin_table):
    half_dim = values.shape[-1] // 2
    turned = jnp.concatenate([-values[..., half_dim:], values[..., :half_dim]], -1)
    return values * cos_table[:, None, :] + turned * sin_table[:, None, :]


def unrotate_heads(values, cos_table, sin_table):
    half_dim = values.shape[-1] // 2
    weighted = values * sin_table[:, None, :]
    turned = jnp.concatenate([weighted[..., half_dim:], -weighted[..., :half_dim]], -1)
    return values * cos_table[:, None, :] + turned


def norm_rows(values, gain_vec):
    row_scale = lax.rsqrt(jnp.mean(values * values, axis=1, keepdims=True) + NORM_EPS)
    return (values * row_scale * gain_vec, row_scale)


def norm_back(row_grad, values, row_scale, gain_vec):
    scaled_grad = row_grad * gain_vec
    gain_part = jnp.sum(row_grad * values * row_scale, axis=0)
    back_grad = row_scale * scaled_grad - values * row_scale**3 * jnp.mean(
        scaled_grad * values, axis=1, keepdims=True
    )
    return (back_grad, gain_part)


def allowed_pairs(seg_row):
    row_index = jnp.arange(seg_row.shape[0])
    return (seg_row[:, None] == seg_row[None, :]) & (row_index[None, :] <= row_index[:, None])


def attend_forward(entries):
    queries, key_rows, value_rows, seg_row = entries
    scores = jnp.einsum(
        "qkgd,pkd->kgqp", queries, key_rows, preferred_element_type=jnp.float32
    ) * queries.shape[-1] ** (-0.5)
    masked = jnp.where(allowed_pairs(seg_row), scores, -1e30)
    top_score = jnp.max(masked, axis=-1, keepdims=True)
    weights = jnp.exp(masked - top_score)
    totals = jnp.sum(weights, axis=-1, keepdims=True)
    prob_rows = weights / totals
    context = jnp.einsum(
        "kgqp,pkd->qkgd",
        prob_rows.astype(jnp.bfloat16),
        value_rows,
        preferred_element_type=jnp.float32,
    )
    return (context, (top_score + jnp.log(totals))[..., 0])


def attend_backward(entries):
    queries, key_rows, value_rows, seg_row, log_sums, ctx_grad = entries
    head_scale = queries.shape[-1] ** (-0.5)
    scores = (
        jnp.einsum("qkgd,pkd->kgqp", queries, key_rows, preferred_element_type=jnp.float32)
        * head_scale
    )
    prob_rows = jnp.where(allowed_pairs(seg_row), jnp.exp(scores - log_sums[..., None]), 0.0)
    value_grad = jnp.einsum(
        "kgqp,qkgd->pkd",
        prob_rows.astype(jnp.bfloat16),
        ctx_grad,
        preferred_element_type=jnp.float32,
    )
    prob_grad = jnp.einsum(
        "qkgd,pkd->kgqp", ctx_grad, value_rows, preferred_element_type=jnp.float32
    )
    delta_rows = jnp.sum(prob_rows * prob_grad, axis=-1, keepdims=True)
    score_grad = (prob_rows * (prob_grad - delta_rows)).astype(jnp.bfloat16)
    query_grad = (
        jnp.einsum("kgqp,pkd->qkgd", score_grad, key_rows, preferred_element_type=jnp.float32)
        * head_scale
    )
    key_grad = (
        jnp.einsum("kgqp,qkgd->pkd", score_grad, queries, preferred_element_type=jnp.float32)
        * head_scale
    )
    return (query_grad, key_grad, value_grad)


def adamw_update(master, grad_sum, first_mom, second_mom, decay_rate, step_rate):
    next_first = BETA_ONE * first_mom + (1.0 - BETA_ONE) * grad_sum
    next_second = BETA_TWO * second_mom + (1.0 - BETA_TWO) * grad_sum * grad_sum
    first_hat = next_first / (1.0 - BETA_ONE**STEP)
    second_hat = next_second / (1.0 - BETA_TWO**STEP)
    next_master = master - step_rate * (
        first_hat / (jnp.sqrt(second_hat) + ADAM_EPS) + decay_rate * master
    )
    return (next_master, next_first, next_second)


def on_device(
    layer_input,
    out_grad,
    segment_ids,
    positions,
    w_query,
    w_key,
    w_value,
    w_out,
    w_gate,
    w_up,
    w_down,
    m_query,
    m_key,
    m_value,
    m_out,
    m_gate,
    m_up,
    m_down,
    v_query,
    v_key,
    v_value,
    v_out,
    v_gate,
    v_up,
    v_down,
    gain_attn,
    gain_ffn,
    m_gain_attn,
    m_gain_ffn,
    v_gain_attn,
    v_gain_ffn,
):
    query_w, key_w, value_w, out_w, gate_w, up_w, down_w = (
        lax.all_gather(w_query.astype(jnp.bfloat16), "dp", axis=0, tiled=True),
        lax.all_gather(w_key.astype(jnp.bfloat16), "dp", axis=0, tiled=True),
        lax.all_gather(w_value.astype(jnp.bfloat16), "dp", axis=0, tiled=True),
        lax.all_gather(w_out.astype(jnp.bfloat16), "dp", axis=1, tiled=True),
        lax.all_gather(w_gate.astype(jnp.bfloat16), "dp", axis=0, tiled=True),
        lax.all_gather(w_up.astype(jnp.bfloat16), "dp", axis=0, tiled=True),
        lax.all_gather(w_down.astype(jnp.bfloat16), "dp", axis=1, tiled=True),
    )
    local_heads = query_w.shape[1] // HD
    local_groups = key_w.shape[1] // HD
    per_group = local_heads // local_groups
    group_rows = segment_ids.shape[0]
    seq_count = group_rows // LEN
    cos_table, sin_table = rope_tables(positions)
    inputs_f = layer_input.astype(jnp.float32)
    normed, scale_one = norm_rows(inputs_f, gain_attn)
    gathered = lax.all_gather(normed.astype(jnp.bfloat16), "tp", axis=0, tiled=True)
    query_pre = jnp.dot(gathered, query_w, preferred_element_type=jnp.float32)
    query_rot = rotate_heads(
        query_pre.reshape(group_rows, local_heads, HD), cos_table, sin_table
    ).astype(jnp.bfloat16)
    key_pre = jnp.dot(gathered, key_w, preferred_element_type=jnp.float32)
    key_rot = rotate_heads(
        key_pre.reshape(group_rows, local_groups, HD), cos_table, sin_table
    ).astype(jnp.bfloat16)
    value_low = jnp.dot(gathered, value_w, preferred_element_type=jnp.float32).astype(jnp.bfloat16)
    seq_queries = query_rot.reshape(seq_count, LEN, local_groups, per_group, HD)
    seq_keys = key_rot.reshape(seq_count, LEN, local_groups, HD)
    seq_values = value_low.reshape(seq_count, LEN, local_groups, HD)
    seq_segments = segment_ids.reshape(seq_count, LEN)
    context, log_sums = lax.map(attend_forward, (seq_queries, seq_keys, seq_values, seq_segments))
    context_low = context.reshape(group_rows, local_heads * HD).astype(jnp.bfloat16)
    rows_here = context_low
    residual = inputs_f + lax.psum_scatter(
        jnp.dot(rows_here, out_w, preferred_element_type=jnp.float32),
        "tp",
        scatter_dimension=0,
        tiled=True,
    )
    normed_two, scale_two = norm_rows(residual, gain_ffn)
    gathered_two = lax.all_gather(normed_two.astype(jnp.bfloat16), "tp", axis=0, tiled=True)
    gate_pre = jnp.dot(gathered_two, gate_w, preferred_element_type=jnp.float32)
    lifted = jnp.dot(gathered_two, up_w, preferred_element_type=jnp.float32)
    sigmoid_gate = jax.nn.sigmoid(gate_pre)
    silu_gate = gate_pre * sigmoid_gate
    act_low = (silu_gate * lifted).astype(jnp.bfloat16)
    rows_here = act_low
    out_value = (
        residual
        + lax.psum_scatter(
            jnp.dot(rows_here, down_w, preferred_element_type=jnp.float32).astype(jnp.bfloat16),
            "tp",
            scatter_dimension=0,
            tiled=True,
        ).astype(jnp.float32)
    ).astype(jnp.bfloat16)
    grad_all = lax.all_gather(out_grad, "tp", axis=0, tiled=True)
    local_down = jnp.einsum("rf,rd->fd", act_low, grad_all, preferred_element_type=jnp.float32)
    act_grad = jnp.einsum("rd,fd->rf", grad_all, down_w, preferred_element_type=jnp.float32)
    gate_grad = (act_grad * lifted * sigmoid_gate * (1.0 + gate_pre * (1.0 - sigmoid_gate))).astype(
        jnp.bfloat16
    )
    lifted_grad = (act_grad * silu_gate).astype(jnp.bfloat16)
    local_gate = jnp.einsum(
        "rd,rf->df", gathered_two, gate_grad, preferred_element_type=jnp.float32
    )
    local_up = jnp.einsum(
        "rd,rf->df", gathered_two, lifted_grad, preferred_element_type=jnp.float32
    )
    grad_gate, grad_up, grad_down = (
        lax.psum_scatter(
            local_gate.astype(jnp.bfloat16), "dp", scatter_dimension=0, tiled=True
        ).astype(jnp.float32),
        lax.psum_scatter(
            local_up.astype(jnp.bfloat16), "dp", scatter_dimension=0, tiled=True
        ).astype(jnp.float32),
        lax.psum_scatter(
            local_down.astype(jnp.bfloat16), "dp", scatter_dimension=1, tiled=True
        ).astype(jnp.float32),
    )
    normed_two_grad = lax.psum_scatter(
        jnp.einsum("rf,df->rd", gate_grad, gate_w, preferred_element_type=jnp.float32)
        + jnp.einsum("rf,df->rd", lifted_grad, up_w, preferred_element_type=jnp.float32),
        "tp",
        scatter_dimension=0,
        tiled=True,
    )
    back_two, gain_ffn_part = norm_back(normed_two_grad, residual, scale_two, gain_ffn)
    residual_grad = out_grad.astype(jnp.float32) + back_two
    residual_all = lax.all_gather(residual_grad.astype(jnp.bfloat16), "tp", axis=0, tiled=True)
    local_out = jnp.einsum(
        "rh,rd->hd", context_low, residual_all, preferred_element_type=jnp.float32
    )
    context_grad = jnp.einsum(
        "rd,hd->rh", residual_all, out_w, preferred_element_type=jnp.float32
    ).astype(jnp.bfloat16)
    seq_ctx_grad = context_grad.reshape(seq_count, LEN, local_groups, per_group, HD)
    query_grad, key_grad, value_grad = lax.map(
        attend_backward, (seq_queries, seq_keys, seq_values, seq_segments, log_sums, seq_ctx_grad)
    )
    query_low = unrotate_heads(
        query_grad.reshape(group_rows, local_heads, HD), cos_table, sin_table
    )
    query_low = query_low.reshape(group_rows, local_heads * HD).astype(jnp.bfloat16)
    key_low = unrotate_heads(key_grad.reshape(group_rows, local_groups, HD), cos_table, sin_table)
    key_low = key_low.reshape(group_rows, local_groups * HD).astype(jnp.bfloat16)
    value_low_grad = value_grad.reshape(group_rows, local_groups * HD).astype(jnp.bfloat16)
    local_query = jnp.einsum("rd,rc->dc", gathered, query_low, preferred_element_type=jnp.float32)
    local_key = jnp.einsum("rd,rc->dc", gathered, key_low, preferred_element_type=jnp.float32)
    local_value = jnp.einsum(
        "rd,rc->dc", gathered, value_low_grad, preferred_element_type=jnp.float32
    )
    normed_grad = lax.psum_scatter(
        (
            jnp.einsum("rc,dc->rd", query_low, query_w, preferred_element_type=jnp.float32)
            + jnp.einsum("rc,dc->rd", key_low, key_w, preferred_element_type=jnp.float32)
            + jnp.einsum("rc,dc->rd", value_low_grad, value_w, preferred_element_type=jnp.float32)
        ).astype(jnp.bfloat16),
        "tp",
        scatter_dimension=0,
        tiled=True,
    ).astype(jnp.float32)
    back_one, gain_attn_part = norm_back(normed_grad, inputs_f, scale_one, gain_attn)
    in_grad = residual_grad + back_one
    grad_gain_attn, grad_gain_ffn = lax.psum((gain_attn_part, gain_ffn_part), ("dp", "tp"))
    grad_query, grad_key, grad_value, grad_out = (
        lax.psum_scatter(
            local_query.astype(jnp.bfloat16), "dp", scatter_dimension=0, tiled=True
        ).astype(jnp.float32),
        lax.psum_scatter(
            local_key.astype(jnp.bfloat16), "dp", scatter_dimension=0, tiled=True
        ).astype(jnp.float32),
        lax.psum_scatter(
            local_value.astype(jnp.bfloat16), "dp", scatter_dimension=0, tiled=True
        ).astype(jnp.float32),
        lax.psum_scatter(
            local_out.astype(jnp.bfloat16), "dp", scatter_dimension=1, tiled=True
        ).astype(jnp.float32),
    )
    next_query, next_m_query, next_v_query = adamw_update(
        w_query, grad_query, m_query, v_query, WEIGHT_DECAY, LEARN_RATE
    )
    next_key, next_m_key, next_v_key = adamw_update(
        w_key, grad_key, m_key, v_key, WEIGHT_DECAY, LEARN_RATE
    )
    next_value, next_m_value, next_v_value = adamw_update(
        w_value, grad_value, m_value, v_value, WEIGHT_DECAY, LEARN_RATE
    )
    next_out, next_m_out, next_v_out = adamw_update(
        w_out, grad_out, m_out, v_out, WEIGHT_DECAY, LEARN_RATE
    )
    next_gate, next_m_gate, next_v_gate = adamw_update(
        w_gate, grad_gate, m_gate, v_gate, WEIGHT_DECAY, LEARN_RATE
    )
    next_up, next_m_up, next_v_up = adamw_update(
        w_up, grad_up, m_up, v_up, WEIGHT_DECAY, LEARN_RATE
    )
    next_down, next_m_down, next_v_down = adamw_update(
        w_down, grad_down, m_down, v_down, WEIGHT_DECAY, LEARN_RATE
    )
    next_gain_attn, next_m_gain_attn, next_v_gain_attn = adamw_update(
        gain_attn, grad_gain_attn, m_gain_attn, v_gain_attn, 0.0, GAIN_RATE
    )
    next_gain_ffn, next_m_gain_ffn, next_v_gain_ffn = adamw_update(
        gain_ffn, grad_gain_ffn, m_gain_ffn, v_gain_ffn, 0.0, GAIN_RATE
    )
    return (
        out_value,
        in_grad,
        grad_query,
        grad_key,
        grad_value,
        grad_out,
        grad_gate,
        grad_up,
        grad_down,
        next_query,
        next_key,
        next_value,
        next_out,
        next_gate,
        next_up,
        next_down,
        next_m_query,
        next_m_key,
        next_m_value,
        next_m_out,
        next_m_gate,
        next_m_up,
        next_m_down,
        next_v_query,
        next_v_key,
        next_v_value,
        next_v_out,
        next_v_gate,
        next_v_up,
        next_v_down,
        grad_gain_attn,
        grad_gain_ffn,
        next_gain_attn,
        next_gain_ffn,
        next_m_gain_attn,
        next_m_gain_ffn,
        next_v_gain_attn,
        next_v_gain_ffn,
    )


def solution(mesh):
    in_specs = (
        P(("dp", "tp"), None),
        P(("dp", "tp"), None),
        P("dp"),
        P("dp"),
        P("dp", "tp"),
        P("dp", "tp"),
        P("dp", "tp"),
        P("tp", "dp"),
        P("dp", "tp"),
        P("dp", "tp"),
        P("tp", "dp"),
        P("dp", "tp"),
        P("dp", "tp"),
        P("dp", "tp"),
        P("tp", "dp"),
        P("dp", "tp"),
        P("dp", "tp"),
        P("tp", "dp"),
        P("dp", "tp"),
        P("dp", "tp"),
        P("dp", "tp"),
        P("tp", "dp"),
        P("dp", "tp"),
        P("dp", "tp"),
        P("tp", "dp"),
        P(),
        P(),
        P(),
        P(),
        P(),
        P(),
    )
    out_specs = (
        P(("dp", "tp"), None),
        P(("dp", "tp"), None),
        P("dp", "tp"),
        P("dp", "tp"),
        P("dp", "tp"),
        P("tp", "dp"),
        P("dp", "tp"),
        P("dp", "tp"),
        P("tp", "dp"),
        P("dp", "tp"),
        P("dp", "tp"),
        P("dp", "tp"),
        P("tp", "dp"),
        P("dp", "tp"),
        P("dp", "tp"),
        P("tp", "dp"),
        P("dp", "tp"),
        P("dp", "tp"),
        P("dp", "tp"),
        P("tp", "dp"),
        P("dp", "tp"),
        P("dp", "tp"),
        P("tp", "dp"),
        P("dp", "tp"),
        P("dp", "tp"),
        P("dp", "tp"),
        P("tp", "dp"),
        P("dp", "tp"),
        P("dp", "tp"),
        P("tp", "dp"),
        P(),
        P(),
        P(),
        P(),
        P(),
        P(),
        P(),
        P(),
    )
    return jax.shard_map(
        on_device, mesh=mesh, in_specs=in_specs, out_specs=out_specs, check_vma=False
    )
```

profile of v0, /device:TPU:9, one launch (start us, length us, event | category | flops | bytes accessed | tf_op | source)
XLA Modules:
  0.0 1720.0 jit_solution(5263861472758188589)
XLA Ops:
  14.8 26.4 %all_gather.35 = bf16[2048,128]{1,0:T(8,128)(2,1)} all-gather(bf16[256,128]{1,0:T(8,128)(2,1)S(1)} %convert_element_type.150), channel_id=1, replica_groups=mesh['dp'=8,'tp'=4] {'dp'}, dimensions={0}, use_global_device_ids=true | all-gather | bytes 589824 | tf_op jit(solution)/shard_map/all_gather | solution.py:157
  41.3 28.4 %all_gather.34 = bf16[2048,128]{1,0:T(8,128)(2,1)} all-gather(bf16[256,128]{1,0:T(8,128)(2,1)S(1)} %convert_element_type.148), channel_id=1, replica_groups=mesh['dp'=8,'tp'=4] {'dp'}, dimensions={0}, use_global_device_ids=true | all-gather | bytes 589824 | tf_op jit(solution)/shard_map/all_gather | solution.py:158
  72.8 31.0 %all-gather.10.cloned.1.call-done = bf16[1024,2048]{1,0:T(8,128)(2,1)} async-done(((bf16[256,2048]{1,0:T(8,128)(2,1)}), bf16[1024,2048]{1,0:T(8,128)(2,1)}) %all-gather.10.cloned.1.call-update) | async-done | bytes 4194320 | tf_op jit(solution)/shard_map/all_gather | solution.py:172
  103.8 5.2 fusion.98
  109.0 2.8 reshape.247
  113.3 3.3 concatenate.43
  116.5 3.1 concatenate.44
  119.6 2.9 fusion.74
  131.0 3.5 convolution_convert_fusion.9
  135.2 13.5 while.26
  138.9 3.2 fusion.173
  145.6 3.2 fusion.173
  148.8 2.9 copy.86
  154.9 7.6 fusion.99
  165.3 69.5 %reduce-scatter.12.cloned.1.call-done = f32[256,2048]{1,0:T(8,128)} async-done(((f32[1024,2048]{1,0:T(8,128)}), f32[256,2048]{1,0:T(8,128)}) %reduce-scatter.12.cloned.1.call-update) | async-done | bytes 2097168 | tf_op jit(solution)/shard_map/reduce_scatter | solution.py:189
  238.1 2.7 convert_element_type.160
  241.6 2.7 convert_element_type.162
  244.4 116.0 %all-gather.18.cloned.1.call-done = bf16[2048,2048]{1,0:T(8,128)(2,1)} async-done(((bf16[256,2048]{1,0:T(8,128)(2,1)}), bf16[2048,2048]{1,0:T(8,128)(2,1)}) %all-gather.18.cloned.1.call-update) | async-done | bytes 8388624 | tf_op jit(solution)/shard_map/all_gather | solution.py:160
  360.3 37.4 %all-gather.16.cloned.1.call-done = bf16[1024,2048]{1,0:T(8,128)(2,1)} async-done(((bf16[256,2048]{1,0:T(8,128)(2,1)}), bf16[1024,2048]{1,0:T(8,128)(2,1)}) %all-gather.16.cloned.1.call-update) | async-done | bytes 4194320 | tf_op jit(solution)/shard_map/all_gather | solution.py:196
  397.8 14.9 fusion.100
  412.7 110.3 %all-gather.20.cloned.1.call-done = bf16[2048,2048]{1,0:T(8,128)(2,1)} async-done(((bf16[256,2048]{1,0:T(8,128)(2,1)}), bf16[2048,2048]{1,0:T(8,128)(2,1)}) %all-gather.20.cloned.1.call-update) | async-done | bytes 8388624 | tf_op jit(solution)/shard_map/all_gather | solution.py:161
  523.0 14.6 fusion.101
  537.6 22.4 %all-gather.24.cloned.1.call-done = bf16[1024,2048]{1,0:T(8,128)(2,1)} async-done(((bf16[256,2048]{1,0:T(8,128)(2,1)}), bf16[1024,2048]{1,0:T(8,128)(2,1)}) %all-gather.24.cloned.1.call-update) | async-done | bytes 4194320 | tf_op jit(solution)/shard_map/all_gather | solution.py:212
  560.0 125.6 %all-gather.22.cloned.1.call-done = bf16[2048,2048]{1,0:T(8,128)(2,1)} async-done(((bf16[2048,256]{1,0:T(8,128)(2,1)}), bf16[2048,2048]{1,0:T(8,128)(2,1)}) %all-gather.22.cloned.1.call-update) | async-done | bytes 8388624 | tf_op jit(solution)/shard_map/all_gather | solution.py:162
  685.6 21.8 %multiply_convert_fusion = (bf16[1024,2048]{1,0:T(8,128)(2,1)}, bf16[1024,2048]{1,0:T(8,128)(2,1)}, bf16[1024,2048]{1,0:T(8,128)(2,1)}) fusion(f32[1024,2048]{1,0:T(8,128)} %fusion.100, f32[1024,2048]{1,0:T(8,128)} %fusion.101, bf16[1024,2048]{1,0:T(8,128)(2,1)} %all-gather.24.cloned.1.call-done, bf16[2048,2048]{1,0:T(8,128)(2,1)} %all-gather.22.cloned.1.call-done), kind=kOutput, calls=%fused_computation.69 | convolution fusion | flops 8621391872 | bytes 41943040 | tf_op jit(solution)/shard_map/rd,fd->rf/dot_general | solution.py:214
  707.4 14.9 fusion.102
  722.3 12.9 convolution_add_fusion
  735.3 13.8 convolution_convert_fusion.3
  749.3 58.4 %reduce-scatter.16.cloned.1.call-done = f32[256,2048]{1,0:T(8,128)} async-done(((f32[1024,2048]{1,0:T(8,128)}), f32[256,2048]{1,0:T(8,128)}) %reduce-scatter.16.cloned.1.call-update) | async-done | bytes 2097168 | tf_op jit(solution)/shard_map/reduce_scatter | solution.py:236
  807.6 2.7 multiply_reduce_fusion
  810.4 44.3 %reduce-scatter.14.cloned.1.call-done = bf16[256,2048]{1,0:T(8,128)(2,1)} async-done(((bf16[1024,2048]{1,0:T(8,128)(2,1)}), bf16[256,2048]{1,0:T(8,128)(2,1)}) %reduce-scatter.14.cloned.1.call-update) | async-done | bytes 1048592 | tf_op jit(solution)/shard_map/reduce_scatter | solution.py:205
  854.7 4.6 fusion.94
  859.4 14.3 convolution_convert_fusion.1
  873.8 14.1 convolution_convert_fusion.2
  887.9 14.5 convolution_convert_fusion
  903.7 5.8 convolution_convert_fusion.8
  911.7 3.0 copy.91
  914.8 86.5 %while.27 = (s32[]{:T(128)}, f32[2,512,2,4,64]{1,0,4,3,2:T(2,128)}, f32[2,512,2,64]{1,0,3,2:T(2,128)}, bf16[2,512,2,64]{1,3,2,0:T(8,128)(2,1)}, bf16[2,512,2,64]...) while((s32[]{:T(128)}, f32[2,512,2,4,64]{1,0,4,3,2:T(2,128)}, ...), condition=%wide.region_12.13_spmd, body=%wide.region_10.12_spmd.sunk | while | flops 1374744576 | bytes 136308048 | solution.py:253
  916.4 2.8 fusion.184
  919.4 2.6 fusion.185
  925.0 19.7 %dynamic_update_slice.29 = f32[2,512,2,4,64]{1,0,4,3,2:T(2,128)} dynamic-update-slice(f32[2,512,2,4,64]{1,0,4,3,2:T(2,128)} %get-tuple-element.422, f32[1,512,2,4,64]{1,0,4,3,2:T(1,128)S(1)} %copy.127, s32[]{:T(128)} %get-tuple-element.421, s32[]{:T(128)} %constant.51.clone.1..sunk, s32[]{:T(128)} %constant.51.clone.1..sunk, s32[]{:T(128)} %constant.51.clone.1..sunk, s32[]{:T(128)} %constant.51.clone.1..sunk) | dynamic-update-slice | bytes 2097156 | tf_op jit(solution)/shard_map/while/body/jit(dynamic_update_index_in_dim)/dynamic_update_slice | solution.py:186
  944.7 3.7 fusion.187
  951.9 6.1 fusion.188
  959.5 2.8 fusion.184
  968.2 19.6 %dynamic_update_slice.29 = f32[2,512,2,4,64]{1,0,4,3,2:T(2,128)} dynamic-update-slice(f32[2,512,2,4,64]{1,0,4,3,2:T(2,128)} %get-tuple-element.422, f32[1,512,2,4,64]{1,0,4,3,2:T(1,128)S(1)} %copy.127, s32[]{:T(128)} %get-tuple-element.421, s32[]{:T(128)} %constant.51.clone.1..sunk, s32[]{:T(128)} %constant.51.clone.1..sunk, s32[]{:T(128)} %constant.51.clone.1..sunk, s32[]{:T(128)} %constant.51.clone.1..sunk) | dynamic-update-slice | bytes 2097156 | tf_op jit(solution)/shard_map/while/body/jit(dynamic_update_index_in_dim)/dynamic_update_slice | solution.py:186
  987.8 3.6 fusion.187
  995.0 6.2 fusion.188
  1008.4 2.8 reshape.251
  1021.8 3.8 convolution_convert_fusion.5
  1026.9 5.9 convolution_convert_fusion.4
  1037.8 3.4 add_convert_fusion
  1041.2 4.4 reduce-scatter.30.cloned.1.call-done
  1045.6 6.5 multiply_subtract_fusion.1
  1052.1 145.0 %reduce-scatter.28.cloned.1.call-done = bf16[256,2048]{1,0:T(8,128)(2,1)} async-done(((bf16[2048,2048]{1,0:T(8,128)(2,1)}), bf16[256,2048]{1,0:T(8,128)(2,1)}) %reduce-scatter.28.cloned.1.call-update) | async-done | bytes 1048592 | tf_op jit(solution)/shard_map/reduce_scatter | solution.py:226
  1197.1 7.1 multiply_subtract_fusion.2
  1204.3 145.2 %reduce-scatter.32.cloned.1.call-done = bf16[2048,256]{1,0:T(8,128)(2,1)} async-done(((bf16[2048,2048]{1,0:T(8,128)(2,1)}), bf16[2048,256]{1,0:T(8,128)(2,1)}) %reduce-scatter.32.cloned.1.call-update) | async-done | bytes 1048592 | tf_op jit(solution)/shard_map/reduce_scatter | solution.py:232
  1349.5 6.3 multiply_subtract_fusion
  1355.7 57.9 %reduce-scatter.22.cloned.1.call-done = bf16[256,128]{1,0:T(8,128)(2,1)} async-done(((bf16[2048,128]{1,0:T(8,128)(2,1)}), bf16[256,128]{1,0:T(8,128)(2,1)}) %reduce-scatter.22.cloned.1.call-update) | async-done | bytes 65552 | tf_op jit(solution)/shard_map/reduce_scatter | solution.py:285
  1415.3 63.4 %reduce-scatter.24.cloned.1.call-done = bf16[256,128]{1,0:T(8,128)(2,1)} async-done(((bf16[2048,128]{1,0:T(8,128)(2,1)}), bf16[256,128]{1,0:T(8,128)(2,1)}) %reduce-scatter.24.cloned.1.call-update) | async-done | bytes 65552 | tf_op jit(solution)/shard_map/reduce_scatter | solution.py:288
  1480.4 68.3 %reduce-scatter.20.cloned.1.call-done = bf16[256,512]{1,0:T(8,128)(2,1)} async-done(((bf16[2048,512]{1,0:T(8,128)(2,1)}), bf16[256,512]{1,0:T(8,128)(2,1)}) %reduce-scatter.20.cloned.1.call-update) | async-done | bytes 262160 | tf_op jit(solution)/shard_map/reduce_scatter | solution.py:282
  1551.3 68.5 %reduce-scatter.26.cloned.1.call-done = bf16[512,256]{1,0:T(8,128)(2,1)} async-done(((bf16[512,2048]{1,0:T(8,128)(2,1)}), bf16[512,256]{1,0:T(8,128)(2,1)}) %reduce-scatter.26.cloned.1.call-update) | async-done | bytes 262160 | tf_op jit(solution)/shard_map/reduce_scatter | solution.py:291
  1622.1 45.5 %reduce-scatter.18.cloned.1.call-done = bf16[256,2048]{1,0:T(8,128)(2,1)} async-done(((bf16[1024,2048]{1,0:T(8,128)(2,1)}), bf16[256,2048]{1,0:T(8,128)(2,1)}) %reduce-scatter.18.cloned.1.call-update) | async-done | bytes 1048592 | tf_op jit(solution)/shard_map/reduce_scatter | solution.py:268
  1669.5 38.7 %all-reduce = (f32[2048]{0:T(1024)S(1)}, f32[2048]{0:T(1024)S(1)}) all-reduce(f32[2048]{0:T(1024)S(1)} %get-tuple-element.171, f32[2048]{0:T(1024)S(1)} %copy-done.58), channel_id=1, replica_groups=mesh['dp'=8,'tp'=4] {'dp','tp'}, use_global_device_ids=true, to_apply=%region_23.24 | all-reduce | flops 4096 | bytes 32768 | tf_op jit(solution)/shard_map/psum | solution.py:280
  1709.5 3.1 fusion.62
  (296 shorter events, 95.8 us)
Async XLA Ops:
  7.2 4.7 copy-start.4
  7.2 4.7 copy-start.48
  7.2 65.5 %all-gather.12.cloned.1.call-start = ((), (), s32[]{:S(2)}) async-start(), calls=%async_computation.12 | async-start | bytes 2359296 | tf_op jit(solution)/shard_map/all_gather | solution.py:156
  9.2 4.2 copy-start.29
  9.2 94.6 %all-gather.10.cloned.1.call-start = ((), (), s32[]{:S(2)}) async-start(), calls=%async_computation.11 | async-start | bytes 5242880 | tf_op jit(solution)/shard_map/all_gather | solution.py:172
  12.0 29.3 %copy-start.41 = (f32[256,128]{1,0:T(8,128)S(1)}, f32[256,128]{1,0:T(8,128)}, u32[]{:S(2)}) copy-start(f32[256,128]{1,0:T(8,128)} %param.41) | copy-start | bytes 393220
  13.2 56.4 %copy-start.69 = (s32[1024]{0:T(1024)S(1)}, s32[1024]{0:T(1024)}, u32[]{:S(2)}) copy-start(s32[1024]{0:T(1024)} %param.37) | copy-start | bytes 12292
  13.3 141.6 %all-gather.14.cloned.1.call-start = ((), (), s32[]{:S(2)}) async-start(), calls=%async_computation.13 | async-start | bytes 2359296 | tf_op jit(solution)/shard_map/all_gather | solution.py:159
  14.1 220.7 %reduce-scatter.12.cloned.1.call-start = ((), (), s32[]{:S(2)}) async-start(), calls=%async_computation.14 | async-start | bytes 10485760 | tf_op jit(solution)/shard_map/reduce_scatter | solution.py:189
  14.2 58.6 %copy-start.70 = (f32[32]{0:T(128)}, f32[32]{0:T(128)S(1)}, u32[]{:S(2)}) copy-start(f32[32]{0:T(128)S(1)} %multiply_power_fusion) | copy-start | bytes 388
  113.3 6.4 copy-start.17
  125.1 4.4 copy-start.27
  148.8 4.1 copy-start.6
  148.8 4.1 copy-start.25
  148.8 4.1 copy-start.44
  162.5 197.8 %all-gather.18.cloned.1.call-start = ((), (), s32[]{:S(2)}) async-start(), calls=%async_computation.16 | async-start | bytes 9437184 | tf_op jit(solution)/shard_map/all_gather | solution.py:160
  165.2 71.6 %copy-start.54 = (f32[2048]{0:T(1024)S(1)}, f32[2048]{0:T(1024)}, u32[]{:S(2)}) copy-start(f32[2048]{0:T(1024)} %param.61) | copy-start | bytes 24580
  165.2 232.5 %all-gather.16.cloned.1.call-start = ((), (), s32[]{:S(2)}) async-start(), calls=%async_computation.15 | async-start | bytes 5242880 | tf_op jit(solution)/shard_map/all_gather | solution.py:196
  238.0 284.9 %all-gather.20.cloned.1.call-start = ((), (), s32[]{:S(2)}) async-start(), calls=%async_computation.17 | async-start | bytes 9437184 | tf_op jit(solution)/shard_map/all_gather | solution.py:161
  240.8 319.2 %all-gather.24.cloned.1.call-start = ((), (), s32[]{:S(2)}) async-start(), calls=%async_computation.20 | async-start | bytes 5242880 | tf_op jit(solution)/shard_map/all_gather | solution.py:212
  241.6 444.0 %all-gather.22.cloned.1.call-start = ((), (), s32[]{:S(2)}) async-start(), calls=%async_computation.18 | async-start | bytes 9437184 | tf_op jit(solution)/shard_map/all_gather | solution.py:162
  244.3 563.3 %reduce-scatter.16.cloned.1.call-start = ((), (), s32[]{:S(2)}) async-start(), calls=%async_computation.21 | async-start | bytes 10485760 | tf_op jit(solution)/shard_map/reduce_scatter | solution.py:236
  707.4 14.9 copy-start.72
  707.4 14.9 copy-start.74
  735.3 119.4 %reduce-scatter.14.cloned.1.call-start = ((), (), s32[]{:S(2)}) async-start(), calls=%async_computation.19 | async-start | bytes 5242880 | tf_op jit(solution)/shard_map/reduce_scatter | solution.py:205
  749.2 105.5 %copy-start.24 = (bf16[256,2048]{1,0:T(8,128)(2,1)S(1)}, bf16[256,2048]{1,0:T(8,128)(2,1)}, u32[]{:S(2)}) copy-start(bf16[256,2048]{1,0:T(8,128)(2,1)} %param.36) | copy-start | bytes 3145732
  749.2 154.5 %all-gather.26.cloned.1.call-start = ((), (), s32[]{:S(2)}) async-start(), calls=%async_computation.22 | async-start | bytes 5242880 | tf_op jit(solution)/shard_map/all_gather | solution.py:245
  859.4 186.2 %reduce-scatter.30.cloned.1.call-start = ((), (), s32[]{:S(2)}) async-start(), calls=%async_computation.29 | async-start | bytes 9437184 | tf_op jit(solution)/shard_map/reduce_scatter | solution.py:229
  873.7 323.4 %reduce-scatter.28.cloned.1.call-start = ((), (), s32[]{:S(2)}) async-start(), calls=%async_computation.28 | async-start | bytes 9437184 | tf_op jit(solution)/shard_map/reduce_scatter | solution.py:226
  887.8 461.6 %reduce-scatter.32.cloned.1.call-start = ((), (), s32[]{:S(2)}) async-start(), calls=%async_computation.30 | async-start | bytes 9437184 | tf_op jit(solution)/shard_map/reduce_scatter | solution.py:232
  902.4 511.3 %reduce-scatter.22.cloned.1.call-start = ((), (), s32[]{:S(2)}) async-start(), calls=%async_computation.25 | async-start | bytes 589824 | tf_op jit(solution)/shard_map/reduce_scatter | solution.py:285
  951.9 6.1 copy-start.9
  995.0 6.2 copy-start.9
  1008.3 470.5 %reduce-scatter.24.cloned.1.call-start = ((), (), s32[]{:S(2)}) async-start(), calls=%async_computation.26 | async-start | bytes 589824 | tf_op jit(solution)/shard_map/reduce_scatter | solution.py:288
  1017.8 531.0 %reduce-scatter.20.cloned.1.call-start = ((), (), s32[]{:S(2)}) async-start(), calls=%async_computation.24 | async-start | bytes 2359296 | tf_op jit(solution)/shard_map/reduce_scatter | solution.py:282
  1025.7 594.1 %reduce-scatter.26.cloned.1.call-start = ((), (), s32[]{:S(2)}) async-start(), calls=%async_computation.27 | async-start | bytes 2359296 | tf_op jit(solution)/shard_map/reduce_scatter | solution.py:291
  1032.8 634.9 %reduce-scatter.18.cloned.1.call-start = ((), (), s32[]{:S(2)}) async-start(), calls=%async_computation.23 | async-start | bytes 5242880 | tf_op jit(solution)/shard_map/reduce_scatter | solution.py:268
  1041.2 4.4 copy-start.10
  1052.1 297.3 %copy-start.12 = (f32[2048,256]{1,0:T(8,128)S(1)}, f32[2048,256]{1,0:T(8,128)}, u32[]{:S(2)}) copy-start(f32[2048,256]{1,0:T(8,128)} %param.45) | copy-start | bytes 6291460
  1204.3 209.4 %copy-start.40 = (f32[256,128]{1,0:T(8,128)S(1)}, f32[256,128]{1,0:T(8,128)}, u32[]{:S(2)}) copy-start(f32[256,128]{1,0:T(8,128)} %param.40) | copy-start | bytes 393220
  1204.3 209.4 %copy-start.50 = (f32[256,128]{1,0:T(8,128)S(1)}, f32[256,128]{1,0:T(8,128)}, u32[]{:S(2)}) copy-start(f32[256,128]{1,0:T(8,128)} %param.47) | copy-start | bytes 393220
  1204.3 209.4 %copy-start.51 = (f32[256,128]{1,0:T(8,128)S(1)}, f32[256,128]{1,0:T(8,128)}, u32[]{:S(2)}) copy-start(f32[256,128]{1,0:T(8,128)} %param.54) | copy-start | bytes 393220
  1204.3 274.5 %copy-start.42 = (f32[256,128]{1,0:T(8,128)S(1)}, f32[256,128]{1,0:T(8,128)}, u32[]{:S(2)}) copy-start(f32[256,128]{1,0:T(8,128)} %param.41) | copy-start | bytes 393220
  1204.3 274.5 %copy-start.52 = (f32[256,128]{1,0:T(8,128)S(1)}, f32[256,128]{1,0:T(8,128)}, u32[]{:S(2)}) copy-start(f32[256,128]{1,0:T(8,128)} %param.48) | copy-start | bytes 393220
  1204.3 274.5 %copy-start.53 = (f32[256,128]{1,0:T(8,128)S(1)}, f32[256,128]{1,0:T(8,128)}, u32[]{:S(2)}) copy-start(f32[256,128]{1,0:T(8,128)} %param.55) | copy-start | bytes 393220
  1355.7 193.0 %copy-start.28 = (f32[256,512]{1,0:T(8,128)S(1)}, f32[256,512]{1,0:T(8,128)}, u32[]{:S(2)}) copy-start(f32[256,512]{1,0:T(8,128)} %param.39) | copy-start | bytes 1572868
  1355.7 193.0 %copy-start.35 = (f32[256,512]{1,0:T(8,128)S(1)}, f32[256,512]{1,0:T(8,128)}, u32[]{:S(2)}) copy-start(f32[256,512]{1,0:T(8,128)} %param.46) | copy-start | bytes 1572868
  1355.7 193.0 %copy-start.36 = (f32[256,512]{1,0:T(8,128)S(1)}, f32[256,512]{1,0:T(8,128)}, u32[]{:S(2)}) copy-start(f32[256,512]{1,0:T(8,128)} %param.53) | copy-start | bytes 1572868
  1480.4 139.3 %copy-start.30 = (f32[512,256]{1,0:T(8,128)S(1)}, f32[512,256]{1,0:T(8,128)}, u32[]{:S(2)}) copy-start(f32[512,256]{1,0:T(8,128)} %param.42) | copy-start | bytes 1572868
  1480.4 139.3 %copy-start.37 = (f32[512,256]{1,0:T(8,128)S(1)}, f32[512,256]{1,0:T(8,128)}, u32[]{:S(2)}) copy-start(f32[512,256]{1,0:T(8,128)} %param.49) | copy-start | bytes 1572868
  1480.4 139.3 %copy-start.38 = (f32[512,256]{1,0:T(8,128)S(1)}, f32[512,256]{1,0:T(8,128)}, u32[]{:S(2)}) copy-start(f32[512,256]{1,0:T(8,128)} %param.56) | copy-start | bytes 1572868
  1551.2 116.5 %copy-start.5 = (bf16[256,2048]{1,0:T(8,128)(2,1)S(1)}, bf16[256,2048]{1,0:T(8,128)(2,1)}, u32[]{:S(2)}) copy-start(bf16[256,2048]{1,0:T(8,128)(2,1)} %param.35) | copy-start | bytes 3145732
  1551.2 116.5 %copy-start.49 = (f32[2048]{0:T(1024)S(1)}, f32[2048]{0:T(1024)}, u32[]{:S(2)}) copy-start(f32[2048]{0:T(1024)} %param.60) | copy-start | bytes 24580
  1551.2 116.5 %copy-start.60 = (f32[256]{0:T(256)S(1)}, f32[256]{0:T(256)}, u32[]{:S(2)}) copy-start(f32[256]{0:T(256)} %copy-done.59) | copy-start | bytes 3076
  1551.2 118.3 %copy-start.58 = (f32[2048]{0:T(1024)S(1)}, f32[2048]{0:T(1024)}, u32[]{:S(2)}) copy-start(f32[2048]{0:T(1024)} %get-tuple-element.169) | copy-start | bytes 24580
  1551.2 157.0 %copy-start.55 = (f32[2048]{0:T(1024)S(1)}, f32[2048]{0:T(1024)}, u32[]{:S(2)}) copy-start(f32[2048]{0:T(1024)} %param.61) | copy-start | bytes 24580
  1551.2 157.0 %copy-start.61 = (f32[2048]{0:T(1024)S(1)}, f32[2048]{0:T(1024)}, u32[]{:S(2)}) copy-start(f32[2048]{0:T(1024)} %param.63) | copy-start | bytes 24580
  1551.2 157.0 %copy-start.62 = (f32[2048]{0:T(1024)S(1)}, f32[2048]{0:T(1024)}, u32[]{:S(2)}) copy-start(f32[2048]{0:T(1024)} %param.65) | copy-start | bytes 24580
  1551.2 157.7 %copy-start.63 = (f32[2048]{0:T(1024)S(1)}, f32[2048]{0:T(1024)}, u32[]{:S(2)}) copy-start(f32[2048]{0:T(1024)} %param.62) | copy-start | bytes 24580
  1551.2 157.7 %copy-start.64 = (f32[2048]{0:T(1024)S(1)}, f32[2048]{0:T(1024)}, u32[]{:S(2)}) copy-start(f32[2048]{0:T(1024)} %param.64) | copy-start | bytes 24580
  1622.1 87.4 %copy-start.13 = (f32[256,2048]{1,0:T(8,128)S(1)}, f32[256,2048]{1,0:T(8,128)}, u32[]{:S(2)}) copy-start(f32[256,2048]{1,0:T(8,128)} %get-tuple-element.244) | copy-start | bytes 6291460
  1622.1 87.4 %copy-start.67 = (f32[256]{0:T(256)S(1)}, f32[256]{0:T(256)}, u32[]{:S(2)}) copy-start(f32[256]{0:T(256)} %get-tuple-element.267) | copy-start | bytes 3076
  1708.2 4.5 copy-start.65
  1708.2 4.5 copy-start.66
  (37 other events, 80.8 us)
Sparse Core Ops, SparseCore 0:
  10.8 56.1 all-gather.11
  69.1 34.6 all-gather.9
  106.4 48.4 all-gather.13
  162.6 72.1 reduce-scatter.11
  237.6 122.6 all-gather.17
  362.4 35.3 all-gather.15
  400.7 122.2 all-gather.19
  524.6 35.3 all-gather.23
  562.8 122.7 all-gather.21
  735.4 72.1 reduce-scatter.15
  810.2 44.4 reduce-scatter.13
  859.5 34.9 all-gather.25
  898.5 147.0 reduce-scatter.29
  1049.1 147.9 reduce-scatter.27
  1201.0 148.3 reduce-scatter.31
  1353.2 60.3 reduce-scatter.21
  1417.8 60.8 reduce-scatter.23
  1482.1 66.5 reduce-scatter.19
  1552.3 67.4 reduce-scatter.25
  1622.1 45.4 reduce-scatter.17
where the time goes:
time: 1730 us; the launch traced here: 1720 us
  waiting for transfers between devices  1220 us (71%)
  matrix products  219 us (13%)
  local copies, waits for them, and re-layouts  95.1 us (5%)
  blocking collectives  93.5 us (5%)
  other arithmetic  78.6 us (5%)
    reduce_scatter x1, waiting for transfers between devices, on_device(): lax.psum_scatter(local_down.astype(jnp.bfloat16), 'dp', scatter_dimension...  145 us
    reduce_scatter x1, waiting for transfers between devices, on_device(): lax.psum_scatter(local_gate.astype(jnp.bfloat16), 'dp', scatter_dimension...  145 us
    all_gather x1, waiting for transfers between devices, on_device(): lax.all_gather(w_down.astype(jnp.bfloat16), 'dp', axis=1, tiled=True)  126 us
    all_gather x1, waiting for transfers between devices, on_device(): lax.all_gather(w_gate.astype(jnp.bfloat16), 'dp', axis=0, tiled=True)  116 us
    all_gather x1, waiting for transfers between devices, on_device(): lax.all_gather(w_up.astype(jnp.bfloat16), 'dp', axis=0, tiled=True)  110 us
    reduce_scatter x1, waiting for transfers between devices, on_device(): lax.psum_scatter(jnp.dot(rows_here, out_w, preferred_element_type=jnp.flo...  69.5 us
    reduce_scatter x1, waiting for transfers between devices, on_device(): lax.psum_scatter(local_out.astype(jnp.bfloat16), 'dp', scatter_dimension=...  68.5 us
    reduce_scatter x1, waiting for transfers between devices, on_device(): lax.psum_scatter(local_query.astype(jnp.bfloat16), 'dp', scatter_dimensio...  68.3 us
  transfers between devices with their start and end apart: 20, of which 18 were waited for; matrix products, arithmetic and copies ran while one was open for 18% of the time, Pallas kernels for 0%

commit v1 on v0

v1 whole, which is shorter than its diff:
```python
import functools

import jax
import jax.numpy as jnp
from jax import lax
from jax.experimental import pallas as pl
from jax.experimental.pallas import tpu as pltpu
from jax.sharding import Mesh
from jax.sharding import PartitionSpec as P

HD = 64
LEN = 512
STEP = 5
CHUNKS = 2

NORM_EPS = 1e-05
ROPE_BASE = 500000.0
BETA_ONE = 0.9
BETA_TWO = 0.95
LEARN_RATE = 0.02
GAIN_RATE = 0.5
WEIGHT_DECAY = 0.1
ADAM_EPS = 1e-08

LOW = jnp.bfloat16
F32 = jnp.float32
MIB = 1024 * 1024

NEAR = [(0, 1), (1, 0), (2, 3), (3, 2)]
MIDDLE = [(1, 2), (2, 1)]
OUTWARD = [(1, 0), (2, 3)]
INWARD = [(0, 1), (3, 2)]
PAIR = [(0, 1), (1, 0)]


def dot(lhs, rhs, lhs_dim, rhs_dim):
    return lax.dot_general(
        lhs, rhs, (((lhs_dim,), (rhs_dim,)), ((), ())), preferred_element_type=F32
    )


def cat(parts, axis):
    return jnp.concatenate(parts, axis)


def line_gather(own):
    near = lax.ppermute(own, "do", NEAR)
    across = lax.ppermute(own, "do", MIDDLE)
    across_near = lax.ppermute(near, "do", MIDDLE)
    out = lax.ppermute(across, "do", OUTWARD)
    out_near = lax.ppermute(across_near, "do", OUTWARD)
    place = lax.axis_index("do")
    inner = (place == 1) | (place == 2)
    return [
        own,
        near,
        jnp.where(inner, across_near, out),
        jnp.where(inner, across, out_near),
    ]


def line_reduce(parts):
    def add(part, *arrived):
        total = part.astype(F32)
        for piece in arrived:
            total = total + piece.astype(F32)
        return total

    far = lax.ppermute(parts[3], "do", INWARD)
    second = add(parts[2], far).astype(LOW)
    crossed = lax.ppermute(second, "do", MIDDLE)
    inward = lax.ppermute(second, "do", INWARD)
    third = add(parts[3], inward).astype(LOW)
    first = add(parts[1], crossed).astype(LOW)
    from_near = lax.ppermute(first, "do", NEAR)
    from_across = lax.ppermute(third, "do", MIDDLE)
    return add(parts[0], from_near, from_across)


class Plan:
    def __init__(self, outer, width, per_device):
        self.outer = outer
        self.width = width
        self.rows = per_device
        self.block = 2 * per_device
        self.line = outer == 4 and per_device % 128 == 0

    def reorder(self, values):
        if not self.line:
            return values
        place = lax.axis_index("do")
        quarter = values.shape[-1] // 4
        a, b, c, d = (values[..., i * quarter : (i + 1) * quarter] for i in range(4))
        values = jnp.where(place % 2 == 1, cat([b, a, d, c], -1), values)
        half = 2 * quarter
        turned = cat([values[..., half:], values[..., :half]], -1)
        return jnp.where(place >= 2, turned, values)

    def by_x(self, low, high):
        return jnp.where(lax.axis_index("di") == 0, low, high)

    def gather(self, row_parts, col_parts):
        if not self.line:
            row_full, col_full = [], []
            for own, other in row_parts:
                theirs = lax.ppermute(other, "di", PAIR)
                block = cat([self.by_x(own, theirs), self.by_x(theirs, own)], 0)
                row_full.append(lax.all_gather(block, "do", axis=0, tiled=True))
            for own, other in col_parts:
                theirs = lax.ppermute(other, "di", PAIR)
                block = cat([self.by_x(own, theirs), self.by_x(theirs, own)], 1)
                col_full.append(lax.all_gather(block, "do", axis=1, tiled=True))
            return row_full, col_full
        rows = self.rows

        def pack(which):
            pieces = [part[which] for part in row_parts]
            for part in col_parts:
                both = part[which]
                pieces += [both[i : i + rows] for i in range(0, both.shape[0], rows)]
            return cat(pieces, 1)

        mine, other = pack(0), pack(1)
        theirs = lax.ppermute(other, "di", PAIR)
        block = cat([self.by_x(mine, theirs), self.by_x(theirs, mine)], 0)
        slots = line_gather(block)
        row_full, col_full, start = [], [], 0
        for own, _ in row_parts:
            stop = start + own.shape[1]
            row_full.append(cat([slot[:, start:stop] for slot in slots], 0))
            start = stop
        for own, _ in col_parts:
            bands = []
            for _ in range(0, own.shape[0], rows):
                bands.append(
                    cat(
                        [
                            slot[x * rows : (x + 1) * rows, start : start + rows]
                            for slot in slots
                            for x in range(2)
                        ],
                        1,
                    )
                )
                start += rows
            col_full.append(cat(bands, 0))
        return row_full, col_full

    def reduce(self, row_grads, col_grads):
        rows = self.rows
        if not self.line:
            row_out, col_out = [], []
            for grad in row_grads:
                total = lax.psum_scatter(grad, "do", scatter_dimension=0, tiled=True)
                row_out.append(self.trade(total[:rows], total[rows:]))
            for grad in col_grads:
                total = lax.psum_scatter(grad, "do", scatter_dimension=1, tiled=True)
                col_out.append(self.trade(total[:, :rows], total[:, rows:]))
            return row_out, col_out
        block = self.block
        parts = []
        for k in range(4):
            pieces = [grad[k * block : (k + 1) * block] for grad in row_grads]
            for grad in col_grads:
                for i in range(0, grad.shape[0], rows):
                    at = k * block
                    pieces.append(
                        cat(
                            [
                                grad[i : i + rows, at : at + rows],
                                grad[i : i + rows, at + rows : at + block],
                            ],
                            0,
                        )
                    )
            parts.append(cat(pieces, 1))
        total = line_reduce(parts)
        mine, theirs = self.trade(total[:rows], total[rows:])
        row_out, col_out, start = [], [], 0
        for grad in row_grads:
            stop = start + grad.shape[1]
            row_out.append((mine[:, start:stop], theirs[:, start:stop]))
            start = stop
        for grad in col_grads:
            own, other = [], []
            for _ in range(0, grad.shape[0], rows):
                own.append(mine[:, start : start + rows])
                other.append(theirs[:, start : start + rows])
                start += rows
            col_out.append((cat(own, 0), cat(other, 0)))
        return row_out, col_out

    def trade(self, low, high):
        mine = self.by_x(low, high).astype(F32)
        theirs = lax.ppermute(self.by_x(high, low).astype(LOW), "di", PAIR)
        return mine, theirs.astype(F32)


def rope_tables(positions):
    half_dim = HD // 2
    inverse_freq = ROPE_BASE ** (-2.0 * jnp.arange(half_dim, dtype=F32) / HD)
    angles = positions.astype(F32)[:, None] * inverse_freq[None, :]
    cosine, sine = jnp.cos(angles), jnp.sin(angles)
    return cat([cosine] * 4, 1), cat([-sine, sine] * 2, 1)


def lanes_of(shape):
    return lax.broadcasted_iota(jnp.int32, shape, 1)


def shuffle_halves(values):
    wide = values.shape[1]
    up = pltpu.roll(values, wide - HD // 2, 1)
    down = pltpu.roll(values, HD // 2, 1)
    return jnp.where(lanes_of(values.shape) % HD < HD // 2, up, down)


def tables(cos_ref, sin_ref, pairs):
    cosine, sine = cos_ref[...], sin_ref[...]
    is_key = lanes_of(cosine.shape) < HD
    return (
        cat([cosine] * pairs + [jnp.where(is_key, cosine, 1.0)], 1),
        cat([sine] * pairs + [jnp.where(is_key, sine, 0.0)], 1),
    )


def split_kv(both):
    is_key = lanes_of(both.shape) < HD
    blank = jnp.zeros_like(both)
    key_low = jnp.where(is_key, both, blank)
    value_high = jnp.where(is_key, blank, both)
    return (
        (key_low, pltpu.roll(key_low.astype(F32), HD, 1).astype(LOW)),
        (pltpu.roll(value_high.astype(F32), HD, 1).astype(LOW), value_high),
    )


def allowed_pairs(seg_col, seg_row):
    shape = (seg_col.shape[0], seg_row.shape[1])
    key_at = lax.broadcasted_iota(jnp.int32, shape, 1)
    query_at = lax.broadcasted_iota(jnp.int32, shape, 0)
    return (seg_col == seg_row) & (key_at <= query_at)


def attn_forward_kernel(
    pairs, x_ref, wqkv_ref, wout_ref, cos_ref, sin_ref, col_ref, row_ref,
    part_ref, ctx_ref, q_ref, kv_ref, lse_ref,
):
    cosine, sine = tables(cos_ref, sin_ref, pairs)
    qkv = dot(x_ref[...], wqkv_ref[...], 1, 0)
    rotated = (qkv * cosine + shuffle_halves(qkv) * sine).astype(LOW)
    queries, both = rotated[:, : pairs * 128], rotated[:, pairs * 128 :]
    q_ref[...] = queries
    kv_ref[...] = both
    keys, values = split_kv(both)
    allowed = allowed_pairs(col_ref[...], row_ref[0])
    lane = lanes_of((both.shape[0], 128))
    log_sums = jnp.zeros((both.shape[0], 128), F32)
    contexts = []
    for pair in range(pairs):
        heads = queries[:, pair * 128 : (pair + 1) * 128]
        context = None
        for side in range(2):
            scores = dot(heads, keys[side], 1, 1) * HD**-0.5
            masked = jnp.where(allowed, scores, -1e30)
            top = jnp.max(masked, axis=1, keepdims=True)
            weights = jnp.exp(masked - top)
            totals = jnp.sum(weights, axis=1, keepdims=True)
            probs = (weights * (1.0 / totals)).astype(LOW)
            piece = dot(probs, values[side], 1, 0)
            context = piece if context is None else context + piece
            log_sums = jnp.where(lane == 2 * pair + side, top + jnp.log(totals), log_sums)
        contexts.append(context.astype(LOW))
    lse_ref[...] = log_sums
    context_low = cat(contexts, 1)
    ctx_ref[...] = context_low
    part_ref[...] = dot(context_low, wout_ref[...], 1, 0).astype(LOW)


def attn_backward_kernel(
    pairs, res_ref, x_ref, ctx_ref, q_ref, kv_ref, lse_ref, wqkv_ref, wout_ref, cos_ref, sin_ref,
    col_ref, row_ref,
    part_ref, gqkv_ref, gout_ref, gain_ref, acc_qkv, acc_out,
):
    step = pl.program_id(0)

    @pl.when(step == 0)
    def _():
        acc_qkv[...] = jnp.zeros_like(acc_qkv)
        acc_out[...] = jnp.zeros_like(acc_out)

    cosine, sine = tables(cos_ref, sin_ref, pairs)
    scale = HD**-0.5
    res = res_ref[...]
    acc_out[...] += dot(ctx_ref[...], res, 0, 0)
    ctx_grad = dot(res, wout_ref[...], 1, 1).astype(LOW)
    keys, values = split_kv(kv_ref[...])
    allowed = allowed_pairs(col_ref[...], row_ref[0])
    lane = lanes_of((res.shape[0], 128))
    log_sums = lse_ref[...]
    query_grads, key_grad, value_grad = [], None, None
    for pair in range(pairs):
        heads = q_ref[:, pair * 128 : (pair + 1) * 128]
        grads = ctx_grad[:, pair * 128 : (pair + 1) * 128]
        query_grad = None
        for side in range(2):
            here = (lane < HD) if side == 0 else (lane >= HD)
            head = jnp.where(here, heads, jnp.zeros_like(heads))
            grad = jnp.where(here, grads, jnp.zeros_like(grads))
            at = 2 * pair + side
            scores = dot(heads, keys[side], 1, 1) * scale
            probs = jnp.where(allowed, jnp.exp(scores - log_sums[:, at : at + 1]), 0.0)
            prob_grad = dot(grads, values[side], 1, 1)
            delta = jnp.sum(probs * prob_grad, axis=1, keepdims=True)
            score_grad = (probs * (prob_grad - delta)).astype(LOW)
            to_value = dot(probs.astype(LOW), grad, 0, 0)
            to_key = dot(score_grad, head, 0, 0)
            to_query = dot(score_grad, keys[side], 1, 0)
            value_grad = to_value if value_grad is None else value_grad + to_value
            key_grad = to_key if key_grad is None else key_grad + to_key
            query_grad = to_query if query_grad is None else query_grad + to_query
        query_grads.append(query_grad * scale)
    key_grad = (key_grad + pltpu.roll(key_grad, HD, 1)) * scale
    value_grad = value_grad + pltpu.roll(value_grad, HD, 1)
    joined = cat(query_grads + [jnp.where(lane < HD, key_grad, value_grad)], 1)
    low = (joined * cosine - shuffle_halves(joined) * sine).astype(LOW)
    part_ref[...] = dot(low, wqkv_ref[...], 1, 1).astype(LOW)
    acc_qkv[...] += dot(x_ref[...], low, 0, 0)

    @pl.when(step == pl.num_programs(0) - 1)
    def _():
        total = acc_qkv[...]
        gqkv_ref[...] = total.astype(LOW)
        gout_ref[...] = acc_out[...].astype(LOW)
        gain_ref[...] = jnp.sum(total * wqkv_ref[...].astype(F32), axis=1, keepdims=True)


def once(shape):
    return pl.BlockSpec(shape, lambda i: (0,) * len(shape), pipeline_mode=pl.Buffered(1))


def per_seq(shape):
    return pl.BlockSpec(shape, lambda i: (i,) + (0,) * (len(shape) - 1))


def attn_forward(normed, wqkv, wout, cosine, sine, seg_col, seg_row):
    rows, width = normed.shape
    heads = wout.shape[0]
    pairs = heads // 128
    seqs = rows // LEN
    return pl.pallas_call(
        functools.partial(attn_forward_kernel, pairs),
        grid=(seqs,),
        in_specs=[
            per_seq((LEN, width)),
            once(wqkv.shape),
            once(wout.shape),
            per_seq((LEN, 128)),
            per_seq((LEN, 128)),
            per_seq((LEN, 1)),
            per_seq((1, 1, LEN)),
        ],
        out_specs=[
            per_seq((LEN, width)),
            per_seq((LEN, heads)),
            per_seq((LEN, heads)),
            per_seq((LEN, 128)),
            per_seq((LEN, 128)),
        ],
        out_shape=[
            jax.ShapeDtypeStruct((rows, width), LOW),
            jax.ShapeDtypeStruct((rows, heads), LOW),
            jax.ShapeDtypeStruct((rows, heads), LOW),
            jax.ShapeDtypeStruct((rows, 128), LOW),
            jax.ShapeDtypeStruct((rows, 128), F32),
        ],
        compiler_params=pltpu.CompilerParams(vmem_limit_bytes=48 * MIB),
        cost_estimate=pl.CostEstimate(
            flops=20 * rows * width * heads, bytes_accessed=10 * rows * width, transcendentals=0
        ),
        name="attn_forward",
    )(normed, wqkv, wout, cosine, sine, seg_col, seg_row)


def attn_backward(res_all, normed, ctx, queries, both, lse, wqkv, wout, cosine, sine, seg_col, seg_row):
    rows, width = normed.shape
    heads = wout.shape[0]
    pairs = heads // 128
    seqs = rows // LEN
    return pl.pallas_call(
        functools.partial(attn_backward_kernel, pairs),
        grid=(seqs,),
        in_specs=[
            per_seq((LEN, width)),
            per_seq((LEN, width)),
            per_seq((LEN, heads)),
            per_seq((LEN, heads)),
            per_seq((LEN, 128)),
            per_seq((LEN, 128)),
            once(wqkv.shape),
            once(wout.shape),
            per_seq((LEN, 128)),
            per_seq((LEN, 128)),
            per_seq((LEN, 1)),
            per_seq((1, 1, LEN)),
        ],
        out_specs=[
            per_seq((LEN, width)),
            once(wqkv.shape),
            once(wout.shape),
            once((width, 1)),
        ],
        out_shape=[
            jax.ShapeDtypeStruct((rows, width), LOW),
            jax.ShapeDtypeStruct(wqkv.shape, LOW),
            jax.ShapeDtypeStruct(wout.shape, LOW),
            jax.ShapeDtypeStruct((width, 1), F32),
        ],
        scratch_shapes=[pltpu.VMEM(wqkv.shape, F32), pltpu.VMEM(wout.shape, F32)],
        compiler_params=pltpu.CompilerParams(vmem_limit_bytes=52 * MIB),
        cost_estimate=pl.CostEstimate(
            flops=40 * rows * width * heads, bytes_accessed=16 * rows * width, transcendentals=0
        ),
        name="attn_backward",
    )(res_all, normed, ctx, queries, both, lse, wqkv, wout, cosine, sine, seg_col, seg_row)


def norm_rows(values, gain_vec):
    row_scale = lax.rsqrt(jnp.mean(values * values, axis=1, keepdims=True) + NORM_EPS)
    return values * row_scale * gain_vec, row_scale


def norm_back(row_grad, values, row_scale, gain_vec):
    scaled_grad = row_grad * gain_vec
    return row_scale * scaled_grad - values * row_scale**3 * jnp.mean(
        scaled_grad * values, axis=1, keepdims=True
    )


def adamw_update(master, grad_sum, first_mom, second_mom, decay_rate, step_rate):
    next_first = BETA_ONE * first_mom + (1.0 - BETA_ONE) * grad_sum
    next_second = BETA_TWO * second_mom + (1.0 - BETA_TWO) * grad_sum * grad_sum
    first_hat = next_first / (1.0 - BETA_ONE**STEP)
    second_hat = next_second / (1.0 - BETA_TWO**STEP)
    next_master = master - step_rate * (
        first_hat / (jnp.sqrt(second_hat) + ADAM_EPS) + decay_rate * master
    )
    return (next_master, next_first, next_second)


def sum_everywhere(values, sizes):
    for axis, size in sizes:
        step = 1
        while step < size:
            values = values + lax.ppermute(values, axis, [(i, i ^ step) for i in range(size)])
            step *= 2
    return values


def on_device(
    sizes,
    layer_input, out_grad, segment_ids, positions,
    w_query, w_key, w_value, w_out, w_gate, w_up, w_down,
    m_query, m_key, m_value, m_out, m_gate, m_up, m_down,
    v_query, v_key, v_value, v_out, v_gate, v_up, v_down,
    gain_attn, gain_ffn, m_gain_attn, m_gain_ffn, v_gain_attn, v_gain_ffn,
):
    width = layer_input.shape[1]
    plan = Plan(sizes["do"], width, w_query.shape[0])
    by_x = plan.by_x
    plane = ("di", "tp")

    def col_halves(weight):
        half = weight.shape[1] // 2
        low = weight.astype(LOW)
        return by_x(low[:, :half], low[:, half:]), by_x(low[:, half:], low[:, :half])

    def row_halves(weight):
        half = weight.shape[0] // 2
        low = weight.astype(LOW)
        return by_x(low[:half], low[half:]), by_x(low[half:], low[:half])

    def col_cut(pair, chunk):
        size = pair[0].shape[1] // CHUNKS
        return tuple(part[:, chunk * size : (chunk + 1) * size] for part in pair)

    def row_cut(pair, chunk):
        size = pair[0].shape[0] // CHUNKS
        return tuple(part[chunk * size : (chunk + 1) * size] for part in pair)

    halves_q, halves_k, halves_v = col_halves(w_query), col_halves(w_key), col_halves(w_value)
    qkv_parts = tuple(cat([q, k, v], 1) for q, k, v in zip(halves_q, halves_k, halves_v))
    (wqkv,), (wout,) = plan.gather([qkv_parts], [row_halves(w_out)])
    halves_g, halves_u, halves_d = col_halves(w_gate), col_halves(w_up), row_halves(w_down)
    ffn_weights = []
    for chunk in range(CHUNKS):
        (gate_up,), (down,) = plan.gather(
            [
                tuple(
                    cat([g, u], 1)
                    for g, u in zip(col_cut(halves_g, chunk), col_cut(halves_u, chunk))
                )
            ],
            [row_cut(halves_d, chunk)],
        )
        ffn_weights.append((gate_up, down))

    marks = cat([segment_ids[None, :], positions[None, :]], 0)
    marks_other = lax.ppermute(marks, "di", PAIR)
    marks_all = cat([by_x(marks, marks_other), by_x(marks_other, marks)], 1)
    seg_all, pos_all = marks_all[0], marks_all[1]
    rows = seg_all.shape[0]
    seqs = rows // LEN
    seg_col, seg_row = seg_all.reshape(rows, 1), seg_all.reshape(seqs, 1, LEN)
    cosine, sine = rope_tables(pos_all)

    gain_one, gain_two = plan.reorder(gain_attn), plan.reorder(gain_ffn)
    inputs_f = plan.reorder(layer_input).astype(F32)
    grad_low = plan.reorder(out_grad)
    normed, scale_one = norm_rows(inputs_f, gain_one)
    normed_all = lax.all_gather(normed.astype(LOW), plane, axis=0, tiled=True)
    grad_all = lax.all_gather(grad_low, plane, axis=0, tiled=True)

    attn_part, ctx, queries, both, lse = attn_forward(
        normed_all, wqkv, wout, cosine, sine, seg_col, seg_row
    )
    residual = inputs_f + lax.psum_scatter(
        attn_part, plane, scatter_dimension=0, tiled=True
    ).astype(F32)
    normed_two, scale_two = norm_rows(residual, gain_two)
    two_all = lax.all_gather(normed_two.astype(LOW), plane, axis=0, tiled=True)

    out_part, back_part, gain_two_part, ffn_grads = None, None, None, []
    for gate_up, down in ffn_weights:
        hidden = down.shape[0]
        pre = dot(two_all, gate_up, 1, 0)
        gate_pre, lifted = pre[:, :hidden], pre[:, hidden:]
        sigmoid_gate = jax.nn.sigmoid(gate_pre)
        silu_gate = gate_pre * sigmoid_gate
        act = (silu_gate * lifted).astype(LOW)
        act_grad = dot(grad_all, down, 1, 1)
        gate_grad = act_grad * lifted * sigmoid_gate * (1.0 + gate_pre * (1.0 - sigmoid_gate))
        both_grad = cat([gate_grad.astype(LOW), (act_grad * silu_gate).astype(LOW)], 1)
        piece = dot(act, down, 1, 0)
        out_part = piece if out_part is None else out_part + piece
        piece = dot(both_grad, gate_up, 1, 1)
        back_part = piece if back_part is None else back_part + piece
        local_gate_up = dot(two_all, both_grad, 0, 0)
        local_down = dot(act, grad_all, 0, 0)
        piece = jnp.sum(local_gate_up * gate_up.astype(F32), axis=1)
        gain_two_part = piece if gain_two_part is None else gain_two_part + piece
        (gate_up_pair,), (down_pair,) = plan.reduce(
            [local_gate_up.astype(LOW)], [local_down.astype(LOW)]
        )
        ffn_grads.append((gate_up_pair, down_pair))

    normed_two_grad = lax.psum_scatter(
        back_part.astype(LOW), plane, scatter_dimension=0, tiled=True
    ).astype(F32)
    out_value = (
        residual
        + lax.psum_scatter(
            out_part.astype(LOW), plane, scatter_dimension=0, tiled=True
        ).astype(F32)
    ).astype(LOW)
    residual_grad = grad_low.astype(F32) + norm_back(normed_two_grad, residual, scale_two, gain_two)
    res_all = lax.all_gather(residual_grad.astype(LOW), plane, axis=0, tiled=True)

    back_one_part, local_qkv, local_out, gain_one_part = attn_backward(
        res_all, normed_all, ctx, queries, both, lse, wqkv, wout, cosine, sine, seg_col, seg_row
    )
    (qkv_pair,), (out_pair,) = plan.reduce([local_qkv], [local_out])
    normed_grad = lax.psum_scatter(
        back_one_part, plane, scatter_dimension=0, tiled=True
    ).astype(F32)
    in_grad = residual_grad + norm_back(normed_grad, inputs_f, scale_one, gain_one)

    gain_parts = jnp.stack([gain_one_part[:, 0] / gain_one, gain_two_part / gain_two])
    gain_sums = sum_everywhere(plan.reorder(gain_parts), list(sizes.items()))
    grad_gain_attn, grad_gain_ffn = gain_sums[0], gain_sums[1]

    def join(pair, axis):
        own, other = pair
        return by_x(cat([own, other], axis), cat([other, own], axis))

    def from_chunks(pairs, axis):
        own = cat([pair[0] for pair in pairs], axis)
        other = cat([pair[1] for pair in pairs], axis)
        return join((own, other), axis)

    def cut(pair, start, stop):
        return tuple(part[:, start:stop] for part in pair)

    at_k = halves_q[0].shape[1]
    at_v = at_k + halves_k[0].shape[1]
    end = at_v + halves_v[0].shape[1]
    grad_query = join(cut(qkv_pair, 0, at_k), 1)
    grad_key = join(cut(qkv_pair, at_k, at_v), 1)
    grad_value = join(cut(qkv_pair, at_v, end), 1)
    grad_out = join(out_pair, 0)
    hidden = ffn_weights[0][1].shape[0]
    grad_gate = from_chunks([cut(gu, 0, hidden) for gu, _ in ffn_grads], 1)
    grad_up = from_chunks([cut(gu, hidden, 2 * hidden) for gu, _ in ffn_grads], 1)
    grad_down = from_chunks([down for _, down in ffn_grads], 0)

    grads = (grad_query, grad_key, grad_value, grad_out, grad_gate, grad_up, grad_down)
    masters = (w_query, w_key, w_value, w_out, w_gate, w_up, w_down)
    firsts = (m_query, m_key, m_value, m_out, m_gate, m_up, m_down)
    seconds = (v_query, v_key, v_value, v_out, v_gate, v_up, v_down)
    updated = [
        adamw_update(w, g, m, v, WEIGHT_DECAY, LEARN_RATE)
        for w, g, m, v in zip(masters, grads, firsts, seconds)
    ]
    gain_updated = [
        adamw_update(gain_attn, grad_gain_attn, m_gain_attn, v_gain_attn, 0.0, GAIN_RATE),
        adamw_update(gain_ffn, grad_gain_ffn, m_gain_ffn, v_gain_ffn, 0.0, GAIN_RATE),
    ]
    return (
        plan.reorder(out_value),
        plan.reorder(in_grad),
        *grads,
        *[u[0] for u in updated],
        *[u[1] for u in updated],
        *[u[2] for u in updated],
        grad_gain_attn,
        grad_gain_ffn,
        *[u[0] for u in gain_updated],
        *[u[1] for u in gain_updated],
        *[u[2] for u in gain_updated],
    )


def solution(mesh):
    dp, tp = mesh.shape["dp"], mesh.shape["tp"]
    split = Mesh(mesh.devices.reshape(dp // 2, 2, tp), ("do", "di", "tp"))
    sizes = {"do": dp // 2, "di": 2, "tp": tp}
    dp_axes = ("do", "di")
    tokens = P(("do", "di", "tp"), None)
    by_rows, by_cols = P(dp_axes, "tp"), P("tp", dp_axes)
    weights = (by_rows, by_rows, by_rows, by_cols, by_rows, by_rows, by_cols)
    gains = (P(),) * 6
    in_specs = (tokens, tokens, P(dp_axes), P(dp_axes)) + weights * 3 + gains
    out_specs = (tokens, tokens) + weights * 4 + (P(),) * 2 + gains
    return jax.shard_map(
        functools.partial(on_device, sizes),
        mesh=split,
        in_specs=in_specs,
        out_specs=out_specs,
        check_vma=False,
    )
```

time: 1730 us -> 1070 us (0.62)
  waiting for transfers between devices: 1220 us -> 551 us
  blocking collectives: 93.5 us -> 0 us
  starting transfers between devices: 1.08 us -> 74.8 us
  matrix products: 219 us -> 155 us
  Pallas kernels: 0 us -> 62.9 us
    reduce_scatter x11 -> x4, waiting for transfers between devices: 770 us -> 151 us  [the longest x1 77.7 us: on_device(): lax.psum_scatter(back_part.astype(LOW), plane, scatter_dimension=0, tiled...]
    all_gather x9 -> x4, waiting for transfers between devices: 445 us -> 26.5 us  [the longest x1 26.5 us: on_device(): lax.all_gather(residual_grad.astype(LOW), plane, axis=0, tiled=True)]
    ppermute x0 -> x42, waiting for transfers between devices: none -> 374 us  [the longest x3 69.5 us: line_gather(): out_near = lax.ppermute(across_near, 'do', OUTWARD)]
    ppermute x0 -> x42, starting transfers between devices: none -> 74 us  [the longest x3 12.5 us: line_gather(): across = lax.ppermute(own, 'do', MIDDLE)]
    dot_general x35 -> x12, matrix products: 219 us -> 155 us  [dot(): lax.dot_general(lhs, rhs, (((lhs_dim,), (rhs_dim,)), ((), ())), preferred...]
    pallas_call x0 -> x2, Pallas kernels: none -> 62.9 us  [the longest x1 41.4 us: attn_backward(): pl.pallas_call(functools.partial(attn_backward_kernel, pairs), grid=(seqs...]
    unnamed x142 -> x308, local copies, waits for them, and re-layouts: 17.7 us -> 77.2 us
    all_gather x2 -> x0, blocking collectives: 54.8 us -> none  [the longest x1 28.4 us: on_device(): lax.all_gather(w_value.astype(jnp.bfloat16), 'dp', axis=0, tiled=True)]
  transfers between devices with their start and end apart: 20 -> 50, of which waited for: 18 -> 27; matrix products, arithmetic and copies ran while one was open for 18% -> 24% of each run, Pallas kernels for 0% -> 0%
where the time goes in v1:
time: 1070 us; the launch traced here: 1060 us
  waiting for transfers between devices  551 us (51%)
  matrix products  155 us (14%)
  local copies, waits for them, and re-layouts  105 us (10%)
  other arithmetic  90.3 us (8%)
  starting transfers between devices  74.8 us (7%)
  Pallas kernels  62.9 us (6%)
  between operations  16.8 us (2%)
    dot_general x12, matrix products, dot(): lax.dot_general(lhs, rhs, (((lhs_dim,), (rhs_dim,)), ((), ())), preferred...  155 us
    reduce_scatter x1, waiting for transfers between devices, on_device(): lax.psum_scatter(back_part.astype(LOW), plane, scatter_dimension=0, tiled...  77.7 us
    unnamed x308, local copies, waits for them, and re-layouts  77.2 us
    reduce_scatter x1, waiting for transfers between devices, on_device(): lax.psum_scatter(attn_part, plane, scatter_dimension=0, tiled=True)  73.3 us
    ppermute x3, waiting for transfers between devices, line_gather(): out_near = lax.ppermute(across_near, 'do', OUTWARD)  69.5 us
    ppermute x3, waiting for transfers between devices, line_gather(): across_near = lax.ppermute(near, 'do', MIDDLE)  68.2 us
    ppermute x3, waiting for transfers between devices, line_reduce(): from_near = lax.ppermute(first, 'do', NEAR)  51.8 us
    ppermute x3, waiting for transfers between devices, gather(): theirs = lax.ppermute(other, 'di', PAIR)  51.3 us
  transfers between devices with their start and end apart: 50, of which 27 were waited for; matrix products, arithmetic and copies ran while one was open for 24% of the time, Pallas kernels for 0%

profile of v1, /device:TPU:9, one launch (start us, length us, event | category | flops | bytes accessed | tf_op | source)
XLA Modules:
  0.0 1056.1 jit_solution(206740268479540383)
XLA Ops:
  14.5 7.2 collective-permute-done.6
  21.8 5.4 fusion.23
  28.5 4.3 collective-permute-start.3
  35.0 3.6 pad_maximum_fusion.18.sin_ref
  38.6 4.6 collective-permute-done.1
  43.2 3.2 collective-permute-start.2
  50.7 8.9 collective-permute-done.2
  61.1 13.3 %collective-permute-done.5 = bf16[512,640]{1,0:T(8,128)(2,1)S(1)} collective-permute-done((bf16[512,640]{1,0:T(8,128)(2,1)S(1)}, bf16[512,640]{1,0:T(8,128)(2,1)S(1)}, u32[]{:S(2)}, u32[]{:S(2)}) %collective-permute-start.5) | collective-permute-done | bytes 655392 | tf_op jit(solution)/shard_map/ppermute | solution.py:51
  77.0 21.5 %attn_forward.1 = (bf16[2048,2048]{1,0:T(8,128)(2,1)}, bf16[2048,256]{1,0:T(8,128)(2,1)S(1)}, bf16[2048,256]{1,0:T(8,128)(2,1)S(1)}, bf16[2048,128]{1,0:T(8,128)(2,1)S(1)}, f32[2048,128]{1,0:T(8,128)S(1)}) custom-call(bf16[2048,2048]{1,0:T(8,128)(2,1)} %all-gather.5.cloned.1.call-done.x_ref, bf16[2048,384]{1,0:T(8,128)(2,1)} %pad_maximum_fusion.12.wqkv_ref, ...), custom_call_target="tpu_custom_call" | custom-call | flops 21474836480 | bytes 41943040 | tf_op jit(solution)/shard_map/attn_forward/pallas_call | solution.py:351
  102.2 73.3 %reduce-scatter.5.cloned.1.call-done = bf16[256,2048]{1,0:T(8,128)(2,1)} async-done(((bf16[2048,2048]{1,0:T(8,128)(2,1)}), bf16[256,2048]{1,0:T(8,128)(2,1)}) %reduce-scatter.5.cloned.1.call-update) | async-done | bytes 1048592 | tf_op jit(solution)/shard_map/reduce_scatter | solution.py:527
  182.4 2.9 copy.133
  185.3 2.9 convert_element_type.241
  188.2 3.1 copy.131
  194.0 2.9 copy.132
  202.1 26.6 %collective-permute-done.7 = bf16[256,1536]{0,1:T(8,128)(2,1)S(1)} collective-permute-done((bf16[256,1536]{0,1:T(8,128)(2,1)S(1)}, bf16[256,1536]{0,1:T(8,128)(2,1)S(1)}, u32[]{:S(2)}, u32[]{:S(2)}) %collective-permute-start.7) | collective-permute-done | bytes 786464 | tf_op jit(solution)/shard_map/ppermute | solution.py:124
  229.3 4.1 collective-permute-start.10
  233.5 24.7 %collective-permute-done.13 = bf16[256,1536]{0,1:T(8,128)(2,1)S(1)} collective-permute-done((bf16[256,1536]{0,1:T(8,128)(2,1)S(1)}, bf16[256,1536]{0,1:T(8,128)(2,1)S(1)}, u32[]{:S(2)}, u32[]{:S(2)}) %collective-permute-start.13) | collective-permute-done | bytes 786464 | tf_op jit(solution)/shard_map/ppermute | solution.py:124
  259.0 4.1 collective-permute-start.16
  268.9 26.4 %collective-permute-done.14 = bf16[512,1536]{0,1:T(8,128)(2,1)S(1)} collective-permute-done((bf16[512,1536]{0,1:T(8,128)(2,1)S(1)}, bf16[512,1536]{0,1:T(8,128)(2,1)S(1)}, u32[]{:S(2)}, u32[]{:S(2)}) %collective-permute-start.14) | collective-permute-done | bytes 1572896 | tf_op jit(solution)/shard_map/ppermute | solution.py:47
  295.3 3.1 collective-permute-start.15
  304.5 27.2 %collective-permute-done.9 = bf16[512,1536]{0,1:T(8,128)(2,1)S(1)} collective-permute-done((bf16[512,1536]{0,1:T(8,128)(2,1)S(1)}, bf16[512,1536]{0,1:T(8,128)(2,1)S(1)}, u32[]{:S(2)}, u32[]{:S(2)}) %collective-permute-start.9) | collective-permute-done | bytes 1572896 | tf_op jit(solution)/shard_map/ppermute | solution.py:49
  333.3 32.1 %collective-permute-done.15 = bf16[512,1536]{0,1:T(8,128)(2,1)S(1)} collective-permute-done((bf16[512,1536]{0,1:T(8,128)(2,1)S(1)}, bf16[512,1536]{0,1:T(8,128)(2,1)S(1)}, u32[]{:S(2)}, u32[]{:S(2)}) %collective-permute-start.15) | collective-permute-done | bytes 1572896 | tf_op jit(solution)/shard_map/ppermute | solution.py:49
  370.7 23.7 %collective-permute-done.12 = bf16[512,1536]{0,1:T(8,128)(2,1)S(1)} collective-permute-done((bf16[512,1536]{0,1:T(8,128)(2,1)S(1)}, bf16[512,1536]{0,1:T(8,128)(2,1)S(1)}, u32[]{:S(2)}, u32[]{:S(2)}) %collective-permute-start.12) | collective-permute-done | bytes 1572896 | tf_op jit(solution)/shard_map/ppermute | solution.py:51
  395.6 32.5 %collective-permute-done.18 = bf16[512,1536]{0,1:T(8,128)(2,1)S(1)} collective-permute-done((bf16[512,1536]{0,1:T(8,128)(2,1)S(1)}, bf16[512,1536]{0,1:T(8,128)(2,1)S(1)}, u32[]{:S(2)}, u32[]{:S(2)}) %collective-permute-start.18) | collective-permute-done | bytes 1572896 | tf_op jit(solution)/shard_map/ppermute | solution.py:51
  432.7 15.5 %fusion.44 = f32[2048,1024]{0,1:T(8,128)} fusion(bf16[2048,2048]{1,0:T(8,128)(2,1)} %all-gather.7.cloned.1.call-done, bf16[512,1024]{0,1:T(8,128)(2,1)} %slice.980, bf16[512,1024]{0,1:T(8,128)(2,1)} %slice.979, bf16[512,1024]{0,1:T(8,128)(2,1)} %slice.978, bf16[512,1024]{0,1:T(8,128)(2,1)} %fusion.18), kind=kOutput, calls=%fused_computation.269 | convolution fusion | flops 8606711808 | bytes 20971520 | tf_op jit(solution)/shard_map/dot_general | solution.py:37
  448.3 11.5 %multiply_convert_fusion.1 = (bf16[2048,512]{0,1:T(8,128)(2,1)S(1)}, bf16[2048,512]{0,1:T(8,128)(2,1)S(1)}, bf16[2048,512]{0,1:T(8,128)(2,1)}) fusion(f32[2048,1024]{0,1:T(8,128)} %fusion.44, bf16[2048,2048]{1,0:T(8,128)(2,1)} %all-gather.9.cloned.1.call-done, bf16[256,2048]{0,1:T(8,128)(2,1)} %get-tuple-element.281, bf16[256,2048]{0,1:T(8,128)(2,1)} %get-tuple-element.280), kind=kOutput, calls=%fused_computation.9 | convolution fusion | flops 4314890240 | bytes 25165824 | tf_op jit(solution)/shard_map/dot_general | solution.py:37
  459.9 13.0 %fusion.3 = f32[2048,2048]{1,0:T(8,128)} fusion(bf16[2048,512]{0,1:T(8,128)(2,1)S(1)} %get-tuple-element.209, bf16[2048,512]{0,1:T(8,128)(2,1)S(1)} %get-tuple-element.208, bf16[512,1024]{0,1:T(8,128)(2,1)S(1)} %copy-done.55, bf16[512,1024]{0,1:T(8,128)(2,1)S(1)} %copy-done.52, bf16[512,1024]{0,1:T(8,128)(2,1)S(1)} %copy-done.49, ...), kind=kOutput, calls=%fused_computation.37 | convolution fusion | flops 8615100416 | bytes 25165824 | tf_op jit(solution)/shard_map/dot_general | solution.py:37
  473.0 13.7 %fusion.45 = f32[2048,1024]{0,1:T(8,128)} fusion(bf16[2048,2048]{1,0:T(8,128)(2,1)} %all-gather.7.cloned.1.call-done, bf16[512,1024]{0,1:T(8,128)(2,1)S(1)} %copy-done.58, bf16[512,1024]{0,1:T(8,128)(2,1)S(1)} %copy-done.57, bf16[512,1024]{0,1:T(8,128)(2,1)S(1)} %copy-done.54, bf16[512,1024]{0,1:T(8,128)(2,1)S(1)} %copy-done.51), kind=kOutput, calls=%fused_computation.270 | convolution fusion | flops 8606711808 | bytes 20971520 | tf_op jit(solution)/shard_map/dot_general | solution.py:37
  486.6 12.9 %multiply_convert_fusion.3 = (bf16[2048,512]{0,1:T(8,128)(2,1)}, bf16[2048,512]{0,1:T(8,128)(2,1)}, bf16[2048,512]{0,1:T(8,128)(2,1)}) fusion(f32[2048,1024]{0,1:T(8,128)} %fusion.45, bf16[2048,2048]{1,0:T(8,128)(2,1)} %all-gather.9.cloned.1.call-done, bf16[256,2048]{0,1:T(8,128)(2,1)S(1)} %copy-done.104, bf16[256,2048]{0,1:T(8,128)(2,1)S(1)} %copy-done.101), kind=kOutput, calls=%fused_computation.11 | convolution fusion | flops 4314890240 | bytes 25165824 | tf_op jit(solution)/shard_map/dot_general | solution.py:37
  499.6 17.0 %add_convert_fusion = bf16[2048,2048]{1,0:T(8,128)(2,1)} fusion(f32[2048,2048]{1,0:T(8,128)} %fusion.3, bf16[2048,512]{0,1:T(8,128)(2,1)} %get-tuple-element.207, bf16[2048,512]{0,1:T(8,128)(2,1)} %get-tuple-element.206, bf16[512,1024]{0,1:T(8,128)(2,1)} %slice.949, bf16[512,1024]{0,1:T(8,128)(2,1)} %slice.948, bf16[512,1024]{0,1:T(8,128)(2,1)} %slice.947, ...), kind=kOutput, calls=%fused_computation | convolution fusion | flops 8623489024 | bytes 33554432 | tf_op jit(solution)/shard_map/dot_general | solution.py:37
  516.8 77.7 %reduce-scatter.9.cloned.1.call-done = bf16[256,2048]{1,0:T(8,128)(2,1)} async-done(((bf16[2048,2048]{1,0:T(8,128)(2,1)}), bf16[256,2048]{1,0:T(8,128)(2,1)}) %reduce-scatter.9.cloned.1.call-update) | async-done | bytes 1048592 | tf_op jit(solution)/shard_map/reduce_scatter | solution.py:557
  598.5 14.4 %multiply_reduce_fusion.1 = (f32[2048]{0:T(1024)}, bf16[2048,1024]{0,1:T(8,128)(2,1)S(1)}) fusion(bf16[512,1024]{0,1:T(8,128)(2,1)} %slice.949, bf16[512,1024]{0,1:T(8,128)(2,1)} %slice.948, bf16[512,1024]{0,1:T(8,128)(2,1)} %slice.947, bf16[512,1024]{0,1:T(8,128)(2,1)} %fusion.19, bf16[2048,2048]{1,0:T(8,128)(2,1)} %all-gather.7.cloned.1.call-done, ...), kind=kOutput, calls=%fused_computation.3 | convolution fusion | flops 8621389824 | bytes 20979712 | tf_op jit(solution)/shard_map/dot_general | solution.py:37
  615.6 11.3 %convolution_convert_fusion.1 = bf16[512,2048]{0,1:T(8,128)(2,1)} fusion(bf16[2048,512]{0,1:T(8,128)(2,1)S(1)} %copy-done.122, bf16[2048,2048]{1,0:T(8,128)(2,1)} %all-gather.9.cloned.1.call-done), kind=kOutput, calls=%fused_computation.35 | convolution fusion | flops 4296015872 | bytes 12582912 | tf_op jit(solution)/shard_map/dot_general | solution.py:37
  626.9 26.5 %all-gather.11.cloned.1.call-done.res_ref = bf16[2048,2048]{1,0:T(8,128)(2,1)} async-done(((bf16[256,2048]{1,0:T(8,128)(2,1)}), bf16[2048,2048]{1,0:T(8,128)(2,1)}) %all-gather.11.cloned.1.call-update) | async-done | bytes 8388624 | tf_op jit(solution)/shard_map/all_gather | solution.py:567
  653.4 41.4 %attn_backward.1 = (bf16[2048,2048]{1,0:T(8,128)(2,1)}, bf16[2048,384]{1,0:T(8,128)(2,1)}, bf16[256,2048]{1,0:T(8,128)(2,1)S(1)}, f32[2048,1]{1,0:T(8,128)}) custom-call(bf16[2048,2048]{1,0:T(8,128)(2,1)} %all-gather.11.cloned.1.call-done.res_ref, bf16[2048,2048]{1,0:T(8,128)(2,1)} %all-gather.5.cloned.1.call-done.x_ref, bf16[2048,256]{1,0:T(8,128)(2,1)} %copy-done.2, ...), custom_call_target="tpu_custom_call" | custom-call | flops 42949672960 | bytes 67108864 | tf_op jit(solution)/shard_map/attn_backward/pallas_call | solution.py:390
  700.1 11.9 %convolution_convert_fusion = bf16[512,2048]{0,1:T(8,128)(2,1)S(1)} fusion(bf16[2048,512]{0,1:T(8,128)(2,1)S(1)} %copy-done.124, bf16[2048,2048]{1,0:T(8,128)(2,1)} %all-gather.9.cloned.1.call-done), kind=kOutput, calls=%fused_computation.34 | convolution fusion | flops 4296015872 | bytes 12582912 | tf_op jit(solution)/shard_map/dot_general | solution.py:37
  712.0 14.1 %multiply_reduce_fusion = (f32[2048]{0:T(1024)S(1)}, bf16[2048,1024]{0,1:T(8,128)(2,1)S(1)}) fusion(bf16[512,1024]{0,1:T(8,128)(2,1)S(1)} %copy-done.56, bf16[512,1024]{0,1:T(8,128)(2,1)S(1)} %copy-done.53, bf16[512,1024]{0,1:T(8,128)(2,1)S(1)} %copy-done.50, bf16[512,1024]{0,1:T(8,128)(2,1)S(1)} %copy-done.48, ...), kind=kOutput, calls=%fused_computation.2 | convolution fusion | flops 8621389824 | bytes 20979712 | tf_op jit(solution)/shard_map/dot_general | solution.py:37
  732.0 2.9 copy.145
  734.9 2.9 copy.146
  751.7 3.1 collective-permute-start.26
  756.1 14.3 %collective-permute-done.30 = bf16[512,1536]{0,1:T(8,128)(2,1)} collective-permute-done((bf16[512,1536]{0,1:T(8,128)(2,1)}, bf16[512,1536]{0,1:T(8,128)(2,1)}, u32[]{:S(2)}, u32[]{:S(2)}) %collective-permute-start.30) | collective-permute-done | bytes 1572896 | tf_op jit(solution)/shard_map/ppermute | solution.py:69
  772.6 3.2 collective-permute-start.31
  775.8 8.6 fusion.17
  785.7 3.4 collective-permute-done.26
  790.9 13.2 %collective-permute-done.28 = bf16[512,1536]{0,1:T(8,128)(2,1)S(1)} collective-permute-done((bf16[512,1536]{0,1:T(8,128)(2,1)S(1)}, bf16[512,1536]{0,1:T(8,128)(2,1)S(1)}, u32[]{:S(2)}, u32[]{:S(2)}) %collective-permute-start.28) | collective-permute-done | bytes 1572896 | tf_op jit(solution)/shard_map/ppermute | solution.py:72
  805.7 3.1 collective-permute-start.29
  808.8 14.0 %collective-permute-done.31 = bf16[512,1536]{0,1:T(8,128)(2,1)S(1)} collective-permute-done((bf16[512,1536]{0,1:T(8,128)(2,1)S(1)}, bf16[512,1536]{0,1:T(8,128)(2,1)S(1)}, u32[]{:S(2)}, u32[]{:S(2)}) %collective-permute-start.31) | collective-permute-done | bytes 1572896 | tf_op jit(solution)/shard_map/ppermute | solution.py:71
  824.5 13.4 %collective-permute-done.33 = bf16[512,1536]{0,1:T(8,128)(2,1)S(1)} collective-permute-done((bf16[512,1536]{0,1:T(8,128)(2,1)S(1)}, bf16[512,1536]{0,1:T(8,128)(2,1)S(1)}, u32[]{:S(2)}, u32[]{:S(2)}) %collective-permute-start.33) | collective-permute-done | bytes 1572896 | tf_op jit(solution)/shard_map/ppermute | solution.py:72
  839.5 3.1 collective-permute-start.34
  842.6 10.8 %add_convert_fusion.1 = bf16[2048,2048]{1,0:T(8,128)(2,1)} fusion(f32[2048,2048]{1,0:T(8,128)} %fusion.17, bf16[2048,512]{0,1:T(8,128)(2,1)S(1)} %copy-done.125, bf16[256,2048]{0,1:T(8,128)(2,1)} %get-tuple-element.281, bf16[256,2048]{0,1:T(8,128)(2,1)} %get-tuple-element.280), kind=kOutput, calls=%fused_computation.1 | convolution fusion | flops 4307550208 | bytes 29360128 | tf_op jit(solution)/shard_map/dot_general | solution.py:37
  854.1 17.5 %collective-permute-done.27 = bf16[512,1536]{0,1:T(8,128)(2,1)} collective-permute-done((bf16[512,1536]{0,1:T(8,128)(2,1)}, bf16[512,1536]{0,1:T(8,128)(2,1)}, u32[]{:S(2)}, u32[]{:S(2)}) %collective-permute-start.27) | collective-permute-done | bytes 1572896 | tf_op jit(solution)/shard_map/ppermute | solution.py:75
  875.6 29.7 %collective-permute-done.32 = bf16[512,1536]{0,1:T(8,128)(2,1)} collective-permute-done((bf16[512,1536]{0,1:T(8,128)(2,1)}, bf16[512,1536]{0,1:T(8,128)(2,1)}, u32[]{:S(2)}, u32[]{:S(2)}) %collective-permute-start.32) | collective-permute-done | bytes 1572896 | tf_op jit(solution)/shard_map/ppermute | solution.py:75
  911.5 24.3 %collective-permute-done.36 = bf16[256,1536]{0,1:T(8,128)(2,1)S(1)} collective-permute-done((bf16[256,1536]{0,1:T(8,128)(2,1)S(1)}, bf16[256,1536]{0,1:T(8,128)(2,1)S(1)}, u32[]{:S(2)}, u32[]{:S(2)}) %collective-permute-start.36) | collective-permute-done | bytes 786464 | tf_op jit(solution)/shard_map/ppermute | solution.py:195
  940.0 4.1 multiply_subtract_fusion
  955.9 4.6 collective-permute-start.40
  960.6 5.1 multiply_subtract_fusion.1
  973.6 3.9 multiply_subtract_fusion.2
  999.5 3.0 copy.149
  1004.3 3.0 copy.155
  1011.4 3.0 collective-permute-start.21
  1018.9 4.7 collective-permute-done.21
  1023.6 4.0 collective-permute-done.23
  1029.0 5.3 collective-permute-done.24
  1041.3 3.5 fusion.13
  (518 shorter events, 185.3 us)
Async XLA Ops:
  7.2 69.8 %all-gather.5.cloned.1.call-start = ((), (), s32[]{:S(2)}) async-start(), calls=%async_computation.4 | async-start | bytes 9437184 | tf_op jit(solution)/shard_map/all_gather | solution.py:521
  12.3 163.2 %reduce-scatter.5.cloned.1.call-start = ((), (), s32[]{:S(2)}) async-start(), calls=%async_computation.5 | async-start | bytes 9437184 | tf_op jit(solution)/shard_map/reduce_scatter | solution.py:527
  12.9 14.2 %collective-permute-start = (bf16[256,640]{1,0:T(8,128)(2,1)S(1)}, bf16[256,640]{1,0:T(8,128)(2,1)S(1)}, u32[]{:S(2)}, u32[]{:S(2)}) collective-permute-start(bf16[256,640]{1,0:T(8,128)(2,1)S(1)} %pad_maximum_fusion.25), channel_id=1, source_target_pairs={{0,4},{4,0},{1,5},{5,1},{2,6},{6,2},{3,7},{7,3},{8,12},{12,8},{9,1... | collective-permute-start | bytes 983048 | tf_op jit(solution)/shard_map/ppermute | solution.py:124
  14.2 7.5 collective-permute-start.6
  28.2 15.0 %collective-permute-start.1 = (bf16[512,640]{1,0:T(8,128)(2,1)}, bf16[512,640]{1,0:T(8,128)(2,1)}, u32[]{:S(2)}, u32[]{:S(2)}) collective-permute-start(bf16[512,640]{1,0:T(8,128)(2,1)} %pad_maximum_fusion.23), channel_id=1, source_target_pairs={{0,8},{8,0},{16,24},{24,16},{1,9},{9,1},{17,25},{25,17},{2,10},{10... | collective-permute-start | bytes 1966088 | tf_op jit(solution)/shard_map/ppermute | solution.py:47
  28.5 18.0 %collective-permute-start.3 = (bf16[512,640]{1,0:T(8,128)(2,1)}, bf16[512,640]{1,0:T(8,128)(2,1)}, u32[]{:S(2)}, u32[]{:S(2)}) collective-permute-start(bf16[512,640]{1,0:T(8,128)(2,1)} %pad_maximum_fusion.23), channel_id=1, source_target_pairs={{8,16},{16,8},{9,17},{17,9},{10,18},{18,10},{11,19},{19,11},{12,20... | collective-permute-start | bytes 1966088 | tf_op jit(solution)/shard_map/ppermute | solution.py:48
  33.6 43.4 %copy-start = (f32[2048,128]{1,0:T(8,128)}, f32[2048,128]{1,0:T(8,128)S(1)}, u32[]{:S(2)}) copy-start(f32[2048,128]{1,0:T(8,128)S(1)} %pad_maximum_fusion.17.cos_ref) | copy-start | bytes 3145732
  43.2 16.3 %collective-permute-start.2 = (bf16[512,640]{1,0:T(8,128)(2,1)}, bf16[512,640]{1,0:T(8,128)(2,1)S(1)}, u32[]{:S(2)}, u32[]{:S(2)}) collective-permute-start(bf16[512,640]{1,0:T(8,128)(2,1)} %collective-permute-done.1), channel_id=1, source_target_pairs={{8,16},{16,8},{9,17},{17,9},{10,18},{18,10},{11,19},{19,11},{12,20... | collective-permute-start | bytes 1966088 | tf_op jit(solution)/shard_map/ppermute | solution.py:49
  46.4 14.5 %collective-permute-start.4 = (bf16[512,640]{1,0:T(8,128)(2,1)}, bf16[512,640]{1,0:T(8,128)(2,1)S(1)}, u32[]{:S(2)}, u32[]{:S(2)}) collective-permute-start(bf16[512,640]{1,0:T(8,128)(2,1)} %collective-permute-done.3), channel_id=1, source_target_pairs={{8,0},{16,24},{9,1},{17,25},{10,2},{18,26},{11,3},{19,27},{12,4},{... | collective-permute-start | bytes 1966088 | tf_op jit(solution)/shard_map/ppermute | solution.py:50
  59.6 14.8 %collective-permute-start.5 = (bf16[512,640]{1,0:T(8,128)(2,1)S(1)}, bf16[512,640]{1,0:T(8,128)(2,1)S(1)}, u32[]{:S(2)}, u32[]{:S(2)}) collective-permute-start(bf16[512,640]{1,0:T(8,128)(2,1)S(1)} %collective-permute-done.2), channel_id=1, source_target_pairs={{8,0},{16,24},{9,1},{17,25},{10,2},{18,26},{11,3},{19,27},{12,4},{... | collective-permute-start | bytes 1966088 | tf_op jit(solution)/shard_map/ppermute | solution.py:51
  101.5 74.0 %copy-start.6 = (bf16[256,2048]{1,0:T(8,128)(2,1)S(1)}, bf16[256,2048]{1,0:T(8,128)(2,1)}, u32[]{:S(2)}) copy-start(bf16[256,2048]{1,0:T(8,128)(2,1)} %copy-done.5) | copy-start | bytes 3145732
  101.5 331.3 %all-gather.7.cloned.1.call-start = ((), (), s32[]{:S(2)}) async-start(), calls=%async_computation.6 | async-start | bytes 9437184 | tf_op jit(solution)/shard_map/all_gather | solution.py:531
  177.2 419.3 %copy-start.108 = (f32[256]{0:T(256)}, f32[256]{0:T(256)S(1)}, u32[]{:S(2)}) copy-start(f32[256]{0:T(256)S(1)} %get-tuple-element.416) | copy-start | bytes 3076
  177.2 419.3 %copy-start.112 = (f32[256]{0:T(256)}, f32[256]{0:T(256)S(1)}, u32[]{:S(2)}) copy-start(f32[256]{0:T(256)S(1)} %get-tuple-element.415) | copy-start | bytes 3076
  178.7 269.5 %all-gather.9.cloned.1.call-start = ((), (), s32[]{:S(2)}) async-start(), calls=%async_computation.8 | async-start | bytes 9437184 | tf_op jit(solution)/shard_map/all_gather | solution.py:522
  182.1 412.4 %reduce-scatter.9.cloned.1.call-start = ((), (), s32[]{:S(2)}) async-start(), calls=%async_computation.9 | async-start | bytes 9437184 | tf_op jit(solution)/shard_map/reduce_scatter | solution.py:557
  200.3 28.4 %collective-permute-start.7 = (bf16[256,1536]{0,1:T(8,128)(2,1)S(1)}, bf16[256,1536]{0,1:T(8,128)(2,1)S(1)}, u32[]{:S(2)}, u32[]{:S(2)}) collective-permute-start(bf16[256,1536]{0,1:T(8,128)(2,1)S(1)} %pad_maximum_fusion.20), channel_id=1, source_target_pairs={{0,4},{4,0},{1,5},{5,1},{2,6},{6,2},{3,7},{7,3},{8,12},{12,8},{9,1... | collective-permute-start | bytes 2359304 | tf_op jit(solution)/shard_map/ppermute | solution.py:124
  201.5 56.7 %collective-permute-start.13 = (bf16[256,1536]{0,1:T(8,128)(2,1)S(1)}, bf16[256,1536]{0,1:T(8,128)(2,1)S(1)}, u32[]{:S(2)}, u32[]{:S(2)}) collective-permute-start(bf16[256,1536]{0,1:T(8,128)(2,1)S(1)} %pad_maximum_fusion.22), channel_id=1, source_target_pairs={{0,4},{4,0},{1,5},{5,1},{2,6},{6,2},{3,7},{7,3},{8,12},{12,8},{9,1... | collective-permute-start | bytes 2359304 | tf_op jit(solution)/shard_map/ppermute | solution.py:124
  229.2 34.7 %collective-permute-start.8 = (bf16[512,1536]{0,1:T(8,128)(2,1)S(1)}, bf16[512,1536]{0,1:T(8,128)(2,1)S(1)}, u32[]{:S(2)}, u32[]{:S(2)}) collective-permute-start(bf16[512,1536]{0,1:T(8,128)(2,1)S(1)} %pad_maximum_fusion.10), channel_id=1, source_target_pairs={{0,8},{8,0},{16,24},{24,16},{1,9},{9,1},{17,25},{25,17},{2,10},{10... | collective-permute-start | bytes 4718600 | tf_op jit(solution)/shard_map/ppermute | solution.py:47
  229.3 36.4 %collective-permute-start.10 = (bf16[512,1536]{0,1:T(8,128)(2,1)S(1)}, bf16[512,1536]{0,1:T(8,128)(2,1)S(1)}, u32[]{:S(2)}, u32[]{:S(2)}) collective-permute-start(bf16[512,1536]{0,1:T(8,128)(2,1)S(1)} %pad_maximum_fusion.10), channel_id=1, source_target_pairs={{8,16},{16,8},{9,17},{17,9},{10,18},{18,10},{11,19},{19,11},{12,20... | collective-permute-start | bytes 4718600 | tf_op jit(solution)/shard_map/ppermute | solution.py:48
  258.7 36.6 %collective-permute-start.14 = (bf16[512,1536]{0,1:T(8,128)(2,1)S(1)}, bf16[512,1536]{0,1:T(8,128)(2,1)S(1)}, u32[]{:S(2)}, u32[]{:S(2)}) collective-permute-start(bf16[512,1536]{0,1:T(8,128)(2,1)S(1)} %pad_maximum_fusion.11), channel_id=1, source_target_pairs={{0,8},{8,0},{16,24},{24,16},{1,9},{9,1},{17,25},{25,17},{2,10},{10... | collective-permute-start | bytes 4718600 | tf_op jit(solution)/shard_map/ppermute | solution.py:47
  259.0 39.5 %collective-permute-start.16 = (bf16[512,1536]{0,1:T(8,128)(2,1)S(1)}, bf16[512,1536]{0,1:T(8,128)(2,1)S(1)}, u32[]{:S(2)}, u32[]{:S(2)}) collective-permute-start(bf16[512,1536]{0,1:T(8,128)(2,1)S(1)} %pad_maximum_fusion.11), channel_id=1, source_target_pairs={{8,16},{16,8},{9,17},{17,9},{10,18},{18,10},{11,19},{19,11},{12,20... | collective-permute-start | bytes 4718600 | tf_op jit(solution)/shard_map/ppermute | solution.py:48
  263.8 67.9 %collective-permute-start.9 = (bf16[512,1536]{0,1:T(8,128)(2,1)S(1)}, bf16[512,1536]{0,1:T(8,128)(2,1)S(1)}, u32[]{:S(2)}, u32[]{:S(2)}) collective-permute-start(bf16[512,1536]{0,1:T(8,128)(2,1)S(1)} %collective-permute-done.8), channel_id=1, source_target_pairs={{8,16},{16,8},{9,17},{17,9},{10,18},{18,10},{11,19},{19,11},{12,20... | collective-permute-start | bytes 4718600 | tf_op jit(solution)/shard_map/ppermute | solution.py:49
  265.7 67.4 %collective-permute-start.11 = (bf16[512,1536]{0,1:T(8,128)(2,1)S(1)}, bf16[512,1536]{0,1:T(8,128)(2,1)S(1)}, u32[]{:S(2)}, u32[]{:S(2)}) collective-permute-start(bf16[512,1536]{0,1:T(8,128)(2,1)S(1)} %collective-permute-done.10), channel_id=1, source_target_pairs={{8,0},{16,24},{9,1},{17,25},{10,2},{18,26},{11,3},{19,27},{12,4},{... | collective-permute-start | bytes 4718600 | tf_op jit(solution)/shard_map/ppermute | solution.py:50
  295.3 70.1 %collective-permute-start.15 = (bf16[512,1536]{0,1:T(8,128)(2,1)S(1)}, bf16[512,1536]{0,1:T(8,128)(2,1)S(1)}, u32[]{:S(2)}, u32[]{:S(2)}) collective-permute-start(bf16[512,1536]{0,1:T(8,128)(2,1)S(1)} %collective-permute-done.14), channel_id=1, source_target_pairs={{8,16},{16,8},{9,17},{17,9},{10,18},{18,10},{11,19},{19,11},{12,20... | collective-permute-start | bytes 4718600 | tf_op jit(solution)/shard_map/ppermute | solution.py:49
  298.4 68.4 %collective-permute-start.17 = (bf16[512,1536]{0,1:T(8,128)(2,1)S(1)}, bf16[512,1536]{0,1:T(8,128)(2,1)S(1)}, u32[]{:S(2)}, u32[]{:S(2)}) collective-permute-start(bf16[512,1536]{0,1:T(8,128)(2,1)S(1)} %collective-permute-done.16), channel_id=1, source_target_pairs={{8,0},{16,24},{9,1},{17,25},{10,2},{18,26},{11,3},{19,27},{12,4},{... | collective-permute-start | bytes 4718600 | tf_op jit(solution)/shard_map/ppermute | solution.py:50
  331.8 62.6 %collective-permute-start.12 = (bf16[512,1536]{0,1:T(8,128)(2,1)S(1)}, bf16[512,1536]{0,1:T(8,128)(2,1)S(1)}, u32[]{:S(2)}, u32[]{:S(2)}) collective-permute-start(bf16[512,1536]{0,1:T(8,128)(2,1)S(1)} %collective-permute-done.9), channel_id=1, source_target_pairs={{8,0},{16,24},{9,1},{17,25},{10,2},{18,26},{11,3},{19,27},{12,4},{... | collective-permute-start | bytes 4718600 | tf_op jit(solution)/shard_map/ppermute | solution.py:51
  365.5 62.6 %collective-permute-start.18 = (bf16[512,1536]{0,1:T(8,128)(2,1)S(1)}, bf16[512,1536]{0,1:T(8,128)(2,1)S(1)}, u32[]{:S(2)}, u32[]{:S(2)}) collective-permute-start(bf16[512,1536]{0,1:T(8,128)(2,1)S(1)} %collective-permute-done.15), channel_id=1, source_target_pairs={{8,0},{16,24},{9,1},{17,25},{10,2},{18,26},{11,3},{19,27},{12,4},{... | collective-permute-start | bytes 4718600 | tf_op jit(solution)/shard_map/ppermute | solution.py:51
  516.6 136.8 %all-gather.11.cloned.1.call-start = ((), (), s32[]{:S(2)}) async-start(), calls=%async_computation.10 | async-start | bytes 9437184 | tf_op jit(solution)/shard_map/all_gather | solution.py:567
  598.4 441.0 %reduce-scatter.11.cloned.1.call-start = ((), (), s32[]{:S(2)}) async-start(), calls=%async_computation.11 | async-start | bytes 9437184 | tf_op jit(solution)/shard_map/reduce_scatter | solution.py:573
  694.8 346.4 %reduce-scatter.7.cloned.1.call-start = ((), (), s32[]{:S(2)}) async-start(), calls=%async_computation.7 | async-start | bytes 9437184 | tf_op jit(solution)/shard_map/reduce_scatter | solution.py:562
  698.7 50.5 %collective-permute-start.25 = (bf16[512,1536]{0,1:T(8,128)(2,1)}, bf16[512,1536]{0,1:T(8,128)(2,1)}, u32[]{:S(2)}, u32[]{:S(2)}) collective-permute-start(bf16[512,1536]{0,1:T(8,128)(2,1)} %maximum_maximum_fusion), channel_id=1, source_target_pairs={{0,8},{24,16},{1,9},{25,17},{2,10},{26,18},{3,11},{27,19},{4,12},{... | collective-permute-start | bytes 4718600 | tf_op jit(solution)/shard_map/ppermute | solution.py:69
  730.7 39.8 %collective-permute-start.30 = (bf16[512,1536]{0,1:T(8,128)(2,1)}, bf16[512,1536]{0,1:T(8,128)(2,1)}, u32[]{:S(2)}, u32[]{:S(2)}) collective-permute-start(bf16[512,1536]{0,1:T(8,128)(2,1)} %maximum_maximum_fusion.1), channel_id=1, source_target_pairs={{0,8},{24,16},{1,9},{25,17},{2,10},{26,18},{3,11},{27,19},{4,12},{... | collective-permute-start | bytes 4718600 | tf_op jit(solution)/shard_map/ppermute | solution.py:69
  751.7 37.4 %collective-permute-start.26 = (bf16[512,1536]{0,1:T(8,128)(2,1)S(1)}, bf16[512,1536]{0,1:T(8,128)(2,1)S(1)}, u32[]{:S(2)}, u32[]{:S(2)}) collective-permute-start(bf16[512,1536]{0,1:T(8,128)(2,1)S(1)} %add_convert_fusion.7), channel_id=1, source_target_pairs={{8,16},{16,8},{9,17},{17,9},{10,18},{18,10},{11,19},{19,11},{12,20... | collective-permute-start | bytes 4718600 | tf_op jit(solution)/shard_map/ppermute | solution.py:71
  754.8 49.2 %collective-permute-start.28 = (bf16[512,1536]{0,1:T(8,128)(2,1)S(1)}, bf16[512,1536]{0,1:T(8,128)(2,1)S(1)}, u32[]{:S(2)}, u32[]{:S(2)}) collective-permute-start(bf16[512,1536]{0,1:T(8,128)(2,1)S(1)} %add_convert_fusion.7), channel_id=1, source_target_pairs={{0,8},{24,16},{1,9},{25,17},{2,10},{26,18},{3,11},{27,19},{4,12},{... | collective-permute-start | bytes 4718600 | tf_op jit(solution)/shard_map/ppermute | solution.py:72
  772.6 50.2 %collective-permute-start.31 = (bf16[512,1536]{0,1:T(8,128)(2,1)S(1)}, bf16[512,1536]{0,1:T(8,128)(2,1)S(1)}, u32[]{:S(2)}, u32[]{:S(2)}) collective-permute-start(bf16[512,1536]{0,1:T(8,128)(2,1)S(1)} %add_convert_fusion.4), channel_id=1, source_target_pairs={{8,16},{16,8},{9,17},{17,9},{10,18},{18,10},{11,19},{19,11},{12,20... | collective-permute-start | bytes 4718600 | tf_op jit(solution)/shard_map/ppermute | solution.py:71
  784.4 53.4 %collective-permute-start.33 = (bf16[512,1536]{0,1:T(8,128)(2,1)S(1)}, bf16[512,1536]{0,1:T(8,128)(2,1)S(1)}, u32[]{:S(2)}, u32[]{:S(2)}) collective-permute-start(bf16[512,1536]{0,1:T(8,128)(2,1)S(1)} %add_convert_fusion.4), channel_id=1, source_target_pairs={{0,8},{24,16},{1,9},{25,17},{2,10},{26,18},{3,11},{27,19},{4,12},{... | collective-permute-start | bytes 4718600 | tf_op jit(solution)/shard_map/ppermute | solution.py:72
  790.8 32.0 %copy-start.33 = (bf16[512,1024]{0,1:T(8,128)(2,1)S(1)}, bf16[512,1024]{0,1:T(8,128)(2,1)}, u32[]{:S(2)}) copy-start(bf16[512,1024]{0,1:T(8,128)(2,1)} %get-tuple-element.223) | copy-start | bytes 3145732
  790.8 32.0 %copy-start.74 = (bf16[256,256]{0,1:T(8,128)(2,1)S(1)}, bf16[256,256]{0,1:T(8,128)(2,1)}, u32[]{:S(2)}) copy-start(bf16[256,256]{0,1:T(8,128)(2,1)} %get-tuple-element.249) | copy-start | bytes 393220
  790.8 32.1 %copy-start.75 = (bf16[256,256]{0,1:T(8,128)(2,1)S(1)}, bf16[256,256]{0,1:T(8,128)(2,1)}, u32[]{:S(2)}) copy-start(bf16[256,256]{0,1:T(8,128)(2,1)} %get-tuple-element.250) | copy-start | bytes 393220
  790.8 32.1 %copy-start.76 = (bf16[256,256]{0,1:T(8,128)(2,1)S(1)}, bf16[256,256]{0,1:T(8,128)(2,1)}, u32[]{:S(2)}) copy-start(bf16[256,256]{0,1:T(8,128)(2,1)} %get-tuple-element.251) | copy-start | bytes 393220
  790.8 32.1 %copy-start.77 = (bf16[256,256]{0,1:T(8,128)(2,1)S(1)}, bf16[256,256]{0,1:T(8,128)(2,1)}, u32[]{:S(2)}) copy-start(bf16[256,256]{0,1:T(8,128)(2,1)} %get-tuple-element.252) | copy-start | bytes 393220
  790.8 80.8 %collective-permute-start.27 = (bf16[512,1536]{0,1:T(8,128)(2,1)}, bf16[512,1536]{0,1:T(8,128)(2,1)}, u32[]{:S(2)}, u32[]{:S(2)}) collective-permute-start(bf16[512,1536]{0,1:T(8,128)(2,1)} %add_convert_fusion.6), channel_id=1, source_target_pairs={{0,8},{8,0},{16,24},{24,16},{1,9},{9,1},{17,25},{25,17},{2,10},{10... | collective-permute-start | bytes 4718600 | tf_op jit(solution)/shard_map/ppermute | solution.py:75
  805.7 65.9 %collective-permute-start.29 = (bf16[512,1536]{0,1:T(8,128)(2,1)}, bf16[512,1536]{0,1:T(8,128)(2,1)}, u32[]{:S(2)}, u32[]{:S(2)}) collective-permute-start(bf16[512,1536]{0,1:T(8,128)(2,1)} %add_convert_fusion.5), channel_id=1, source_target_pairs={{8,16},{16,8},{9,17},{17,9},{10,18},{18,10},{11,19},{19,11},{12,20... | collective-permute-start | bytes 4718600 | tf_op jit(solution)/shard_map/ppermute | solution.py:76
  824.5 80.8 %collective-permute-start.32 = (bf16[512,1536]{0,1:T(8,128)(2,1)}, bf16[512,1536]{0,1:T(8,128)(2,1)}, u32[]{:S(2)}, u32[]{:S(2)}) collective-permute-start(bf16[512,1536]{0,1:T(8,128)(2,1)} %add_convert_fusion.3), channel_id=1, source_target_pairs={{0,8},{8,0},{16,24},{24,16},{1,9},{9,1},{17,25},{25,17},{2,10},{10... | collective-permute-start | bytes 4718600 | tf_op jit(solution)/shard_map/ppermute | solution.py:75
  839.5 65.8 %collective-permute-start.34 = (bf16[512,1536]{0,1:T(8,128)(2,1)}, bf16[512,1536]{0,1:T(8,128)(2,1)}, u32[]{:S(2)}, u32[]{:S(2)}) collective-permute-start(bf16[512,1536]{0,1:T(8,128)(2,1)} %add_convert_fusion.2), channel_id=1, source_target_pairs={{8,16},{16,8},{9,17},{17,9},{10,18},{18,10},{11,19},{19,11},{12,20... | collective-permute-start | bytes 4718600 | tf_op jit(solution)/shard_map/ppermute | solution.py:76
  874.1 31.2 %copy-start.31 = (bf16[512,1024]{0,1:T(8,128)(2,1)S(1)}, bf16[512,1024]{0,1:T(8,128)(2,1)}, u32[]{:S(2)}) copy-start(bf16[512,1024]{0,1:T(8,128)(2,1)} %get-tuple-element.220) | copy-start | bytes 3145732
  874.1 31.2 %copy-start.60 = (bf16[256,256]{0,1:T(8,128)(2,1)S(1)}, bf16[256,256]{0,1:T(8,128)(2,1)}, u32[]{:S(2)}) copy-start(bf16[256,256]{0,1:T(8,128)(2,1)} %get-tuple-element.240) | copy-start | bytes 393220
  874.1 31.2 %copy-start.61 = (bf16[256,256]{0,1:T(8,128)(2,1)S(1)}, bf16[256,256]{0,1:T(8,128)(2,1)}, u32[]{:S(2)}) copy-start(bf16[256,256]{0,1:T(8,128)(2,1)} %get-tuple-element.253) | copy-start | bytes 393220
  874.1 31.2 %copy-start.62 = (bf16[256,256]{0,1:T(8,128)(2,1)S(1)}, bf16[256,256]{0,1:T(8,128)(2,1)}, u32[]{:S(2)}) copy-start(bf16[256,256]{0,1:T(8,128)(2,1)} %get-tuple-element.254) | copy-start | bytes 393220
  874.1 31.2 %copy-start.63 = (bf16[256,256]{0,1:T(8,128)(2,1)S(1)}, bf16[256,256]{0,1:T(8,128)(2,1)}, u32[]{:S(2)}) copy-start(bf16[256,256]{0,1:T(8,128)(2,1)} %get-tuple-element.255) | copy-start | bytes 393220
  874.3 37.1 %collective-permute-start.35 = (bf16[256,1536]{0,1:T(8,128)(2,1)S(1)}, bf16[256,1536]{0,1:T(8,128)(2,1)S(1)}, u32[]{:S(2)}, u32[]{:S(2)}) collective-permute-start(bf16[256,1536]{0,1:T(8,128)(2,1)S(1)} %select_convert_fusion.1), channel_id=1, source_target_pairs={{0,4},{4,0},{1,5},{5,1},{2,6},{6,2},{3,7},{7,3},{8,12},{12,8},{9,1... | collective-permute-start | bytes 2359304 | tf_op jit(solution)/shard_map/ppermute | solution.py:195
  908.0 27.9 %collective-permute-start.36 = (bf16[256,1536]{0,1:T(8,128)(2,1)S(1)}, bf16[256,1536]{0,1:T(8,128)(2,1)S(1)}, u32[]{:S(2)}, u32[]{:S(2)}) collective-permute-start(bf16[256,1536]{0,1:T(8,128)(2,1)S(1)} %select_convert_fusion), channel_id=1, source_target_pairs={{0,4},{4,0},{1,5},{5,1},{2,6},{6,2},{3,7},{7,3},{8,12},{12,8},{9,1... | collective-permute-start | bytes 2359304 | tf_op jit(solution)/shard_map/ppermute | solution.py:195
  945.8 2.7 collective-permute-start.37
  948.5 3.6 collective-permute-start.38
  952.1 3.8 collective-permute-start.39
  954.6 13.9 %collective-permute-start.19 = (bf16[512,640]{1,0:T(8,128)(2,1)S(1)}, bf16[512,640]{1,0:T(8,128)(2,1)S(1)}, u32[]{:S(2)}, u32[]{:S(2)}) collective-permute-start(bf16[512,640]{1,0:T(8,128)(2,1)S(1)} %maximum_maximum_fusion.2), channel_id=1, source_target_pairs={{0,8},{24,16},{1,9},{25,17},{2,10},{26,18},{3,11},{27,19},{4,12},{... | collective-permute-start | bytes 1966088 | tf_op jit(solution)/shard_map/ppermute | solution.py:69
  955.9 9.8 collective-permute-start.40
  966.3 43.0 %collective-permute-start.41 = (f32[2,2048]{1,0:T(2,128)}, f32[2,2048]{1,0:T(2,128)}, u32[]{:S(2)}, u32[]{:S(2)}) collective-permute-start(f32[2,2048]{1,0:T(2,128)} %add.313), channel_id=1, source_target_pairs={{0,2},{1,3},{2,0},{3,1},{4,6},{5,7},{6,4},{7,5},{8,10},{9,11},{10,... | collective-permute-start | bytes 49160 | tf_op jit(solution)/shard_map/ppermute | solution.py:455
  969.6 40.5 %collective-permute-start.20 = (bf16[512,640]{1,0:T(8,128)(2,1)}, bf16[512,640]{1,0:T(8,128)(2,1)}, u32[]{:S(2)}, u32[]{:S(2)}) collective-permute-start(bf16[512,640]{1,0:T(8,128)(2,1)} %add_convert_fusion.11), channel_id=1, source_target_pairs={{8,16},{16,8},{9,17},{17,9},{10,18},{18,10},{11,19},{19,11},{12,20... | collective-permute-start | bytes 1966088 | tf_op jit(solution)/shard_map/ppermute | solution.py:71
  972.3 42.1 %collective-permute-start.22 = (bf16[512,640]{1,0:T(8,128)(2,1)}, bf16[512,640]{1,0:T(8,128)(2,1)}, u32[]{:S(2)}, u32[]{:S(2)}) collective-permute-start(bf16[512,640]{1,0:T(8,128)(2,1)} %add_convert_fusion.11), channel_id=1, source_target_pairs={{0,8},{24,16},{1,9},{25,17},{2,10},{26,18},{3,11},{27,19},{4,12},{... | collective-permute-start | bytes 1966088 | tf_op jit(solution)/shard_map/ppermute | solution.py:72
  1011.4 12.2 %collective-permute-start.21 = (bf16[512,640]{1,0:T(8,128)(2,1)S(1)}, bf16[512,640]{1,0:T(8,128)(2,1)S(1)}, u32[]{:S(2)}, u32[]{:S(2)}) collective-permute-start(bf16[512,640]{1,0:T(8,128)(2,1)S(1)} %add_convert_fusion.10), channel_id=1, source_target_pairs={{0,8},{8,0},{16,24},{24,16},{1,9},{9,1},{17,25},{25,17},{2,10},{10... | collective-permute-start | bytes 1966088 | tf_op jit(solution)/shard_map/ppermute | solution.py:75
  1015.6 12.0 %collective-permute-start.23 = (bf16[512,640]{1,0:T(8,128)(2,1)S(1)}, bf16[512,640]{1,0:T(8,128)(2,1)S(1)}, u32[]{:S(2)}, u32[]{:S(2)}) collective-permute-start(bf16[512,640]{1,0:T(8,128)(2,1)S(1)} %add_convert_fusion.9), channel_id=1, source_target_pairs={{8,16},{16,8},{9,17},{17,9},{10,18},{18,10},{11,19},{19,11},{12,20... | collective-permute-start | bytes 1966088 | tf_op jit(solution)/shard_map/ppermute | solution.py:76
  1028.1 6.2 collective-permute-start.24
  (114 other events, 903.9 us)
Sparse Core Ops, SparseCore 0:
  12.4 55.9 all-gather.4
  101.6 73.8 reduce-scatter.4
  178.9 77.0 all-gather.6
  257.8 54.4 all-gather.8
  516.7 77.7 reduce-scatter.8
  598.5 54.7 all-gather.10
  694.9 70.8 reduce-scatter.10
  853.5 92.2 reduce-scatter.6

commit v2 on v1

v2 whole, which is shorter than its diff:
```python
import functools

import jax
import jax.numpy as jnp
from jax import lax
from jax.experimental import pallas as pl
from jax.experimental.pallas import tpu as pltpu
from jax.sharding import Mesh
from jax.sharding import PartitionSpec as P

HD = 64
LEN = 512
STEP = 5
CHUNKS = 2

NORM_EPS = 1e-05
ROPE_BASE = 500000.0
BETA_ONE = 0.9
BETA_TWO = 0.95
LEARN_RATE = 0.02
GAIN_RATE = 0.5
WEIGHT_DECAY = 0.1
ADAM_EPS = 1e-08

LOW = jnp.bfloat16
F32 = jnp.float32
MIB = 1024 * 1024

NEAR = [(0, 1), (1, 0), (2, 3), (3, 2)]
MIDDLE = [(1, 2), (2, 1)]
OUTWARD = [(1, 0), (2, 3)]
INWARD = [(0, 1), (3, 2)]
PAIR = [(0, 1), (1, 0)]


def dot(lhs, rhs, lhs_dim, rhs_dim):
    return lax.dot_general(
        lhs, rhs, (((lhs_dim,), (rhs_dim,)), ((), ())), preferred_element_type=F32
    )


def cat(parts, axis):
    return jnp.concatenate(parts, axis)


def after(value, *earlier):
    return lax.optimization_barrier((value, earlier))[0]


def line_near(own):
    return lax.ppermute(own, "do", NEAR), lax.ppermute(own, "do", MIDDLE)


def line_far(near, across):
    return lax.ppermute(near, "do", MIDDLE), lax.ppermute(across, "do", OUTWARD)


def line_last(across_near):
    return lax.ppermute(across_near, "do", OUTWARD)


def add(part, *arrived):
    total = part.astype(F32)
    for piece in arrived:
        total = total + piece.astype(F32)
    return total


def sum_far(parts):
    return lax.ppermute(parts[3], "do", INWARD)


def sum_middle(parts, far):
    second = add(parts[2], far).astype(LOW)
    return lax.ppermute(second, "do", MIDDLE), lax.ppermute(second, "do", INWARD)


def sum_near(parts, crossed, inward):
    first = add(parts[1], crossed).astype(LOW)
    third = add(parts[3], inward).astype(LOW)
    return lax.ppermute(first, "do", NEAR), lax.ppermute(third, "do", MIDDLE)


def sum_own(parts, from_near, from_across):
    return add(parts[0], from_near, from_across)


class Plan:
    def __init__(self, outer, per_device):
        self.rows = per_device
        self.block = 2 * per_device
        self.line = outer == 4 and per_device == 256

    def reorder(self, values):
        if not self.line:
            return values
        place = lax.axis_index("do")
        quarter = values.shape[-1] // 4
        a, b, c, d = (values[..., i * quarter : (i + 1) * quarter] for i in range(4))
        values = jnp.where(place % 2 == 1, cat([b, a, d, c], -1), values)
        half = 2 * quarter
        turned = cat([values[..., half:], values[..., :half]], -1)
        return jnp.where(place >= 2, turned, values)

    def by_x(self, low, high):
        return jnp.where(lax.axis_index("di") == 0, low, high)

    def inner(self):
        place = lax.axis_index("do")
        return ((place == 1) | (place == 2)).astype(jnp.int32).reshape(1)

    def blocks(self, row_part, col_part):
        if not self.line:
            out = []
            for (own, other), axis in ((row_part, 0), (col_part, 1)):
                theirs = lax.ppermute(other, "di", PAIR)
                out.append(cat([self.by_x(own, theirs), self.by_x(theirs, own)], axis))
            return tuple(out)
        rows = self.rows

        def pack(which):
            side = col_part[which]
            pieces = [side[i : i + rows] for i in range(0, side.shape[0], rows)]
            return cat([row_part[which]] + pieces, 1)

        mine, other = pack(0), pack(1)
        theirs = lax.ppermute(other, "di", PAIR)
        return cat([self.by_x(mine, theirs), self.by_x(theirs, mine)], 0)

    def plain_gather(self, blocks):
        return (
            lax.all_gather(blocks[0], "do", axis=0, tiled=True),
            lax.all_gather(blocks[1], "do", axis=1, tiled=True),
        )

    def plain_sum(self, grads):
        row, col = grads
        row = lax.psum_scatter(row, "do", scatter_dimension=0, tiled=True)
        col = lax.psum_scatter(col, "do", scatter_dimension=1, tiled=True)
        rows = self.rows
        return self.trade(row[:rows], row[rows:]), self.trade(col[:, :rows], col[:, rows:])

    def unpack(self, total, wide):
        rows = self.rows
        mine, theirs = self.trade(total[:rows], total[rows:])
        cuts = range(wide, total.shape[1], rows)
        return (
            (mine[:, :wide], theirs[:, :wide]),
            tuple(cat([side[:, i : i + rows] for i in cuts], 0) for side in (mine, theirs)),
        )

    def trade(self, low, high):
        mine = self.by_x(low, high).astype(F32)
        theirs = lax.ppermute(self.by_x(high, low).astype(LOW), "di", PAIR)
        return mine, theirs.astype(F32)


ANY = pl.BlockSpec(memory_space=pl.ANY)
SMALL = pl.CostEstimate(flops=1, bytes_accessed=1, transcendentals=0)


class Loader:
    def __init__(self, plan, weights, row_shape, col_shape):
        self.plan, self.row_shape, self.col_shape = plan, row_shape, col_shape
        rows, wide = plan.rows, row_shape[1]
        self.moves = []
        if plan.line:
            self.operands = [plan.inner(), *weights]
            for k in range(4):
                at = k * plan.block
                self.moves.append((k, 0, (0, 0), (at, 0), (plan.block, wide)))
                for i in range(0, col_shape[0], rows):
                    for x in range(2):
                        self.moves.append(
                            (k, 1, (x * rows, wide + i), (i, at + x * rows), (rows, rows))
                        )
        else:
            self.operands = list(weights)
            self.moves.append((0, 0, (0, 0), (0, 0), row_shape))
            self.moves.append((1, 1, (0, 0), (0, 0), col_shape))
        self.count = len(self.operands)

    def specs(self):
        if not self.plan.line:
            return [ANY] * 2
        return [pl.BlockSpec(memory_space=pltpu.SMEM)] + [ANY] * 6

    def scratch(self):
        return [
            pltpu.VMEM(self.row_shape, LOW),
            pltpu.VMEM(self.col_shape, LOW),
            pltpu.SemaphoreType.DMA((len(self.moves),)),
        ]

    def load(self, refs, row_ref, col_ref, sems):
        def copies(sources, chosen):
            made = []
            for i, (k, which, here, there, size) in enumerate(self.moves):
                if k in chosen:
                    target = (row_ref, col_ref)[which]
                    made.append(
                        pltpu.make_async_copy(
                            sources[k].at[pl.ds(here[0], size[0]), pl.ds(here[1], size[1])],
                            target.at[pl.ds(there[0], size[0]), pl.ds(there[1], size[1])],
                            sems.at[i],
                        )
                    )
            return made

        if not self.plan.line:
            for copy in copies(refs, (0, 1)):
                copy.start()
            for copy in copies(refs, (0, 1)):
                copy.wait()
            return
        inner, own, near, across_near, out, across, out_near = refs
        is_inner = inner[0] == 1
        for copy in copies((own, near), (0, 1)):
            copy.start()

        @pl.when(is_inner)
        def _():
            for copy in copies((None, None, across_near, across), (2, 3)):
                copy.start()

        @pl.when(jnp.logical_not(is_inner))
        def _():
            for copy in copies((None, None, out, out_near), (2, 3)):
                copy.start()

        for copy in copies((own, near, out, out_near), (0, 1, 2, 3)):
            copy.wait()


def pack_grads(plan, row_grad, col_grad, out_refs):
    if not plan.line:
        out_refs[0][...] = row_grad[...].astype(LOW)
        out_refs[1][...] = col_grad[...].astype(LOW)
        return
    rows, block, wide = plan.rows, plan.block, row_grad.shape[1]
    for k, out in enumerate(out_refs):
        at = k * block
        out[:, :wide] = row_grad[at : at + block, :].astype(LOW)
        for i in range(0, col_grad.shape[0], rows):
            for x in range(2):
                out[x * rows : (x + 1) * rows, wide + i : wide + i + rows] = col_grad[
                    i : i + rows, at + x * rows : at + (x + 1) * rows
                ].astype(LOW)


def packed_shapes(plan, row_shape, col_shape):
    if not plan.line:
        return [row_shape, col_shape]
    return [(plan.block, row_shape[1] + col_shape[0])] * 4


def rope_tables(positions):
    half_dim = HD // 2
    inverse_freq = ROPE_BASE ** (-2.0 * jnp.arange(half_dim, dtype=F32) / HD)
    angles = positions.astype(F32)[:, None] * inverse_freq[None, :]
    cosine, sine = jnp.cos(angles), jnp.sin(angles)
    return cat([cosine] * 4, 1), cat([-sine, sine] * 2, 1)


def lanes_of(shape):
    return lax.broadcasted_iota(jnp.int32, shape, 1)


def shuffle_halves(values):
    wide = values.shape[1]
    up = pltpu.roll(values, wide - HD // 2, 1)
    down = pltpu.roll(values, HD // 2, 1)
    return jnp.where(lanes_of(values.shape) % HD < HD // 2, up, down)


def tables(cos_ref, sin_ref, pairs):
    cosine, sine = cos_ref[...], sin_ref[...]
    is_key = lanes_of(cosine.shape) < HD
    return (
        cat([cosine] * pairs + [jnp.where(is_key, cosine, 1.0)], 1),
        cat([sine] * pairs + [jnp.where(is_key, sine, 0.0)], 1),
    )


def split_kv(both):
    is_key = lanes_of(both.shape) < HD
    blank = jnp.zeros_like(both)
    key_low = jnp.where(is_key, both, blank)
    value_high = jnp.where(is_key, blank, both)
    return (
        (key_low, pltpu.roll(key_low.astype(F32), HD, 1).astype(LOW)),
        (pltpu.roll(value_high.astype(F32), HD, 1).astype(LOW), value_high),
    )


def allowed_pairs(seg_col, seg_row):
    shape = (seg_col.shape[0], seg_row.shape[1])
    key_at = lax.broadcasted_iota(jnp.int32, shape, 1)
    query_at = lax.broadcasted_iota(jnp.int32, shape, 0)
    return (seg_col == seg_row) & (key_at <= query_at)


def attn_forward_kernel(pairs, loader, *refs):
    weights, refs = refs[: loader.count], refs[loader.count :]
    x_ref, cos_ref, sin_ref, col_ref, row_ref = refs[:5]
    part_ref, ctx_ref, q_ref, kv_ref, lse_ref, wqkv_ref, wout_ref, sems = refs[5:]

    @pl.when(pl.program_id(0) == 0)
    def _():
        loader.load(weights, wqkv_ref, wout_ref, sems)

    cosine, sine = tables(cos_ref, sin_ref, pairs)
    qkv = dot(x_ref[...], wqkv_ref[...], 1, 0)
    rotated = (qkv * cosine + shuffle_halves(qkv) * sine).astype(LOW)
    queries, both = rotated[:, : pairs * 128], rotated[:, pairs * 128 :]
    q_ref[...] = queries
    kv_ref[...] = both
    keys, values = split_kv(both)
    allowed = allowed_pairs(col_ref[...], row_ref[0])
    lane = lanes_of((both.shape[0], 128))
    log_sums = jnp.zeros((both.shape[0], 128), F32)
    contexts = []
    for pair in range(pairs):
        heads = queries[:, pair * 128 : (pair + 1) * 128]
        context = None
        for side in range(2):
            scores = dot(heads, keys[side], 1, 1) * HD**-0.5
            masked = jnp.where(allowed, scores, -1e30)
            top = jnp.max(masked, axis=1, keepdims=True)
            weights = jnp.exp(masked - top)
            totals = jnp.sum(weights, axis=1, keepdims=True)
            probs = (weights * (1.0 / totals)).astype(LOW)
            piece = dot(probs, values[side], 1, 0)
            context = piece if context is None else context + piece
            log_sums = jnp.where(lane == 2 * pair + side, top + jnp.log(totals), log_sums)
        contexts.append(context.astype(LOW))
    lse_ref[...] = log_sums
    context_low = cat(contexts, 1)
    ctx_ref[...] = context_low
    part_ref[...] = dot(context_low, wout_ref[...], 1, 0).astype(LOW)


def attn_backward_kernel(pairs, loader, *refs):
    weights, refs = refs[: loader.count], refs[loader.count :]
    res_ref, x_ref, ctx_ref, q_ref, kv_ref, lse_ref, cos_ref, sin_ref, col_ref, row_ref = refs[:10]
    part_ref, gain_ref, *grad_refs = refs[10:-5]
    wqkv_ref, wout_ref, sems, acc_qkv, acc_out = refs[-5:]
    step = pl.program_id(0)

    @pl.when(step == 0)
    def _():
        loader.load(weights, wqkv_ref, wout_ref, sems)
        acc_qkv[...] = jnp.zeros_like(acc_qkv)
        acc_out[...] = jnp.zeros_like(acc_out)

    cosine, sine = tables(cos_ref, sin_ref, pairs)
    scale = HD**-0.5
    res = res_ref[...]
    acc_out[...] += dot(ctx_ref[...], res, 0, 0)
    ctx_grad = dot(res, wout_ref[...], 1, 1).astype(LOW)
    keys, values = split_kv(kv_ref[...])
    allowed = allowed_pairs(col_ref[...], row_ref[0])
    lane = lanes_of((res.shape[0], 128))
    log_sums = lse_ref[...]
    query_grads, key_grad, value_grad = [], None, None
    for pair in range(pairs):
        heads = q_ref[:, pair * 128 : (pair + 1) * 128]
        grads = ctx_grad[:, pair * 128 : (pair + 1) * 128]
        query_grad = None
        for side in range(2):
            here = (lane < HD) if side == 0 else (lane >= HD)
            head = jnp.where(here, heads, jnp.zeros_like(heads))
            grad = jnp.where(here, grads, jnp.zeros_like(grads))
            at = 2 * pair + side
            scores = dot(heads, keys[side], 1, 1) * scale
            probs = jnp.where(allowed, jnp.exp(scores - log_sums[:, at : at + 1]), 0.0)
            prob_grad = dot(grads, values[side], 1, 1)
            delta = jnp.sum(probs * prob_grad, axis=1, keepdims=True)
            score_grad = (probs * (prob_grad - delta)).astype(LOW)
            to_value = dot(probs.astype(LOW), grad, 0, 0)
            to_key = dot(score_grad, head, 0, 0)
            to_query = dot(score_grad, keys[side], 1, 0)
            value_grad = to_value if value_grad is None else value_grad + to_value
            key_grad = to_key if key_grad is None else key_grad + to_key
            query_grad = to_query if query_grad is None else query_grad + to_query
        query_grads.append(query_grad * scale)
    key_grad = (key_grad + pltpu.roll(key_grad, HD, 1)) * scale
    value_grad = value_grad + pltpu.roll(value_grad, HD, 1)
    joined = cat(query_grads + [jnp.where(lane < HD, key_grad, value_grad)], 1)
    low = (joined * cosine - shuffle_halves(joined) * sine).astype(LOW)
    part_ref[...] = dot(low, wqkv_ref[...], 1, 1).astype(LOW)
    acc_qkv[...] += dot(x_ref[...], low, 0, 0)

    @pl.when(step == pl.num_programs(0) - 1)
    def _():
        pack_grads(loader.plan, acc_qkv, acc_out, grad_refs)
        gain_ref[...] = jnp.sum(acc_qkv[...] * wqkv_ref[...].astype(F32), axis=1, keepdims=True)


def once(shape):
    return pl.BlockSpec(shape, lambda i: (0,) * len(shape), pipeline_mode=pl.Buffered(1))


def per_seq(shape):
    return pl.BlockSpec(shape, lambda i: (i,) + (0,) * (len(shape) - 1))


def attn_forward(loader, normed, cosine, sine, seg_col, seg_row):
    rows, width = normed.shape
    heads = loader.col_shape[0]
    return pl.pallas_call(
        functools.partial(attn_forward_kernel, heads // 128, loader),
        grid=(rows // LEN,),
        in_specs=[
            *loader.specs(),
            per_seq((LEN, width)),
            per_seq((LEN, 128)),
            per_seq((LEN, 128)),
            per_seq((LEN, 1)),
            per_seq((1, 1, LEN)),
        ],
        out_specs=[
            per_seq((LEN, width)),
            per_seq((LEN, heads)),
            per_seq((LEN, heads)),
            per_seq((LEN, 128)),
            per_seq((LEN, 128)),
        ],
        out_shape=[
            jax.ShapeDtypeStruct((rows, width), LOW),
            jax.ShapeDtypeStruct((rows, heads), LOW),
            jax.ShapeDtypeStruct((rows, heads), LOW),
            jax.ShapeDtypeStruct((rows, 128), LOW),
            jax.ShapeDtypeStruct((rows, 128), F32),
        ],
        scratch_shapes=loader.scratch(),
        compiler_params=pltpu.CompilerParams(vmem_limit_bytes=48 * MIB),
        cost_estimate=SMALL,
        name="attn_forward",
    )(*loader.operands, normed, cosine, sine, seg_col, seg_row)


def attn_backward(loader, res_all, normed, ctx, queries, both, lse, cosine, sine, seg_col, seg_row):
    rows, width = normed.shape
    heads = loader.col_shape[0]
    grads = packed_shapes(loader.plan, loader.row_shape, loader.col_shape)
    return pl.pallas_call(
        functools.partial(attn_backward_kernel, heads // 128, loader),
        grid=(rows // LEN,),
        in_specs=[
            *loader.specs(),
            per_seq((LEN, width)),
            per_seq((LEN, width)),
            per_seq((LEN, heads)),
            per_seq((LEN, heads)),
            per_seq((LEN, 128)),
            per_seq((LEN, 128)),
            per_seq((LEN, 128)),
            per_seq((LEN, 128)),
            per_seq((LEN, 1)),
            per_seq((1, 1, LEN)),
        ],
        out_specs=[per_seq((LEN, width)), once((width, 1))] + [once(shape) for shape in grads],
        out_shape=[
            jax.ShapeDtypeStruct((rows, width), LOW),
            jax.ShapeDtypeStruct((width, 1), F32),
        ]
        + [jax.ShapeDtypeStruct(shape, LOW) for shape in grads],
        scratch_shapes=[
            *loader.scratch(),
            pltpu.VMEM(loader.row_shape, F32),
            pltpu.VMEM(loader.col_shape, F32),
        ],
        compiler_params=pltpu.CompilerParams(vmem_limit_bytes=52 * MIB),
        cost_estimate=SMALL,
        name="attn_backward",
    )(*loader.operands, res_all, normed, ctx, queries, both, lse, cosine, sine, seg_col, seg_row)


TILE = 512


def ffn_main_kernel(loader, more, *refs):
    weights, refs = refs[: loader.count], refs[loader.count :]
    x_ref, grad_ref = refs[:2]
    back_ref, act_ref, both_ref, gate_up_ref, down_ref, sems = refs[2 + more :]

    @pl.when(pl.program_id(0) == 0)
    def _():
        loader.load(weights, gate_up_ref, down_ref, sems)

    hidden = down_ref.shape[0]
    pre = dot(x_ref[...], gate_up_ref[...], 1, 0)
    gate_pre, lifted = pre[:, :hidden], pre[:, hidden:]
    sigmoid_gate = jax.nn.sigmoid(gate_pre)
    silu_gate = gate_pre * sigmoid_gate
    act_ref[...] = (silu_gate * lifted).astype(LOW)
    act_grad = dot(grad_ref[...], down_ref[...], 1, 1)
    gate_grad = act_grad * lifted * sigmoid_gate * (1.0 + gate_pre * (1.0 - sigmoid_gate))
    both_grad = cat([gate_grad.astype(LOW), (act_grad * silu_gate).astype(LOW)], 1)
    both_ref[...] = both_grad
    back = dot(both_grad, gate_up_ref[...], 1, 1)
    if more:
        back = back + refs[2][...].astype(F32)
    back_ref[...] = back.astype(LOW)


def ffn_main(loader, tokens, grads, earlier):
    rows, width = tokens.shape
    hidden = loader.col_shape[0]
    more = [] if earlier is None else [earlier]
    return pl.pallas_call(
        functools.partial(ffn_main_kernel, loader, len(more)),
        grid=(rows // TILE,),
        in_specs=[
            *loader.specs(),
            per_seq((TILE, width)),
            per_seq((TILE, width)),
            *[per_seq((TILE, width))] * len(more),
        ],
        out_specs=[
            per_seq((TILE, width)),
            per_seq((TILE, hidden)),
            per_seq((TILE, 2 * hidden)),
        ],
        out_shape=[
            jax.ShapeDtypeStruct((rows, width), LOW),
            jax.ShapeDtypeStruct((rows, hidden), LOW),
            jax.ShapeDtypeStruct((rows, 2 * hidden), LOW),
        ],
        scratch_shapes=loader.scratch(),
        compiler_params=pltpu.CompilerParams(vmem_limit_bytes=58 * MIB),
        cost_estimate=SMALL,
        name="ffn_main",
    )(*loader.operands, tokens, grads, *more)


def ffn_weights_kernel(loader, more, *refs):
    weights, refs = refs[: loader.count], refs[loader.count :]
    x_ref, grad_ref, act_ref, both_ref = refs[:4]
    out_ref, gain_ref, *grad_refs = refs[4 + more : -5]
    gate_up_ref, down_ref, sems, acc_gate_up, acc_down = refs[-5:]
    step = pl.program_id(0)

    @pl.when(step == 0)
    def _():
        loader.load(weights, gate_up_ref, down_ref, sems)
        acc_gate_up[...] = jnp.zeros_like(acc_gate_up)
        acc_down[...] = jnp.zeros_like(acc_down)

    act = act_ref[...]
    acc_down[...] += dot(act, grad_ref[...], 0, 0)
    acc_gate_up[...] += dot(x_ref[...], both_ref[...], 0, 0)
    out = dot(act, down_ref[...], 1, 0)
    if more:
        out = out + refs[4][...].astype(F32)
    out_ref[...] = out.astype(LOW)

    @pl.when(step == pl.num_programs(0) - 1)
    def _():
        pack_grads(loader.plan, acc_gate_up, acc_down, grad_refs)
        gain_ref[...] = jnp.sum(
            acc_gate_up[...] * gate_up_ref[...].astype(F32), axis=1, keepdims=True
        )


def ffn_weights(loader, tokens, grads, act, both_grad, earlier):
    rows, width = tokens.shape
    hidden = loader.col_shape[0]
    more = [] if earlier is None else [earlier]
    packed = packed_shapes(loader.plan, loader.row_shape, loader.col_shape)
    return pl.pallas_call(
        functools.partial(ffn_weights_kernel, loader, len(more)),
        grid=(rows // TILE,),
        in_specs=[
            *loader.specs(),
            per_seq((TILE, width)),
            per_seq((TILE, width)),
            per_seq((TILE, hidden)),
            per_seq((TILE, 2 * hidden)),
            *[per_seq((TILE, width))] * len(more),
        ],
        out_specs=[per_seq((TILE, width)), once((width, 1))] + [once(shape) for shape in packed],
        out_shape=[
            jax.ShapeDtypeStruct((rows, width), LOW),
            jax.ShapeDtypeStruct((width, 1), F32),
        ]
        + [jax.ShapeDtypeStruct(shape, LOW) for shape in packed],
        scratch_shapes=[
            *loader.scratch(),
            pltpu.VMEM(loader.row_shape, F32),
            pltpu.VMEM(loader.col_shape, F32),
        ],
        compiler_params=pltpu.CompilerParams(vmem_limit_bytes=60 * MIB),
        cost_estimate=SMALL,
        name="ffn_weights",
    )(*loader.operands, tokens, grads, act, both_grad, *more)


def norm_rows(values, gain_vec):
    row_scale = lax.rsqrt(jnp.mean(values * values, axis=1, keepdims=True) + NORM_EPS)
    return values * row_scale * gain_vec, row_scale


def norm_back(row_grad, values, row_scale, gain_vec):
    scaled_grad = row_grad * gain_vec
    return row_scale * scaled_grad - values * row_scale**3 * jnp.mean(
        scaled_grad * values, axis=1, keepdims=True
    )


def adamw_update(master, grad_sum, first_mom, second_mom, decay_rate, step_rate):
    next_first = BETA_ONE * first_mom + (1.0 - BETA_ONE) * grad_sum
    next_second = BETA_TWO * second_mom + (1.0 - BETA_TWO) * grad_sum * grad_sum
    first_hat = next_first / (1.0 - BETA_ONE**STEP)
    second_hat = next_second / (1.0 - BETA_TWO**STEP)
    next_master = master - step_rate * (
        first_hat / (jnp.sqrt(second_hat) + ADAM_EPS) + decay_rate * master
    )
    return (next_master, next_first, next_second)


def sum_everywhere(values, sizes):
    for axis, size in sizes:
        step = 1
        while step < size:
            values = values + lax.ppermute(values, axis, [(i, i ^ step) for i in range(size)])
            step *= 2
    return values


def pick(index, low, high):
    return jnp.where(index == 0, low, high)


class Plane:
    def __init__(self, tp):
        self.tp = tp
        self.half = tp // 2
        self.x = lax.axis_index("di")
        self.y = lax.axis_index("tp") // self.half
        self.far = [(i, (i + self.half) % tp) for i in range(tp)]

    def swap_y(self, value):
        return lax.ppermute(value, "tp", self.far)

    def swap_x(self, value):
        return lax.ppermute(value, "di", PAIR)

    def swap_core(self, value):
        return lax.ppermute(value, "tp", [(i, i ^ 1) for i in range(self.tp)])


def on_device(
    sizes,
    layer_input, out_grad, segment_ids, positions,
    w_query, w_key, w_value, w_out, w_gate, w_up, w_down,
    m_query, m_key, m_value, m_out, m_gate, m_up, m_down,
    v_query, v_key, v_value, v_out, v_gate, v_up, v_down,
    gain_attn, gain_ffn, m_gain_attn, m_gain_ffn, v_gain_attn, v_gain_ffn,
):
    width = layer_input.shape[1]
    plan = Plan(sizes["do"], w_query.shape[0])
    by_x = plan.by_x
    axes = ("di", "tp")
    plane = Plane(sizes["tp"])

    gain_one, gain_two = plan.reorder(gain_attn), plan.reorder(gain_ffn)
    inputs_f = plan.reorder(layer_input).astype(F32)
    grad_low = plan.reorder(out_grad)
    normed, scale_one = norm_rows(inputs_f, gain_one)
    normed_all = lax.all_gather(normed.astype(LOW), axes, axis=0, tiled=True)

    marks = cat([segment_ids[None, :], positions[None, :]], 0)
    marks_other = lax.ppermute(marks, "di", PAIR)
    marks_all = cat([by_x(marks, marks_other), by_x(marks_other, marks)], 1)
    seg_all, pos_all = marks_all[0], marks_all[1]
    rows = seg_all.shape[0]
    seqs = rows // LEN
    seg_col, seg_row = seg_all.reshape(rows, 1), seg_all.reshape(seqs, 1, LEN)
    cosine, sine = rope_tables(pos_all)

    def col_halves(weight):
        half = weight.shape[1] // 2
        low = weight.astype(LOW)
        return by_x(low[:, :half], low[:, half:]), by_x(low[:, half:], low[:, :half])

    def row_halves(weight):
        half = weight.shape[0] // 2
        low = weight.astype(LOW)
        return by_x(low[:half], low[half:]), by_x(low[half:], low[:half])

    def col_cut(pair, chunk):
        size = pair[0].shape[1] // CHUNKS
        return tuple(part[:, chunk * size : (chunk + 1) * size] for part in pair)

    def row_cut(pair, chunk):
        size = pair[0].shape[0] // CHUNKS
        return tuple(part[chunk * size : (chunk + 1) * size] for part in pair)

    halves_q, halves_k, halves_v = col_halves(w_query), col_halves(w_key), col_halves(w_value)
    qkv_parts = tuple(cat([q, k, v], 1) for q, k, v in zip(halves_q, halves_k, halves_v))
    out_parts = row_halves(w_out)
    halves_g, halves_u, halves_d = col_halves(w_gate), col_halves(w_up), row_halves(w_down)

    def ffn_parts(chunk):
        gate_up = tuple(
            cat([g, u], 1) for g, u in zip(col_cut(halves_g, chunk), col_cut(halves_u, chunk))
        )
        return gate_up, row_cut(halves_d, chunk)

    attn_block = plan.blocks(qkv_parts, out_parts)
    ffn_blocks = [plan.blocks(*ffn_parts(chunk)) for chunk in range(CHUNKS)]
    hidden = halves_d[0].shape[0] // CHUNKS
    attn_shapes = (width, qkv_parts[0].shape[1]), (out_parts[0].shape[0], width)
    ffn_shapes = (width, 2 * hidden), (hidden, width)

    if plan.line:
        near, across = line_near(attn_block)
        across_near, out = line_far(near, across)
        out_near = line_last(across_near)
        attn_weights = (attn_block, near, across_near, out, across, out_near)
        first_block = after(ffn_blocks[0], out_near)
        near_1, across_1 = line_near(first_block)
    else:
        attn_weights = plan.plain_gather(attn_block)
    attn_loader = Loader(plan, attn_weights, *attn_shapes)

    attn_part, ctx, queries, both, lse = attn_forward(
        attn_loader, normed_all, cosine, sine, seg_col, seg_row
    )
    attn_sum = lax.psum_scatter(attn_part, axes, scatter_dimension=0, tiled=True)

    grad_y = plane.swap_y(after(grad_low, normed_all))
    grad_half = cat([pick(plane.y, grad_low, grad_y), pick(plane.y, grad_y, grad_low)], 0)

    if plan.line:
        near_1, across_1 = after((near_1, across_1), attn_part)
        across_near_1, out_1 = line_far(near_1, across_1)
        attn_sum = after(attn_sum, across_near_1, out_1, grad_y)
        second_block = after(ffn_blocks[1], out_1, across_near_1)
        near_2, across_2 = line_near(second_block)
        out_near_1 = line_last(across_near_1)
        first_weights = (first_block, near_1, across_near_1, out_1, across_1, out_near_1)
    else:
        first_weights = plan.plain_gather(ffn_blocks[0])
        second_weights = plan.plain_gather(ffn_blocks[1])

    residual = inputs_f + attn_sum.astype(F32)
    normed_two, scale_two = norm_rows(residual, gain_two)
    two_all = lax.all_gather(normed_two.astype(LOW), axes, axis=0, tiled=True)

    grad_x = plane.swap_x(grad_half)
    grad_core = cat([by_x(grad_half, grad_x), by_x(grad_x, grad_half)], 0)
    grad_other = plane.swap_core(grad_core)
    own_rows = layer_input.shape[0]
    core = lax.axis_index("tp") % 2
    groups = (rows // own_rows // 2, 1, own_rows, width)
    mine, theirs = grad_core.reshape(groups), grad_other.reshape(groups)
    grad_all = cat([pick(core, mine, theirs), pick(core, theirs, mine)], 1).reshape(rows, width)

    first = Loader(plan, first_weights, *ffn_shapes)
    if plan.line:
        two_all = after(two_all, near_2, across_2)
        across_near_2, out_2 = line_far(near_2, across_2)
    back_1, act_1, both_1 = ffn_main(first, two_all, grad_all, None)
    if plan.line:
        act_1 = after(act_1, across_near_2, out_2)
        out_near_2 = line_last(across_near_2)
        second_weights = (second_block, near_2, across_near_2, out_2, across_2, out_near_2)
    out_1_part, gain_1, *grads_1 = ffn_weights(first, two_all, grad_all, act_1, both_1, None)
    second = Loader(plan, second_weights, *ffn_shapes)
    if plan.line:
        far_1 = sum_far(grads_1)
        back_1 = after(back_1, out_1_part)
    back_2, act_2, both_2 = ffn_main(second, two_all, grad_all, back_1)
    back_sum = lax.psum_scatter(back_2, axes, scatter_dimension=0, tiled=True)
    if plan.line:
        far_1 = after(far_1, back_2)
        crossed_1, inward_1 = sum_middle(grads_1, far_1)
        act_2 = after(act_2, far_1)
    out_2_part, gain_2, *grads_2 = ffn_weights(second, two_all, grad_all, act_2, both_2, out_1_part)
    if plan.line:
        far_2 = sum_far(grads_2)
        crossed_1, inward_1 = after((crossed_1, inward_1), out_2_part)
        near_sum_1, across_sum_1 = sum_near(grads_1, crossed_1, inward_1)
        back_sum = after(back_sum, crossed_1, inward_1, far_2)
        crossed_2, inward_2 = sum_middle(grads_2, far_2)

    out_shape = (rows // own_rows // 2, 2, own_rows, width)
    parts = out_2_part.reshape(out_shape)
    mine, theirs = pick(core, parts[:, 0], parts[:, 1]), pick(core, parts[:, 1], parts[:, 0])
    summed = add(mine, plane.swap_core(theirs)).astype(LOW)
    low, high = summed[: out_shape[0] // 2], summed[out_shape[0] // 2 :]
    summed = add(by_x(low, high), plane.swap_x(by_x(high, low))).astype(LOW)
    low, high = summed[: summed.shape[0] // 2], summed[summed.shape[0] // 2 :]
    summed = add(pick(plane.y, low, high), plane.swap_y(pick(plane.y, high, low)))
    out_value = (residual + summed.reshape(own_rows, width)).astype(LOW)

    normed_two_grad = back_sum.astype(F32)
    residual_grad = grad_low.astype(F32) + norm_back(normed_two_grad, residual, scale_two, gain_two)
    res_all = lax.all_gather(residual_grad.astype(LOW), axes, axis=0, tiled=True)
    if plan.line:
        res_all = after(res_all, near_sum_1, across_sum_1, crossed_2, inward_2)
        near_sum_2, across_sum_2 = sum_near(grads_2, crossed_2, inward_2)

    back_one_part, gain_one_part, *grads_attn = attn_backward(
        attn_loader, res_all, normed_all, ctx, queries, both, lse, cosine, sine, seg_col, seg_row
    )
    back_one = lax.psum_scatter(back_one_part, axes, scatter_dimension=0, tiled=True)
    if plan.line:
        far = sum_far(grads_attn)
        total_1 = sum_own(grads_1, near_sum_1, across_sum_1)
        total_2 = sum_own(grads_2, near_sum_2, across_sum_2)
        crossed, inward = sum_middle(grads_attn, far)
        from_near, from_across = sum_near(grads_attn, crossed, inward)
        total = sum_own(grads_attn, from_near, from_across)
        qkv_pair, out_pair = plan.unpack(total, attn_shapes[0][1])
        ffn_grads = [plan.unpack(each, 2 * hidden) for each in (total_1, total_2)]
    else:
        qkv_pair, out_pair = plan.plain_sum(grads_attn)
        ffn_grads = [plan.plain_sum(each) for each in (grads_1, grads_2)]
    in_grad = residual_grad + norm_back(back_one.astype(F32), inputs_f, scale_one, gain_one)

    gain_parts = jnp.stack(
        [gain_one_part[:, 0] / gain_one, (gain_1[:, 0] + gain_2[:, 0]) / gain_two]
    )
    gain_sums = sum_everywhere(plan.reorder(gain_parts), list(sizes.items()))
    grad_gain_attn, grad_gain_ffn = gain_sums[0], gain_sums[1]

    def join(pair, axis):
        own, other = pair
        return by_x(cat([own, other], axis), cat([other, own], axis))

    def from_chunks(pairs, axis):
        own = cat([pair[0] for pair in pairs], axis)
        other = cat([pair[1] for pair in pairs], axis)
        return join((own, other), axis)

    def cut(pair, start, stop):
        return tuple(part[:, start:stop] for part in pair)

    at_k = halves_q[0].shape[1]
    at_v = at_k + halves_k[0].shape[1]
    end = at_v + halves_v[0].shape[1]
    grad_query = join(cut(qkv_pair, 0, at_k), 1)
    grad_key = join(cut(qkv_pair, at_k, at_v), 1)
    grad_value = join(cut(qkv_pair, at_v, end), 1)
    grad_out = join(out_pair, 0)
    grad_gate = from_chunks([cut(gu, 0, hidden) for gu, _ in ffn_grads], 1)
    grad_up = from_chunks([cut(gu, hidden, 2 * hidden) for gu, _ in ffn_grads], 1)
    grad_down = from_chunks([down for _, down in ffn_grads], 0)

    grads = (grad_query, grad_key, grad_value, grad_out, grad_gate, grad_up, grad_down)
    masters = (w_query, w_key, w_value, w_out, w_gate, w_up, w_down)
    firsts = (m_query, m_key, m_value, m_out, m_gate, m_up, m_down)
    seconds = (v_query, v_key, v_value, v_out, v_gate, v_up, v_down)
    updated = [
        adamw_update(w, g, m, v, WEIGHT_DECAY, LEARN_RATE)
        for w, g, m, v in zip(masters, grads, firsts, seconds)
    ]
    gain_updated = [
        adamw_update(gain_attn, grad_gain_attn, m_gain_attn, v_gain_attn, 0.0, GAIN_RATE),
        adamw_update(gain_ffn, grad_gain_ffn, m_gain_ffn, v_gain_ffn, 0.0, GAIN_RATE),
    ]
    return (
        plan.reorder(out_value),
        plan.reorder(in_grad),
        *grads,
        *[u[0] for u in updated],
        *[u[1] for u in updated],
        *[u[2] for u in updated],
        grad_gain_attn,
        grad_gain_ffn,
        *[u[0] for u in gain_updated],
        *[u[1] for u in gain_updated],
        *[u[2] for u in gain_updated],
    )


def solution(mesh):
    dp, tp = mesh.shape["dp"], mesh.shape["tp"]
    split = Mesh(mesh.devices.reshape(dp // 2, 2, tp), ("do", "di", "tp"))
    sizes = {"do": dp // 2, "di": 2, "tp": tp}
    dp_axes = ("do", "di")
    tokens = P(("do", "di", "tp"), None)
    by_rows, by_cols = P(dp_axes, "tp"), P("tp", dp_axes)
    weights = (by_rows, by_rows, by_rows, by_cols, by_rows, by_rows, by_cols)
    gains = (P(),) * 6
    in_specs = (tokens, tokens, P(dp_axes), P(dp_axes)) + weights * 3 + gains
    out_specs = (tokens, tokens) + weights * 4 + (P(),) * 2 + gains
    return jax.shard_map(
        functools.partial(on_device, sizes),
        mesh=split,
        in_specs=in_specs,
        out_specs=out_specs,
        check_vma=False,
    )
```

time: 1070 us -> 872 us (0.81)
  the two profiles are of different devices: /device:TPU:9 before, /device:TPU:20 now
where the time goes in v2:
time: 872 us; the launch traced here: 862 us
  waiting for transfers between devices  434 us (50%)
  Pallas kernels  189 us (22%)
  other arithmetic  111 us (13%)
  starting transfers between devices  75.5 us (9%)
  local copies, waits for them, and re-layouts  36.1 us (4%)
  between operations  16.4 us (2%)
    ppermute x2, waiting for transfers between devices, swap_x(): return lax.ppermute(value, 'di', PAIR)  77.9 us
    ppermute x3, waiting for transfers between devices, sum_far(): return lax.ppermute(parts[3], 'do', INWARD)  77.3 us
    ppermute x6, waiting for transfers between devices, line_near(): return (lax.ppermute(own, 'do', NEAR), lax.ppermute(own, 'do', MIDDLE))  74.3 us
    pallas_call x2, Pallas kernels, ffn_weights(): pl.pallas_call(functools.partial(ffn_weights_kernel, loader, len(more)),...  63.5 us
    pallas_call x2, Pallas kernels, ffn_main(): pl.pallas_call(functools.partial(ffn_main_kernel, loader, len(more)), gri...  61.8 us
    ppermute x6, waiting for transfers between devices, sum_near(): return (lax.ppermute(first, 'do', NEAR), lax.ppermute(third, 'do', MIDDLE))  54.6 us
    pallas_call x1, Pallas kernels, attn_backward(): pl.pallas_call(functools.partial(attn_backward_kernel, heads // 128, load...  42.5 us
    ppermute x3, waiting for transfers between devices, line_far(): lax.ppermute(near, 'do', MIDDLE)  37.6 us
  transfers between devices with their start and end apart: 54, of which 29 were waited for; matrix products, arithmetic and copies ran while one was open for 13% of the time, Pallas kernels for 16%

profile of v2, /device:TPU:20, one launch (start us, length us, event | category | flops | bytes accessed | tf_op | source)
XLA Modules:
  0.0 862.4 jit_solution(2687037641968196659)
XLA Ops:
  14.7 8.0 collective-permute-done
  26.4 12.1 %collective-permute-done.1.refs_2_ = bf16[512,640]{1,0:T(8,128)(2,1)S(1)} collective-permute-done((bf16[512,640]{1,0:T(8,128)(2,1)S(1)}, bf16[512,640]{1,0:T(8,128)(2,1)S(1)}, u32[]{:S(2)}, u32[]{:S(2)}) %collective-permute-start.1) | collective-permute-done | bytes 655392 | tf_op jit(solution)/shard_map/ppermute | solution.py:51
  38.6 2.3 collective-permute-start.2
  42.5 2.1 collective-permute-done.6
  46.6 9.2 %collective-permute-done.2.refs_3_ = bf16[512,640]{1,0:T(8,128)(2,1)S(1)} collective-permute-done((bf16[512,640]{1,0:T(8,128)(2,1)S(1)}, bf16[512,640]{1,0:T(8,128)(2,1)S(1)}, u32[]{:S(2)}, u32[]{:S(2)}) %collective-permute-start.2) | collective-permute-done | bytes 655392 | tf_op jit(solution)/shard_map/ppermute | solution.py:55
  55.8 2.2 collective-permute-start.5
  58.0 5.7 fusion.14
  65.1 4.3 pad_maximum_fusion.5.refs_8_.refs_13_
  71.7 21.3 %attn_forward.1 = (bf16[2048,2048]{1,0:T(8,128)(2,1)}, bf16[2048,256]{1,0:T(8,128)(2,1)S(1)}, bf16[2048,256]{1,0:T(8,128)(2,1)}, bf16[2048,128]{1,0:T(8,128)(2,1)S(1)}, f32[2048,128]{1,0:T(8,128)}) custom-call(s32[1]{0:T(128)} %bitcast.refs_0_, bf16[512,640]{1,0:T(8,128)(2,1)S(1)} %pad_maximum_fusion.11.refs_1_, ...), custom_call_target="tpu_custom_call" | custom-call | flops 1 | bytes 1 | tf_op jit(solution)/shard_map/attn_forward/pallas_call | solution.py:411
  102.9 14.4 %collective-permute-done.7 = bf16[256,1536]{1,0:T(8,128)(2,1)S(1)} collective-permute-done((bf16[256,1536]{1,0:T(8,128)(2,1)S(1)}, bf16[256,1536]{1,0:T(8,128)(2,1)S(1)}, u32[]{:S(2)}, u32[]{:S(2)}) %collective-permute-start.7) | collective-permute-done | bytes 786464 | tf_op jit(solution)/shard_map/ppermute | solution.py:127
  117.7 3.8 collective-permute-start.8
  121.5 2.2 collective-permute-start.9
  124.2 28.9 %collective-permute-done.8.refs_2_ = bf16[512,1536]{1,0:T(8,128)(2,1)S(1)} collective-permute-done((bf16[512,1536]{1,0:T(8,128)(2,1)S(1)}, bf16[512,1536]{1,0:T(8,128)(2,1)S(1)}, u32[]{:S(2)}, u32[]{:S(2)}) %collective-permute-start.8) | collective-permute-done | bytes 1572896 | tf_op jit(solution)/shard_map/ppermute | solution.py:51
  153.1 3.3 collective-permute-done.9.refs_5_
  157.8 2.2 collective-permute-start.10
  162.1 27.3 %collective-permute-done.12 = bf16[256,2048]{1,0:T(8,128)(2,1)S(1)} collective-permute-done((bf16[256,2048]{1,0:T(8,128)(2,1)S(1)}, bf16[256,2048]{1,0:T(8,128)(2,1)S(1)}, u32[]{:S(2)}, u32[]{:S(2)}) %collective-permute-start.12) | collective-permute-done | bytes 1048608 | tf_op jit(solution)/shard_map/ppermute | solution.py:645
  199.9 77.8 %collective-permute-done.19 = bf16[512,2048]{1,0:T(8,128)(2,1)S(1)} collective-permute-done((bf16[512,2048]{1,0:T(8,128)(2,1)S(1)}, bf16[512,2048]{1,0:T(8,128)(2,1)S(1)}, u32[]{:S(2)}, u32[]{:S(2)}) %collective-permute-start.19) | collective-permute-done | bytes 2097184 | tf_op jit(solution)/shard_map/ppermute | solution.py:648
  279.0 2.6 pad_maximum_fusion.1
  282.2 11.7 %collective-permute-done.13 = bf16[256,1536]{1,0:T(8,128)(2,1)S(1)} collective-permute-done((bf16[256,1536]{1,0:T(8,128)(2,1)S(1)}, bf16[256,1536]{1,0:T(8,128)(2,1)S(1)}, u32[]{:S(2)}, u32[]{:S(2)}) %collective-permute-start.13) | collective-permute-done | bytes 786464 | tf_op jit(solution)/shard_map/ppermute | solution.py:127
  297.9 30.0 %collective-permute-done.14.refs_2_ = bf16[512,1536]{1,0:T(8,128)(2,1)S(1)} collective-permute-done((bf16[512,1536]{1,0:T(8,128)(2,1)S(1)}, bf16[512,1536]{1,0:T(8,128)(2,1)S(1)}, u32[]{:S(2)}, u32[]{:S(2)}) %collective-permute-start.14) | collective-permute-done | bytes 1572896 | tf_op jit(solution)/shard_map/ppermute | solution.py:51
  327.9 2.4 collective-permute-start.15
  330.3 4.2 collective-permute-start.21
  334.5 2.4 collective-permute-start.17
  337.0 28.0 %collective-permute-done.15.refs_3_ = bf16[512,1536]{1,0:T(8,128)(2,1)} collective-permute-done((bf16[512,1536]{1,0:T(8,128)(2,1)S(1)}, bf16[512,1536]{1,0:T(8,128)(2,1)}, u32[]{:S(2)}, u32[]{:S(2)}) %collective-permute-start.15) | collective-permute-done | bytes 1572896 | tf_op jit(solution)/shard_map/ppermute | solution.py:55
  365.0 2.5 collective-permute-start.18
  367.4 6.8 broadcast_select_fusion.1
  374.2 7.5 pad_maximum_fusion
  381.7 8.4 copy.77
  390.1 30.3 %ffn_main.2 = (bf16[2048,2048]{1,0:T(8,128)(2,1)}, bf16[2048,512]{1,0:T(8,128)(2,1)}, bf16[2048,1024]{1,0:T(8,128)(2,1)}) custom-call(s32[1]{0:T(128)} %bitcast.refs_0_, bf16[512,1536]{1,0:T(8,128)(2,1)} %copy-done.22, bf16[512,1536]{1,0:T(8,128)(2,1)} %copy-done.30, bf16[512,1536]{1,0:T(8,128)(2,1)} %collective-permute-done.10.refs_3_, ...), custom_call_target="tpu_custom_call" | custom-call | flops 1 | bytes 1 | tf_op jit(solution)/shard_map/ffn_main/pallas_call | solution.py:512
  420.4 31.2 %ffn_weights.2 = (bf16[2048,2048]{1,0:T(8,128)(2,1)}, f32[2048,1]{1,0:T(8,128)}, bf16[512,1536]{1,0:T(8,128)(2,1)}, bf16[512,1536]{1,0:T(8,128)(2,1)}, bf16[512,...) custom-call(s32[1]{0:T(128)} %bitcast.refs_0_, bf16[512,1536]{1,0:T(8,128)(2,1)} %copy-done.22, bf16[512,1536]{1,0:T(8,128)(2,1)} %copy-done.30, ...), custom_call_target="tpu_custom_call" | custom-call | flops 1 | bytes 1 | tf_op jit(solution)/shard_map/ffn_weights/pallas_call | solution.py:572
  451.6 31.5 %ffn_main.3 = (bf16[2048,2048]{1,0:T(8,128)(2,1)}, bf16[2048,512]{1,0:T(8,128)(2,1)}, bf16[2048,1024]{1,0:T(8,128)(2,1)}) custom-call(s32[1]{0:T(128)} %bitcast.refs_0_, bf16[512,1536]{1,0:T(8,128)(2,1)} %copy-done.21, bf16[512,1536]{1,0:T(8,128)(2,1)} %copy-done.29, bf16[512,1536]{1,0:T(8,128)(2,1)} %collective-permute-done.15.refs_3_, ...), custom_call_target="tpu_custom_call" | custom-call | flops 1 | bytes 1 | tf_op jit(solution)/shard_map/ffn_main/pallas_call | solution.py:512
  484.5 34.9 %collective-permute-done.22 = bf16[512,1536]{1,0:T(8,128)(2,1)S(1)} collective-permute-done((bf16[512,1536]{1,0:T(8,128)(2,1)}, bf16[512,1536]{1,0:T(8,128)(2,1)S(1)}, u32[]{:S(2)}, u32[]{:S(2)}) %collective-permute-start.22) | collective-permute-done | bytes 1572896 | tf_op jit(solution)/shard_map/ppermute | solution.py:70
  519.3 2.9 add_convert_fusion.6
  522.3 2.1 collective-permute-start.26
  525.7 32.4 %ffn_weights.3 = (bf16[2048,2048]{1,0:T(8,128)(2,1)}, f32[2048,1]{1,0:T(8,128)}, bf16[512,1536]{1,0:T(8,128)(2,1)}, bf16[512,1536]{1,0:T(8,128)(2,1)}, bf16[512,...) custom-call(s32[1]{0:T(128)} %bitcast.refs_0_, bf16[512,1536]{1,0:T(8,128)(2,1)} %copy-done.21, bf16[512,1536]{1,0:T(8,128)(2,1)} %copy-done.29, ...), custom_call_target="tpu_custom_call" | custom-call | flops 1 | bytes 1 | tf_op jit(solution)/shard_map/ffn_weights/pallas_call | solution.py:572
  559.7 35.0 %collective-permute-done.28 = bf16[512,1536]{1,0:T(8,128)(2,1)} collective-permute-done((bf16[512,1536]{1,0:T(8,128)(2,1)}, bf16[512,1536]{1,0:T(8,128)(2,1)}, u32[]{:S(2)}, u32[]{:S(2)}) %collective-permute-start.28) | collective-permute-done | bytes 1572896 | tf_op jit(solution)/shard_map/ppermute | solution.py:70
  596.6 3.1 fusion.26
  599.7 2.4 add_convert_fusion.5
  604.0 3.5 collective-permute-start.30
  607.5 4.4 select_bitcast_fusion
  615.8 2.4 collective-permute-start.31
  618.2 21.3 %collective-permute-done.29 = bf16[512,1536]{1,0:T(8,128)(2,1)S(1)} collective-permute-done((bf16[512,1536]{1,0:T(8,128)(2,1)S(1)}, bf16[512,1536]{1,0:T(8,128)(2,1)S(1)}, u32[]{:S(2)}, u32[]{:S(2)}) %collective-permute-start.29) | collective-permute-done | bytes 1572896 | tf_op jit(solution)/shard_map/ppermute | solution.py:81
  639.5 3.7 collective-permute-done.30
  645.5 22.6 %collective-permute-done.32 = bf16[512,1536]{1,0:T(8,128)(2,1)S(1)} collective-permute-done((bf16[512,1536]{1,0:T(8,128)(2,1)S(1)}, bf16[512,1536]{1,0:T(8,128)(2,1)S(1)}, u32[]{:S(2)}, u32[]{:S(2)}) %collective-permute-start.32) | collective-permute-done | bytes 1572896 | tf_op jit(solution)/shard_map/ppermute | solution.py:75
  668.6 3.5 collective-permute-start.40
  672.0 3.4 collective-permute-done.31
  678.8 2.9 fusion
  685.8 19.8 %collective-permute-done.40 = bf16[512,1536]{1,0:T(8,128)(2,1)S(1)} collective-permute-done((bf16[512,1536]{1,0:T(8,128)(2,1)S(1)}, bf16[512,1536]{1,0:T(8,128)(2,1)S(1)}, u32[]{:S(2)}, u32[]{:S(2)}) %collective-permute-start.40) | collective-permute-done | bytes 1572896 | tf_op jit(solution)/shard_map/ppermute | solution.py:81
  710.2 42.5 %attn_backward.1 = (bf16[2048,2048]{1,0:T(8,128)(2,1)}, f32[2048,1]{1,0:T(8,128)}, bf16[512,640]{1,0:T(8,128)(2,1)S(1)}, bf16[512,640]{1,0:T(8,128)(2,1)S(1)}, b...) custom-call(s32[1]{0:T(128)} %bitcast.refs_0_, bf16[512,640]{1,0:T(8,128)(2,1)} %copy-done, bf16[512,640]{1,0:T(8,128)(2,1)} %copy-done.1, ...), custom_call_target="tpu_custom_call" | custom-call | flops 1 | bytes 1 | tf_op jit(solution)/shard_map/attn_backward/pallas_call | solution.py:447
  752.8 3.4 slice_select_fusion
  761.7 2.3 slice_dynamic-update-slice_fusion.5
  764.4 4.4 multiply_subtract_fusion
  771.9 2.5 collective-permute-done.43
  774.9 7.2 multiply_subtract_fusion.2
  784.9 4.4 multiply_subtract_fusion.1
  789.4 7.5 collective-permute-done.33
  798.4 2.8 add_convert_fusion
  806.6 3.4 collective-permute-done.36
  810.2 2.5 collective-permute-start.37
  812.7 9.5 %collective-permute-done.34 = bf16[512,640]{1,0:T(8,128)(2,1)S(1)} collective-permute-done((bf16[512,640]{1,0:T(8,128)(2,1)S(1)}, bf16[512,640]{1,0:T(8,128)(2,1)S(1)}, u32[]{:S(2)}, u32[]{:S(2)}) %collective-permute-start.34) | collective-permute-done | bytes 655392 | tf_op jit(solution)/shard_map/ppermute | solution.py:75
  823.2 6.0 collective-permute-done.37
  829.3 3.8 collective-permute-done.35
  834.4 6.1 collective-permute-done.38
  847.0 4.0 fusion.9
  (409 shorter events, 106.4 us)
Async XLA Ops:
  7.2 64.4 %all-gather.4.cloned.1.call-start = ((), (), s32[]{:S(2)}) async-start(), calls=%async_computation.3 | async-start | bytes 9437184 | tf_op jit(solution)/shard_map/all_gather | solution.py:672
  12.5 179.4 %reduce-scatter.4.cloned.1.call-start = ((), (), s32[]{:S(2)}) async-start(), calls=%async_computation.4 | async-start | bytes 9437184 | tf_op jit(solution)/shard_map/reduce_scatter | solution.py:732
  12.9 28.0 %copy-start.86 = (s32[1024]{0:T(1024)S(1)}, s32[1024]{0:T(1024)}, u32[]{:S(2)}) copy-start(s32[1024]{0:T(1024)} %param.34) | copy-start | bytes 12292
  13.1 9.5 %collective-permute-start = (bf16[256,640]{1,0:T(8,128)(2,1)S(1)}, bf16[256,640]{1,0:T(8,128)(2,1)S(1)}, u32[]{:S(2)}, u32[]{:S(2)}) collective-permute-start(bf16[256,640]{1,0:T(8,128)(2,1)S(1)} %pad_maximum_fusion.13), channel_id=1, source_target_pairs={{0,4},{4,0},{1,5},{5,1},{2,6},{6,2},{3,7},{7,3},{8,12},{12,8},{9,1... | collective-permute-start | bytes 983048 | tf_op jit(solution)/shard_map/ppermute | solution.py:127
  22.9 48.8 %copy-start = (bf16[512,640]{1,0:T(8,128)(2,1)}, bf16[512,640]{1,0:T(8,128)(2,1)S(1)}, u32[]{:S(2)}) copy-start(bf16[512,640]{1,0:T(8,128)(2,1)S(1)} %pad_maximum_fusion.11.refs_1_) | copy-start | bytes 1966084
  22.9 15.7 %collective-permute-start.1 = (bf16[512,640]{1,0:T(8,128)(2,1)S(1)}, bf16[512,640]{1,0:T(8,128)(2,1)S(1)}, u32[]{:S(2)}, u32[]{:S(2)}) collective-permute-start(bf16[512,640]{1,0:T(8,128)(2,1)S(1)} %pad_maximum_fusion.11.refs_1_), channel_id=1, source_target_pairs={{0,8},{8,0},{16,24},{24,16},{1,9},{9,1},{17,25},{25,17},{2,10},{10... | collective-permute-start | bytes 1966088 | tf_op jit(solution)/shard_map/ppermute | solution.py:51
  24.5 20.2 %collective-permute-start.3 = (bf16[512,640]{1,0:T(8,128)(2,1)S(1)}, bf16[512,640]{1,0:T(8,128)(2,1)S(1)}, u32[]{:S(2)}, u32[]{:S(2)}) collective-permute-start(bf16[512,640]{1,0:T(8,128)(2,1)S(1)} %pad_maximum_fusion.11.refs_1_), channel_id=1, source_target_pairs={{8,16},{16,8},{9,17},{17,9},{10,18},{18,10},{11,19},{19,11},{12,20... | collective-permute-start | bytes 1966088 | tf_op jit(solution)/shard_map/ppermute | solution.py:51
  38.6 33.1 %copy-start.1 = (bf16[512,640]{1,0:T(8,128)(2,1)}, bf16[512,640]{1,0:T(8,128)(2,1)S(1)}, u32[]{:S(2)}) copy-start(bf16[512,640]{1,0:T(8,128)(2,1)S(1)} %collective-permute-done.1.refs_2_) | copy-start | bytes 1966084
  38.6 17.2 %collective-permute-start.2 = (bf16[512,640]{1,0:T(8,128)(2,1)S(1)}, bf16[512,640]{1,0:T(8,128)(2,1)S(1)}, u32[]{:S(2)}, u32[]{:S(2)}) collective-permute-start(bf16[512,640]{1,0:T(8,128)(2,1)S(1)} %collective-permute-done.1.refs_2_), channel_id=1, source_target_pairs={{8,16},{16,8},{9,17},{17,9},{10,18},{18,10},{11,19},{19,11},{12,20... | collective-permute-start | bytes 1966088 | tf_op jit(solution)/shard_map/ppermute | solution.py:55
  41.0 3.7 collective-permute-start.6
  44.7 26.5 %collective-permute-start.4 = (bf16[512,640]{1,0:T(8,128)(2,1)S(1)}, bf16[512,640]{1,0:T(8,128)(2,1)S(1)}, u32[]{:S(2)}, u32[]{:S(2)}) collective-permute-start(bf16[512,640]{1,0:T(8,128)(2,1)S(1)} %collective-permute-done.3.refs_5_), channel_id=1, source_target_pairs={{8,0},{16,24},{9,1},{17,25},{10,2},{18,26},{11,3},{19,27},{12,4},{... | collective-permute-start | bytes 1966088 | tf_op jit(solution)/shard_map/ppermute | solution.py:55
  55.8 15.9 %collective-permute-start.5 = (bf16[512,640]{1,0:T(8,128)(2,1)S(1)}, bf16[512,640]{1,0:T(8,128)(2,1)}, u32[]{:S(2)}, u32[]{:S(2)}) collective-permute-start(bf16[512,640]{1,0:T(8,128)(2,1)S(1)} %collective-permute-done.2.refs_3_), channel_id=1, source_target_pairs={{8,0},{16,24},{9,1},{17,25},{10,2},{18,26},{11,3},{19,27},{12,4},{... | collective-permute-start | bytes 1966088 | tf_op jit(solution)/shard_map/ppermute | solution.py:59
  94.8 295.3 %all-gather.6.cloned.1.call-start = ((), (), s32[]{:S(2)}) async-start(), calls=%async_computation.5 | async-start | bytes 9437184 | tf_op jit(solution)/shard_map/all_gather | solution.py:751
  99.9 17.4 %collective-permute-start.7 = (bf16[256,1536]{1,0:T(8,128)(2,1)S(1)}, bf16[256,1536]{1,0:T(8,128)(2,1)S(1)}, u32[]{:S(2)}, u32[]{:S(2)}) collective-permute-start(bf16[256,1536]{1,0:T(8,128)(2,1)S(1)} %pad_maximum_fusion.8), channel_id=1, source_target_pairs={{0,4},{4,0},{1,5},{5,1},{2,6},{6,2},{3,7},{7,3},{8,12},{12,8},{9,1... | collective-permute-start | bytes 2359304 | tf_op jit(solution)/shard_map/ppermute | solution.py:127
  117.7 35.3 %collective-permute-start.8 = (bf16[512,1536]{1,0:T(8,128)(2,1)S(1)}, bf16[512,1536]{1,0:T(8,128)(2,1)S(1)}, u32[]{:S(2)}, u32[]{:S(2)}) collective-permute-start(bf16[512,1536]{1,0:T(8,128)(2,1)S(1)} %pad_maximum_fusion.3.refs_1_), channel_id=1, source_target_pairs={{0,8},{8,0},{16,24},{24,16},{1,9},{9,1},{17,25},{25,17},{2,10},{10... | collective-permute-start | bytes 4718600 | tf_op jit(solution)/shard_map/ppermute | solution.py:51
  121.5 34.9 %collective-permute-start.9 = (bf16[512,1536]{1,0:T(8,128)(2,1)S(1)}, bf16[512,1536]{1,0:T(8,128)(2,1)S(1)}, u32[]{:S(2)}, u32[]{:S(2)}) collective-permute-start(bf16[512,1536]{1,0:T(8,128)(2,1)S(1)} %pad_maximum_fusion.3.refs_1_), channel_id=1, source_target_pairs={{8,16},{16,8},{9,17},{17,9},{10,18},{18,10},{11,19},{19,11},{12,20... | collective-permute-start | bytes 4718600 | tf_op jit(solution)/shard_map/ppermute | solution.py:51
  156.4 33.0 %collective-permute-start.11 = (bf16[512,1536]{1,0:T(8,128)(2,1)S(1)}, bf16[512,1536]{1,0:T(8,128)(2,1)S(1)}, u32[]{:S(2)}, u32[]{:S(2)}) collective-permute-start(bf16[512,1536]{1,0:T(8,128)(2,1)S(1)} %collective-permute-done.9.refs_5_), channel_id=1, source_target_pairs={{8,0},{16,24},{9,1},{17,25},{10,2},{18,26},{11,3},{19,27},{12,4},{... | collective-permute-start | bytes 4718600 | tf_op jit(solution)/shard_map/ppermute | solution.py:55
  157.8 34.1 %collective-permute-start.10 = (bf16[512,1536]{1,0:T(8,128)(2,1)S(1)}, bf16[512,1536]{1,0:T(8,128)(2,1)}, u32[]{:S(2)}, u32[]{:S(2)}) collective-permute-start(bf16[512,1536]{1,0:T(8,128)(2,1)S(1)} %collective-permute-done.8.refs_2_), channel_id=1, source_target_pairs={{8,16},{16,8},{9,17},{17,9},{10,18},{18,10},{11,19},{19,11},{12,20... | collective-permute-start | bytes 4718600 | tf_op jit(solution)/shard_map/ppermute | solution.py:55
  160.1 31.8 %copy-start.9 = (bf16[256,2048]{1,0:T(8,128)(2,1)S(1)}, bf16[256,2048]{1,0:T(8,128)(2,1)}, u32[]{:S(2)}) copy-start(bf16[256,2048]{1,0:T(8,128)(2,1)} %copy-done.8) | copy-start | bytes 3145732
  161.5 27.9 %collective-permute-start.12 = (bf16[256,2048]{1,0:T(8,128)(2,1)S(1)}, bf16[256,2048]{1,0:T(8,128)(2,1)S(1)}, u32[]{:S(2)}, u32[]{:S(2)}) collective-permute-start(bf16[256,2048]{1,0:T(8,128)(2,1)S(1)} %maximum_select_fusion.7), channel_id=1, source_target_pairs={{0,2},{1,3},{2,0},{3,1},{4,6},{5,7},{6,4},{7,5},{8,10},{9,11},{10,... | collective-permute-start | bytes 3145736 | tf_op jit(solution)/shard_map/ppermute | solution.py:645
  195.7 399.0 %reduce-scatter.6.cloned.1.call-start = ((), (), s32[]{:S(2)}) async-start(), calls=%async_computation.6 | async-start | bytes 9437184 | tf_op jit(solution)/shard_map/reduce_scatter | solution.py:777
  197.7 80.1 %collective-permute-start.19 = (bf16[512,2048]{1,0:T(8,128)(2,1)S(1)}, bf16[512,2048]{1,0:T(8,128)(2,1)S(1)}, u32[]{:S(2)}, u32[]{:S(2)}) collective-permute-start(bf16[512,2048]{1,0:T(8,128)(2,1)S(1)} %pad_maximum_fusion.2), channel_id=1, source_target_pairs={{0,4},{4,0},{1,5},{5,1},{2,6},{6,2},{3,7},{7,3},{8,12},{12,8},{9,1... | collective-permute-start | bytes 6291464 | tf_op jit(solution)/shard_map/ppermute | solution.py:648
  199.3 94.6 %collective-permute-start.13 = (bf16[256,1536]{1,0:T(8,128)(2,1)S(1)}, bf16[256,1536]{1,0:T(8,128)(2,1)S(1)}, u32[]{:S(2)}, u32[]{:S(2)}) collective-permute-start(bf16[256,1536]{1,0:T(8,128)(2,1)S(1)} %pad_maximum_fusion.10), channel_id=1, source_target_pairs={{0,4},{4,0},{1,5},{5,1},{2,6},{6,2},{3,7},{7,3},{8,12},{12,8},{9,1... | collective-permute-start | bytes 2359304 | tf_op jit(solution)/shard_map/ppermute | solution.py:127
  282.2 85.2 %collective-permute-start.20 = (bf16[1024,2048]{1,0:T(8,128)(2,1)}, bf16[1024,2048]{1,0:T(8,128)(2,1)}, u32[]{:S(2)}, u32[]{:S(2)}) collective-permute-start(bf16[1024,2048]{1,0:T(8,128)(2,1)} %pad_maximum_fusion.1), channel_id=1, source_target_pairs={{0,1},{1,0},{2,3},{3,2},{4,5},{5,4},{6,7},{7,6},{8,9},{9,8},{10,11... | collective-permute-start | bytes 12582920 | tf_op jit(solution)/shard_map/ppermute | solution.py:651
  294.3 33.6 %collective-permute-start.14 = (bf16[512,1536]{1,0:T(8,128)(2,1)S(1)}, bf16[512,1536]{1,0:T(8,128)(2,1)S(1)}, u32[]{:S(2)}, u32[]{:S(2)}) collective-permute-start(bf16[512,1536]{1,0:T(8,128)(2,1)S(1)} %pad_maximum_fusion.4.refs_1_), channel_id=1, source_target_pairs={{0,8},{8,0},{16,24},{24,16},{1,9},{9,1},{17,25},{25,17},{2,10},{10... | collective-permute-start | bytes 4718600 | tf_op jit(solution)/shard_map/ppermute | solution.py:51
  295.8 38.7 %collective-permute-start.16 = (bf16[512,1536]{1,0:T(8,128)(2,1)S(1)}, bf16[512,1536]{1,0:T(8,128)(2,1)}, u32[]{:S(2)}, u32[]{:S(2)}) collective-permute-start(bf16[512,1536]{1,0:T(8,128)(2,1)S(1)} %pad_maximum_fusion.4.refs_1_), channel_id=1, source_target_pairs={{8,16},{16,8},{9,17},{17,9},{10,18},{18,10},{11,19},{19,11},{12,20... | collective-permute-start | bytes 4718600 | tf_op jit(solution)/shard_map/ppermute | solution.py:51
  327.9 37.1 %collective-permute-start.15 = (bf16[512,1536]{1,0:T(8,128)(2,1)S(1)}, bf16[512,1536]{1,0:T(8,128)(2,1)}, u32[]{:S(2)}, u32[]{:S(2)}) collective-permute-start(bf16[512,1536]{1,0:T(8,128)(2,1)S(1)} %collective-permute-done.14.refs_2_), channel_id=1, source_target_pairs={{8,16},{16,8},{9,17},{17,9},{10,18},{18,10},{11,19},{19,11},{12,20... | collective-permute-start | bytes 4718600 | tf_op jit(solution)/shard_map/ppermute | solution.py:55
  330.3 59.8 %collective-permute-start.21 = (bf16[512,1536]{1,0:T(8,128)(2,1)}, bf16[512,1536]{1,0:T(8,128)(2,1)}, u32[]{:S(2)}, u32[]{:S(2)}) collective-permute-start(bf16[512,1536]{1,0:T(8,128)(2,1)} %collective-permute-done.10.refs_3_), channel_id=1, source_target_pairs={{8,0},{16,24},{9,1},{17,25},{10,2},{18,26},{11,3},{19,27},{12,4},{... | collective-permute-start | bytes 4718600 | tf_op jit(solution)/shard_map/ppermute | solution.py:59
  334.5 85.9 %collective-permute-start.17 = (bf16[512,1536]{1,0:T(8,128)(2,1)}, bf16[512,1536]{1,0:T(8,128)(2,1)}, u32[]{:S(2)}, u32[]{:S(2)}) collective-permute-start(bf16[512,1536]{1,0:T(8,128)(2,1)} %collective-permute-done.16.refs_5_), channel_id=1, source_target_pairs={{8,0},{16,24},{9,1},{17,25},{10,2},{18,26},{11,3},{19,27},{12,4},{... | collective-permute-start | bytes 4718600 | tf_op jit(solution)/shard_map/ppermute | solution.py:55
  365.0 86.6 %collective-permute-start.18 = (bf16[512,1536]{1,0:T(8,128)(2,1)}, bf16[512,1536]{1,0:T(8,128)(2,1)}, u32[]{:S(2)}, u32[]{:S(2)}) collective-permute-start(bf16[512,1536]{1,0:T(8,128)(2,1)} %collective-permute-done.15.refs_3_), channel_id=1, source_target_pairs={{8,0},{16,24},{9,1},{17,25},{10,2},{18,26},{11,3},{19,27},{12,4},{... | collective-permute-start | bytes 4718600 | tf_op jit(solution)/shard_map/ppermute | solution.py:59
  483.1 227.1 %all-gather.8.cloned.1.call-start = ((), (), s32[]{:S(2)}) async-start(), calls=%async_computation.7 | async-start | bytes 9437184 | tf_op jit(solution)/shard_map/all_gather | solution.py:802
  483.2 36.2 %collective-permute-start.22 = (bf16[512,1536]{1,0:T(8,128)(2,1)}, bf16[512,1536]{1,0:T(8,128)(2,1)S(1)}, u32[]{:S(2)}, u32[]{:S(2)}) collective-permute-start(bf16[512,1536]{1,0:T(8,128)(2,1)} %get-tuple-element.97), channel_id=1, source_target_pairs={{0,8},{24,16},{1,9},{25,17},{2,10},{26,18},{3,11},{27,19},{4,12},{... | collective-permute-start | bytes 4718600 | tf_op jit(solution)/shard_map/ppermute | solution.py:70
  522.3 37.1 %collective-permute-start.26 = (bf16[512,1536]{1,0:T(8,128)(2,1)}, bf16[512,1536]{1,0:T(8,128)(2,1)}, u32[]{:S(2)}, u32[]{:S(2)}) collective-permute-start(bf16[512,1536]{1,0:T(8,128)(2,1)} %add_convert_fusion.6), channel_id=1, source_target_pairs={{8,16},{16,8},{9,17},{17,9},{10,18},{18,10},{11,19},{19,11},{12,20... | collective-permute-start | bytes 4718600 | tf_op jit(solution)/shard_map/ppermute | solution.py:75
  524.4 35.3 %collective-permute-start.27 = (bf16[512,1536]{1,0:T(8,128)(2,1)}, bf16[512,1536]{1,0:T(8,128)(2,1)}, u32[]{:S(2)}, u32[]{:S(2)}) collective-permute-start(bf16[512,1536]{1,0:T(8,128)(2,1)} %add_convert_fusion.6), channel_id=1, source_target_pairs={{0,8},{24,16},{1,9},{25,17},{2,10},{26,18},{3,11},{27,19},{4,12},{... | collective-permute-start | bytes 4718600 | tf_op jit(solution)/shard_map/ppermute | solution.py:75
  558.1 38.5 %copy-start.89 = (f32[256]{0:T(256)S(1)}, f32[256]{0:T(256)}, u32[]{:S(2)}) copy-start(f32[256]{0:T(256)} %copy-done.88) | copy-start | bytes 3076
  558.1 38.5 %copy-start.93 = (f32[256]{0:T(256)S(1)}, f32[256]{0:T(256)}, u32[]{:S(2)}) copy-start(f32[256]{0:T(256)} %get-tuple-element.283) | copy-start | bytes 3076
  558.1 36.6 %collective-permute-start.28 = (bf16[512,1536]{1,0:T(8,128)(2,1)}, bf16[512,1536]{1,0:T(8,128)(2,1)}, u32[]{:S(2)}, u32[]{:S(2)}) collective-permute-start(bf16[512,1536]{1,0:T(8,128)(2,1)} %get-tuple-element.106), channel_id=1, source_target_pairs={{0,8},{24,16},{1,9},{25,17},{2,10},{26,18},{3,11},{27,19},{4,12},{... | collective-permute-start | bytes 4718600 | tf_op jit(solution)/shard_map/ppermute | solution.py:70
  599.7 245.4 %reduce-scatter.8.cloned.1.call-start = ((), (), s32[]{:S(2)}) async-start(), calls=%async_computation.8 | async-start | bytes 9437184 | tf_op jit(solution)/shard_map/reduce_scatter | solution.py:810
  602.1 37.4 %collective-permute-start.29 = (bf16[512,1536]{1,0:T(8,128)(2,1)S(1)}, bf16[512,1536]{1,0:T(8,128)(2,1)S(1)}, u32[]{:S(2)}, u32[]{:S(2)}) collective-permute-start(bf16[512,1536]{1,0:T(8,128)(2,1)S(1)} %add_convert_fusion.5), channel_id=1, source_target_pairs={{0,8},{8,0},{16,24},{24,16},{1,9},{9,1},{17,25},{25,17},{2,10},{10... | collective-permute-start | bytes 4718600 | tf_op jit(solution)/shard_map/ppermute | solution.py:81
  604.0 39.2 %collective-permute-start.30 = (bf16[512,1536]{1,0:T(8,128)(2,1)S(1)}, bf16[512,1536]{1,0:T(8,128)(2,1)S(1)}, u32[]{:S(2)}, u32[]{:S(2)}) collective-permute-start(bf16[512,1536]{1,0:T(8,128)(2,1)S(1)} %add_convert_fusion.4), channel_id=1, source_target_pairs={{8,16},{16,8},{9,17},{17,9},{10,18},{18,10},{11,19},{19,11},{12,20... | collective-permute-start | bytes 4718600 | tf_op jit(solution)/shard_map/ppermute | solution.py:81
  611.9 66.8 %collective-permute-start.23 = (bf16[4,256,2048]{2,1,0:T(8,128)(2,1)S(1)}, bf16[4,256,2048]{2,1,0:T(8,128)(2,1)S(1)}, u32[]{:S(2)}, u32[]{:S(2)}) collective-permute-start(bf16[4,256,2048]{2,1,0:T(8,128)(2,1)S(1)} %select_bitcast_fusion), channel_id=1, source_target_pairs={{0,1},{1,0},{2,3},{3,2},{4,5},{5,4},{6,7},{7,6},{8,9},{9,8},{10,11... | collective-permute-start | bytes 12582920 | tf_op jit(solution)/shard_map/ppermute | solution.py:651
  614.0 29.3 %copy-start.56 = (bf16[512,1536]{1,0:T(8,128)(2,1)S(1)}, bf16[512,1536]{1,0:T(8,128)(2,1)}, u32[]{:S(2)}) copy-start(bf16[512,1536]{1,0:T(8,128)(2,1)} %get-tuple-element.120) | copy-start | bytes 4718596
  614.0 54.2 %collective-permute-start.32 = (bf16[512,1536]{1,0:T(8,128)(2,1)S(1)}, bf16[512,1536]{1,0:T(8,128)(2,1)S(1)}, u32[]{:S(2)}, u32[]{:S(2)}) collective-permute-start(bf16[512,1536]{1,0:T(8,128)(2,1)S(1)} %add_convert_fusion.3), channel_id=1, source_target_pairs={{0,8},{24,16},{1,9},{25,17},{2,10},{26,18},{3,11},{27,19},{4,12},{... | collective-permute-start | bytes 4718600 | tf_op jit(solution)/shard_map/ppermute | solution.py:75
  615.8 59.7 %collective-permute-start.31 = (bf16[512,1536]{1,0:T(8,128)(2,1)S(1)}, bf16[512,1536]{1,0:T(8,128)(2,1)S(1)}, u32[]{:S(2)}, u32[]{:S(2)}) collective-permute-start(bf16[512,1536]{1,0:T(8,128)(2,1)S(1)} %add_convert_fusion.3), channel_id=1, source_target_pairs={{8,16},{16,8},{9,17},{17,9},{10,18},{18,10},{11,19},{19,11},{12,20... | collective-permute-start | bytes 4718600 | tf_op jit(solution)/shard_map/ppermute | solution.py:75
  643.8 32.3 %copy-start.14 = (f32[512,1536]{1,0:T(8,128)}, f32[512,1536]{1,0:T(8,128)S(1)}, u32[]{:S(2)}) copy-start(f32[512,1536]{1,0:T(8,128)S(1)} %convert_add_fusion.3) | copy-start | bytes 9437188
  643.8 34.9 %slice-start = ((s8[8388608]{0:T(1024)(128)(4,1)}), s8[4194304]{0:T(1024)(128)(4,1)S(1)}, s32[]{:S(2)}) async-start(s8[8388608]{0:T(1024)(128)(4,1)} %bitcast.43), calls=%async_computation.9 | async-start | bytes 8388608
  644.0 31.5 %copy-start.51 = (bf16[512,1536]{1,0:T(8,128)(2,1)S(1)}, bf16[512,1536]{1,0:T(8,128)(2,1)}, u32[]{:S(2)}) copy-start(bf16[512,1536]{1,0:T(8,128)(2,1)} %get-tuple-element.122) | copy-start | bytes 4718596
  644.0 32.0 %collective-permute-start.41 = (bf16[256,1536]{1,0:T(8,128)(2,1)S(1)}, bf16[256,1536]{1,0:T(8,128)(2,1)S(1)}, u32[]{:S(2)}, u32[]{:S(2)}) collective-permute-start(bf16[256,1536]{1,0:T(8,128)(2,1)S(1)} %select_convert_fusion.1), channel_id=1, source_target_pairs={{0,4},{4,0},{1,5},{5,1},{2,6},{6,2},{3,7},{7,3},{8,12},{12,8},{9,1... | collective-permute-start | bytes 2359304 | tf_op jit(solution)/shard_map/ppermute | solution.py:154
  668.6 37.0 %collective-permute-start.40 = (bf16[512,1536]{1,0:T(8,128)(2,1)S(1)}, bf16[512,1536]{1,0:T(8,128)(2,1)S(1)}, u32[]{:S(2)}, u32[]{:S(2)}) collective-permute-start(bf16[512,1536]{1,0:T(8,128)(2,1)S(1)} %add_convert_fusion.1), channel_id=1, source_target_pairs={{8,16},{16,8},{9,17},{17,9},{10,18},{18,10},{11,19},{19,11},{12,20... | collective-permute-start | bytes 4718600 | tf_op jit(solution)/shard_map/ppermute | solution.py:81
  675.9 29.7 %collective-permute-start.39 = (bf16[512,1536]{1,0:T(8,128)(2,1)S(1)}, bf16[512,1536]{1,0:T(8,128)(2,1)S(1)}, u32[]{:S(2)}, u32[]{:S(2)}) collective-permute-start(bf16[512,1536]{1,0:T(8,128)(2,1)S(1)} %add_convert_fusion.2), channel_id=1, source_target_pairs={{0,8},{8,0},{16,24},{24,16},{1,9},{9,1},{17,25},{25,17},{2,10},{10... | collective-permute-start | bytes 4718600 | tf_op jit(solution)/shard_map/ppermute | solution.py:81
  684.3 114.1 %collective-permute-start.24 = (bf16[2,256,2048]{2,1,0:T(8,128)(2,1)}, bf16[2,256,2048]{2,1,0:T(8,128)(2,1)}, u32[]{:S(2)}, u32[]{:S(2)}) collective-permute-start(bf16[2,256,2048]{2,1,0:T(8,128)(2,1)} %broadcast_select_fusion.4), channel_id=1, source_target_pairs={{0,4},{4,0},{1,5},{5,1},{2,6},{6,2},{3,7},{7,3},{8,12},{12,8},{9,1... | collective-permute-start | bytes 6291464 | tf_op jit(solution)/shard_map/ppermute | solution.py:648
  708.9 49.4 %collective-permute-start.42 = (bf16[256,1536]{1,0:T(8,128)(2,1)}, bf16[256,1536]{1,0:T(8,128)(2,1)}, u32[]{:S(2)}, u32[]{:S(2)}) collective-permute-start(bf16[256,1536]{1,0:T(8,128)(2,1)} %select_convert_fusion), channel_id=1, source_target_pairs={{0,4},{4,0},{1,5},{5,1},{2,6},{6,2},{3,7},{7,3},{8,12},{12,8},{9,1... | collective-permute-start | bytes 2359304 | tf_op jit(solution)/shard_map/ppermute | solution.py:154
  770.6 3.8 collective-permute-start.43
  774.4 9.2 %collective-permute-start.44 = (f32[2,2048]{1,0:T(2,128)S(1)}, f32[2,2048]{1,0:T(2,128)S(1)}, u32[]{:S(2)}, u32[]{:S(2)}) collective-permute-start(f32[2,2048]{1,0:T(2,128)S(1)} %add.305), channel_id=1, source_target_pairs={{0,16},{8,24},{16,0},{24,8},{1,17},{9,25},{17,1},{25,9},{2,18},{10... | collective-permute-start | bytes 49160 | tf_op jit(solution)/shard_map/ppermute | solution.py:627
  782.2 14.7 %collective-permute-start.33 = (bf16[512,640]{1,0:T(8,128)(2,1)S(1)}, bf16[512,640]{1,0:T(8,128)(2,1)S(1)}, u32[]{:S(2)}, u32[]{:S(2)}) collective-permute-start(bf16[512,640]{1,0:T(8,128)(2,1)S(1)} %copy-done.61), channel_id=1, source_target_pairs={{0,8},{24,16},{1,9},{25,17},{2,10},{26,18},{3,11},{27,19},{4,12},{... | collective-permute-start | bytes 1966088 | tf_op jit(solution)/shard_map/ppermute | solution.py:70
  783.6 5.7 collective-permute-start.45
  789.3 11.9 %collective-permute-start.46 = (f32[2,2048]{1,0:T(2,128)S(1)}, f32[2,2048]{1,0:T(2,128)S(1)}, u32[]{:S(2)}, u32[]{:S(2)}) collective-permute-start(f32[2,2048]{1,0:T(2,128)S(1)} %add.307), channel_id=1, source_target_pairs={{0,1},{1,0},{2,3},{3,2},{4,5},{5,4},{6,7},{7,6},{8,9},{9,8},{10,11... | collective-permute-start | bytes 49160 | tf_op jit(solution)/shard_map/ppermute | solution.py:627
  797.1 13.0 %collective-permute-start.36 = (bf16[512,640]{1,0:T(8,128)(2,1)S(1)}, bf16[512,640]{1,0:T(8,128)(2,1)S(1)}, u32[]{:S(2)}, u32[]{:S(2)}) collective-permute-start(bf16[512,640]{1,0:T(8,128)(2,1)S(1)} %add_convert_fusion.9), channel_id=1, source_target_pairs={{0,8},{24,16},{1,9},{25,17},{2,10},{26,18},{3,11},{27,19},{4,12},{... | collective-permute-start | bytes 1966088 | tf_op jit(solution)/shard_map/ppermute | solution.py:75
  801.3 5.3 collective-permute-start.47
  803.3 19.0 %collective-permute-start.34 = (bf16[512,640]{1,0:T(8,128)(2,1)S(1)}, bf16[512,640]{1,0:T(8,128)(2,1)S(1)}, u32[]{:S(2)}, u32[]{:S(2)}) collective-permute-start(bf16[512,640]{1,0:T(8,128)(2,1)S(1)} %add_convert_fusion.9), channel_id=1, source_target_pairs={{8,16},{16,8},{9,17},{17,9},{10,18},{18,10},{11,19},{19,11},{12,20... | collective-permute-start | bytes 1966088 | tf_op jit(solution)/shard_map/ppermute | solution.py:75
  806.3 40.6 %collective-permute-start.25 = (bf16[1,256,2048]{2,1,0:T(8,128)(2,1)}, bf16[1,256,2048]{2,1,0:T(8,128)(2,1)}, u32[]{:S(2)}, u32[]{:S(2)}) collective-permute-start(bf16[1,256,2048]{2,1,0:T(8,128)(2,1)} %broadcast_select_fusion.8), channel_id=1, source_target_pairs={{0,2},{1,3},{2,0},{3,1},{4,6},{5,7},{6,4},{7,5},{8,10},{9,11},{10,... | collective-permute-start | bytes 3145736 | tf_op jit(solution)/shard_map/ppermute | solution.py:645
  810.2 19.1 %collective-permute-start.37 = (bf16[512,640]{1,0:T(8,128)(2,1)S(1)}, bf16[512,640]{1,0:T(8,128)(2,1)S(1)}, u32[]{:S(2)}, u32[]{:S(2)}) collective-permute-start(bf16[512,640]{1,0:T(8,128)(2,1)S(1)} %add_convert_fusion.7), channel_id=1, source_target_pairs={{8,16},{16,8},{9,17},{17,9},{10,18},{18,10},{11,19},{19,11},{12,20... | collective-permute-start | bytes 1966088 | tf_op jit(solution)/shard_map/ppermute | solution.py:81
  822.4 10.7 %collective-permute-start.35 = (bf16[512,640]{1,0:T(8,128)(2,1)S(1)}, bf16[512,640]{1,0:T(8,128)(2,1)S(1)}, u32[]{:S(2)}, u32[]{:S(2)}) collective-permute-start(bf16[512,640]{1,0:T(8,128)(2,1)S(1)} %add_convert_fusion.8), channel_id=1, source_target_pairs={{0,8},{8,0},{16,24},{24,16},{1,9},{9,1},{17,25},{25,17},{2,10},{10... | collective-permute-start | bytes 1966088 | tf_op jit(solution)/shard_map/ppermute | solution.py:81
  833.4 7.1 collective-permute-start.38
  (94 other events, 595.9 us)
Sparse Core Ops, SparseCore 0:
  12.6 55.1 all-gather.3
  94.9 79.0 reduce-scatter.3
  195.8 91.8 all-gather.5
  483.2 71.3 reduce-scatter.5
  599.8 66.7 all-gather.7
  752.9 79.0 reduce-scatter.7

commit v3 on v2

--- a/solution.py
+++ b/solution.py
@@ -30,6 +30,8 @@
 MIDDLE = [(1, 2), (2, 1)]
 OUTWARD = [(1, 0), (2, 3)]
 INWARD = [(0, 1), (3, 2)]
+CROSS = [(0, 2), (1, 3), (2, 0), (3, 1)]
+MIRROR = [(0, 3), (1, 2), (2, 1), (3, 0)]
 PAIR = [(0, 1), (1, 0)]
 
 
@@ -43,8 +45,8 @@
     return jnp.concatenate(parts, axis)
 
 
-def after(value, *earlier):
-    return lax.optimization_barrier((value, earlier))[0]
+def fence(*values):
+    return lax.optimization_barrier(values)
 
 
 def line_near(own):
@@ -85,11 +87,18 @@
     return add(parts[0], from_near, from_across)
 
 
+def send_direct(parts):
+    return [
+        lax.ppermute(part, "do", perm) for part, perm in zip(parts[1:], (NEAR, CROSS, MIRROR))
+    ]
+
+
 class Plan:
     def __init__(self, outer, per_device):
         self.rows = per_device
         self.block = 2 * per_device
         self.line = outer == 4 and per_device == 256
+        self.cuts = 4 if self.line else 1
 
     def reorder(self, values):
         if not self.line:
@@ -109,36 +118,25 @@
         place = lax.axis_index("do")
         return ((place == 1) | (place == 2)).astype(jnp.int32).reshape(1)
 
-    def blocks(self, row_part, col_part):
-        if not self.line:
-            out = []
-            for (own, other), axis in ((row_part, 0), (col_part, 1)):
-                theirs = lax.ppermute(other, "di", PAIR)
-                out.append(cat([self.by_x(own, theirs), self.by_x(theirs, own)], axis))
-            return tuple(out)
-        rows = self.rows
-
-        def pack(which):
-            side = col_part[which]
+    def pack(self, row_part, col_part):
+        rows, packs = self.rows, []
+        for row_side, side in zip(row_part, col_part):
             pieces = [side[i : i + rows] for i in range(0, side.shape[0], rows)]
-            return cat([row_part[which]] + pieces, 1)
-
-        mine, other = pack(0), pack(1)
-        theirs = lax.ppermute(other, "di", PAIR)
-        return cat([self.by_x(mine, theirs), self.by_x(theirs, mine)], 0)
-
-    def plain_gather(self, blocks):
-        return (
-            lax.all_gather(blocks[0], "do", axis=0, tiled=True),
-            lax.all_gather(blocks[1], "do", axis=1, tiled=True),
-        )
-
-    def plain_sum(self, grads):
-        row, col = grads
-        row = lax.psum_scatter(row, "do", scatter_dimension=0, tiled=True)
-        col = lax.psum_scatter(col, "do", scatter_dimension=1, tiled=True)
-        rows = self.rows
-        return self.trade(row[:rows], row[rows:]), self.trade(col[:, :rows], col[:, rows:])
+            packs.append(cat([row_side] + pieces, 1))
+        return packs
+
+    def swap(self, other):
+        return lax.ppermute(other, "di", PAIR)
+
+    def join(self, own, theirs, axis=0):
+        return cat([self.by_x(own, theirs), self.by_x(theirs, own)], axis)
+
+    def plain_gather(self, row_part, col_part):
+        full = []
+        for (own, other), axis in ((row_part, 0), (col_part, 1)):
+            block = self.join(own, self.swap(other), axis)
+            full.append(lax.all_gather(block, "do", axis=axis, tiled=True))
+        return tuple(full)
 
     def unpack(self, total, wide):
         rows = self.rows
@@ -148,6 +146,14 @@
             (mine[:, :wide], theirs[:, :wide]),
             tuple(cat([side[:, i : i + rows] for i in cuts], 0) for side in (mine, theirs)),
         )
+
+    def plain_sum_row(self, grad):
+        total = lax.psum_scatter(grad, "do", scatter_dimension=0, tiled=True)
+        return self.trade(total[: self.rows], total[self.rows :])
+
+    def plain_sum_col(self, grad):
+        total = lax.psum_scatter(grad, "do", scatter_dimension=1, tiled=True)
+        return self.trade(total[:, : self.rows], total[:, self.rows :])
 
     def trade(self, low, high):
         mine = self.by_x(low, high).astype(F32)
@@ -303,7 +309,7 @@
 def attn_forward_kernel(pairs, loader, *refs):
     weights, refs = refs[: loader.count], refs[loader.count :]
     x_ref, cos_ref, sin_ref, col_ref, row_ref = refs[:5]
-    part_ref, ctx_ref, q_ref, kv_ref, lse_ref, wqkv_ref, wout_ref, sems = refs[5:]
+    part_ref, ctx_ref, q_ref, kv_ref, lse_ref, wout_ref, wqkv_ref, _, sems = refs[5:]
 
     @pl.when(pl.program_id(0) == 0)
     def _():
@@ -342,25 +348,22 @@
 
 def attn_backward_kernel(pairs, loader, *refs):
     weights, refs = refs[: loader.count], refs[loader.count :]
-    res_ref, x_ref, ctx_ref, q_ref, kv_ref, lse_ref, cos_ref, sin_ref, col_ref, row_ref = refs[:10]
-    part_ref, gain_ref, *grad_refs = refs[10:-5]
-    wqkv_ref, wout_ref, sems, acc_qkv, acc_out = refs[-5:]
+    cg_ref, x_ref, q_ref, kv_ref, lse_ref, cos_ref, sin_ref, col_ref, row_ref = refs[:9]
+    part_ref, gain_ref, *grad_refs = refs[9:-4]
+    wqkv_ref, wout_ref, sems, acc_qkv = refs[-4:]
     step = pl.program_id(0)
 
     @pl.when(step == 0)
     def _():
         loader.load(weights, wqkv_ref, wout_ref, sems)
         acc_qkv[...] = jnp.zeros_like(acc_qkv)
-        acc_out[...] = jnp.zeros_like(acc_out)
 
     cosine, sine = tables(cos_ref, sin_ref, pairs)
     scale = HD**-0.5
-    res = res_ref[...]
-    acc_out[...] += dot(ctx_ref[...], res, 0, 0)
-    ctx_grad = dot(res, wout_ref[...], 1, 1).astype(LOW)
+    ctx_grad = cg_ref[...]
     keys, values = split_kv(kv_ref[...])
     allowed = allowed_pairs(col_ref[...], row_ref[0])
-    lane = lanes_of((res.shape[0], 128))
+    lane = lanes_of((ctx_grad.shape[0], 128))
     log_sums = lse_ref[...]
     query_grads, key_grad, value_grad = [], None, None
     for pair in range(pairs):
@@ -393,7 +396,9 @@
 
     @pl.when(step == pl.num_programs(0) - 1)
     def _():
-        pack_grads(loader.plan, acc_qkv, acc_out, grad_refs)
+        cut = acc_qkv.shape[0] // len(grad_refs)
+        for i, out in enumerate(grad_refs):
+            out[...] = acc_qkv[i * cut : (i + 1) * cut, :].astype(LOW)
         gain_ref[...] = jnp.sum(acc_qkv[...] * wqkv_ref[...].astype(F32), axis=1, keepdims=True)
 
 
@@ -425,6 +430,7 @@
             per_seq((LEN, heads)),
             per_seq((LEN, 128)),
             per_seq((LEN, 128)),
+            once(loader.col_shape),
         ],
         out_shape=[
             jax.ShapeDtypeStruct((rows, width), LOW),
@@ -432,6 +438,7 @@
             jax.ShapeDtypeStruct((rows, heads), LOW),
             jax.ShapeDtypeStruct((rows, 128), LOW),
             jax.ShapeDtypeStruct((rows, 128), F32),
+            jax.ShapeDtypeStruct(loader.col_shape, LOW),
         ],
         scratch_shapes=loader.scratch(),
         compiler_params=pltpu.CompilerParams(vmem_limit_bytes=48 * MIB),
@@ -440,18 +447,18 @@
     )(*loader.operands, normed, cosine, sine, seg_col, seg_row)
 
 
-def attn_backward(loader, res_all, normed, ctx, queries, both, lse, cosine, sine, seg_col, seg_row):
+def attn_backward(loader, ctx_grad, normed, queries, both, lse, cosine, sine, seg_col, seg_row):
     rows, width = normed.shape
     heads = loader.col_shape[0]
-    grads = packed_shapes(loader.plan, loader.row_shape, loader.col_shape)
+    cuts = loader.plan.cuts
+    grad = (width // cuts, loader.row_shape[1])
     return pl.pallas_call(
         functools.partial(attn_backward_kernel, heads // 128, loader),
         grid=(rows // LEN,),
         in_specs=[
             *loader.specs(),
+            per_seq((LEN, heads)),
             per_seq((LEN, width)),
-            per_seq((LEN, width)),
-            per_seq((LEN, heads)),
             per_seq((LEN, heads)),
             per_seq((LEN, 128)),
             per_seq((LEN, 128)),
@@ -460,21 +467,97 @@
             per_seq((LEN, 1)),
             per_seq((1, 1, LEN)),
         ],
-        out_specs=[per_seq((LEN, width)), once((width, 1))] + [once(shape) for shape in grads],
+        out_specs=[per_seq((LEN, width)), once((width, 1))] + [once(grad)] * cuts,
         out_shape=[
             jax.ShapeDtypeStruct((rows, width), LOW),
             jax.ShapeDtypeStruct((width, 1), F32),
         ]
-        + [jax.ShapeDtypeStruct(shape, LOW) for shape in grads],
-        scratch_shapes=[
-            *loader.scratch(),
-            pltpu.VMEM(loader.row_shape, F32),
-            pltpu.VMEM(loader.col_shape, F32),
-        ],
+        + [jax.ShapeDtypeStruct(grad, LOW)] * cuts,
+        scratch_shapes=[*loader.scratch(), pltpu.VMEM(loader.row_shape, F32)],
         compiler_params=pltpu.CompilerParams(vmem_limit_bytes=52 * MIB),
         cost_estimate=SMALL,
         name="attn_backward",
-    )(*loader.operands, res_all, normed, ctx, queries, both, lse, cosine, sine, seg_col, seg_row)
+    )(*loader.operands, ctx_grad, normed, queries, both, lse, cosine, sine, seg_col, seg_row)
+
+
+def out_weights_kernel(ctx_ref, res_ref, *refs):
+    grad_refs, acc = refs[:-1], refs[-1]
+    step = pl.program_id(0)
+
+    @pl.when(step == 0)
+    def _():
+        acc[...] = jnp.zeros_like(acc)
+
+    acc[...] += dot(ctx_ref[...], res_ref[...], 0, 0)
+
+    @pl.when(step == pl.num_programs(0) - 1)
+    def _():
+        cut = acc.shape[1] // len(grad_refs)
+        for i, out in enumerate(grad_refs):
+            out[...] = acc[:, i * cut : (i + 1) * cut].astype(LOW)
+
+
+def out_weights(plan, ctx, res_all):
+    rows, width = res_all.shape
+    heads = ctx.shape[1]
+    grad = (heads, width // plan.cuts)
+    return pl.pallas_call(
+        out_weights_kernel,
+        grid=(rows // LEN,),
+        in_specs=[per_seq((LEN, heads)), per_seq((LEN, width))],
+        out_specs=[once(grad)] * plan.cuts,
+        out_shape=[jax.ShapeDtypeStruct(grad, LOW)] * plan.cuts,
+        scratch_shapes=[pltpu.VMEM((heads, width), F32)],
+        compiler_params=pltpu.CompilerParams(vmem_limit_bytes=40 * MIB),
+        cost_estimate=SMALL,
+        name="out_weights",
+    )(ctx, res_all)
+
+
+def residual_backward_kernel(
+    back_ref, residual_ref, scale_ref, gain_ref, grad_ref, wout_ref, res_grad_ref, low_ref, ctx_ref
+):
+    @pl.when(pl.program_id(0) == 0)
+    def _():
+        back = norm_back(
+            back_ref[...].astype(F32), residual_ref[...], scale_ref[...], gain_ref[...]
+        )
+        total = grad_ref[...].astype(F32) + back
+        res_grad_ref[...] = total
+        low_ref[...] = total.astype(LOW)
+
+    ctx_ref[...] = dot(low_ref[...], wout_ref[...], 1, 1).astype(LOW)
+
+
+def residual_backward(back_sum, residual, scale, gain, grad_low, wout_all):
+    rows, width = residual.shape
+    heads = wout_all.shape[0]
+    step = 512
+    return pl.pallas_call(
+        residual_backward_kernel,
+        grid=(heads // step,),
+        in_specs=[
+            once((rows, width)),
+            once((rows, width)),
+            once((rows, 1)),
+            once((1, width)),
+            once((rows, width)),
+            per_seq((step, width)),
+        ],
+        out_specs=[
+            once((rows, width)),
+            once((rows, width)),
+            pl.BlockSpec((rows, step), lambda i: (0, i)),
+        ],
+        out_shape=[
+            jax.ShapeDtypeStruct((rows, width), F32),
+            jax.ShapeDtypeStruct((rows, width), LOW),
+            jax.ShapeDtypeStruct((rows, heads), LOW),
+        ],
+        compiler_params=pltpu.CompilerParams(vmem_limit_bytes=40 * MIB),
+        cost_estimate=SMALL,
+        name="residual_backward",
+    )(back_sum, residual, scale, gain[None, :], grad_low, wout_all)
 
 
 TILE = 512
@@ -709,83 +792,101 @@
         )
         return gate_up, row_cut(halves_d, chunk)
 
-    attn_block = plan.blocks(qkv_parts, out_parts)
-    ffn_blocks = [plan.blocks(*ffn_parts(chunk)) for chunk in range(CHUNKS)]
     hidden = halves_d[0].shape[0] // CHUNKS
     attn_shapes = (width, qkv_parts[0].shape[1]), (out_parts[0].shape[0], width)
     ffn_shapes = (width, 2 * hidden), (hidden, width)
-
-    if plan.line:
+    own_rows = layer_input.shape[0]
+    core = lax.axis_index("tp") % 2
+
+    if plan.line:
+        attn_own, attn_other = plan.pack(qkv_parts, out_parts)
+        own_1, other_1 = plan.pack(*ffn_parts(0))
+        own_2, other_2 = plan.pack(*ffn_parts(1))
+        attn_theirs = plan.swap(attn_other)
+        attn_theirs, marks_all = fence(attn_theirs, marks_all)
+        attn_block = plan.join(attn_own, attn_theirs)
         near, across = line_near(attn_block)
+        theirs_1 = plan.swap(other_1)
+        near, across, theirs_1 = fence(near, across, theirs_1)
         across_near, out = line_far(near, across)
+        theirs_2 = plan.swap(other_2)
+        block_1 = plan.join(own_1, theirs_1)
+        across_near, out, theirs_2, block_1 = fence(across_near, out, theirs_2, block_1)
         out_near = line_last(across_near)
+        block_2 = plan.join(own_2, theirs_2)
+        out_near, normed_all, cosine, sine, block_1, block_2 = fence(
+            out_near, normed_all, cosine, sine, block_1, block_2
+        )
         attn_weights = (attn_block, near, across_near, out, across, out_near)
-        first_block = after(ffn_blocks[0], out_near)
-        near_1, across_1 = line_near(first_block)
+        near_1, across_1 = line_near(block_1)
     else:
-        attn_weights = plan.plain_gather(attn_block)
+        attn_weights = plan.plain_gather(qkv_parts, out_parts)
+        first_weights = plan.plain_gather(*ffn_parts(0))
+        second_weights = plan.plain_gather(*ffn_parts(1))
     attn_loader = Loader(plan, attn_weights, *attn_shapes)
 
-    attn_part, ctx, queries, both, lse = attn_forward(
+    attn_part, ctx, queries, both, lse, wout = attn_forward(
         attn_loader, normed_all, cosine, sine, seg_col, seg_row
     )
+    grad_y, grad_x = plane.swap_y(grad_low), plane.swap_x(grad_low)
+    if plan.line:
+        attn_part, near_1, across_1, grad_y, grad_x = fence(
+            attn_part, near_1, across_1, grad_y, grad_x
+        )
+        across_near_1, out_1 = line_far(near_1, across_1)
     attn_sum = lax.psum_scatter(attn_part, axes, scatter_dimension=0, tiled=True)
-
-    grad_y = plane.swap_y(after(grad_low, normed_all))
-    grad_half = cat([pick(plane.y, grad_low, grad_y), pick(plane.y, grad_y, grad_low)], 0)
-
-    if plan.line:
-        near_1, across_1 = after((near_1, across_1), attn_part)
-        across_near_1, out_1 = line_far(near_1, across_1)
-        attn_sum = after(attn_sum, across_near_1, out_1, grad_y)
-        second_block = after(ffn_blocks[1], out_1, across_near_1)
-        near_2, across_2 = line_near(second_block)
+    grad_xy = plane.swap_x(grad_y)
+    if plan.line:
+        across_near_1, out_1, grad_xy, block_2 = fence(across_near_1, out_1, grad_xy, block_2)
         out_near_1 = line_last(across_near_1)
-        first_weights = (first_block, near_1, across_near_1, out_1, across_1, out_near_1)
-    else:
-        first_weights = plan.plain_gather(ffn_blocks[0])
-        second_weights = plan.plain_gather(ffn_blocks[1])
-
+        across_2 = lax.ppermute(block_2, "do", MIDDLE)
+    over_y = cat([pick(plane.y, grad_low, grad_y), pick(plane.y, grad_y, grad_low)], 0)
+    over_xy = cat([pick(plane.y, grad_x, grad_xy), pick(plane.y, grad_xy, grad_x)], 0)
+    grad_core = cat([by_x(over_y, over_xy), by_x(over_xy, over_y)], 0)
+    grad_other = plane.swap_core(grad_core)
+    groups = (rows // own_rows // 2, 1, own_rows, width)
+    mine, theirs = grad_core.reshape(groups), grad_other.reshape(groups)
+    grad_all = cat([pick(core, mine, theirs), pick(core, theirs, mine)], 1).reshape(rows, width)
+
+    if plan.line:
+        attn_sum, out_near_1, across_2, grad_all, block_2 = fence(
+            attn_sum, out_near_1, across_2, grad_all, block_2
+        )
+        first_weights = (block_1, near_1, across_near_1, out_1, across_1, out_near_1)
+        near_2 = lax.ppermute(block_2, "do", NEAR)
     residual = inputs_f + attn_sum.astype(F32)
     normed_two, scale_two = norm_rows(residual, gain_two)
     two_all = lax.all_gather(normed_two.astype(LOW), axes, axis=0, tiled=True)
 
-    grad_x = plane.swap_x(grad_half)
-    grad_core = cat([by_x(grad_half, grad_x), by_x(grad_x, grad_half)], 0)
-    grad_other = plane.swap_core(grad_core)
-    own_rows = layer_input.shape[0]
-    core = lax.axis_index("tp") % 2
-    groups = (rows // own_rows // 2, 1, own_rows, width)
-    mine, theirs = grad_core.reshape(groups), grad_other.reshape(groups)
-    grad_all = cat([pick(core, mine, theirs), pick(core, theirs, mine)], 1).reshape(rows, width)
-
+    if plan.line:
+        near_2, across_2 = fence(near_2, across_2)
+        across_near_2, out_2 = line_far(near_2, across_2)
     first = Loader(plan, first_weights, *ffn_shapes)
-    if plan.line:
-        two_all = after(two_all, near_2, across_2)
-        across_near_2, out_2 = line_far(near_2, across_2)
     back_1, act_1, both_1 = ffn_main(first, two_all, grad_all, None)
-    if plan.line:
-        act_1 = after(act_1, across_near_2, out_2)
+    two_all, wout = fence(two_all, wout)
+    wout_all = lax.all_gather(wout, axes, axis=0, tiled=True)
+    if plan.line:
+        back_1, act_1, both_1, across_near_2, out_2 = fence(
+            back_1, act_1, both_1, across_near_2, out_2
+        )
         out_near_2 = line_last(across_near_2)
-        second_weights = (second_block, near_2, across_near_2, out_2, across_2, out_near_2)
     out_1_part, gain_1, *grads_1 = ffn_weights(first, two_all, grad_all, act_1, both_1, None)
+    if plan.line:
+        back_1, out_1_part, grads_1, out_near_2 = fence(back_1, out_1_part, grads_1, out_near_2)
+        second_weights = (block_2, near_2, across_near_2, out_2, across_2, out_near_2)
+        far_1 = sum_far(grads_1)
     second = Loader(plan, second_weights, *ffn_shapes)
-    if plan.line:
-        far_1 = sum_far(grads_1)
-        back_1 = after(back_1, out_1_part)
     back_2, act_2, both_2 = ffn_main(second, two_all, grad_all, back_1)
+    if plan.line:
+        back_2, act_2, both_2, far_1, wout_all = fence(back_2, act_2, both_2, far_1, wout_all)
+        crossed_1, inward_1 = sum_middle(grads_1, far_1)
     back_sum = lax.psum_scatter(back_2, axes, scatter_dimension=0, tiled=True)
-    if plan.line:
-        far_1 = after(far_1, back_2)
-        crossed_1, inward_1 = sum_middle(grads_1, far_1)
-        act_2 = after(act_2, far_1)
     out_2_part, gain_2, *grads_2 = ffn_weights(second, two_all, grad_all, act_2, both_2, out_1_part)
     if plan.line:
+        out_2_part, grads_2, crossed_1, inward_1 = fence(out_2_part, grads_2, crossed_1, inward_1)
+        near_sum_1, across_sum_1 = sum_near(grads_1, crossed_1, inward_1)
         far_2 = sum_far(grads_2)
-        crossed_1, inward_1 = after((crossed_1, inward_1), out_2_part)
-        near_sum_1, across_sum_1 = sum_near(grads_1, crossed_1, inward_1)
-        back_sum = after(back_sum, crossed_1, inward_1, far_2)
-        crossed_2, inward_2 = sum_middle(grads_2, far_2)
+        back_sum, near_sum_1, across_sum_1 = fence(back_sum, near_sum_1, across_sum_1)
 
     out_shape = (rows // own_rows // 2, 2, own_rows, width)
     parts = out_2_part.reshape(out_shape)
@@ -797,29 +898,42 @@
     summed = add(pick(plane.y, low, high), plane.swap_y(pick(plane.y, high, low)))
     out_value = (residual + summed.reshape(own_rows, width)).astype(LOW)
 
-    normed_two_grad = back_sum.astype(F32)
-    residual_grad = grad_low.astype(F32) + norm_back(normed_two_grad, residual, scale_two, gain_two)
-    res_all = lax.all_gather(residual_grad.astype(LOW), axes, axis=0, tiled=True)
-    if plan.line:
-        res_all = after(res_all, near_sum_1, across_sum_1, crossed_2, inward_2)
+    residual_grad, res_low, ctx_grad = residual_backward(
+        back_sum, residual, scale_two, gain_two, grad_low, wout_all
+    )
+    res_all = lax.all_gather(res_low, axes, axis=0, tiled=True)
+    ctx_grad = lax.all_to_all(ctx_grad, axes, split_axis=1, concat_axis=0, tiled=True)
+    if plan.line:
+        ctx_grad, far_2 = fence(ctx_grad, far_2)
+        crossed_2, inward_2 = sum_middle(grads_2, far_2)
+    back_one_part, gain_one_part, *grads_qkv = attn_backward(
+        attn_loader, ctx_grad, normed_all, queries, both, lse, cosine, sine, seg_col, seg_row
+    )
+    if plan.line:
+        back_one_part, grads_qkv, crossed_2, inward_2 = fence(
+            back_one_part, grads_qkv, crossed_2, inward_2
+        )
+    back_one = lax.psum_scatter(back_one_part, axes, scatter_dimension=0, tiled=True)
+    grads_out = out_weights(plan, ctx, res_all)
+    if plan.line:
+        direct_qkv = send_direct(grads_qkv)
+        gain_one_part, *direct_qkv = fence(gain_one_part, *direct_qkv)
+        direct_out = send_direct(grads_out)
         near_sum_2, across_sum_2 = sum_near(grads_2, crossed_2, inward_2)
-
-    back_one_part, gain_one_part, *grads_attn = attn_backward(
-        attn_loader, res_all, normed_all, ctx, queries, both, lse, cosine, sine, seg_col, seg_row
-    )
-    back_one = lax.psum_scatter(back_one_part, axes, scatter_dimension=0, tiled=True)
-    if plan.line:
-        far = sum_far(grads_attn)
+        total = add(grads_qkv[0], *direct_qkv)
+        half = plan.rows
+        qkv_pair = plan.trade(total[:half], total[half:])
+        total = add(grads_out[0], *direct_out)
+        out_pair = plan.trade(total[:, :half], total[:, half:])
         total_1 = sum_own(grads_1, near_sum_1, across_sum_1)
         total_2 = sum_own(grads_2, near_sum_2, across_sum_2)
-        crossed, inward = sum_middle(grads_attn, far)
-        from_near, from_across = sum_near(grads_attn, crossed, inward)
-        total = sum_own(grads_attn, from_near, from_across)
-        qkv_pair, out_pair = plan.unpack(total, attn_shapes[0][1])
         ffn_grads = [plan.unpack(each, 2 * hidden) for each in (total_1, total_2)]
     else:
-        qkv_pair, out_pair = plan.plain_sum(grads_attn)
-        ffn_grads = [plan.plain_sum(each) for each in (grads_1, grads_2)]
+        qkv_pair = plan.plain_sum_row(grads_qkv[0])
+        out_pair = plan.plain_sum_col(grads_out[0])
+        ffn_grads = [
+            (plan.plain_sum_row(row), plan.plain_sum_col(col)) for row, col in (grads_1, grads_2)
+        ]
     in_grad = residual_grad + norm_back(back_one.astype(F32), inputs_f, scale_one, gain_one)
 
     gain_parts = jnp.stack(

time: 872 us -> 914 us (1.048)
  the two profiles are of different devices: /device:TPU:20 before, /device:TPU:9 now
where the time goes in v3:
time: 914 us; the launch traced here: 901 us
  waiting for transfers between devices  413 us (45%)
  Pallas kernels  192 us (21%)
  starting transfers between devices  119 us (13%)
  other arithmetic  114 us (12%)
  local copies, waits for them, and re-layouts  47 us (5%)
  between operations  16.2 us (2%)
    pallas_call x2, Pallas kernels, ffn_weights(): pl.pallas_call(functools.partial(ffn_weights_kernel, loader, len(more)),...  66.1 us
    pallas_call x2, Pallas kernels, ffn_main(): pl.pallas_call(functools.partial(ffn_main_kernel, loader, len(more)), gri...  61.9 us
    ppermute x1, waiting for transfers between devices, on_device(): marks_other = lax.ppermute(marks, 'di', PAIR)  57.2 us
    all_to_all x1, waiting for transfers between devices, on_device(): lax.all_to_all(ctx_grad, axes, split_axis=1, concat_axis=0, tiled=True)  57.1 us
    all_gather x1, waiting for transfers between devices, on_device(): two_all = lax.all_gather(normed_two.astype(LOW), axes, axis=0, tiled=True)  53.8 us
    ppermute x6, waiting for transfers between devices, send_direct(): lax.ppermute(part, 'do', perm)  43.6 us
    ppermute x1, waiting for transfers between devices, on_device(): near_2 = lax.ppermute(block_2, 'do', NEAR)  35.8 us
    pallas_call x1, Pallas kernels, attn_backward(): pl.pallas_call(functools.partial(attn_backward_kernel, heads // 128, load...  33 us
  transfers between devices with their start and end apart: 59, of which 31 were waited for; matrix products, arithmetic and copies ran while one was open for 13% of the time, Pallas kernels for 21%

profile of v3, /device:TPU:9, one launch (start us, length us, event | category | flops | bytes accessed | tf_op | source)
XLA Modules:
  0.0 900.7 jit_solution(4212892914123975352)
XLA Ops:
  21.6 57.2 %collective-permute-done.1 = s32[2,1024]{1,0:T(2,128)S(1)} collective-permute-done((s32[2,1024]{1,0:T(2,128)S(1)}, s32[2,1024]{1,0:T(2,128)S(1)}, u32[]{:S(2)}, u32[]{:S(2)}) %collective-permute-start.1) | collective-permute-done | bytes 8224 | tf_op jit(solution)/shard_map/ppermute | solution.py:758
  79.4 4.4 collective-permute-start.3
  83.9 3.7 fusion.14
  91.7 3.2 collective-permute-done.3.refs_5_
  94.9 3.1 collective-permute-start.5
  100.9 7.5 collective-permute-done.5.refs_3_
  108.4 4.1 collective-permute-start.8
  114.0 7.5 collective-permute-done.8.refs_6_
  138.4 21.3 %attn_forward.1 = (bf16[2048,2048]{1,0:T(8,128)(2,1)}, bf16[2048,256]{1,0:T(8,128)(2,1)S(1)}, bf16[2048,256]{1,0:T(8,128)(2,1)}, bf16[2048,128]{1,0:T(8,128)(2,1...) custom-call(s32[1]{0:T(128)} %bitcast.refs_0_, bf16[512,640]{1,0:T(8,128)(2,1)S(1)} %pad_maximum_fusion.12.refs_1_, ...), custom_call_target="tpu_custom_call" | custom-call | flops 1 | bytes 1 | tf_op jit(solution)/shard_map/attn_forward/pallas_call | solution.py:416
  167.4 13.3 %collective-permute-done.15 = bf16[256,2048]{1,0:T(8,128)(2,1)} collective-permute-done((bf16[256,2048]{1,0:T(8,128)(2,1)}, bf16[256,2048]{1,0:T(8,128)(2,1)}, u32[]{:S(2)}, u32[]{:S(2)}) %collective-permute-start.15) | collective-permute-done | bytes 1048608 | tf_op jit(solution)/shard_map/ppermute | solution.py:731
  180.7 9.2 %collective-permute-done.13.refs_3_ = bf16[512,1536]{1,0:T(8,128)(2,1)S(1)} collective-permute-done((bf16[512,1536]{1,0:T(8,128)(2,1)}, bf16[512,1536]{1,0:T(8,128)(2,1)S(1)}, u32[]{:S(2)}, u32[]{:S(2)}) %collective-permute-start.13) | collective-permute-done | bytes 1572896 | tf_op jit(solution)/shard_map/ppermute | solution.py:57
  196.2 10.6 %collective-permute-start.18 = (bf16[1024,2048]{1,0:T(8,128)(2,1)}, bf16[1024,2048]{1,0:T(8,128)(2,1)}, u32[]{:S(2)}, u32[]{:S(2)}) collective-permute-start(bf16[1024,2048]{1,0:T(8,128)(2,1)} %pad_maximum_fusion.1), channel_id=1, source_target_pairs={{0,1},{1,0},{2,3},{3,2},{4,5},{5,4},{6,7},{7,6},{8,9},{9,8},{10,11... | collective-permute-start | bytes 12582920 | tf_op jit(solution)/shard_map/ppermute | solution.py:734
  206.8 4.0 collective-permute-start.16
  210.8 3.3 collective-permute-start.17
  214.2 6.5 broadcast_select_fusion.1
  220.7 7.5 pad_maximum_fusion
  228.2 8.6 copy.80
  236.8 6.9 collective-permute-done.16.refs_6_
  243.7 5.0 collective-permute-done.17.refs_5_
  253.2 53.8 %all-gather.7.cloned.1.call-done.refs_7_ = bf16[2048,2048]{1,0:T(8,128)(2,1)} async-done(((bf16[256,2048]{1,0:T(8,128)(2,1)}), bf16[2048,2048]{1,0:T(8,128)(2,1)}) %all-gather.7.cloned.1.call-update) | async-done | bytes 8388624 | tf_op jit(solution)/shard_map/all_gather | solution.py:859
  307.4 35.8 %collective-permute-done.19.refs_2_ = bf16[512,1536]{1,0:T(8,128)(2,1)S(1)} collective-permute-done((bf16[512,1536]{1,0:T(8,128)(2,1)}, bf16[512,1536]{1,0:T(8,128)(2,1)S(1)}, u32[]{:S(2)}, u32[]{:S(2)}) %collective-permute-start.19) | collective-permute-done | bytes 1572896 | tf_op jit(solution)/shard_map/ppermute | solution.py:856
  343.2 3.1 collective-permute-start.20
  346.3 13.3 %collective-permute-start.21 = (bf16[512,1536]{1,0:T(8,128)(2,1)}, bf16[512,1536]{1,0:T(8,128)(2,1)}, u32[]{:S(2)}, u32[]{:S(2)}) collective-permute-start(bf16[512,1536]{1,0:T(8,128)(2,1)} %collective-permute-done.17.refs_5_), channel_id=1, source_target_pairs={{8,0},{16,24},{9,1},{17,25},{10,2},{18,26},{11,3},{19,27},{12,4},{... | collective-permute-start | bytes 4718600 | tf_op jit(solution)/shard_map/ppermute | solution.py:57
  359.6 30.4 %ffn_main.2 = (bf16[2048,2048]{1,0:T(8,128)(2,1)}, bf16[2048,512]{1,0:T(8,128)(2,1)}, bf16[2048,1024]{1,0:T(8,128)(2,1)}) custom-call(s32[1]{0:T(128)} %bitcast.refs_0_, bf16[512,1536]{1,0:T(8,128)(2,1)} %pad_maximum_fusion.4.refs_1_, bf16[512,1536]{1,0:T(8,128)(2,1)} %collective-permute-done.9.refs_2_, bf16[512,1536]{1,0:T(8,128)(2,1)} %copy-done.36, ...), custom_call_target="tpu_custom_call" | custom-call | flops 1 | bytes 1 | tf_op jit(solution)/shard_map/ffn_main/pallas_call | solution.py:595
  392.5 30.7 %ffn_weights.2 = (bf16[2048,2048]{1,0:T(8,128)(2,1)}, f32[2048,1]{1,0:T(8,128)}, bf16[512,1536]{1,0:T(8,128)(2,1)}, bf16[512,1536]{1,0:T(8,128)(2,1)}, bf16[512,...) custom-call(s32[1]{0:T(128)} %bitcast.refs_0_, bf16[512,1536]{1,0:T(8,128)(2,1)} %pad_maximum_fusion.4.refs_1_, ...), custom_call_target="tpu_custom_call" | custom-call | flops 1 | bytes 1 | tf_op jit(solution)/shard_map/ffn_weights/pallas_call | solution.py:655
  425.6 31.5 %ffn_main.3 = (bf16[2048,2048]{1,0:T(8,128)(2,1)}, bf16[2048,512]{1,0:T(8,128)(2,1)}, bf16[2048,1024]{1,0:T(8,128)(2,1)}) custom-call(s32[1]{0:T(128)} %bitcast.refs_0_, bf16[512,1536]{1,0:T(8,128)(2,1)} %pad_maximum_fusion.5.refs_1_, bf16[512,1536]{1,0:T(8,128)(2,1)} %copy-done.35, bf16[512,1536]{1,0:T(8,128)(2,1)} %collective-permute-done.20.refs_3_, ...), custom_call_target="tpu_custom_call" | custom-call | flops 1 | bytes 1 | tf_op jit(solution)/shard_map/ffn_main/pallas_call | solution.py:595
  457.1 3.6 collective-permute-done.23
  460.9 3.4 add_convert_fusion.6
  464.3 3.6 collective-permute-start.24
  469.6 35.4 %ffn_weights.3 = (bf16[2048,2048]{1,0:T(8,128)(2,1)}, f32[2048,1]{1,0:T(8,128)}, bf16[512,1536]{1,0:T(8,128)(2,1)}, bf16[512,1536]{1,0:T(8,128)(2,1)}, bf16[512,...) custom-call(s32[1]{0:T(128)} %bitcast.refs_0_, bf16[512,1536]{1,0:T(8,128)(2,1)} %pad_maximum_fusion.5.refs_1_, ...), custom_call_target="tpu_custom_call" | custom-call | flops 1 | bytes 1 | tf_op jit(solution)/shard_map/ffn_weights/pallas_call | solution.py:655
  505.0 3.5 add_convert_fusion.5
  510.8 2.9 add_convert_fusion.4
  516.7 27.1 %collective-permute-done.29 = bf16[512,1536]{1,0:T(8,128)(2,1)} collective-permute-done((bf16[512,1536]{1,0:T(8,128)(2,1)}, bf16[512,1536]{1,0:T(8,128)(2,1)}, u32[]{:S(2)}, u32[]{:S(2)}) %collective-permute-start.29) | collective-permute-done | bytes 1572896 | tf_op jit(solution)/shard_map/ppermute | solution.py:83
  543.8 5.7 collective-permute-done.30
  550.7 6.5 residual_backward.1
  560.5 3.8 select_bitcast_fusion
  564.3 3.3 collective-permute-start.26
  569.0 5.5 collective-permute-done.26
  574.4 4.7 fusion
  585.2 4.1 all-to-all-start
  589.5 2.9 convert_add_fusion.3
  596.6 9.0 %collective-permute-done.31 = bf16[512,1536]{1,0:T(8,128)(2,1)} collective-permute-done((bf16[512,1536]{1,0:T(8,128)(2,1)S(1)}, bf16[512,1536]{1,0:T(8,128)(2,1)}, u32[]{:S(2)}, u32[]{:S(2)}) %collective-permute-start.31) | collective-permute-done | bytes 1572896 | tf_op jit(solution)/shard_map/ppermute | solution.py:72
  605.6 57.1 %all-to-all-done = bf16[256,8,256]{2,0,1:T(8,128)(2,1)S(1)} async-done(((bf16[256,8,256]{2,0,1:T(8,128)(2,1)}), bf16[256,8,256]{2,0,1:T(8,128)(2,1)S(1)}, u32[]{:S(2)}, u32[]{:S(2)}) %all-to-all-start) | async-done | bytes 1048608 | tf_op jit(solution)/shard_map/all_to_all | solution.py:905
  669.6 2.9 add_convert_fusion
  674.7 5.0 collective-permute-done.44
  682.4 33.0 %attn_backward.1 = (bf16[2048,2048]{1,0:T(8,128)(2,1)}, f32[2048,1]{1,0:T(8,128)}, bf16[512,384]{1,0:T(8,128)(2,1)S(1)}, bf16[512,384]{1,0:T(8,128)(2,1)S(1)}, b...) custom-call(s32[1]{0:T(128)} %bitcast.refs_0_, bf16[512,640]{1,0:T(8,128)(2,1)} %copy-done.1, ...), custom_call_target="tpu_custom_call" | custom-call | flops 1 | bytes 1 | tf_op jit(solution)/shard_map/attn_backward/pallas_call | solution.py:455
  718.2 3.4 add_convert_fusion.1
  721.6 3.2 collective-permute-start.43
  724.8 5.4 collective-permute-done.34
  730.2 4.1 collective-permute-done.35
  734.3 17.2 %collective-permute-done.36 = bf16[512,384]{1,0:T(8,128)(2,1)} collective-permute-done((bf16[512,384]{1,0:T(8,128)(2,1)S(1)}, bf16[512,384]{1,0:T(8,128)(2,1)}, u32[]{:S(2)}, u32[]{:S(2)}) %collective-permute-start.36) | collective-permute-done | bytes 393248 | tf_op jit(solution)/shard_map/ppermute | solution.py:92
  759.3 29.0 %collective-permute-done.47 = f32[2,2048]{1,0:T(2,128)S(1)} collective-permute-done((f32[2,2048]{1,0:T(2,128)S(1)}, f32[2,2048]{1,0:T(2,128)S(1)}, u32[]{:S(2)}, u32[]{:S(2)}) %collective-permute-start.47) | collective-permute-done | bytes 16416 | tf_op jit(solution)/shard_map/ppermute | solution.py:710
  791.7 5.8 collective-permute-start.49
  801.8 3.8 collective-permute-done.37
  813.6 15.3 %collective-permute-done.45 = bf16[256,1536]{1,0:T(8,128)(2,1)S(1)} collective-permute-done((bf16[256,1536]{1,0:T(8,128)(2,1)S(1)}, bf16[256,1536]{1,0:T(8,128)(2,1)S(1)}, u32[]{:S(2)}, u32[]{:S(2)}) %collective-permute-start.45) | collective-permute-done | bytes 786464 | tf_op jit(solution)/shard_map/ppermute | solution.py:160
  835.8 4.6 multiply_subtract_fusion.2
  841.5 4.1 multiply_subtract_fusion
  845.6 3.4 copy-done
  849.0 3.2 out_weights.1
  855.0 3.7 multiply_subtract_fusion.1
  858.7 12.5 %collective-permute-done.40 = bf16[256,512]{1,0:T(8,128)(2,1)S(1)} collective-permute-done((bf16[256,512]{1,0:T(8,128)(2,1)S(1)}, bf16[256,512]{1,0:T(8,128)(2,1)S(1)}, u32[]{:S(2)}, u32[]{:S(2)}) %collective-permute-start.40) | collective-permute-done | bytes 262176 | tf_op jit(solution)/shard_map/ppermute | solution.py:92
  871.2 4.4 collective-permute-done.39
  878.3 3.4 collective-permute-done.41
  885.2 4.0 fusion.9
  (383 shorter events, 145.2 us)
Async XLA Ops:
  7.2 115.2 %all-gather.5.cloned.1.call-start = ((), (), s32[]{:S(2)}) async-start(), calls=%async_computation.4 | async-start | bytes 9437184 | tf_op jit(solution)/shard_map/all_gather | solution.py:755
  12.5 236.2 %reduce-scatter.4.cloned.1.call-start = ((), (), s32[]{:S(2)}) async-start(), calls=%async_computation.5 | async-start | bytes 9437184 | tf_op jit(solution)/shard_map/reduce_scatter | solution.py:837
  13.1 65.8 %collective-permute-start = (bf16[256,640]{1,0:T(8,128)(2,1)S(1)}, bf16[256,640]{1,0:T(8,128)(2,1)S(1)}, u32[]{:S(2)}, u32[]{:S(2)}) collective-permute-start(bf16[256,640]{1,0:T(8,128)(2,1)S(1)} %pad_maximum_fusion.14), channel_id=1, source_target_pairs={{0,4},{4,0},{1,5},{5,1},{2,6},{6,2},{3,7},{7,3},{8,12},{12,8},{9,1... | collective-permute-start | bytes 983048 | tf_op jit(solution)/shard_map/ppermute | solution.py:129
  17.1 74.3 %collective-permute-start.4 = (bf16[256,1536]{1,0:T(8,128)(2,1)S(1)}, bf16[256,1536]{1,0:T(8,128)(2,1)S(1)}, u32[]{:S(2)}, u32[]{:S(2)}) collective-permute-start(bf16[256,1536]{1,0:T(8,128)(2,1)S(1)} %pad_maximum_fusion.8), channel_id=1, source_target_pairs={{0,4},{4,0},{1,5},{5,1},{2,6},{6,2},{3,7},{7,3},{8,12},{12,8},{9,1... | collective-permute-start | bytes 2359304 | tf_op jit(solution)/shard_map/ppermute | solution.py:129
  18.4 82.4 %collective-permute-start.7 = (bf16[256,1536]{1,0:T(8,128)(2,1)S(1)}, bf16[256,1536]{1,0:T(8,128)(2,1)S(1)}, u32[]{:S(2)}, u32[]{:S(2)}) collective-permute-start(bf16[256,1536]{1,0:T(8,128)(2,1)S(1)} %pad_maximum_fusion.9), channel_id=1, source_target_pairs={{0,4},{4,0},{1,5},{5,1},{2,6},{6,2},{3,7},{7,3},{8,12},{12,8},{9,1... | collective-permute-start | bytes 2359304 | tf_op jit(solution)/shard_map/ppermute | solution.py:129
  18.7 60.1 %collective-permute-start.1 = (s32[2,1024]{1,0:T(2,128)S(1)}, s32[2,1024]{1,0:T(2,128)S(1)}, u32[]{:S(2)}, u32[]{:S(2)}) collective-permute-start(s32[2,1024]{1,0:T(2,128)S(1)} %pad_add_fusion.1), channel_id=1, source_target_pairs={{0,4},{4,0},{1,5},{5,1},{2,6},{6,2},{3,7},{7,3},{8,12},{12,8},{9,1... | collective-permute-start | bytes 24584 | tf_op jit(solution)/shard_map/ppermute | solution.py:758
  79.1 56.0 %copy-start.1 = (bf16[512,640]{1,0:T(8,128)(2,1)}, bf16[512,640]{1,0:T(8,128)(2,1)S(1)}, u32[]{:S(2)}) copy-start(bf16[512,640]{1,0:T(8,128)(2,1)S(1)} %pad_maximum_fusion.12.refs_1_) | copy-start | bytes 1966084
  79.1 12.5 %collective-permute-start.2 = (bf16[512,640]{1,0:T(8,128)(2,1)S(1)}, bf16[512,640]{1,0:T(8,128)(2,1)S(1)}, u32[]{:S(2)}, u32[]{:S(2)}) collective-permute-start(bf16[512,640]{1,0:T(8,128)(2,1)S(1)} %pad_maximum_fusion.12.refs_1_), channel_id=1, source_target_pairs={{0,8},{8,0},{16,24},{24,16},{1,9},{9,1},{17,25},{25,17},{2,10},{10... | collective-permute-start | bytes 1966088 | tf_op jit(solution)/shard_map/ppermute | solution.py:53
  79.4 15.5 %collective-permute-start.3 = (bf16[512,640]{1,0:T(8,128)(2,1)S(1)}, bf16[512,640]{1,0:T(8,128)(2,1)S(1)}, u32[]{:S(2)}, u32[]{:S(2)}) collective-permute-start(bf16[512,640]{1,0:T(8,128)(2,1)S(1)} %pad_maximum_fusion.12.refs_1_), channel_id=1, source_target_pairs={{8,16},{16,8},{9,17},{17,9},{10,18},{18,10},{11,19},{19,11},{12,20... | collective-permute-start | bytes 1966088 | tf_op jit(solution)/shard_map/ppermute | solution.py:53
  91.7 43.5 %copy-start.2 = (bf16[512,640]{1,0:T(8,128)(2,1)}, bf16[512,640]{1,0:T(8,128)(2,1)S(1)}, u32[]{:S(2)}) copy-start(bf16[512,640]{1,0:T(8,128)(2,1)S(1)} %collective-permute-done.2.refs_2_) | copy-start | bytes 1966084
  94.9 13.5 %collective-permute-start.5 = (bf16[512,640]{1,0:T(8,128)(2,1)S(1)}, bf16[512,640]{1,0:T(8,128)(2,1)S(1)}, u32[]{:S(2)}, u32[]{:S(2)}) collective-permute-start(bf16[512,640]{1,0:T(8,128)(2,1)S(1)} %collective-permute-done.2.refs_2_), channel_id=1, source_target_pairs={{8,16},{16,8},{9,17},{17,9},{10,18},{18,10},{11,19},{19,11},{12,20... | collective-permute-start | bytes 1966088 | tf_op jit(solution)/shard_map/ppermute | solution.py:57
  98.0 10.4 %collective-permute-start.6 = (bf16[512,640]{1,0:T(8,128)(2,1)S(1)}, bf16[512,640]{1,0:T(8,128)(2,1)S(1)}, u32[]{:S(2)}, u32[]{:S(2)}) collective-permute-start(bf16[512,640]{1,0:T(8,128)(2,1)S(1)} %collective-permute-done.3.refs_5_), channel_id=1, source_target_pairs={{8,0},{16,24},{9,1},{17,25},{10,2},{18,26},{11,3},{19,27},{12,4},{... | collective-permute-start | bytes 1966088 | tf_op jit(solution)/shard_map/ppermute | solution.py:57
  108.4 13.2 %collective-permute-start.8 = (bf16[512,640]{1,0:T(8,128)(2,1)S(1)}, bf16[512,640]{1,0:T(8,128)(2,1)S(1)}, u32[]{:S(2)}, u32[]{:S(2)}) collective-permute-start(bf16[512,640]{1,0:T(8,128)(2,1)S(1)} %collective-permute-done.5.refs_3_), channel_id=1, source_target_pairs={{8,0},{16,24},{9,1},{17,25},{10,2},{18,26},{11,3},{19,27},{12,4},{... | collective-permute-start | bytes 1966088 | tf_op jit(solution)/shard_map/ppermute | solution.py:61
  122.4 39.1 %collective-permute-start.9 = (bf16[512,1536]{1,0:T(8,128)(2,1)}, bf16[512,1536]{1,0:T(8,128)(2,1)}, u32[]{:S(2)}, u32[]{:S(2)}) collective-permute-start(bf16[512,1536]{1,0:T(8,128)(2,1)} %pad_maximum_fusion.4.refs_1_), channel_id=1, source_target_pairs={{0,8},{8,0},{16,24},{24,16},{1,9},{9,1},{17,25},{25,17},{2,10},{10... | collective-permute-start | bytes 4718600 | tf_op jit(solution)/shard_map/ppermute | solution.py:53
  124.6 36.9 %collective-permute-start.10 = (bf16[512,1536]{1,0:T(8,128)(2,1)}, bf16[512,1536]{1,0:T(8,128)(2,1)}, u32[]{:S(2)}, u32[]{:S(2)}) collective-permute-start(bf16[512,1536]{1,0:T(8,128)(2,1)} %pad_maximum_fusion.4.refs_1_), channel_id=1, source_target_pairs={{8,16},{16,8},{9,17},{17,9},{10,18},{18,10},{11,19},{19,11},{12,20... | collective-permute-start | bytes 4718600 | tf_op jit(solution)/shard_map/ppermute | solution.py:53
  130.3 31.3 %collective-permute-start.11 = (bf16[256,2048]{1,0:T(8,128)(2,1)S(1)}, bf16[256,2048]{1,0:T(8,128)(2,1)}, u32[]{:S(2)}, u32[]{:S(2)}) collective-permute-start(bf16[256,2048]{1,0:T(8,128)(2,1)S(1)} %maximum_select_fusion.7.grad_ref), channel_id=1, source_target_pairs={{0,2},{1,3},{2,0},{3,1},{4,6},{5,7},{6,4},{7,5},{8,10},{9,11},{10,... | collective-permute-start | bytes 3145736 | tf_op jit(solution)/shard_map/ppermute | solution.py:728
  131.6 29.9 %collective-permute-start.12 = (bf16[256,2048]{1,0:T(8,128)(2,1)S(1)}, bf16[256,2048]{1,0:T(8,128)(2,1)}, u32[]{:S(2)}, u32[]{:S(2)}) collective-permute-start(bf16[256,2048]{1,0:T(8,128)(2,1)S(1)} %maximum_select_fusion.7.grad_ref), channel_id=1, source_target_pairs={{0,4},{4,0},{1,5},{5,1},{2,6},{6,2},{3,7},{7,3},{8,12},{12,8},{9,1... | collective-permute-start | bytes 3145736 | tf_op jit(solution)/shard_map/ppermute | solution.py:731
  161.5 145.4 %all-gather.7.cloned.1.call-start = ((), (), s32[]{:S(2)}) async-start(), calls=%async_computation.6 | async-start | bytes 9437184 | tf_op jit(solution)/shard_map/all_gather | solution.py:859
  161.6 28.3 %collective-permute-start.13 = (bf16[512,1536]{1,0:T(8,128)(2,1)}, bf16[512,1536]{1,0:T(8,128)(2,1)S(1)}, u32[]{:S(2)}, u32[]{:S(2)}) collective-permute-start(bf16[512,1536]{1,0:T(8,128)(2,1)} %collective-permute-done.9.refs_2_), channel_id=1, source_target_pairs={{8,16},{16,8},{9,17},{17,9},{10,18},{18,10},{11,19},{19,11},{12,20... | collective-permute-start | bytes 4718600 | tf_op jit(solution)/shard_map/ppermute | solution.py:57
  163.5 26.4 %collective-permute-start.14 = (bf16[512,1536]{1,0:T(8,128)(2,1)}, bf16[512,1536]{1,0:T(8,128)(2,1)}, u32[]{:S(2)}, u32[]{:S(2)}) collective-permute-start(bf16[512,1536]{1,0:T(8,128)(2,1)} %collective-permute-done.10.refs_5_), channel_id=1, source_target_pairs={{8,0},{16,24},{9,1},{17,25},{10,2},{18,26},{11,3},{19,27},{12,4},{... | collective-permute-start | bytes 4718600 | tf_op jit(solution)/shard_map/ppermute | solution.py:57
  166.0 14.7 %collective-permute-start.15 = (bf16[256,2048]{1,0:T(8,128)(2,1)}, bf16[256,2048]{1,0:T(8,128)(2,1)}, u32[]{:S(2)}, u32[]{:S(2)}) collective-permute-start(bf16[256,2048]{1,0:T(8,128)(2,1)} %collective-permute-done.11), channel_id=1, source_target_pairs={{0,4},{4,0},{1,5},{5,1},{2,6},{6,2},{3,7},{7,3},{8,12},{12,8},{9,1... | collective-permute-start | bytes 3145736 | tf_op jit(solution)/shard_map/ppermute | solution.py:731
  196.2 17.9 %collective-permute-start.18 = (bf16[1024,2048]{1,0:T(8,128)(2,1)}, bf16[1024,2048]{1,0:T(8,128)(2,1)}, u32[]{:S(2)}, u32[]{:S(2)}) collective-permute-start(bf16[1024,2048]{1,0:T(8,128)(2,1)} %pad_maximum_fusion.1), channel_id=1, source_target_pairs={{0,1},{1,0},{2,3},{3,2},{4,5},{5,4},{6,7},{7,6},{8,9},{9,8},{10,11... | collective-permute-start | bytes 12582920 | tf_op jit(solution)/shard_map/ppermute | solution.py:734
  206.8 36.9 %collective-permute-start.16 = (bf16[512,1536]{1,0:T(8,128)(2,1)}, bf16[512,1536]{1,0:T(8,128)(2,1)}, u32[]{:S(2)}, u32[]{:S(2)}) collective-permute-start(bf16[512,1536]{1,0:T(8,128)(2,1)} %copy-done.36), channel_id=1, source_target_pairs={{8,0},{16,24},{9,1},{17,25},{10,2},{18,26},{11,3},{19,27},{12,4},{... | collective-permute-start | bytes 4718600 | tf_op jit(solution)/shard_map/ppermute | solution.py:61
  210.8 37.9 %collective-permute-start.17 = (bf16[512,1536]{1,0:T(8,128)(2,1)}, bf16[512,1536]{1,0:T(8,128)(2,1)}, u32[]{:S(2)}, u32[]{:S(2)}) collective-permute-start(bf16[512,1536]{1,0:T(8,128)(2,1)} %pad_maximum_fusion.5.refs_1_), channel_id=1, source_target_pairs={{8,16},{16,8},{9,17},{17,9},{10,18},{18,10},{11,19},{19,11},{12,20... | collective-permute-start | bytes 4718600 | tf_op jit(solution)/shard_map/ppermute | solution.py:842
  253.1 207.6 %all-gather.9.cloned.1.call-start = ((), (), s32[]{:S(2)}) async-start(), calls=%async_computation.7 | async-start | bytes 9437184 | tf_op jit(solution)/shard_map/all_gather | solution.py:867
  307.0 242.5 %reduce-scatter.6.cloned.1.call-start = ((), (), s32[]{:S(2)}) async-start(), calls=%async_computation.8 | async-start | bytes 9437184 | tf_op jit(solution)/shard_map/reduce_scatter | solution.py:883
  307.0 36.1 %collective-permute-start.19 = (bf16[512,1536]{1,0:T(8,128)(2,1)}, bf16[512,1536]{1,0:T(8,128)(2,1)S(1)}, u32[]{:S(2)}, u32[]{:S(2)}) collective-permute-start(bf16[512,1536]{1,0:T(8,128)(2,1)} %pad_maximum_fusion.5.refs_1_), channel_id=1, source_target_pairs={{0,8},{8,0},{16,24},{24,16},{1,9},{9,1},{17,25},{25,17},{2,10},{10... | collective-permute-start | bytes 4718600 | tf_op jit(solution)/shard_map/ppermute | solution.py:856
  343.2 46.8 %copy-start.35 = (bf16[512,1536]{1,0:T(8,128)(2,1)}, bf16[512,1536]{1,0:T(8,128)(2,1)S(1)}, u32[]{:S(2)}) copy-start(bf16[512,1536]{1,0:T(8,128)(2,1)S(1)} %collective-permute-done.19.refs_2_) | copy-start | bytes 4718596
  343.2 46.8 %collective-permute-start.20 = (bf16[512,1536]{1,0:T(8,128)(2,1)S(1)}, bf16[512,1536]{1,0:T(8,128)(2,1)}, u32[]{:S(2)}, u32[]{:S(2)}) collective-permute-start(bf16[512,1536]{1,0:T(8,128)(2,1)S(1)} %collective-permute-done.19.refs_2_), channel_id=1, source_target_pairs={{8,16},{16,8},{9,17},{17,9},{10,18},{18,10},{11,19},{19,11},{12,20... | collective-permute-start | bytes 4718600 | tf_op jit(solution)/shard_map/ppermute | solution.py:57
  346.3 43.7 %collective-permute-start.21 = (bf16[512,1536]{1,0:T(8,128)(2,1)}, bf16[512,1536]{1,0:T(8,128)(2,1)}, u32[]{:S(2)}, u32[]{:S(2)}) collective-permute-start(bf16[512,1536]{1,0:T(8,128)(2,1)} %collective-permute-done.17.refs_5_), channel_id=1, source_target_pairs={{8,0},{16,24},{9,1},{17,25},{10,2},{18,26},{11,3},{19,27},{12,4},{... | collective-permute-start | bytes 4718600 | tf_op jit(solution)/shard_map/ppermute | solution.py:57
  390.0 34.3 %collective-permute-start.22 = (bf16[512,1536]{1,0:T(8,128)(2,1)}, bf16[512,1536]{1,0:T(8,128)(2,1)}, u32[]{:S(2)}, u32[]{:S(2)}) collective-permute-start(bf16[512,1536]{1,0:T(8,128)(2,1)} %collective-permute-done.20.refs_3_), channel_id=1, source_target_pairs={{8,0},{16,24},{9,1},{17,25},{10,2},{18,26},{11,3},{19,27},{12,4},{... | collective-permute-start | bytes 4718600 | tf_op jit(solution)/shard_map/ppermute | solution.py:61
  424.3 36.4 %collective-permute-start.23 = (bf16[512,1536]{1,0:T(8,128)(2,1)}, bf16[512,1536]{1,0:T(8,128)(2,1)}, u32[]{:S(2)}, u32[]{:S(2)}) collective-permute-start(bf16[512,1536]{1,0:T(8,128)(2,1)} %get-tuple-element.198), channel_id=1, source_target_pairs={{0,8},{24,16},{1,9},{25,17},{2,10},{26,18},{3,11},{27,19},{4,12},{... | collective-permute-start | bytes 4718600 | tf_op jit(solution)/shard_map/ppermute | solution.py:72
  460.8 384.8 %all-gather.11.cloned.1.call-start = ((), (), s32[]{:S(2)}) async-start(), calls=%async_computation.10 | async-start | bytes 9437184 | tf_op jit(solution)/shard_map/all_gather | solution.py:904
  464.3 40.7 %collective-permute-start.24 = (bf16[512,1536]{1,0:T(8,128)(2,1)}, bf16[512,1536]{1,0:T(8,128)(2,1)}, u32[]{:S(2)}, u32[]{:S(2)}) collective-permute-start(bf16[512,1536]{1,0:T(8,128)(2,1)} %add_convert_fusion.6), channel_id=1, source_target_pairs={{8,16},{16,8},{9,17},{17,9},{10,18},{18,10},{11,19},{19,11},{12,20... | collective-permute-start | bytes 4718600 | tf_op jit(solution)/shard_map/ppermute | solution.py:77
  467.9 37.1 %collective-permute-start.25 = (bf16[512,1536]{1,0:T(8,128)(2,1)}, bf16[512,1536]{1,0:T(8,128)(2,1)}, u32[]{:S(2)}, u32[]{:S(2)}) collective-permute-start(bf16[512,1536]{1,0:T(8,128)(2,1)} %add_convert_fusion.6), channel_id=1, source_target_pairs={{0,8},{24,16},{1,9},{25,17},{2,10},{26,18},{3,11},{27,19},{4,12},{... | collective-permute-start | bytes 4718600 | tf_op jit(solution)/shard_map/ppermute | solution.py:77
  508.5 35.2 %collective-permute-start.29 = (bf16[512,1536]{1,0:T(8,128)(2,1)}, bf16[512,1536]{1,0:T(8,128)(2,1)}, u32[]{:S(2)}, u32[]{:S(2)}) collective-permute-start(bf16[512,1536]{1,0:T(8,128)(2,1)} %add_convert_fusion.5), channel_id=1, source_target_pairs={{0,8},{8,0},{16,24},{24,16},{1,9},{9,1},{17,25},{25,17},{2,10},{10... | collective-permute-start | bytes 4718600 | tf_op jit(solution)/shard_map/ppermute | solution.py:83
  513.7 35.8 %collective-permute-start.30 = (bf16[512,1536]{1,0:T(8,128)(2,1)}, bf16[512,1536]{1,0:T(8,128)(2,1)}, u32[]{:S(2)}, u32[]{:S(2)}) collective-permute-start(bf16[512,1536]{1,0:T(8,128)(2,1)} %add_convert_fusion.4), channel_id=1, source_target_pairs={{8,16},{16,8},{9,17},{17,9},{10,18},{18,10},{11,19},{19,11},{12,20... | collective-permute-start | bytes 4718600 | tf_op jit(solution)/shard_map/ppermute | solution.py:83
  564.3 10.1 %collective-permute-start.26 = (bf16[4,256,2048]{2,1,0:T(8,128)(2,1)S(1)}, bf16[4,256,2048]{2,1,0:T(8,128)(2,1)S(1)}, u32[]{:S(2)}, u32[]{:S(2)}) collective-permute-start(bf16[4,256,2048]{2,1,0:T(8,128)(2,1)S(1)} %select_bitcast_fusion), channel_id=1, source_target_pairs={{0,1},{1,0},{2,3},{3,2},{4,5},{5,4},{6,7},{7,6},{8,9},{9,8},{10,11... | collective-permute-start | bytes 12582920 | tf_op jit(solution)/shard_map/ppermute | solution.py:734
  567.7 38.0 %collective-permute-start.31 = (bf16[512,1536]{1,0:T(8,128)(2,1)S(1)}, bf16[512,1536]{1,0:T(8,128)(2,1)}, u32[]{:S(2)}, u32[]{:S(2)}) collective-permute-start(bf16[512,1536]{1,0:T(8,128)(2,1)S(1)} %copy-done.53), channel_id=1, source_target_pairs={{0,8},{24,16},{1,9},{25,17},{2,10},{26,18},{3,11},{27,19},{4,12},{... | collective-permute-start | bytes 4718600 | tf_op jit(solution)/shard_map/ppermute | solution.py:72
  582.0 87.6 %collective-permute-start.27 = (bf16[2,256,2048]{2,1,0:T(8,128)(2,1)}, bf16[2,256,2048]{2,1,0:T(8,128)(2,1)}, u32[]{:S(2)}, u32[]{:S(2)}) collective-permute-start(bf16[2,256,2048]{2,1,0:T(8,128)(2,1)} %broadcast_select_fusion.2), channel_id=1, source_target_pairs={{0,4},{4,0},{1,5},{5,1},{2,6},{6,2},{3,7},{7,3},{8,12},{12,8},{9,1... | collective-permute-start | bytes 6291464 | tf_op jit(solution)/shard_map/ppermute | solution.py:731
  585.2 77.5 %all-to-all-start = ((bf16[256,8,256]{2,0,1:T(8,128)(2,1)}), bf16[256,8,256]{2,0,1:T(8,128)(2,1)S(1)}, u32[]{:S(2)}, u32[]{:S(2)}) async-start(bf16[256,8,256]{2,0,1:T(8,128)(2,1)} %bitcast.43), calls=%async_computation.2 | async-start | bytes 2097152 | tf_op jit(solution)/shard_map/all_to_all | solution.py:905
  589.3 293.9 %reduce-scatter.8.cloned.1.call-start = ((), (), s32[]{:S(2)}) async-start(), calls=%async_computation.9 | async-start | bytes 9437184 | tf_op jit(solution)/shard_map/reduce_scatter | solution.py:916
  595.4 84.3 %collective-permute-start.44 = (bf16[256,1536]{1,0:T(8,128)(2,1)}, bf16[256,1536]{1,0:T(8,128)(2,1)S(1)}, u32[]{:S(2)}, u32[]{:S(2)}) collective-permute-start(bf16[256,1536]{1,0:T(8,128)(2,1)} %select_convert_fusion.1), channel_id=1, source_target_pairs={{0,4},{4,0},{1,5},{5,1},{2,6},{6,2},{3,7},{7,3},{8,12},{12,8},{9,1... | collective-permute-start | bytes 2359304 | tf_op jit(solution)/shard_map/ppermute | solution.py:160
  665.5 50.0 %collective-permute-start.32 = (bf16[512,1536]{1,0:T(8,128)(2,1)S(1)}, bf16[512,1536]{1,0:T(8,128)(2,1)}, u32[]{:S(2)}, u32[]{:S(2)}) collective-permute-start(bf16[512,1536]{1,0:T(8,128)(2,1)S(1)} %add_convert_fusion.3), channel_id=1, source_target_pairs={{8,16},{16,8},{9,17},{17,9},{10,18},{18,10},{11,19},{19,11},{12,20... | collective-permute-start | bytes 4718600 | tf_op jit(solution)/shard_map/ppermute | solution.py:77
  668.3 47.2 %collective-permute-start.33 = (bf16[512,1536]{1,0:T(8,128)(2,1)S(1)}, bf16[512,1536]{1,0:T(8,128)(2,1)}, u32[]{:S(2)}, u32[]{:S(2)}) collective-permute-start(bf16[512,1536]{1,0:T(8,128)(2,1)S(1)} %add_convert_fusion.3), channel_id=1, source_target_pairs={{0,8},{24,16},{1,9},{25,17},{2,10},{26,18},{3,11},{27,19},{4,12},{... | collective-permute-start | bytes 4718600 | tf_op jit(solution)/shard_map/ppermute | solution.py:77
  673.7 211.5 %collective-permute-start.28 = (bf16[1,256,2048]{2,1,0:T(8,128)(2,1)}, bf16[1,256,2048]{2,1,0:T(8,128)(2,1)}, u32[]{:S(2)}, u32[]{:S(2)}) collective-permute-start(bf16[1,256,2048]{2,1,0:T(8,128)(2,1)} %broadcast_select_fusion.6), channel_id=1, source_target_pairs={{0,2},{1,3},{2,0},{3,1},{4,6},{5,7},{6,4},{7,5},{8,10},{9,11},{10,... | collective-permute-start | bytes 3145736 | tf_op jit(solution)/shard_map/ppermute | solution.py:728
  715.5 14.7 %collective-permute-start.34 = (bf16[512,384]{1,0:T(8,128)(2,1)S(1)}, bf16[512,384]{1,0:T(8,128)(2,1)}, u32[]{:S(2)}, u32[]{:S(2)}) collective-permute-start(bf16[512,384]{1,0:T(8,128)(2,1)S(1)} %get-tuple-element.234), channel_id=1, source_target_pairs={{0,8},{8,0},{16,24},{24,16},{1,9},{9,1},{17,25},{25,17},{2,10},{10... | collective-permute-start | bytes 1179656 | tf_op jit(solution)/shard_map/ppermute | solution.py:92
  715.6 18.7 %collective-permute-start.35 = (bf16[512,384]{1,0:T(8,128)(2,1)S(1)}, bf16[512,384]{1,0:T(8,128)(2,1)}, u32[]{:S(2)}, u32[]{:S(2)}) collective-permute-start(bf16[512,384]{1,0:T(8,128)(2,1)S(1)} %get-tuple-element.235), channel_id=1, source_target_pairs={{0,16},{8,24},{16,0},{24,8},{1,17},{9,25},{17,1},{25,9},{2,18},{10... | collective-permute-start | bytes 1179656 | tf_op jit(solution)/shard_map/ppermute | solution.py:92
  717.6 33.8 %collective-permute-start.36 = (bf16[512,384]{1,0:T(8,128)(2,1)S(1)}, bf16[512,384]{1,0:T(8,128)(2,1)}, u32[]{:S(2)}, u32[]{:S(2)}) collective-permute-start(bf16[512,384]{1,0:T(8,128)(2,1)S(1)} %get-tuple-element.236), channel_id=1, source_target_pairs={{0,24},{8,16},{16,8},{24,0},{1,25},{9,17},{17,9},{25,1},{2,26},{10... | collective-permute-start | bytes 1179656 | tf_op jit(solution)/shard_map/ppermute | solution.py:92
  721.6 86.9 %collective-permute-start.43 = (bf16[512,1536]{1,0:T(8,128)(2,1)}, bf16[512,1536]{1,0:T(8,128)(2,1)}, u32[]{:S(2)}, u32[]{:S(2)}) collective-permute-start(bf16[512,1536]{1,0:T(8,128)(2,1)} %add_convert_fusion.1), channel_id=1, source_target_pairs={{8,16},{16,8},{9,17},{17,9},{10,18},{18,10},{11,19},{19,11},{12,20... | collective-permute-start | bytes 4718600 | tf_op jit(solution)/shard_map/ppermute | solution.py:83
  753.1 3.9 collective-permute-start.46
  755.5 53.0 %collective-permute-start.42 = (bf16[512,1536]{1,0:T(8,128)(2,1)S(1)}, bf16[512,1536]{1,0:T(8,128)(2,1)S(1)}, u32[]{:S(2)}, u32[]{:S(2)}) collective-permute-start(bf16[512,1536]{1,0:T(8,128)(2,1)S(1)} %add_convert_fusion.2), channel_id=1, source_target_pairs={{0,8},{8,0},{16,24},{24,16},{1,9},{9,1},{17,25},{25,17},{2,10},{10... | collective-permute-start | bytes 4718600 | tf_op jit(solution)/shard_map/ppermute | solution.py:83
  757.0 31.3 %collective-permute-start.47 = (f32[2,2048]{1,0:T(2,128)S(1)}, f32[2,2048]{1,0:T(2,128)S(1)}, u32[]{:S(2)}, u32[]{:S(2)}) collective-permute-start(f32[2,2048]{1,0:T(2,128)S(1)} %add.307), channel_id=1, source_target_pairs={{0,16},{8,24},{16,0},{24,8},{1,17},{9,25},{17,1},{25,9},{2,18},{10... | collective-permute-start | bytes 49160 | tf_op jit(solution)/shard_map/ppermute | solution.py:710
  759.2 41.9 %copy-start.70 = (f32[2048]{0:T(1024)S(1)}, f32[2048]{0:T(1024)}, u32[]{:S(2)}) copy-start(f32[2048]{0:T(1024)} %param.56) | copy-start | bytes 24580
  759.2 41.9 %copy-start.72 = (f32[2048]{0:T(1024)S(1)}, f32[2048]{0:T(1024)}, u32[]{:S(2)}) copy-start(f32[2048]{0:T(1024)} %param.57) | copy-start | bytes 24580
  788.4 3.4 collective-permute-start.48
  791.7 6.6 collective-permute-start.49
  798.4 2.7 collective-permute-start.50
  799.7 5.9 collective-permute-start.37
  811.3 17.6 %collective-permute-start.45 = (bf16[256,1536]{1,0:T(8,128)(2,1)S(1)}, bf16[256,1536]{1,0:T(8,128)(2,1)S(1)}, u32[]{:S(2)}, u32[]{:S(2)}) collective-permute-start(bf16[256,1536]{1,0:T(8,128)(2,1)S(1)} %select_convert_fusion), channel_id=1, source_target_pairs={{0,4},{4,0},{1,5},{5,1},{2,6},{6,2},{3,7},{7,3},{8,12},{12,8},{9,1... | collective-permute-start | bytes 2359304 | tf_op jit(solution)/shard_map/ppermute | solution.py:160
  852.2 19.0 %collective-permute-start.40 = (bf16[256,512]{1,0:T(8,128)(2,1)S(1)}, bf16[256,512]{1,0:T(8,128)(2,1)S(1)}, u32[]{:S(2)}, u32[]{:S(2)}) collective-permute-start(bf16[256,512]{1,0:T(8,128)(2,1)S(1)} %get-tuple-element.245), channel_id=1, source_target_pairs={{0,24},{8,16},{16,8},{24,0},{1,25},{9,17},{17,9},{25,1},{2,26},{10... | collective-permute-start | bytes 786440 | tf_op jit(solution)/shard_map/ppermute | solution.py:92
  852.8 22.8 %collective-permute-start.39 = (bf16[256,512]{1,0:T(8,128)(2,1)S(1)}, bf16[256,512]{1,0:T(8,128)(2,1)S(1)}, u32[]{:S(2)}, u32[]{:S(2)}) collective-permute-start(bf16[256,512]{1,0:T(8,128)(2,1)S(1)} %get-tuple-element.244), channel_id=1, source_target_pairs={{0,16},{8,24},{16,0},{24,8},{1,17},{9,25},{17,1},{25,9},{2,18},{10... | collective-permute-start | bytes 786440 | tf_op jit(solution)/shard_map/ppermute | solution.py:92
  853.2 22.4 %collective-permute-start.38 = (bf16[256,512]{1,0:T(8,128)(2,1)S(1)}, bf16[256,512]{1,0:T(8,128)(2,1)S(1)}, u32[]{:S(2)}, u32[]{:S(2)}) collective-permute-start(bf16[256,512]{1,0:T(8,128)(2,1)S(1)} %get-tuple-element.243), channel_id=1, source_target_pairs={{0,8},{8,0},{16,24},{24,16},{1,9},{9,1},{17,25},{25,17},{2,10},{10... | collective-permute-start | bytes 786440 | tf_op jit(solution)/shard_map/ppermute | solution.py:92
  875.8 5.9 collective-permute-start.41
  (80 other events, 631.4 us)
Sparse Core Ops, SparseCore 0:
  12.6 79.6 all-gather.4
  161.7 77.5 reduce-scatter.3
  253.3 53.6 all-gather.6
  309.4 54.3 all-gather.8
  460.9 72.8 reduce-scatter.5
  560.6 80.6 all-gather.10
  724.9 71.7 reduce-scatter.7

commit v4 on v3

--- a/solution.py
+++ b/solution.py
@@ -28,8 +28,6 @@
 
 NEAR = [(0, 1), (1, 0), (2, 3), (3, 2)]
 MIDDLE = [(1, 2), (2, 1)]
-OUTWARD = [(1, 0), (2, 3)]
-INWARD = [(0, 1), (3, 2)]
 CROSS = [(0, 2), (1, 3), (2, 0), (3, 1)]
 MIRROR = [(0, 3), (1, 2), (2, 1), (3, 0)]
 PAIR = [(0, 1), (1, 0)]
@@ -54,11 +52,11 @@
 
 
 def line_far(near, across):
-    return lax.ppermute(near, "do", MIDDLE), lax.ppermute(across, "do", OUTWARD)
+    return lax.ppermute(near, "do", MIDDLE), lax.ppermute(across, "do", NEAR)
 
 
 def line_last(across_near):
-    return lax.ppermute(across_near, "do", OUTWARD)
+    return lax.ppermute(across_near, "do", NEAR)
 
 
 def add(part, *arrived):
@@ -68,23 +66,34 @@
     return total
 
 
+def is_inner():
+    place = lax.axis_index("do")
+    return (place == 1) | (place == 2)
+
+
+def add_inner(part, arrived):
+    return add(part, jnp.where(is_inner(), arrived, jnp.zeros_like(arrived)))
+
+
 def sum_far(parts):
-    return lax.ppermute(parts[3], "do", INWARD)
+    return lax.ppermute(parts[3], "do", NEAR)
 
 
 def sum_middle(parts, far):
-    second = add(parts[2], far).astype(LOW)
-    return lax.ppermute(second, "do", MIDDLE), lax.ppermute(second, "do", INWARD)
-
-
-def sum_near(parts, crossed, inward):
-    first = add(parts[1], crossed).astype(LOW)
-    third = add(parts[3], inward).astype(LOW)
+    second = add_inner(parts[2], far).astype(LOW)
+    return lax.ppermute(second, "do", MIDDLE), lax.ppermute(second, "do", NEAR)
+
+
+def sum_near_parts(parts, crossed, inward):
+    return add_inner(parts[1], crossed).astype(LOW), add_inner(parts[3], inward).astype(LOW)
+
+
+def sum_near_send(first, third):
     return lax.ppermute(first, "do", NEAR), lax.ppermute(third, "do", MIDDLE)
 
 
 def sum_own(parts, from_near, from_across):
-    return add(parts[0], from_near, from_across)
+    return add_inner(parts[0], from_across) + from_near.astype(F32)
 
 
 def send_direct(parts):
@@ -115,8 +124,7 @@
         return jnp.where(lax.axis_index("di") == 0, low, high)
 
     def inner(self):
-        place = lax.axis_index("do")
-        return ((place == 1) | (place == 2)).astype(jnp.int32).reshape(1)
+        return is_inner().astype(jnp.int32).reshape(1)
 
     def pack(self, row_part, col_part):
         rows, packs = self.rows, []
@@ -718,20 +726,35 @@
 
 class Plane:
     def __init__(self, tp):
-        self.tp = tp
-        self.half = tp // 2
+        self.tp, self.half = tp, tp // 2
         self.x = lax.axis_index("di")
         self.y = lax.axis_index("tp") // self.half
-        self.far = [(i, (i + self.half) % tp) for i in range(tp)]
-
-    def swap_y(self, value):
-        return lax.ppermute(value, "tp", self.far)
-
-    def swap_x(self, value):
-        return lax.ppermute(value, "di", PAIR)
+        self.core = lax.axis_index("tp") % 2
+        self.place = self.x * 2 + self.y
+        self.axes = ("di", "tp")
+
+    def pairs(self, first):
+        def other(index):
+            x, t = divmod(index, self.tp)
+            along_x = (t % 2 == 0) == first
+            return (1 - x) * self.tp + t if along_x else x * self.tp + (t + self.half) % self.tp
+
+        return [(index, other(index)) for index in range(2 * self.tp)]
+
+    def swap_first(self, value):
+        return lax.ppermute(value, self.axes, self.pairs(True))
+
+    def swap_second(self, value):
+        return lax.ppermute(value, self.axes, self.pairs(False))
 
     def swap_core(self, value):
         return lax.ppermute(value, "tp", [(i, i ^ 1) for i in range(self.tp)])
+
+    def first_step(self):
+        return jnp.where(self.core == 0, 2, 1)
+
+    def at(self, blocks, step):
+        return lax.dynamic_index_in_dim(blocks, self.place ^ step, 0, keepdims=False)
 
 
 def on_device(
@@ -803,20 +826,20 @@
         own_1, other_1 = plan.pack(*ffn_parts(0))
         own_2, other_2 = plan.pack(*ffn_parts(1))
         attn_theirs = plan.swap(attn_other)
-        attn_theirs, marks_all = fence(attn_theirs, marks_all)
+        attn_theirs, marks_all, own_1, other_1 = fence(attn_theirs, marks_all, own_1, other_1)
         attn_block = plan.join(attn_own, attn_theirs)
         near, across = line_near(attn_block)
         theirs_1 = plan.swap(other_1)
-        near, across, theirs_1 = fence(near, across, theirs_1)
+        near, across, cosine, sine, own_2, other_2 = fence(
+            near, across, cosine, sine, own_2, other_2
+        )
         across_near, out = line_far(near, across)
-        theirs_2 = plan.swap(other_2)
+        across_near, out, theirs_1 = fence(across_near, out, theirs_1)
+        out_near = line_last(across_near)
+        out_near, normed_all, theirs_1, grad_low, other_2 = fence(
+            out_near, normed_all, theirs_1, grad_low, other_2
+        )
         block_1 = plan.join(own_1, theirs_1)
-        across_near, out, theirs_2, block_1 = fence(across_near, out, theirs_2, block_1)
-        out_near = line_last(across_near)
-        block_2 = plan.join(own_2, theirs_2)
-        out_near, normed_all, cosine, sine, block_1, block_2 = fence(
-            out_near, normed_all, cosine, sine, block_1, block_2
-        )
         attn_weights = (attn_block, near, across_near, out, across, out_near)
         near_1, across_1 = line_near(block_1)
     else:
@@ -828,18 +851,25 @@
     attn_part, ctx, queries, both, lse, wout = attn_forward(
         attn_loader, normed_all, cosine, sine, seg_col, seg_row
     )
-    grad_y, grad_x = plane.swap_y(grad_low), plane.swap_x(grad_low)
-    if plan.line:
-        attn_part, near_1, across_1, grad_y, grad_x = fence(
-            attn_part, near_1, across_1, grad_y, grad_x
+    grad_second = plane.swap_second(grad_low)
+    if plan.line:
+        theirs_2 = plan.swap(other_2)
+        attn_part, near_1, across_1, grad_second, theirs_2, grad_low = fence(
+            attn_part, near_1, across_1, grad_second, theirs_2, grad_low
         )
         across_near_1, out_1 = line_far(near_1, across_1)
+    grad_first = plane.swap_first(grad_low)
     attn_sum = lax.psum_scatter(attn_part, axes, scatter_dimension=0, tiled=True)
-    grad_xy = plane.swap_x(grad_y)
-    if plan.line:
-        across_near_1, out_1, grad_xy, block_2 = fence(across_near_1, out_1, grad_xy, block_2)
+    grad_xy = plane.swap_first(grad_second)
+    if plan.line:
+        across_near_1, out_1, grad_xy, theirs_2, grad_first = fence(
+            across_near_1, out_1, grad_xy, theirs_2, grad_first
+        )
+        block_2 = plan.join(own_2, theirs_2)
         out_near_1 = line_last(across_near_1)
         across_2 = lax.ppermute(block_2, "do", MIDDLE)
+    grad_x = pick(core, grad_first, grad_second)
+    grad_y = pick(core, grad_second, grad_first)
     over_y = cat([pick(plane.y, grad_low, grad_y), pick(plane.y, grad_y, grad_low)], 0)
     over_xy = cat([pick(plane.y, grad_x, grad_xy), pick(plane.y, grad_xy, grad_x)], 0)
     grad_core = cat([by_x(over_y, over_xy), by_x(over_xy, over_y)], 0)
@@ -849,21 +879,21 @@
     grad_all = cat([pick(core, mine, theirs), pick(core, theirs, mine)], 1).reshape(rows, width)
 
     if plan.line:
-        attn_sum, out_near_1, across_2, grad_all, block_2 = fence(
-            attn_sum, out_near_1, across_2, grad_all, block_2
-        )
+        attn_sum, grad_all = fence(attn_sum, grad_all)
+    residual = inputs_f + attn_sum.astype(F32)
+    normed_two, scale_two = norm_rows(residual, gain_two)
+    two_low = normed_two.astype(LOW)
+    two_all = lax.all_gather(two_low, axes, axis=0, tiled=True)
+
+    if plan.line:
+        out_near_1, across_2, block_2, _ = fence(out_near_1, across_2, block_2, two_low)
         first_weights = (block_1, near_1, across_near_1, out_1, across_1, out_near_1)
         near_2 = lax.ppermute(block_2, "do", NEAR)
-    residual = inputs_f + attn_sum.astype(F32)
-    normed_two, scale_two = norm_rows(residual, gain_two)
-    two_all = lax.all_gather(normed_two.astype(LOW), axes, axis=0, tiled=True)
-
-    if plan.line:
-        near_2, across_2 = fence(near_2, across_2)
+        two_all, near_2, across_2 = fence(two_all, near_2, across_2)
         across_near_2, out_2 = line_far(near_2, across_2)
+    two_all, wout = fence(two_all, wout)
     first = Loader(plan, first_weights, *ffn_shapes)
     back_1, act_1, both_1 = ffn_main(first, two_all, grad_all, None)
-    two_all, wout = fence(two_all, wout)
     wout_all = lax.all_gather(wout, axes, axis=0, tiled=True)
     if plan.line:
         back_1, act_1, both_1, across_near_2, out_2 = fence(
@@ -884,62 +914,76 @@
     out_2_part, gain_2, *grads_2 = ffn_weights(second, two_all, grad_all, act_2, both_2, out_1_part)
     if plan.line:
         out_2_part, grads_2, crossed_1, inward_1 = fence(out_2_part, grads_2, crossed_1, inward_1)
-        near_sum_1, across_sum_1 = sum_near(grads_1, crossed_1, inward_1)
         far_2 = sum_far(grads_2)
-        back_sum, near_sum_1, across_sum_1 = fence(back_sum, near_sum_1, across_sum_1)
+
+    residual_grad, res_low, ctx_grad = residual_backward(
+        back_sum, residual, scale_two, gain_two, grad_low, wout_all
+    )
+    ctx_grad = lax.all_to_all(ctx_grad, axes, split_axis=1, concat_axis=0, tiled=True)
 
     out_shape = (rows // own_rows // 2, 2, own_rows, width)
     parts = out_2_part.reshape(out_shape)
     mine, theirs = pick(core, parts[:, 0], parts[:, 1]), pick(core, parts[:, 1], parts[:, 0])
     summed = add(mine, plane.swap_core(theirs)).astype(LOW)
-    low, high = summed[: out_shape[0] // 2], summed[out_shape[0] // 2 :]
-    summed = add(by_x(low, high), plane.swap_x(by_x(high, low))).astype(LOW)
-    low, high = summed[: summed.shape[0] // 2], summed[summed.shape[0] // 2 :]
-    summed = add(pick(plane.y, low, high), plane.swap_y(pick(plane.y, high, low)))
-    out_value = (residual + summed.reshape(own_rows, width)).astype(LOW)
-
-    residual_grad, res_low, ctx_grad = residual_backward(
-        back_sum, residual, scale_two, gain_two, grad_low, wout_all
-    )
+    step = plane.first_step()
+    goes = jnp.stack([plane.at(summed, step), plane.at(summed, 3)])
+    goes_on, stays = plane.at(summed, 3 - step), plane.at(summed, 0)
+
+    if plan.line:
+        far_2, grads_1, _ = fence(far_2, grads_1, res_low)
+        crossed_2, inward_2 = sum_middle(grads_2, far_2)
+        first_1, third_1 = sum_near_parts(grads_1, crossed_1, inward_1)
+        ctx_grad, res_low, stays, goes, goes_on, first_1, third_1 = fence(
+            ctx_grad, res_low, stays, goes, goes_on, first_1, third_1
+        )
+        near_sum_1, across_sum_1 = sum_near_send(first_1, third_1)
+    arrives = plane.swap_first(goes)
     res_all = lax.all_gather(res_low, axes, axis=0, tiled=True)
-    ctx_grad = lax.all_to_all(ctx_grad, axes, split_axis=1, concat_axis=0, tiled=True)
-    if plan.line:
-        ctx_grad, far_2 = fence(ctx_grad, far_2)
-        crossed_2, inward_2 = sum_middle(grads_2, far_2)
     back_one_part, gain_one_part, *grads_qkv = attn_backward(
         attn_loader, ctx_grad, normed_all, queries, both, lse, cosine, sine, seg_col, seg_row
     )
     if plan.line:
-        back_one_part, grads_qkv, crossed_2, inward_2 = fence(
-            back_one_part, grads_qkv, crossed_2, inward_2
-        )
+        back_one_part, grads_qkv, gain_one_part, crossed_2, inward_2, res_all = fence(
+            back_one_part, grads_qkv, gain_one_part, crossed_2, inward_2, res_all
+        )
+        near_sum_1, across_sum_1, _ = fence(near_sum_1, across_sum_1, back_one_part)
+        total_1 = sum_own(grads_1, near_sum_1, across_sum_1)
+        ffn_grad_1 = plan.unpack(total_1, 2 * hidden)
     back_one = lax.psum_scatter(back_one_part, axes, scatter_dimension=0, tiled=True)
     grads_out = out_weights(plan, ctx, res_all)
     if plan.line:
-        direct_qkv = send_direct(grads_qkv)
-        gain_one_part, *direct_qkv = fence(gain_one_part, *direct_qkv)
-        direct_out = send_direct(grads_out)
-        near_sum_2, across_sum_2 = sum_near(grads_2, crossed_2, inward_2)
+        near_sum_2, across_sum_2 = sum_near_send(*sum_near_parts(grads_2, crossed_2, inward_2))
+        near_sum_2, across_sum_2, grads_qkv, grads_out, arrives, ffn_grad_1 = fence(
+            near_sum_2, across_sum_2, grads_qkv, grads_out, arrives, ffn_grad_1
+        )
+        direct_qkv, direct_out = send_direct(grads_qkv), send_direct(grads_out)
+        total_2 = sum_own(grads_2, near_sum_2, across_sum_2)
+        ffn_grad_2 = plan.unpack(total_2, 2 * hidden)
+    summed = add(stays, arrives[0])
+    arrives = plane.swap_second(add(goes_on, arrives[1]).astype(LOW))
+    if plan.line:
+        ffn_grad_2, direct_qkv, direct_out, arrives, gain_one_part = fence(
+            ffn_grad_2, direct_qkv, direct_out, arrives, gain_one_part
+        )
+        half = plan.rows
         total = add(grads_qkv[0], *direct_qkv)
-        half = plan.rows
         qkv_pair = plan.trade(total[:half], total[half:])
         total = add(grads_out[0], *direct_out)
         out_pair = plan.trade(total[:, :half], total[:, half:])
-        total_1 = sum_own(grads_1, near_sum_1, across_sum_1)
-        total_2 = sum_own(grads_2, near_sum_2, across_sum_2)
-        ffn_grads = [plan.unpack(each, 2 * hidden) for each in (total_1, total_2)]
+        ffn_grads = [ffn_grad_1, ffn_grad_2]
     else:
         qkv_pair = plan.plain_sum_row(grads_qkv[0])
         out_pair = plan.plain_sum_col(grads_out[0])
         ffn_grads = [
             (plan.plain_sum_row(row), plan.plain_sum_col(col)) for row, col in (grads_1, grads_2)
         ]
-    in_grad = residual_grad + norm_back(back_one.astype(F32), inputs_f, scale_one, gain_one)
-
     gain_parts = jnp.stack(
         [gain_one_part[:, 0] / gain_one, (gain_1[:, 0] + gain_2[:, 0]) / gain_two]
     )
-    gain_sums = sum_everywhere(plan.reorder(gain_parts), list(sizes.items()))
+    gain_sums = sum_everywhere(plan.reorder(gain_parts), list(sizes.items())[::-1])
+    out_value = (residual + add(summed, arrives)).astype(LOW)
+    in_grad = residual_grad + norm_back(back_one.astype(F32), inputs_f, scale_one, gain_one)
+
     grad_gain_attn, grad_gain_ffn = gain_sums[0], gain_sums[1]
 
     def join(pair, axis):

time: 914 us -> 741 us (0.81)
  waiting for transfers between devices: 413 us -> 285 us
  starting transfers between devices: 119 us -> 82.1 us
  local copies, waits for them, and re-layouts: 47 us -> 36.8 us
    ppermute x1, waiting for transfers between devices: 57.2 us -> 1.91 us  [on_device(): marks_other = lax.ppermute(marks, 'di', PAIR)]
    all_gather x1, waiting for transfers between devices: 53.8 us -> 0.01 us  [on_device(): two_all = lax.all_gather(two_low, axes, axis=0, tiled=True)]
    all_to_all x1, waiting for transfers between devices: 57.1 us -> 5.46 us  [on_device(): lax.all_to_all(ctx_grad, axes, split_axis=1, concat_axis=0, tiled=True)]
    ppermute x5, waiting for transfers between devices: 32.4 us -> 3.6 us  [sum_everywhere(): lax.ppermute(values, axis, [(i, i ^ step) for i in range(size)])]
    all_gather x1, waiting for transfers between devices: 0.01 us -> 24.9 us  [on_device(): res_all = lax.all_gather(res_low, axes, axis=0, tiled=True)]
    ppermute x22, starting transfers between devices: 56.7 us -> 34 us  [the longest x6 19.4 us: line_far(): return (lax.ppermute(near, 'do', MIDDLE), lax.ppermute(across, 'do', NEAR))]
    unnamed x180 -> x182, local copies, waits for them, and re-layouts: 29.2 us -> 16.3 us
    ppermute x4, waiting for transfers between devices: 27.6 us -> 14.9 us  [trade(): theirs = lax.ppermute(self.by_x(high, low).astype(LOW), 'di', PAIR)]
  transfers between devices with their start and end apart: 59 -> 59, of which waited for: 31 -> 35; matrix products, arithmetic and copies ran while one was open for 13% -> 16% of each run, Pallas kernels for 21% -> 26%
where the time goes in v4:
time: 741 us; the launch traced here: 730 us
  waiting for transfers between devices  285 us (38%)
  Pallas kernels  193 us (26%)
  other arithmetic  117 us (16%)
  starting transfers between devices  82.1 us (11%)
  local copies, waits for them, and re-layouts  36.8 us (5%)
  between operations  16.4 us (2%)
    pallas_call x2, Pallas kernels, ffn_weights(): pl.pallas_call(functools.partial(ffn_weights_kernel, loader, len(more)),...  66 us
    pallas_call x2, Pallas kernels, ffn_main(): pl.pallas_call(functools.partial(ffn_main_kernel, loader, len(more)), gri...  61.7 us
    ppermute x6, waiting for transfers between devices, send_direct(): lax.ppermute(part, 'do', perm)  53.8 us
    ppermute x3, waiting for transfers between devices, line_last(): return lax.ppermute(across_near, 'do', NEAR)  44 us
    ppermute x1, waiting for transfers between devices, on_device(): near_2 = lax.ppermute(block_2, 'do', NEAR)  33.5 us
    pallas_call x1, Pallas kernels, attn_backward(): pl.pallas_call(functools.partial(attn_backward_kernel, heads // 128, load...  33 us
    ppermute x3, waiting for transfers between devices, swap_first(): return lax.ppermute(value, self.axes, self.pairs(True))  27.3 us
    all_gather x1, waiting for transfers between devices, on_device(): res_all = lax.all_gather(res_low, axes, axis=0, tiled=True)  24.9 us
  transfers between devices with their start and end apart: 59, of which 35 were waited for; matrix products, arithmetic and copies ran while one was open for 16% of the time, Pallas kernels for 26%

profile of v4, /device:TPU:9, one launch (start us, length us, event | category | flops | bytes accessed | tf_op | source)
XLA Modules:
  0.0 729.8 jit_solution(519448038694173369)
XLA Ops:
  22.5 4.2 collective-permute-start.3
  26.8 3.7 fusion.17
  37.0 3.0 collective-permute-done.3.refs_5_
  40.0 3.1 collective-permute-start.4
  43.6 10.7 %collective-permute-done.6 = bf16[256,1536]{1,0:T(8,128)(2,1)S(1)} collective-permute-done((bf16[256,1536]{1,0:T(8,128)(2,1)S(1)}, bf16[256,1536]{1,0:T(8,128)(2,1)S(1)}, u32[]{:S(2)}, u32[]{:S(2)}) %collective-permute-start.6) | collective-permute-done | bytes 786464 | tf_op jit(solution)/shard_map/ppermute | solution.py:137
  57.5 12.2 %collective-permute-done.7.refs_6_ = bf16[512,640]{1,0:T(8,128)(2,1)S(1)} collective-permute-done((bf16[512,640]{1,0:T(8,128)(2,1)S(1)}, bf16[512,640]{1,0:T(8,128)(2,1)S(1)}, u32[]{:S(2)}, u32[]{:S(2)}) %collective-permute-start.7) | collective-permute-done | bytes 655392 | tf_op jit(solution)/shard_map/ppermute | solution.py:59
  70.6 6.3 all-gather.5.cloned.1.call-done.refs_7_.refs_8_
  79.8 4.3 collective-permute-start.9
  90.3 21.3 %attn_forward.1 = (bf16[2048,2048]{1,0:T(8,128)(2,1)}, bf16[2048,256]{1,0:T(8,128)(2,1)S(1)}, bf16[2048,256]{1,0:T(8,128)(2,1)}, bf16[2048,128]{1,0:T(8,128)(2,1...) custom-call(s32[1]{0:T(128)} %bitcast.refs_0_, bf16[512,640]{1,0:T(8,128)(2,1)S(1)} %pad_maximum_fusion.13.refs_1_, ...), custom_call_target="tpu_custom_call" | custom-call | flops 1 | bytes 1 | tf_op jit(solution)/shard_map/attn_forward/pallas_call | solution.py:424
  115.6 2.8 collective-permute-done.9.refs_5_
  118.5 3.0 collective-permute-start.12
  123.2 12.8 %collective-permute-done.14 = bf16[256,2048]{1,0:T(8,128)(2,1)} collective-permute-done((bf16[256,2048]{1,0:T(8,128)(2,1)}, bf16[256,2048]{1,0:T(8,128)(2,1)}, u32[]{:S(2)}, u32[]{:S(2)}) %collective-permute-start.14) | collective-permute-done | bytes 1048608 | tf_op jit(solution)/shard_map/ppermute | solution.py:745
  136.0 14.5 %collective-permute-done.15 = bf16[256,2048]{1,0:T(8,128)(2,1)} collective-permute-done((bf16[256,2048]{1,0:T(8,128)(2,1)S(1)}, bf16[256,2048]{1,0:T(8,128)(2,1)}, u32[]{:S(2)}, u32[]{:S(2)}) %collective-permute-start.15) | collective-permute-done | bytes 1048608 | tf_op jit(solution)/shard_map/ppermute | solution.py:745
  150.5 5.1 collective-permute-done.12.refs_3_
  160.5 2.9 collective-permute-start.16
  163.5 6.7 collective-permute-done.16
  170.2 4.5 broadcast_select_fusion.1
  174.7 7.5 %pad_maximum_fusion = bf16[4,2,256,2048]{3,2,0,1:T(8,128)(2,1)} fusion(bf16[4,1,256,2048]{3,2,0,1:T(8,128)(2,1)} %bitcast.64, bf16[4,1,256,2048]{3,2,0,1:T(8,128)(2,1)} %bitcast.63), kind=kLoop, calls=%fused_computation | loop fusion | flops 4194304 | bytes 16777216 | tf_op jit(solution)/shard_map/concatenate | solution.py:43
  182.3 8.5 %copy.80 = bf16[4,2,256,2048]{3,2,1,0:T(8,128)(2,1)} copy(bf16[4,2,256,2048]{3,2,0,1:T(8,128)(2,1)} %pad_maximum_fusion) | data formatting | bytes 16777216 | tf_op jit(solution)/shard_map/concatenate | solution.py:43
  199.1 2.6 collective-permute-start.18
  201.7 30.1 %collective-permute-done.17.refs_6_ = bf16[512,1536]{1,0:T(8,128)(2,1)S(1)} collective-permute-done((bf16[512,1536]{1,0:T(8,128)(2,1)}, bf16[512,1536]{1,0:T(8,128)(2,1)S(1)}, u32[]{:S(2)}, u32[]{:S(2)}) %collective-permute-start.17) | collective-permute-done | bytes 1572896 | tf_op jit(solution)/shard_map/ppermute | solution.py:59
  231.9 4.6 collective-permute-done.18.refs_5_
  237.6 33.5 %collective-permute-done.19.refs_2_ = bf16[512,1536]{1,0:T(8,128)(2,1)} collective-permute-done((bf16[512,1536]{1,0:T(8,128)(2,1)S(1)}, bf16[512,1536]{1,0:T(8,128)(2,1)}, u32[]{:S(2)}, u32[]{:S(2)}) %collective-permute-start.19) | collective-permute-done | bytes 1572896 | tf_op jit(solution)/shard_map/ppermute | solution.py:891
  271.2 13.1 %collective-permute-start.20 = (bf16[512,1536]{1,0:T(8,128)(2,1)}, bf16[512,1536]{1,0:T(8,128)(2,1)}, u32[]{:S(2)}, u32[]{:S(2)}) collective-permute-start(bf16[512,1536]{1,0:T(8,128)(2,1)} %collective-permute-done.19.refs_2_), channel_id=1, source_target_pairs={{8,16},{16,8},{9,17},{17,9},{10,18},{18,10},{11,19},{19,11},{12,20... | collective-permute-start | bytes 4718600 | tf_op jit(solution)/shard_map/ppermute | solution.py:55
  284.4 30.3 %ffn_main.2 = (bf16[2048,2048]{1,0:T(8,128)(2,1)}, bf16[2048,512]{1,0:T(8,128)(2,1)}, bf16[2048,1024]{1,0:T(8,128)(2,1)}) custom-call(s32[1]{0:T(128)} %bitcast.refs_0_, bf16[512,1536]{1,0:T(8,128)(2,1)} %pad_maximum_fusion.5.refs_1_, bf16[512,1536]{1,0:T(8,128)(2,1)} %collective-permute-done.8.refs_2_, bf16[512,1536]{1,0:T(8,128)(2,1)} %copy-done.28, ...), custom_call_target="tpu_custom_call" | custom-call | flops 1 | bytes 1 | tf_op jit(solution)/shard_map/ffn_main/pallas_call | solution.py:603
  314.7 3.1 collective-permute-done.21.refs_4_
  318.1 30.9 %ffn_weights.2 = (bf16[2048,2048]{1,0:T(8,128)(2,1)}, f32[2048,1]{1,0:T(8,128)}, bf16[512,1536]{1,0:T(8,128)(2,1)}, bf16[512,1536]{1,0:T(8,128)(2,1)}, bf16[512,...) custom-call(s32[1]{0:T(128)} %bitcast.refs_0_, bf16[512,1536]{1,0:T(8,128)(2,1)} %pad_maximum_fusion.5.refs_1_, ...), custom_call_target="tpu_custom_call" | custom-call | flops 1 | bytes 1 | tf_op jit(solution)/shard_map/ffn_weights/pallas_call | solution.py:663
  350.9 31.4 %ffn_main.3 = (bf16[2048,2048]{1,0:T(8,128)(2,1)}, bf16[2048,512]{1,0:T(8,128)(2,1)}, bf16[2048,1024]{1,0:T(8,128)(2,1)}) custom-call(s32[1]{0:T(128)} %bitcast.refs_0_, bf16[512,1536]{1,0:T(8,128)(2,1)} %copy-done.19, bf16[512,1536]{1,0:T(8,128)(2,1)} %collective-permute-done.19.refs_2_, bf16[512,1536]{1,0:T(8,128)(2,1)} %collective-permute-done.20.refs_3_, ...), custom_call_target="tpu_custom_call" | custom-call | flops 1 | bytes 1 | tf_op jit(solution)/shard_map/ffn_main/pallas_call | solution.py:603
  383.5 3.5 add_convert_fusion.5
  387.0 3.6 collective-permute-start.24
  390.7 35.1 %ffn_weights.3 = (bf16[2048,2048]{1,0:T(8,128)(2,1)}, f32[2048,1]{1,0:T(8,128)}, bf16[512,1536]{1,0:T(8,128)(2,1)}, bf16[512,1536]{1,0:T(8,128)(2,1)}, bf16[512,...) custom-call(s32[1]{0:T(128)} %bitcast.refs_0_, bf16[512,1536]{1,0:T(8,128)(2,1)} %copy-done.19, ...), custom_call_target="tpu_custom_call" | custom-call | flops 1 | bytes 1 | tf_op jit(solution)/shard_map/ffn_weights/pallas_call | solution.py:663
  425.8 5.7 select_bitcast_fusion
  431.5 5.4 collective-permute-start.26
  438.0 6.0 collective-permute-done.26
  444.0 6.6 fusion
  450.6 2.2 dynamic-slice_bitcast_fusion
  452.8 6.3 reduce-scatter.6.cloned.1.call-done.back_ref
  460.3 7.2 residual_backward.1
  469.9 4.1 all-to-all-start
  474.1 2.7 pad_maximum_fusion.4
  476.8 5.4 add_convert_fusion.3
  482.2 5.5 all-to-all-done
  488.0 2.8 add_convert_fusion.2
  490.8 3.1 collective-permute-start.28
  499.8 33.0 %attn_backward.1 = (bf16[2048,2048]{1,0:T(8,128)(2,1)}, f32[2048,1]{1,0:T(8,128)}, bf16[512,384]{1,0:T(8,128)(2,1)S(1)}, bf16[512,384]{1,0:T(8,128)(2,1)S(1)}, b...) custom-call(s32[1]{0:T(128)} %bitcast.refs_0_, bf16[512,640]{1,0:T(8,128)(2,1)} %copy-done, ...), custom_call_target="tpu_custom_call" | custom-call | flops 1 | bytes 1 | tf_op jit(solution)/shard_map/attn_backward/pallas_call | solution.py:463
  532.8 24.9 %all-gather.11.cloned.1.call-done.res_ref = bf16[2048,2048]{1,0:T(8,128)(2,1)} async-done(((bf16[256,2048]{1,0:T(8,128)(2,1)}), bf16[2048,2048]{1,0:T(8,128)(2,1)}) %all-gather.11.cloned.1.call-update) | async-done | bytes 8388624 | tf_op jit(solution)/shard_map/all_gather | solution.py:941
  561.1 2.5 add_convert_fusion
  563.6 3.6 collective-permute-start.31
  567.2 2.6 convert_add_fusion.3
  571.5 3.2 out_weights.1
  575.6 13.1 %collective-permute-done.35 = bf16[256,1536]{1,0:T(8,128)(2,1)S(1)} collective-permute-done((bf16[256,1536]{1,0:T(8,128)(2,1)S(1)}, bf16[256,1536]{1,0:T(8,128)(2,1)S(1)}, u32[]{:S(2)}, u32[]{:S(2)}) %collective-permute-start.35) | collective-permute-done | bytes 786464 | tf_op jit(solution)/shard_map/ppermute | solution.py:168
  589.7 7.8 %collective-permute-done.30 = bf16[512,1536]{1,0:T(8,128)(2,1)S(1)} collective-permute-done((bf16[512,1536]{1,0:T(8,128)(2,1)S(1)}, bf16[512,1536]{1,0:T(8,128)(2,1)S(1)}, u32[]{:S(2)}, u32[]{:S(2)}) %collective-permute-start.30) | collective-permute-done | bytes 1572896 | tf_op jit(solution)/shard_map/ppermute | solution.py:92
  597.5 4.1 collective-permute-done.31
  601.6 2.2 convert_add_fusion.2
  607.7 2.2 fusion.11
  612.4 11.6 %collective-permute-done.40 = bf16[256,512]{1,0:T(8,128)(2,1)S(1)} collective-permute-done((bf16[256,512]{1,0:T(8,128)(2,1)S(1)}, bf16[256,512]{1,0:T(8,128)(2,1)S(1)}, u32[]{:S(2)}, u32[]{:S(2)}) %collective-permute-start.40) | collective-permute-done | bytes 262176 | tf_op jit(solution)/shard_map/ppermute | solution.py:101
  624.0 2.7 collective-permute-start.38
  631.1 42.1 %collective-permute-done.42 = bf16[256,512]{1,0:T(8,128)(2,1)S(1)} collective-permute-done((bf16[256,512]{1,0:T(8,128)(2,1)S(1)}, bf16[256,512]{1,0:T(8,128)(2,1)S(1)}, u32[]{:S(2)}, u32[]{:S(2)}) %collective-permute-start.42) | collective-permute-done | bytes 262176 | tf_op jit(solution)/shard_map/ppermute | solution.py:101
  676.5 2.2 reduce
  683.1 5.6 multiply_subtract_fusion.2
  689.2 4.6 multiply_subtract_fusion.1
  695.2 3.8 multiply_subtract_fusion
  699.7 3.0 collective-permute-done.50
  714.1 4.2 fusion.9
  (400 shorter events, 112.1 us)
Async XLA Ops:
  7.2 69.6 %all-gather.5.cloned.1.call-start = ((), (), s32[]{:S(2)}) async-start(), calls=%async_computation.4 | async-start | bytes 9437184 | tf_op jit(solution)/shard_map/all_gather | solution.py:778
  12.4 179.9 %reduce-scatter.4.cloned.1.call-start = ((), (), s32[]{:S(2)}) async-start(), calls=%async_computation.5 | async-start | bytes 9437184 | tf_op jit(solution)/shard_map/reduce_scatter | solution.py:862
  13.1 8.9 %collective-permute-start = (bf16[256,640]{1,0:T(8,128)(2,1)S(1)}, bf16[256,640]{1,0:T(8,128)(2,1)S(1)}, u32[]{:S(2)}, u32[]{:S(2)}) collective-permute-start(bf16[256,640]{1,0:T(8,128)(2,1)S(1)} %pad_maximum_fusion.19), channel_id=1, source_target_pairs={{0,4},{4,0},{1,5},{5,1},{2,6},{6,2},{3,7},{7,3},{8,12},{12,8},{9,1... | collective-permute-start | bytes 983048 | tf_op jit(solution)/shard_map/ppermute | solution.py:137
  14.4 7.5 %collective-permute-start.1 = (s32[2,1024]{1,0:T(2,128)S(1)}, s32[2,1024]{1,0:T(2,128)S(1)}, u32[]{:S(2)}, u32[]{:S(2)}) collective-permute-start(s32[2,1024]{1,0:T(2,128)S(1)} %pad_add_fusion.1), channel_id=1, source_target_pairs={{0,4},{4,0},{1,5},{5,1},{2,6},{6,2},{3,7},{7,3},{8,12},{12,8},{9,1... | collective-permute-start | bytes 24584 | tf_op jit(solution)/shard_map/ppermute | solution.py:781
  22.2 64.9 %copy-start = (bf16[512,640]{1,0:T(8,128)(2,1)}, bf16[512,640]{1,0:T(8,128)(2,1)S(1)}, u32[]{:S(2)}) copy-start(bf16[512,640]{1,0:T(8,128)(2,1)S(1)} %pad_maximum_fusion.13.refs_1_) | copy-start | bytes 1966084
  22.2 14.7 %collective-permute-start.2 = (bf16[512,640]{1,0:T(8,128)(2,1)S(1)}, bf16[512,640]{1,0:T(8,128)(2,1)S(1)}, u32[]{:S(2)}, u32[]{:S(2)}) collective-permute-start(bf16[512,640]{1,0:T(8,128)(2,1)S(1)} %pad_maximum_fusion.13.refs_1_), channel_id=1, source_target_pairs={{0,8},{8,0},{16,24},{24,16},{1,9},{9,1},{17,25},{25,17},{2,10},{10... | collective-permute-start | bytes 1966088 | tf_op jit(solution)/shard_map/ppermute | solution.py:51
  22.5 17.5 %collective-permute-start.3 = (bf16[512,640]{1,0:T(8,128)(2,1)S(1)}, bf16[512,640]{1,0:T(8,128)(2,1)S(1)}, u32[]{:S(2)}, u32[]{:S(2)}) collective-permute-start(bf16[512,640]{1,0:T(8,128)(2,1)S(1)} %pad_maximum_fusion.13.refs_1_), channel_id=1, source_target_pairs={{8,16},{16,8},{9,17},{17,9},{10,18},{18,10},{11,19},{19,11},{12,20... | collective-permute-start | bytes 1966088 | tf_op jit(solution)/shard_map/ppermute | solution.py:51
  32.4 21.9 %collective-permute-start.6 = (bf16[256,1536]{1,0:T(8,128)(2,1)S(1)}, bf16[256,1536]{1,0:T(8,128)(2,1)S(1)}, u32[]{:S(2)}, u32[]{:S(2)}) collective-permute-start(bf16[256,1536]{1,0:T(8,128)(2,1)S(1)} %pad_maximum_fusion.10), channel_id=1, source_target_pairs={{0,4},{4,0},{1,5},{5,1},{2,6},{6,2},{3,7},{7,3},{8,12},{12,8},{9,1... | collective-permute-start | bytes 2359304 | tf_op jit(solution)/shard_map/ppermute | solution.py:137
  37.0 50.1 %copy-start.1 = (bf16[512,640]{1,0:T(8,128)(2,1)}, bf16[512,640]{1,0:T(8,128)(2,1)S(1)}, u32[]{:S(2)}) copy-start(bf16[512,640]{1,0:T(8,128)(2,1)S(1)} %collective-permute-done.2.refs_2_) | copy-start | bytes 1966084
  40.0 47.1 %copy-start.2 = (bf16[512,640]{1,0:T(8,128)(2,1)}, bf16[512,640]{1,0:T(8,128)(2,1)S(1)}, u32[]{:S(2)}) copy-start(bf16[512,640]{1,0:T(8,128)(2,1)S(1)} %collective-permute-done.3.refs_5_) | copy-start | bytes 1966084
  40.0 15.7 %collective-permute-start.4 = (bf16[512,640]{1,0:T(8,128)(2,1)S(1)}, bf16[512,640]{1,0:T(8,128)(2,1)S(1)}, u32[]{:S(2)}, u32[]{:S(2)}) collective-permute-start(bf16[512,640]{1,0:T(8,128)(2,1)S(1)} %collective-permute-done.2.refs_2_), channel_id=1, source_target_pairs={{8,16},{16,8},{9,17},{17,9},{10,18},{18,10},{11,19},{19,11},{12,20... | collective-permute-start | bytes 1966088 | tf_op jit(solution)/shard_map/ppermute | solution.py:55
  43.1 13.4 %collective-permute-start.5 = (bf16[512,640]{1,0:T(8,128)(2,1)S(1)}, bf16[512,640]{1,0:T(8,128)(2,1)S(1)}, u32[]{:S(2)}, u32[]{:S(2)}) collective-permute-start(bf16[512,640]{1,0:T(8,128)(2,1)S(1)} %collective-permute-done.3.refs_5_), channel_id=1, source_target_pairs={{0,8},{8,0},{16,24},{24,16},{1,9},{9,1},{17,25},{25,17},{2,10},{10... | collective-permute-start | bytes 1966088 | tf_op jit(solution)/shard_map/ppermute | solution.py:55
  56.4 13.3 %collective-permute-start.7 = (bf16[512,640]{1,0:T(8,128)(2,1)S(1)}, bf16[512,640]{1,0:T(8,128)(2,1)S(1)}, u32[]{:S(2)}, u32[]{:S(2)}) collective-permute-start(bf16[512,640]{1,0:T(8,128)(2,1)S(1)} %collective-permute-done.4.refs_3_), channel_id=1, source_target_pairs={{0,8},{8,0},{16,24},{24,16},{1,9},{9,1},{17,25},{25,17},{2,10},{10... | collective-permute-start | bytes 1966088 | tf_op jit(solution)/shard_map/ppermute | solution.py:59
  79.6 36.0 %collective-permute-start.8 = (bf16[512,1536]{1,0:T(8,128)(2,1)}, bf16[512,1536]{1,0:T(8,128)(2,1)}, u32[]{:S(2)}, u32[]{:S(2)}) collective-permute-start(bf16[512,1536]{1,0:T(8,128)(2,1)} %pad_maximum_fusion.5.refs_1_), channel_id=1, source_target_pairs={{0,8},{8,0},{16,24},{24,16},{1,9},{9,1},{17,25},{25,17},{2,10},{10... | collective-permute-start | bytes 4718600 | tf_op jit(solution)/shard_map/ppermute | solution.py:51
  79.8 38.6 %collective-permute-start.9 = (bf16[512,1536]{1,0:T(8,128)(2,1)}, bf16[512,1536]{1,0:T(8,128)(2,1)}, u32[]{:S(2)}, u32[]{:S(2)}) collective-permute-start(bf16[512,1536]{1,0:T(8,128)(2,1)} %pad_maximum_fusion.5.refs_1_), channel_id=1, source_target_pairs={{8,16},{16,8},{9,17},{17,9},{10,18},{18,10},{11,19},{19,11},{12,20... | collective-permute-start | bytes 4718600 | tf_op jit(solution)/shard_map/ppermute | solution.py:51
  84.2 31.0 %collective-permute-start.10 = (bf16[256,2048]{1,0:T(8,128)(2,1)S(1)}, bf16[256,2048]{1,0:T(8,128)(2,1)}, u32[]{:S(2)}, u32[]{:S(2)}) collective-permute-start(bf16[256,2048]{1,0:T(8,128)(2,1)S(1)} %maximum_select_fusion.8.grad_ref), channel_id=1, source_target_pairs={{0,2},{1,5},{2,0},{3,7},{4,6},{5,1},{6,4},{7,3},{8,10},{9,13},{10,... | collective-permute-start | bytes 3145736 | tf_op jit(solution)/shard_map/ppermute | solution.py:748
  84.5 30.6 %collective-permute-start.11 = (bf16[256,1536]{1,0:T(8,128)(2,1)}, bf16[256,1536]{1,0:T(8,128)(2,1)}, u32[]{:S(2)}, u32[]{:S(2)}) collective-permute-start(bf16[256,1536]{1,0:T(8,128)(2,1)} %pad_maximum_fusion.12), channel_id=1, source_target_pairs={{0,4},{4,0},{1,5},{5,1},{2,6},{6,2},{3,7},{7,3},{8,12},{12,8},{9,1... | collective-permute-start | bytes 2359304 | tf_op jit(solution)/shard_map/ppermute | solution.py:137
  118.5 152.7 %all-gather.7.cloned.1.call-start = ((), (), s32[]{:S(2)}) async-start(), calls=%async_computation.6 | async-start | bytes 9437184 | tf_op jit(solution)/shard_map/all_gather | solution.py:886
  118.5 37.0 %collective-permute-start.12 = (bf16[512,1536]{1,0:T(8,128)(2,1)}, bf16[512,1536]{1,0:T(8,128)(2,1)S(1)}, u32[]{:S(2)}, u32[]{:S(2)}) collective-permute-start(bf16[512,1536]{1,0:T(8,128)(2,1)} %collective-permute-done.8.refs_2_), channel_id=1, source_target_pairs={{8,16},{16,8},{9,17},{17,9},{10,18},{18,10},{11,19},{19,11},{12,20... | collective-permute-start | bytes 4718600 | tf_op jit(solution)/shard_map/ppermute | solution.py:55
  121.6 34.6 %collective-permute-start.13 = (bf16[512,1536]{1,0:T(8,128)(2,1)}, bf16[512,1536]{1,0:T(8,128)(2,1)}, u32[]{:S(2)}, u32[]{:S(2)}) collective-permute-start(bf16[512,1536]{1,0:T(8,128)(2,1)} %collective-permute-done.9.refs_5_), channel_id=1, source_target_pairs={{0,8},{8,0},{16,24},{24,16},{1,9},{9,1},{17,25},{25,17},{2,10},{10... | collective-permute-start | bytes 4718600 | tf_op jit(solution)/shard_map/ppermute | solution.py:55
  121.7 14.3 %collective-permute-start.14 = (bf16[256,2048]{1,0:T(8,128)(2,1)}, bf16[256,2048]{1,0:T(8,128)(2,1)}, u32[]{:S(2)}, u32[]{:S(2)}) collective-permute-start(bf16[256,2048]{1,0:T(8,128)(2,1)} %collective-permute-done.10), channel_id=1, source_target_pairs={{0,4},{1,3},{2,6},{3,1},{4,0},{5,7},{6,2},{7,5},{8,12},{9,11},{10,... | collective-permute-start | bytes 3145736 | tf_op jit(solution)/shard_map/ppermute | solution.py:745
  122.9 27.5 %collective-permute-start.15 = (bf16[256,2048]{1,0:T(8,128)(2,1)S(1)}, bf16[256,2048]{1,0:T(8,128)(2,1)}, u32[]{:S(2)}, u32[]{:S(2)}) collective-permute-start(bf16[256,2048]{1,0:T(8,128)(2,1)S(1)} %maximum_select_fusion.8.grad_ref), channel_id=1, source_target_pairs={{0,4},{1,3},{2,6},{3,1},{4,0},{5,7},{6,2},{7,5},{8,12},{9,11},{10,... | collective-permute-start | bytes 3145736 | tf_op jit(solution)/shard_map/ppermute | solution.py:745
  160.5 9.7 %collective-permute-start.16 = (bf16[1024,2048]{1,0:T(8,128)(2,1)S(1)}, bf16[1024,2048]{1,0:T(8,128)(2,1)S(1)}, u32[]{:S(2)}, u32[]{:S(2)}) collective-permute-start(bf16[1024,2048]{1,0:T(8,128)(2,1)S(1)} %pad_maximum_fusion.1), channel_id=1, source_target_pairs={{0,1},{1,0},{2,3},{3,2},{4,5},{5,4},{6,7},{7,6},{8,9},{9,8},{10,11... | collective-permute-start | bytes 12582920 | tf_op jit(solution)/shard_map/ppermute | solution.py:751
  195.7 187.8 %all-gather.9.cloned.1.call-start = ((), (), s32[]{:S(2)}) async-start(), calls=%async_computation.7 | async-start | bytes 9437184 | tf_op jit(solution)/shard_map/all_gather | solution.py:897
  195.8 36.1 %collective-permute-start.17 = (bf16[512,1536]{1,0:T(8,128)(2,1)}, bf16[512,1536]{1,0:T(8,128)(2,1)S(1)}, u32[]{:S(2)}, u32[]{:S(2)}) collective-permute-start(bf16[512,1536]{1,0:T(8,128)(2,1)} %copy-done.28), channel_id=1, source_target_pairs={{0,8},{8,0},{16,24},{24,16},{1,9},{9,1},{17,25},{25,17},{2,10},{10... | collective-permute-start | bytes 4718600 | tf_op jit(solution)/shard_map/ppermute | solution.py:59
  199.1 37.4 %copy-start.19 = (bf16[512,1536]{1,0:T(8,128)(2,1)}, bf16[512,1536]{1,0:T(8,128)(2,1)S(1)}, u32[]{:S(2)}) copy-start(bf16[512,1536]{1,0:T(8,128)(2,1)S(1)} %pad_maximum_fusion.6.refs_1_) | copy-start | bytes 4718596
  199.1 37.4 %collective-permute-start.18 = (bf16[512,1536]{1,0:T(8,128)(2,1)S(1)}, bf16[512,1536]{1,0:T(8,128)(2,1)S(1)}, u32[]{:S(2)}, u32[]{:S(2)}) collective-permute-start(bf16[512,1536]{1,0:T(8,128)(2,1)S(1)} %pad_maximum_fusion.6.refs_1_), channel_id=1, source_target_pairs={{8,16},{16,8},{9,17},{17,9},{10,18},{18,10},{11,19},{19,11},{12,20... | collective-permute-start | bytes 4718600 | tf_op jit(solution)/shard_map/ppermute | solution.py:870
  236.5 34.7 %collective-permute-start.19 = (bf16[512,1536]{1,0:T(8,128)(2,1)S(1)}, bf16[512,1536]{1,0:T(8,128)(2,1)}, u32[]{:S(2)}, u32[]{:S(2)}) collective-permute-start(bf16[512,1536]{1,0:T(8,128)(2,1)S(1)} %pad_maximum_fusion.6.refs_1_), channel_id=1, source_target_pairs={{0,8},{8,0},{16,24},{24,16},{1,9},{9,1},{17,25},{25,17},{2,10},{10... | collective-permute-start | bytes 4718600 | tf_op jit(solution)/shard_map/ppermute | solution.py:891
  271.2 187.9 %reduce-scatter.6.cloned.1.call-start = ((), (), s32[]{:S(2)}) async-start(), calls=%async_computation.8 | async-start | bytes 9437184 | tf_op jit(solution)/shard_map/reduce_scatter | solution.py:913
  271.2 43.5 %collective-permute-start.20 = (bf16[512,1536]{1,0:T(8,128)(2,1)}, bf16[512,1536]{1,0:T(8,128)(2,1)}, u32[]{:S(2)}, u32[]{:S(2)}) collective-permute-start(bf16[512,1536]{1,0:T(8,128)(2,1)} %collective-permute-done.19.refs_2_), channel_id=1, source_target_pairs={{8,16},{16,8},{9,17},{17,9},{10,18},{18,10},{11,19},{19,11},{12,20... | collective-permute-start | bytes 4718600 | tf_op jit(solution)/shard_map/ppermute | solution.py:55
  284.3 33.5 %collective-permute-start.21 = (bf16[512,1536]{1,0:T(8,128)(2,1)}, bf16[512,1536]{1,0:T(8,128)(2,1)}, u32[]{:S(2)}, u32[]{:S(2)}) collective-permute-start(bf16[512,1536]{1,0:T(8,128)(2,1)} %copy-done.27), channel_id=1, source_target_pairs={{0,8},{8,0},{16,24},{24,16},{1,9},{9,1},{17,25},{25,17},{2,10},{10... | collective-permute-start | bytes 4718600 | tf_op jit(solution)/shard_map/ppermute | solution.py:55
  317.8 32.9 %collective-permute-start.22 = (bf16[512,1536]{1,0:T(8,128)(2,1)}, bf16[512,1536]{1,0:T(8,128)(2,1)}, u32[]{:S(2)}, u32[]{:S(2)}) collective-permute-start(bf16[512,1536]{1,0:T(8,128)(2,1)} %collective-permute-done.20.refs_3_), channel_id=1, source_target_pairs={{0,8},{8,0},{16,24},{24,16},{1,9},{9,1},{17,25},{25,17},{2,10},{10... | collective-permute-start | bytes 4718600 | tf_op jit(solution)/shard_map/ppermute | solution.py:59
  350.6 32.8 %collective-permute-start.23 = (bf16[512,1536]{1,0:T(8,128)(2,1)}, bf16[512,1536]{1,0:T(8,128)(2,1)}, u32[]{:S(2)}, u32[]{:S(2)}) collective-permute-start(bf16[512,1536]{1,0:T(8,128)(2,1)} %get-tuple-element.265), channel_id=1, source_target_pairs={{0,8},{8,0},{16,24},{24,16},{1,9},{9,1},{17,25},{25,17},{2,10},{10... | collective-permute-start | bytes 4718600 | tf_op jit(solution)/shard_map/ppermute | solution.py:79
  387.0 38.8 %collective-permute-start.24 = (bf16[512,1536]{1,0:T(8,128)(2,1)}, bf16[512,1536]{1,0:T(8,128)(2,1)}, u32[]{:S(2)}, u32[]{:S(2)}) collective-permute-start(bf16[512,1536]{1,0:T(8,128)(2,1)} %add_convert_fusion.5), channel_id=1, source_target_pairs={{8,16},{16,8},{9,17},{17,9},{10,18},{18,10},{11,19},{19,11},{12,20... | collective-permute-start | bytes 4718600 | tf_op jit(solution)/shard_map/ppermute | solution.py:84
  390.6 35.2 %collective-permute-start.25 = (bf16[512,1536]{1,0:T(8,128)(2,1)}, bf16[512,1536]{1,0:T(8,128)(2,1)}, u32[]{:S(2)}, u32[]{:S(2)}) collective-permute-start(bf16[512,1536]{1,0:T(8,128)(2,1)} %add_convert_fusion.5), channel_id=1, source_target_pairs={{0,8},{8,0},{16,24},{24,16},{1,9},{9,1},{17,25},{25,17},{2,10},{10... | collective-permute-start | bytes 4718600 | tf_op jit(solution)/shard_map/ppermute | solution.py:84
  431.5 12.5 %collective-permute-start.26 = (bf16[4,256,2048]{2,1,0:T(8,128)(2,1)}, bf16[4,256,2048]{2,1,0:T(8,128)(2,1)}, u32[]{:S(2)}, u32[]{:S(2)}) collective-permute-start(bf16[4,256,2048]{2,1,0:T(8,128)(2,1)} %select_bitcast_fusion), channel_id=1, source_target_pairs={{0,1},{1,0},{2,3},{3,2},{4,5},{5,4},{6,7},{7,6},{8,9},{9,8},{10,11... | collective-permute-start | bytes 12582920 | tf_op jit(solution)/shard_map/ppermute | solution.py:751
  436.9 39.9 %collective-permute-start.27 = (bf16[512,1536]{1,0:T(8,128)(2,1)}, bf16[512,1536]{1,0:T(8,128)(2,1)}, u32[]{:S(2)}, u32[]{:S(2)}) collective-permute-start(bf16[512,1536]{1,0:T(8,128)(2,1)} %get-tuple-element.260), channel_id=1, source_target_pairs={{0,8},{8,0},{16,24},{24,16},{1,9},{9,1},{17,25},{25,17},{2,10},{10... | collective-permute-start | bytes 4718600 | tf_op jit(solution)/shard_map/ppermute | solution.py:79
  469.9 17.7 %all-to-all-start = ((bf16[256,8,256]{2,0,1:T(8,128)(2,1)}), bf16[256,8,256]{2,0,1:T(8,128)(2,1)S(1)}, u32[]{:S(2)}, u32[]{:S(2)}) async-start(bf16[256,8,256]{2,0,1:T(8,128)(2,1)} %bitcast.66), calls=%async_computation.2 | async-start | bytes 2097152 | tf_op jit(solution)/shard_map/all_to_all | solution.py:922
  474.1 83.6 %all-gather.11.cloned.1.call-start = ((), (), s32[]{:S(2)}) async-start(), calls=%async_computation.9 | async-start | bytes 9437184 | tf_op jit(solution)/shard_map/all_gather | solution.py:941
  487.7 224.5 %reduce-scatter.8.cloned.1.call-start = ((), (), s32[]{:S(2)}) async-start(), calls=%async_computation.10 | async-start | bytes 9437184 | tf_op jit(solution)/shard_map/reduce_scatter | solution.py:952
  490.8 42.0 %collective-permute-start.28 = (bf16[512,1536]{1,0:T(8,128)(2,1)S(1)}, bf16[512,1536]{1,0:T(8,128)(2,1)}, u32[]{:S(2)}, u32[]{:S(2)}) collective-permute-start(bf16[512,1536]{1,0:T(8,128)(2,1)S(1)} %add_convert_fusion.2), channel_id=1, source_target_pairs={{8,16},{16,8},{9,17},{17,9},{10,18},{18,10},{11,19},{19,11},{12,20... | collective-permute-start | bytes 4718600 | tf_op jit(solution)/shard_map/ppermute | solution.py:84
  493.9 38.9 %collective-permute-start.29 = (bf16[512,1536]{1,0:T(8,128)(2,1)S(1)}, bf16[512,1536]{1,0:T(8,128)(2,1)}, u32[]{:S(2)}, u32[]{:S(2)}) collective-permute-start(bf16[512,1536]{1,0:T(8,128)(2,1)S(1)} %add_convert_fusion.2), channel_id=1, source_target_pairs={{0,8},{8,0},{16,24},{24,16},{1,9},{9,1},{17,25},{25,17},{2,10},{10... | collective-permute-start | bytes 4718600 | tf_op jit(solution)/shard_map/ppermute | solution.py:84
  494.0 73.2 %collective-permute-start.33 = (bf16[512,1536]{1,0:T(8,128)(2,1)}, bf16[512,1536]{1,0:T(8,128)(2,1)}, u32[]{:S(2)}, u32[]{:S(2)}) collective-permute-start(bf16[512,1536]{1,0:T(8,128)(2,1)} %get-tuple-element.296), channel_id=1, source_target_pairs={{0,8},{8,0},{16,24},{24,16},{1,9},{9,1},{17,25},{25,17},{2,10},{10... | collective-permute-start | bytes 4718600 | tf_op jit(solution)/shard_map/ppermute | solution.py:92
  495.4 71.8 %collective-permute-start.34 = (bf16[512,1536]{1,0:T(8,128)(2,1)}, bf16[512,1536]{1,0:T(8,128)(2,1)}, u32[]{:S(2)}, u32[]{:S(2)}) collective-permute-start(bf16[512,1536]{1,0:T(8,128)(2,1)} %get-tuple-element.297), channel_id=1, source_target_pairs={{8,16},{16,8},{9,17},{17,9},{10,18},{18,10},{11,19},{19,11},{12,20... | collective-permute-start | bytes 4718600 | tf_op jit(solution)/shard_map/ppermute | solution.py:92
  498.6 91.1 %collective-permute-start.32 = (bf16[2,256,2048]{2,1,0:T(8,128)(2,1)}, bf16[2,256,2048]{2,1,0:T(8,128)(2,1)}, u32[]{:S(2)}, u32[]{:S(2)}) collective-permute-start(bf16[2,256,2048]{2,1,0:T(8,128)(2,1)} %pad_maximum_fusion.4), channel_id=1, source_target_pairs={{0,4},{1,3},{2,6},{3,1},{4,0},{5,7},{6,2},{7,5},{8,12},{9,11},{10,... | collective-permute-start | bytes 6291464 | tf_op jit(solution)/shard_map/ppermute | solution.py:745
  561.0 36.5 %collective-permute-start.30 = (bf16[512,1536]{1,0:T(8,128)(2,1)S(1)}, bf16[512,1536]{1,0:T(8,128)(2,1)S(1)}, u32[]{:S(2)}, u32[]{:S(2)}) collective-permute-start(bf16[512,1536]{1,0:T(8,128)(2,1)S(1)} %add_convert_fusion.1), channel_id=1, source_target_pairs={{0,8},{8,0},{16,24},{24,16},{1,9},{9,1},{17,25},{25,17},{2,10},{10... | collective-permute-start | bytes 4718600 | tf_op jit(solution)/shard_map/ppermute | solution.py:92
  563.6 38.0 %collective-permute-start.31 = (bf16[512,1536]{1,0:T(8,128)(2,1)S(1)}, bf16[512,1536]{1,0:T(8,128)(2,1)}, u32[]{:S(2)}, u32[]{:S(2)}) collective-permute-start(bf16[512,1536]{1,0:T(8,128)(2,1)S(1)} %add_convert_fusion), channel_id=1, source_target_pairs={{8,16},{16,8},{9,17},{17,9},{10,18},{18,10},{11,19},{19,11},{12,20... | collective-permute-start | bytes 4718600 | tf_op jit(solution)/shard_map/ppermute | solution.py:92
  570.0 18.8 %collective-permute-start.35 = (bf16[256,1536]{1,0:T(8,128)(2,1)S(1)}, bf16[256,1536]{1,0:T(8,128)(2,1)S(1)}, u32[]{:S(2)}, u32[]{:S(2)}) collective-permute-start(bf16[256,1536]{1,0:T(8,128)(2,1)S(1)} %select_convert_fusion.1), channel_id=1, source_target_pairs={{0,4},{4,0},{1,5},{5,1},{2,6},{6,2},{3,7},{7,3},{8,12},{12,8},{9,1... | collective-permute-start | bytes 2359304 | tf_op jit(solution)/shard_map/ppermute | solution.py:168
  604.0 24.5 %collective-permute-start.36 = (bf16[256,1536]{1,0:T(8,128)(2,1)S(1)}, bf16[256,1536]{1,0:T(8,128)(2,1)S(1)}, u32[]{:S(2)}, u32[]{:S(2)}) collective-permute-start(bf16[256,1536]{1,0:T(8,128)(2,1)S(1)} %select_convert_fusion), channel_id=1, source_target_pairs={{0,4},{4,0},{1,5},{5,1},{2,6},{6,2},{3,7},{7,3},{8,12},{12,8},{9,1... | collective-permute-start | bytes 2359304 | tf_op jit(solution)/shard_map/ppermute | solution.py:168
  605.3 67.9 %collective-permute-start.37 = (bf16[512,384]{1,0:T(8,128)(2,1)S(1)}, bf16[512,384]{1,0:T(8,128)(2,1)S(1)}, u32[]{:S(2)}, u32[]{:S(2)}) collective-permute-start(bf16[512,384]{1,0:T(8,128)(2,1)S(1)} %get-tuple-element.305), channel_id=1, source_target_pairs={{0,8},{8,0},{16,24},{24,16},{1,9},{9,1},{17,25},{25,17},{2,10},{10... | collective-permute-start | bytes 1179656 | tf_op jit(solution)/shard_map/ppermute | solution.py:101
  605.3 18.8 %collective-permute-start.40 = (bf16[256,512]{1,0:T(8,128)(2,1)S(1)}, bf16[256,512]{1,0:T(8,128)(2,1)S(1)}, u32[]{:S(2)}, u32[]{:S(2)}) collective-permute-start(bf16[256,512]{1,0:T(8,128)(2,1)S(1)} %get-tuple-element.308), channel_id=1, source_target_pairs={{0,8},{8,0},{16,24},{24,16},{1,9},{9,1},{17,25},{25,17},{2,10},{10... | collective-permute-start | bytes 786440 | tf_op jit(solution)/shard_map/ppermute | solution.py:101
  606.7 23.2 %collective-permute-start.41 = (bf16[256,512]{1,0:T(8,128)(2,1)S(1)}, bf16[256,512]{1,0:T(8,128)(2,1)S(1)}, u32[]{:S(2)}, u32[]{:S(2)}) collective-permute-start(bf16[256,512]{1,0:T(8,128)(2,1)S(1)} %get-tuple-element.309), channel_id=1, source_target_pairs={{0,16},{8,24},{16,0},{24,8},{1,17},{9,25},{17,1},{25,9},{2,18},{10... | collective-permute-start | bytes 786440 | tf_op jit(solution)/shard_map/ppermute | solution.py:101
  609.9 63.3 %collective-permute-start.43 = (bf16[256,2048]{1,0:T(8,128)(2,1)S(1)}, bf16[256,2048]{1,0:T(8,128)(2,1)S(1)}, u32[]{:S(2)}, u32[]{:S(2)}) collective-permute-start(bf16[256,2048]{1,0:T(8,128)(2,1)S(1)} %fusion.11), channel_id=1, source_target_pairs={{0,2},{1,5},{2,0},{3,7},{4,6},{5,1},{6,4},{7,3},{8,10},{9,13},{10,... | collective-permute-start | bytes 3145736 | tf_op jit(solution)/shard_map/ppermute | solution.py:748
  624.0 49.2 %collective-permute-start.38 = (bf16[512,384]{1,0:T(8,128)(2,1)S(1)}, bf16[512,384]{1,0:T(8,128)(2,1)S(1)}, u32[]{:S(2)}, u32[]{:S(2)}) collective-permute-start(bf16[512,384]{1,0:T(8,128)(2,1)S(1)} %get-tuple-element.306), channel_id=1, source_target_pairs={{0,16},{8,24},{16,0},{24,8},{1,17},{9,25},{17,1},{25,9},{2,18},{10... | collective-permute-start | bytes 1179656 | tf_op jit(solution)/shard_map/ppermute | solution.py:101
  628.5 44.7 %collective-permute-start.39 = (bf16[512,384]{1,0:T(8,128)(2,1)S(1)}, bf16[512,384]{1,0:T(8,128)(2,1)S(1)}, u32[]{:S(2)}, u32[]{:S(2)}) collective-permute-start(bf16[512,384]{1,0:T(8,128)(2,1)S(1)} %get-tuple-element.307), channel_id=1, source_target_pairs={{0,24},{8,16},{16,8},{24,0},{1,25},{9,17},{17,9},{25,1},{2,26},{10... | collective-permute-start | bytes 1179656 | tf_op jit(solution)/shard_map/ppermute | solution.py:101
  629.9 43.3 %collective-permute-start.42 = (bf16[256,512]{1,0:T(8,128)(2,1)S(1)}, bf16[256,512]{1,0:T(8,128)(2,1)S(1)}, u32[]{:S(2)}, u32[]{:S(2)}) collective-permute-start(bf16[256,512]{1,0:T(8,128)(2,1)S(1)} %get-tuple-element.310), channel_id=1, source_target_pairs={{0,24},{8,16},{16,8},{24,0},{1,25},{9,17},{17,9},{25,1},{2,26},{10... | collective-permute-start | bytes 786440 | tf_op jit(solution)/shard_map/ppermute | solution.py:101
  673.5 26.1 %copy-start.37 = (f32[256,384]{1,0:T(8,128)}, f32[256,384]{1,0:T(8,128)S(1)}, u32[]{:S(2)}) copy-start(f32[256,384]{1,0:T(8,128)S(1)} %slice_select_fusion.2) | copy-start | bytes 1179652
  674.3 32.3 %collective-permute-start.44 = (bf16[256,384]{1,0:T(8,128)(2,1)}, bf16[256,384]{1,0:T(8,128)(2,1)}, u32[]{:S(2)}, u32[]{:S(2)}) collective-permute-start(bf16[256,384]{1,0:T(8,128)(2,1)} %select_convert_fusion.2), channel_id=1, source_target_pairs={{0,4},{4,0},{1,5},{5,1},{2,6},{6,2},{3,7},{7,3},{8,12},{12,8},{9,1... | collective-permute-start | bytes 589832 | tf_op jit(solution)/shard_map/ppermute | solution.py:168
  675.3 28.7 %collective-permute-start.45 = (bf16[256,256]{1,0:T(8,128)(2,1)}, bf16[256,256]{1,0:T(8,128)(2,1)}, u32[]{:S(2)}, u32[]{:S(2)}) collective-permute-start(bf16[256,256]{1,0:T(8,128)(2,1)} %select_convert_fusion.3), channel_id=1, source_target_pairs={{0,4},{4,0},{1,5},{5,1},{2,6},{6,2},{3,7},{7,3},{8,12},{12,8},{9,1... | collective-permute-start | bytes 393224 | tf_op jit(solution)/shard_map/ppermute | solution.py:168
  679.6 2.0 collective-permute-start.46
  681.5 7.2 collective-permute-start.47
  688.8 5.0 collective-permute-start.48
  693.9 5.2 collective-permute-start.49
  699.1 3.6 collective-permute-start.50
  (89 other events, 412.2 us)
Sparse Core Ops, SparseCore 0:
  12.6 64.2 all-gather.4
  118.6 73.6 reduce-scatter.3
  195.8 54.7 all-gather.6
  271.3 54.5 all-gather.8
  383.6 75.4 reduce-scatter.5
  487.8 69.8 all-gather.10
  561.2 87.8 reduce-scatter.7

commit v5 on v4

--- a/solution.py
+++ b/solution.py
@@ -30,6 +30,8 @@
 MIDDLE = [(1, 2), (2, 1)]
 CROSS = [(0, 2), (1, 3), (2, 0), (3, 1)]
 MIRROR = [(0, 3), (1, 2), (2, 1), (3, 0)]
+OUTWARD = [(1, 0), (2, 3)]
+INWARD = [(0, 1), (3, 2)]
 PAIR = [(0, 1), (1, 0)]
 
 
@@ -55,8 +57,8 @@
     return lax.ppermute(near, "do", MIDDLE), lax.ppermute(across, "do", NEAR)
 
 
-def line_last(across_near):
-    return lax.ppermute(across_near, "do", NEAR)
+def line_last(across_near, perm=NEAR):
+    return lax.ppermute(across_near, "do", perm)
 
 
 def add(part, *arrived):
@@ -75,8 +77,8 @@
     return add(part, jnp.where(is_inner(), arrived, jnp.zeros_like(arrived)))
 
 
-def sum_far(parts):
-    return lax.ppermute(parts[3], "do", NEAR)
+def sum_far(part, perm=NEAR):
+    return lax.ppermute(part, "do", perm)
 
 
 def sum_middle(parts, far):
@@ -146,13 +148,11 @@
             full.append(lax.all_gather(block, "do", axis=axis, tiled=True))
         return tuple(full)
 
-    def unpack(self, total, wide):
-        rows = self.rows
-        mine, theirs = self.trade(total[:rows], total[rows:])
-        cuts = range(wide, total.shape[1], rows)
+    def unpack(self, pair, wide):
+        cuts = range(wide, pair[0].shape[1], self.rows)
         return (
-            (mine[:, :wide], theirs[:, :wide]),
-            tuple(cat([side[:, i : i + rows] for i in cuts], 0) for side in (mine, theirs)),
+            tuple(side[:, :wide] for side in pair),
+            tuple(cat([side[:, i : i + self.rows] for i in cuts], 0) for side in pair),
         )
 
     def plain_sum_row(self, grad):
@@ -164,9 +164,8 @@
         return self.trade(total[:, : self.rows], total[:, self.rows :])
 
     def trade(self, low, high):
-        mine = self.by_x(low, high).astype(F32)
         theirs = lax.ppermute(self.by_x(high, low).astype(LOW), "di", PAIR)
-        return mine, theirs.astype(F32)
+        return self.by_x(low, high).astype(F32), theirs
 
 
 ANY = pl.BlockSpec(memory_space=pl.ANY)
@@ -179,25 +178,23 @@
         rows, wide = plan.rows, row_shape[1]
         self.moves = []
         if plan.line:
-            self.operands = [plan.inner(), *weights]
+            *whole, last = weights
+            self.operands = [plan.inner(), *whole, *last]
             for k in range(4):
-                at = k * plan.block
-                self.moves.append((k, 0, (0, 0), (at, 0), (plan.block, wide)))
-                for i in range(0, col_shape[0], rows):
-                    for x in range(2):
-                        self.moves.append(
-                            (k, 1, (x * rows, wide + i), (i, at + x * rows), (rows, rows))
-                        )
+                for x in range(2):
+                    at = k * plan.block + x * rows
+                    self.moves.append((k, x, 0, 0, (at, 0), wide))
+                    for i in range(0, col_shape[0], rows):
+                        self.moves.append((k, x, 1, wide + i, (i, at), rows))
         else:
             self.operands = list(weights)
-            self.moves.append((0, 0, (0, 0), (0, 0), row_shape))
-            self.moves.append((1, 1, (0, 0), (0, 0), col_shape))
+            self.moves = [None, None]
         self.count = len(self.operands)
 
     def specs(self):
         if not self.plan.line:
             return [ANY] * 2
-        return [pl.BlockSpec(memory_space=pltpu.SMEM)] + [ANY] * 6
+        return [pl.BlockSpec(memory_space=pltpu.SMEM)] + [ANY] * (self.count - 1)
 
     def scratch(self):
         return [
@@ -207,65 +204,53 @@
         ]
 
     def load(self, refs, row_ref, col_ref, sems):
-        def copies(sources, chosen):
-            made = []
-            for i, (k, which, here, there, size) in enumerate(self.moves):
-                if k in chosen:
-                    target = (row_ref, col_ref)[which]
-                    made.append(
-                        pltpu.make_async_copy(
-                            sources[k].at[pl.ds(here[0], size[0]), pl.ds(here[1], size[1])],
-                            target.at[pl.ds(there[0], size[0]), pl.ds(there[1], size[1])],
-                            sems.at[i],
-                        )
-                    )
-            return made
-
         if not self.plan.line:
-            for copy in copies(refs, (0, 1)):
+            pairs = zip(refs, (row_ref, col_ref))
+            made = [pltpu.make_async_copy(*pair, sems.at[i]) for i, pair in enumerate(pairs)]
+            for copy in made:
                 copy.start()
-            for copy in copies(refs, (0, 1)):
+            for copy in made:
                 copy.wait()
             return
-        inner, own, near, across_near, out, across, out_near = refs
+        rows = self.plan.rows
+
+        def copies(sources):
+            made = []
+            for i, (k, x, which, column, there, wide) in enumerate(self.moves):
+                if sources[k] is None:
+                    continue
+                if isinstance(sources[k], tuple):
+                    source, row = sources[k][x], 0
+                else:
+                    source, row = sources[k], x * rows
+                target = (row_ref, col_ref)[which]
+                made.append(
+                    pltpu.make_async_copy(
+                        source.at[pl.ds(row, rows), pl.ds(column, wide)],
+                        target.at[pl.ds(there[0], rows), pl.ds(there[1], wide)],
+                        sems.at[i],
+                    )
+                )
+            return made
+
+        inner, own, near, across_near, out, across, *last = refs
+        out_near = tuple(last) if len(last) == 2 else last[0]
         is_inner = inner[0] == 1
-        for copy in copies((own, near), (0, 1)):
+        for copy in copies((own, near, None, None)):
             copy.start()
 
         @pl.when(is_inner)
         def _():
-            for copy in copies((None, None, across_near, across), (2, 3)):
+            for copy in copies((None, None, across_near, across)):
                 copy.start()
 
         @pl.when(jnp.logical_not(is_inner))
         def _():
-            for copy in copies((None, None, out, out_near), (2, 3)):
+            for copy in copies((None, None, out, out_near)):
                 copy.start()
 
-        for copy in copies((own, near, out, out_near), (0, 1, 2, 3)):
+        for copy in copies((own, near, out, out_near)):
             copy.wait()
-
-
-def pack_grads(plan, row_grad, col_grad, out_refs):
-    if not plan.line:
-        out_refs[0][...] = row_grad[...].astype(LOW)
-        out_refs[1][...] = col_grad[...].astype(LOW)
-        return
-    rows, block, wide = plan.rows, plan.block, row_grad.shape[1]
-    for k, out in enumerate(out_refs):
-        at = k * block
-        out[:, :wide] = row_grad[at : at + block, :].astype(LOW)
-        for i in range(0, col_grad.shape[0], rows):
-            for x in range(2):
-                out[x * rows : (x + 1) * rows, wide + i : wide + i + rows] = col_grad[
-                    i : i + rows, at + x * rows : at + (x + 1) * rows
-                ].astype(LOW)
-
-
-def packed_shapes(plan, row_shape, col_shape):
-    if not plan.line:
-        return [row_shape, col_shape]
-    return [(plan.block, row_shape[1] + col_shape[0])] * 4
 
 
 def rope_tables(positions):
@@ -365,6 +350,7 @@
     def _():
         loader.load(weights, wqkv_ref, wout_ref, sems)
         acc_qkv[...] = jnp.zeros_like(acc_qkv)
+        gain_ref[...] = jnp.zeros_like(gain_ref)
 
     cosine, sine = tables(cos_ref, sin_ref, pairs)
     scale = HD**-0.5
@@ -399,7 +385,9 @@
     value_grad = value_grad + pltpu.roll(value_grad, HD, 1)
     joined = cat(query_grads + [jnp.where(lane < HD, key_grad, value_grad)], 1)
     low = (joined * cosine - shuffle_halves(joined) * sine).astype(LOW)
-    part_ref[...] = dot(low, wqkv_ref[...], 1, 1).astype(LOW)
+    part = dot(low, wqkv_ref[...], 1, 1)
+    part_ref[...] = part.astype(LOW)
+    gain_ref[...] += jnp.sum(part * x_ref[...].astype(F32), axis=0, keepdims=True)
     acc_qkv[...] += dot(x_ref[...], low, 0, 0)
 
     @pl.when(step == pl.num_programs(0) - 1)
@@ -407,7 +395,6 @@
         cut = acc_qkv.shape[0] // len(grad_refs)
         for i, out in enumerate(grad_refs):
             out[...] = acc_qkv[i * cut : (i + 1) * cut, :].astype(LOW)
-        gain_ref[...] = jnp.sum(acc_qkv[...] * wqkv_ref[...].astype(F32), axis=1, keepdims=True)
 
 
 def once(shape):
@@ -449,7 +436,7 @@
             jax.ShapeDtypeStruct(loader.col_shape, LOW),
         ],
         scratch_shapes=loader.scratch(),
-        compiler_params=pltpu.CompilerParams(vmem_limit_bytes=48 * MIB),
+        compiler_params=pltpu.CompilerParams(vmem_limit_bytes=60 * MIB),
         cost_estimate=SMALL,
         name="attn_forward",
     )(*loader.operands, normed, cosine, sine, seg_col, seg_row)
@@ -475,21 +462,22 @@
             per_seq((LEN, 1)),
             per_seq((1, 1, LEN)),
         ],
-        out_specs=[per_seq((LEN, width)), once((width, 1))] + [once(grad)] * cuts,
+        out_specs=[per_seq((LEN, width)), once((1, width))] + [once(grad)] * cuts,
         out_shape=[
             jax.ShapeDtypeStruct((rows, width), LOW),
-            jax.ShapeDtypeStruct((width, 1), F32),
+            jax.ShapeDtypeStruct((1, width), F32),
         ]
         + [jax.ShapeDtypeStruct(grad, LOW)] * cuts,
         scratch_shapes=[*loader.scratch(), pltpu.VMEM(loader.row_shape, F32)],
-        compiler_params=pltpu.CompilerParams(vmem_limit_bytes=52 * MIB),
+        compiler_params=pltpu.CompilerParams(vmem_limit_bytes=60 * MIB),
         cost_estimate=SMALL,
         name="attn_backward",
     )(*loader.operands, ctx_grad, normed, queries, both, lse, cosine, sine, seg_col, seg_row)
 
 
-def out_weights_kernel(ctx_ref, res_ref, *refs):
-    grad_refs, acc = refs[:-1], refs[-1]
+def out_weights_kernel(plan, ctx_ref, res_ref, *refs):
+    count = plan.cuts
+    qkv_refs, grad_refs, acc = refs[:-1][: count * plan.line], refs[-1 - count : -1], refs[-1]
     step = pl.program_id(0)
 
     @pl.when(step == 0)
@@ -500,26 +488,34 @@
 
     @pl.when(step == pl.num_programs(0) - 1)
     def _():
-        cut = acc.shape[1] // len(grad_refs)
-        for i, out in enumerate(grad_refs):
-            out[...] = acc[:, i * cut : (i + 1) * cut].astype(LOW)
-
-
-def out_weights(plan, ctx, res_all):
+        if not plan.line:
+            grad_refs[0][...] = acc[...].astype(LOW)
+            return
+        rows = plan.rows
+        for k, (qkv, out) in enumerate(zip(qkv_refs, grad_refs)):
+            wide = qkv.shape[1]
+            out[:, :wide] = qkv[...]
+            for x in range(2):
+                at = k * plan.block + x * rows
+                out[x * rows : (x + 1) * rows, wide:] = acc[:, at : at + rows].astype(LOW)
+
+
+def out_weights(plan, ctx, res_all, grads_qkv):
     rows, width = res_all.shape
     heads = ctx.shape[1]
-    grad = (heads, width // plan.cuts)
+    extra = list(grads_qkv) if plan.line else []
+    shape = (plan.block, extra[0].shape[1] + heads) if plan.line else (heads, width)
     return pl.pallas_call(
-        out_weights_kernel,
+        functools.partial(out_weights_kernel, plan),
         grid=(rows // LEN,),
-        in_specs=[per_seq((LEN, heads)), per_seq((LEN, width))],
-        out_specs=[once(grad)] * plan.cuts,
-        out_shape=[jax.ShapeDtypeStruct(grad, LOW)] * plan.cuts,
+        in_specs=[per_seq((LEN, heads)), per_seq((LEN, width))] + [once(g.shape) for g in extra],
+        out_specs=[once(shape)] * plan.cuts,
+        out_shape=[jax.ShapeDtypeStruct(shape, LOW)] * plan.cuts,
         scratch_shapes=[pltpu.VMEM((heads, width), F32)],
         compiler_params=pltpu.CompilerParams(vmem_limit_bytes=40 * MIB),
         cost_estimate=SMALL,
         name="out_weights",
-    )(ctx, res_all)
+    )(ctx, res_all, *extra)
 
 
 def residual_backward_kernel(
@@ -562,7 +558,7 @@
             jax.ShapeDtypeStruct((rows, width), LOW),
             jax.ShapeDtypeStruct((rows, heads), LOW),
         ],
-        compiler_params=pltpu.CompilerParams(vmem_limit_bytes=40 * MIB),
+        compiler_params=pltpu.CompilerParams(vmem_limit_bytes=60 * MIB),
         cost_estimate=SMALL,
         name="residual_backward",
     )(back_sum, residual, scale, gain[None, :], grad_low, wout_all)
@@ -574,7 +570,7 @@
 def ffn_main_kernel(loader, more, *refs):
     weights, refs = refs[: loader.count], refs[loader.count :]
     x_ref, grad_ref = refs[:2]
-    back_ref, act_ref, both_ref, gate_up_ref, down_ref, sems = refs[2 + more :]
+    back_ref, act_ref, both_ref, down_ref, gate_up_ref, _, sems = refs[2 + more :]
 
     @pl.when(pl.program_id(0) == 0)
     def _():
@@ -613,79 +609,102 @@
             per_seq((TILE, width)),
             per_seq((TILE, hidden)),
             per_seq((TILE, 2 * hidden)),
+            once(loader.col_shape),
         ],
         out_shape=[
             jax.ShapeDtypeStruct((rows, width), LOW),
             jax.ShapeDtypeStruct((rows, hidden), LOW),
             jax.ShapeDtypeStruct((rows, 2 * hidden), LOW),
+            jax.ShapeDtypeStruct(loader.col_shape, LOW),
         ],
         scratch_shapes=loader.scratch(),
-        compiler_params=pltpu.CompilerParams(vmem_limit_bytes=58 * MIB),
+        compiler_params=pltpu.CompilerParams(vmem_limit_bytes=60 * MIB),
         cost_estimate=SMALL,
         name="ffn_main",
     )(*loader.operands, tokens, grads, *more)
 
 
-def ffn_weights_kernel(loader, more, *refs):
-    weights, refs = refs[: loader.count], refs[loader.count :]
-    x_ref, grad_ref, act_ref, both_ref = refs[:4]
-    out_ref, gain_ref, *grad_refs = refs[4 + more : -5]
-    gate_up_ref, down_ref, sems, acc_gate_up, acc_down = refs[-5:]
-    step = pl.program_id(0)
-
-    @pl.when(step == 0)
-    def _():
-        loader.load(weights, gate_up_ref, down_ref, sems)
-        acc_gate_up[...] = jnp.zeros_like(acc_gate_up)
-        acc_down[...] = jnp.zeros_like(acc_down)
-
-    act = act_ref[...]
-    acc_down[...] += dot(act, grad_ref[...], 0, 0)
-    acc_gate_up[...] += dot(x_ref[...], both_ref[...], 0, 0)
-    out = dot(act, down_ref[...], 1, 0)
-    if more:
-        out = out + refs[4][...].astype(F32)
-    out_ref[...] = out.astype(LOW)
-
-    @pl.when(step == pl.num_programs(0) - 1)
-    def _():
-        pack_grads(loader.plan, acc_gate_up, acc_down, grad_refs)
-        gain_ref[...] = jnp.sum(
-            acc_gate_up[...] * gate_up_ref[...].astype(F32), axis=1, keepdims=True
-        )
-
-
-def ffn_weights(loader, tokens, grads, act, both_grad, earlier):
+def ffn_weights_kernel(plan, x_ref, grad_ref, act_ref, both_ref, *out_refs):
+    row = dot(x_ref[...], both_ref[...], 0, 0).astype(LOW)
+    col = dot(act_ref[...], grad_ref[...], 0, 0).astype(LOW)
+    if not plan.line:
+        out_refs[0][...], out_refs[1][...] = row, col
+        return
+    rows, wide, out = plan.rows, row.shape[1], out_refs[0]
+    out[:, :wide] = row
+    for i in range(0, col.shape[0], rows):
+        for x in range(2):
+            out[x * rows : (x + 1) * rows, wide + i : wide + i + rows] = col[
+                i : i + rows, x * rows : (x + 1) * rows
+            ]
+
+
+def ffn_weights(plan, tokens, grads, act, both_grad, first, count):
     rows, width = tokens.shape
-    hidden = loader.col_shape[0]
-    more = [] if earlier is None else [earlier]
-    packed = packed_shapes(loader.plan, loader.row_shape, loader.col_shape)
+    block = width // 4
+    wide, hidden = both_grad.shape[1], act.shape[1]
+
+    def columns(shift):
+        return pl.BlockSpec((rows, block), lambda i: (0, i + shift))
+
+    if plan.line:
+        out_specs = [pl.BlockSpec((block, wide + hidden), lambda i: (i, 0))]
+        out_shape = [jax.ShapeDtypeStruct((count * block, wide + hidden), LOW)]
+    else:
+        out_specs = [
+            pl.BlockSpec((block, wide), lambda i: (i, 0)),
+            pl.BlockSpec((hidden, block), lambda i: (0, i)),
+        ]
+        out_shape = [
+            jax.ShapeDtypeStruct((count * block, wide), LOW),
+            jax.ShapeDtypeStruct((hidden, count * block), LOW),
+        ]
     return pl.pallas_call(
-        functools.partial(ffn_weights_kernel, loader, len(more)),
-        grid=(rows // TILE,),
-        in_specs=[
-            *loader.specs(),
-            per_seq((TILE, width)),
-            per_seq((TILE, width)),
-            per_seq((TILE, hidden)),
-            per_seq((TILE, 2 * hidden)),
-            *[per_seq((TILE, width))] * len(more),
-        ],
-        out_specs=[per_seq((TILE, width)), once((width, 1))] + [once(shape) for shape in packed],
-        out_shape=[
-            jax.ShapeDtypeStruct((rows, width), LOW),
-            jax.ShapeDtypeStruct((width, 1), F32),
-        ]
-        + [jax.ShapeDtypeStruct(shape, LOW) for shape in packed],
-        scratch_shapes=[
-            *loader.scratch(),
-            pltpu.VMEM(loader.row_shape, F32),
-            pltpu.VMEM(loader.col_shape, F32),
-        ],
+        functools.partial(ffn_weights_kernel, plan),
+        grid=(count,),
+        in_specs=[columns(first), columns(first), once(act.shape), once(both_grad.shape)],
+        out_specs=out_specs,
+        out_shape=out_shape,
         compiler_params=pltpu.CompilerParams(vmem_limit_bytes=60 * MIB),
         cost_estimate=SMALL,
         name="ffn_weights",
-    )(*loader.operands, tokens, grads, act, both_grad, *more)
+    )(tokens, grads, act, both_grad)
+
+
+def ffn_out_kernel(act_1, act_2, down_1, down_2, back_ref, x_ref, out_ref, gain_ref):
+    @pl.when(pl.program_id(0) == 0)
+    def _():
+        gain_ref[...] = jnp.zeros_like(gain_ref)
+
+    out = dot(act_1[...], down_1[...], 1, 0) + dot(act_2[...], down_2[...], 1, 0)
+    out_ref[...] = out.astype(LOW)
+    product = back_ref[...].astype(F32) * x_ref[...].astype(F32)
+    gain_ref[...] += jnp.sum(product, axis=0, keepdims=True)
+
+
+def ffn_out(act_1, act_2, down_1, down_2, back, tokens):
+    rows, width = tokens.shape
+    hidden = act_1.shape[1]
+    return pl.pallas_call(
+        ffn_out_kernel,
+        grid=(rows // TILE,),
+        in_specs=[
+            per_seq((TILE, hidden)),
+            per_seq((TILE, hidden)),
+            once(down_1.shape),
+            once(down_2.shape),
+            per_seq((TILE, width)),
+            per_seq((TILE, width)),
+        ],
+        out_specs=[per_seq((TILE, width)), once((1, width))],
+        out_shape=[
+            jax.ShapeDtypeStruct((rows, width), LOW),
+            jax.ShapeDtypeStruct((1, width), F32),
+        ],
+        compiler_params=pltpu.CompilerParams(vmem_limit_bytes=60 * MIB),
+        cost_estimate=SMALL,
+        name="ffn_out",
+    )(act_1, act_2, down_1, down_2, back, tokens)
 
 
 def norm_rows(values, gain_vec):
@@ -711,7 +730,7 @@
     return (next_master, next_first, next_second)
 
 
-def sum_everywhere(values, sizes):
+def sum_over(values, sizes):
     for axis, size in sizes:
         step = 1
         while step < size:
@@ -770,6 +789,7 @@
     by_x = plan.by_x
     axes = ("di", "tp")
     plane = Plane(sizes["tp"])
+    plane_sizes = (("tp", sizes["tp"]), ("di", sizes["di"]))
 
     gain_one, gain_two = plan.reorder(gain_attn), plan.reorder(gain_ffn)
     inputs_f = plan.reorder(layer_input).astype(F32)
@@ -836,11 +856,11 @@
         across_near, out = line_far(near, across)
         across_near, out, theirs_1 = fence(across_near, out, theirs_1)
         out_near = line_last(across_near)
-        out_near, normed_all, theirs_1, grad_low, other_2 = fence(
-            out_near, normed_all, theirs_1, grad_low, other_2
-        )
         block_1 = plan.join(own_1, theirs_1)
-        attn_weights = (attn_block, near, across_near, out, across, out_near)
+        out_near, normed_all, block_1, grad_low, other_2, seg_col, seg_row = fence(
+            out_near, normed_all, block_1, grad_low, other_2, seg_col, seg_row
+        )
+        attn_weights = (attn_block, near, across_near, out, across, (out_near,))
         near_1, across_1 = line_near(block_1)
     else:
         attn_weights = plan.plain_gather(qkv_parts, out_parts)
@@ -866,7 +886,8 @@
             across_near_1, out_1, grad_xy, theirs_2, grad_first
         )
         block_2 = plan.join(own_2, theirs_2)
-        out_near_1 = line_last(across_near_1)
+        half = plan.rows
+        out_near_low = line_last(across_near_1[:half])
         across_2 = lax.ppermute(block_2, "do", MIDDLE)
     grad_x = pick(core, grad_first, grad_second)
     grad_y = pick(core, grad_second, grad_first)
@@ -879,42 +900,55 @@
     grad_all = cat([pick(core, mine, theirs), pick(core, theirs, mine)], 1).reshape(rows, width)
 
     if plan.line:
-        attn_sum, grad_all = fence(attn_sum, grad_all)
+        attn_sum, grad_all, out_near_low, across_2 = fence(
+            attn_sum, grad_all, out_near_low, across_2
+        )
     residual = inputs_f + attn_sum.astype(F32)
     normed_two, scale_two = norm_rows(residual, gain_two)
     two_low = normed_two.astype(LOW)
     two_all = lax.all_gather(two_low, axes, axis=0, tiled=True)
 
     if plan.line:
-        out_near_1, across_2, block_2, _ = fence(out_near_1, across_2, block_2, two_low)
+        across_near_1, across_2, block_2, _ = fence(across_near_1, across_2, block_2, two_low)
+        out_near_high = line_last(across_near_1[half:])
+        near_2 = lax.ppermute(block_2, "do", NEAR)
+        near_2, across_2, wout, out_near_high = fence(near_2, across_2, wout, out_near_high)
+        across_near_2, out_2 = line_far(near_2, across_2)
+        out_near_1 = (out_near_low, out_near_high)
         first_weights = (block_1, near_1, across_near_1, out_1, across_1, out_near_1)
-        near_2 = lax.ppermute(block_2, "do", NEAR)
-        two_all, near_2, across_2 = fence(two_all, near_2, across_2)
-        across_near_2, out_2 = line_far(near_2, across_2)
-    two_all, wout = fence(two_all, wout)
+    wout_all = lax.all_gather(wout, axes, axis=0, tiled=True)
     first = Loader(plan, first_weights, *ffn_shapes)
-    back_1, act_1, both_1 = ffn_main(first, two_all, grad_all, None)
-    wout_all = lax.all_gather(wout, axes, axis=0, tiled=True)
+    back_1, act_1, both_1, down_1 = ffn_main(first, two_all, grad_all, None)
     if plan.line:
         back_1, act_1, both_1, across_near_2, out_2 = fence(
             back_1, act_1, both_1, across_near_2, out_2
         )
-        out_near_2 = line_last(across_near_2)
-    out_1_part, gain_1, *grads_1 = ffn_weights(first, two_all, grad_all, act_1, both_1, None)
-    if plan.line:
-        back_1, out_1_part, grads_1, out_near_2 = fence(back_1, out_1_part, grads_1, out_near_2)
-        second_weights = (block_2, near_2, across_near_2, out_2, across_2, out_near_2)
-        far_1 = sum_far(grads_1)
+        out_near_2 = line_last(across_near_2, OUTWARD)
+        (last_1,) = ffn_weights(plan, two_all, grad_all, act_1, both_1, 3, 1)
+        last_1, both_1 = fence(last_1, both_1)
+        far_1 = sum_far(last_1, INWARD)
+        (rest_1,) = ffn_weights(plan, two_all, grad_all, act_1, both_1, 0, 3)
+        back_1, rest_1, out_near_2 = fence(back_1, rest_1, out_near_2)
+        second_weights = (block_2, near_2, across_near_2, out_2, across_2, (out_near_2,))
+    else:
+        grads_1 = ffn_weights(plan, two_all, grad_all, act_1, both_1, 0, 4)
     second = Loader(plan, second_weights, *ffn_shapes)
-    back_2, act_2, both_2 = ffn_main(second, two_all, grad_all, back_1)
+    back_2, act_2, both_2, down_2 = ffn_main(second, two_all, grad_all, back_1)
     if plan.line:
         back_2, act_2, both_2, far_1, wout_all = fence(back_2, act_2, both_2, far_1, wout_all)
+        block = plan.block
+        grads_1 = [rest_1[:block], rest_1[block : 2 * block], rest_1[2 * block :], last_1]
         crossed_1, inward_1 = sum_middle(grads_1, far_1)
     back_sum = lax.psum_scatter(back_2, axes, scatter_dimension=0, tiled=True)
-    out_2_part, gain_2, *grads_2 = ffn_weights(second, two_all, grad_all, act_2, both_2, out_1_part)
-    if plan.line:
-        out_2_part, grads_2, crossed_1, inward_1 = fence(out_2_part, grads_2, crossed_1, inward_1)
-        far_2 = sum_far(grads_2)
+    grads_2 = ffn_weights(plan, two_all, grad_all, act_2, both_2, 0, 4)
+    if plan.line:
+        grads_2, act_2, crossed_1, inward_1 = fence(grads_2, act_2, crossed_1, inward_1)
+        (grads_2,) = grads_2
+        grads_2 = [grads_2[k * block : (k + 1) * block] for k in range(4)]
+        far_2 = sum_far(grads_2[3])
+    out_part, gain_two_part = ffn_out(act_1, act_2, down_1, down_2, back_2, two_all)
+    if plan.line:
+        back_sum, out_part, far_2 = fence(back_sum, out_part, far_2)
 
     residual_grad, res_low, ctx_grad = residual_backward(
         back_sum, residual, scale_two, gain_two, grad_low, wout_all
@@ -922,7 +956,7 @@
     ctx_grad = lax.all_to_all(ctx_grad, axes, split_axis=1, concat_axis=0, tiled=True)
 
     out_shape = (rows // own_rows // 2, 2, own_rows, width)
-    parts = out_2_part.reshape(out_shape)
+    parts = out_part.reshape(out_shape)
     mine, theirs = pick(core, parts[:, 0], parts[:, 1]), pick(core, parts[:, 1], parts[:, 0])
     summed = add(mine, plane.swap_core(theirs)).astype(LOW)
     step = plane.first_step()
@@ -930,64 +964,60 @@
     goes_on, stays = plane.at(summed, 3 - step), plane.at(summed, 0)
 
     if plan.line:
-        far_2, grads_1, _ = fence(far_2, grads_1, res_low)
         crossed_2, inward_2 = sum_middle(grads_2, far_2)
-        first_1, third_1 = sum_near_parts(grads_1, crossed_1, inward_1)
-        ctx_grad, res_low, stays, goes, goes_on, first_1, third_1 = fence(
-            ctx_grad, res_low, stays, goes, goes_on, first_1, third_1
-        )
-        near_sum_1, across_sum_1 = sum_near_send(first_1, third_1)
+        near_sum_1, across_sum_1 = sum_near_send(*sum_near_parts(grads_1, crossed_1, inward_1))
+        ctx_grad, res_low, goes, goes_on, stays, near_sum_1, across_sum_1 = fence(
+            ctx_grad, res_low, goes, goes_on, stays, near_sum_1, across_sum_1
+        )
     arrives = plane.swap_first(goes)
     res_all = lax.all_gather(res_low, axes, axis=0, tiled=True)
     back_one_part, gain_one_part, *grads_qkv = attn_backward(
         attn_loader, ctx_grad, normed_all, queries, both, lse, cosine, sine, seg_col, seg_row
     )
     if plan.line:
-        back_one_part, grads_qkv, gain_one_part, crossed_2, inward_2, res_all = fence(
-            back_one_part, grads_qkv, gain_one_part, crossed_2, inward_2, res_all
-        )
-        near_sum_1, across_sum_1, _ = fence(near_sum_1, across_sum_1, back_one_part)
-        total_1 = sum_own(grads_1, near_sum_1, across_sum_1)
-        ffn_grad_1 = plan.unpack(total_1, 2 * hidden)
+        gain_parts = jnp.stack([gain_one_part[0] / gain_one, gain_two_part[0] / gain_two])
+        gain_parts = sum_over(plan.reorder(gain_parts), plane_sizes + (("do", sizes["do"]),))
+        back_one_part, grads_qkv, res_all, crossed_2, inward_2, gain_parts, arrives = fence(
+            back_one_part, grads_qkv, res_all, crossed_2, inward_2, gain_parts, arrives
+        )
+    else:
+        gain_parts = jnp.stack([gain_one_part[0] / gain_one, gain_two_part[0] / gain_two])
+        gain_parts = sum_over(gain_parts, plane_sizes)
     back_one = lax.psum_scatter(back_one_part, axes, scatter_dimension=0, tiled=True)
-    grads_out = out_weights(plan, ctx, res_all)
-    if plan.line:
+    grads_attn = out_weights(plan, ctx, res_all, grads_qkv)
+    if plan.line:
+
+        def trade(total):
+            return plan.trade(total[:half], total[half:])
+
         near_sum_2, across_sum_2 = sum_near_send(*sum_near_parts(grads_2, crossed_2, inward_2))
-        near_sum_2, across_sum_2, grads_qkv, grads_out, arrives, ffn_grad_1 = fence(
-            near_sum_2, across_sum_2, grads_qkv, grads_out, arrives, ffn_grad_1
-        )
-        direct_qkv, direct_out = send_direct(grads_qkv), send_direct(grads_out)
-        total_2 = sum_own(grads_2, near_sum_2, across_sum_2)
-        ffn_grad_2 = plan.unpack(total_2, 2 * hidden)
+        ffn_pair_1 = trade(sum_own(grads_1, near_sum_1, across_sum_1))
+        near_sum_2, across_sum_2, grads_attn = fence(near_sum_2, across_sum_2, grads_attn)
+        direct = send_direct(grads_attn)
+        ffn_pair_2 = trade(sum_own(grads_2, near_sum_2, across_sum_2))
     summed = add(stays, arrives[0])
     arrives = plane.swap_second(add(goes_on, arrives[1]).astype(LOW))
     if plan.line:
-        ffn_grad_2, direct_qkv, direct_out, arrives, gain_one_part = fence(
-            ffn_grad_2, direct_qkv, direct_out, arrives, gain_one_part
-        )
-        half = plan.rows
-        total = add(grads_qkv[0], *direct_qkv)
-        qkv_pair = plan.trade(total[:half], total[half:])
-        total = add(grads_out[0], *direct_out)
-        out_pair = plan.trade(total[:, :half], total[:, half:])
-        ffn_grads = [ffn_grad_1, ffn_grad_2]
+        direct, ffn_pair_1, ffn_pair_2, arrives, back_one, gain_parts = fence(
+            direct, ffn_pair_1, ffn_pair_2, arrives, back_one, gain_parts
+        )
+        attn_pair = trade(add(grads_attn[0], *direct))
+        gain_sums = gain_parts
+        qkv_pair, out_pair = plan.unpack(attn_pair, attn_shapes[0][1])
+        ffn_grads = [plan.unpack(pair, 2 * hidden) for pair in (ffn_pair_1, ffn_pair_2)]
     else:
         qkv_pair = plan.plain_sum_row(grads_qkv[0])
-        out_pair = plan.plain_sum_col(grads_out[0])
+        out_pair = plan.plain_sum_col(grads_attn[0])
         ffn_grads = [
             (plan.plain_sum_row(row), plan.plain_sum_col(col)) for row, col in (grads_1, grads_2)
         ]
-    gain_parts = jnp.stack(
-        [gain_one_part[:, 0] / gain_one, (gain_1[:, 0] + gain_2[:, 0]) / gain_two]
-    )
-    gain_sums = sum_everywhere(plan.reorder(gain_parts), list(sizes.items())[::-1])
-    out_value = (residual + add(summed, arrives)).astype(LOW)
+        gain_sums = sum_over(gain_parts, (("do", sizes["do"]),))
     in_grad = residual_grad + norm_back(back_one.astype(F32), inputs_f, scale_one, gain_one)
-
+    out_value = residual + add(summed, arrives)
     grad_gain_attn, grad_gain_ffn = gain_sums[0], gain_sums[1]
 
     def join(pair, axis):
-        own, other = pair
+        own, other = pair[0], pair[1].astype(F32)
         return by_x(cat([own, other], axis), cat([other, own], axis))
 
     def from_chunks(pairs, axis):
@@ -1022,7 +1052,7 @@
         adamw_update(gain_ffn, grad_gain_ffn, m_gain_ffn, v_gain_ffn, 0.0, GAIN_RATE),
     ]
     return (
-        plan.reorder(out_value),
+        plan.reorder(out_value.astype(LOW)),
         plan.reorder(in_grad),
         *grads,
         *[u[0] for u in updated],

time: 741 us -> 711 us (0.960)
  starting transfers between devices: 82.1 us -> 71.5 us
  waiting for transfers between devices: 285 us -> 276 us
    ppermute x10 -> x11, waiting for transfers between devices: 48.7 us -> 86 us  [the longest x4 63.4 us: line_last(): return lax.ppermute(across_near, 'do', perm)]
    ppermute x1, waiting for transfers between devices: 33.5 us -> 0.01 us  [on_device(): near_2 = lax.ppermute(block_2, 'do', NEAR)]
    ppermute x4, waiting for transfers between devices: 11.9 us -> 32.7 us  [sum_near_send(): return (lax.ppermute(first, 'do', NEAR), lax.ppermute(third, 'do', MIDDLE))]
    ppermute x6 -> x3, waiting for transfers between devices: 53.8 us -> 33 us  [send_direct(): lax.ppermute(part, 'do', perm)]
    all_gather x1, waiting for transfers between devices: 24.9 us -> 4.96 us  [on_device(): res_all = lax.all_gather(res_low, axes, axis=0, tiled=True)]
    ppermute x2, waiting for transfers between devices: 0.01 us -> 19.6 us  [swap_second(): return lax.ppermute(value, self.axes, self.pairs(False))]
    ppermute x4 -> x3, waiting for transfers between devices: 14.9 us -> 0.01 us  [trade(): theirs = lax.ppermute(self.by_x(high, low).astype(LOW), 'di', PAIR)]
    ppermute x2, waiting for transfers between devices: 12.8 us -> 0.01 us  [swap_core(): return lax.ppermute(value, 'tp', [(i, i ^ 1) for i in range(self.tp)])]
  transfers between devices with their start and end apart: 59 -> 56, of which waited for: 35 -> 38; matrix products, arithmetic and copies ran while one was open for 16% -> 16% of each run, Pallas kernels for 26% -> 27%
where the time goes in v5:
time: 711 us; the launch traced here: 700 us
  waiting for transfers between devices  276 us (39%)
  Pallas kernels  191 us (27%)
  other arithmetic  110 us (15%)
  starting transfers between devices  71.5 us (10%)
  local copies, waits for them, and re-layouts  35.1 us (5%)
  between operations  16.4 us (2%)
    ppermute x4, waiting for transfers between devices, line_last(): return lax.ppermute(across_near, 'do', perm)  63.4 us
    pallas_call x2, Pallas kernels, ffn_main(): pl.pallas_call(functools.partial(ffn_main_kernel, loader, len(more)), gri...  62 us
    pallas_call x3, Pallas kernels, ffn_weights(): pl.pallas_call(functools.partial(ffn_weights_kernel, plan), grid=(count,)...  44.3 us
    pallas_call x1, Pallas kernels, attn_backward(): pl.pallas_call(functools.partial(attn_backward_kernel, heads // 128, load...  33.4 us
    ppermute x3, waiting for transfers between devices, send_direct(): lax.ppermute(part, 'do', perm)  33 us
    ppermute x4, waiting for transfers between devices, sum_near_send(): return (lax.ppermute(first, 'do', NEAR), lax.ppermute(third, 'do', MIDDLE))  32.7 us
    ppermute x3, waiting for transfers between devices, swap_first(): return lax.ppermute(value, self.axes, self.pairs(True))  27.3 us
    pallas_call x1, Pallas kernels, attn_forward(): pl.pallas_call(functools.partial(attn_forward_kernel, heads // 128, loade...  23.1 us
  transfers between devices with their start and end apart: 56, of which 38 were waited for; matrix products, arithmetic and copies ran while one was open for 16% of the time, Pallas kernels for 27%

profile of v5, /device:TPU:9, one launch (start us, length us, event | category | flops | bytes accessed | tf_op | source)
XLA Modules:
  0.0 700.2 jit_solution(3981049932553020673)
XLA Ops:
  21.8 4.2 collective-permute-start.3
  26.1 3.7 fusion.17
  36.2 3.0 collective-permute-done.3.refs_5_
  39.3 3.1 collective-permute-start.4
  42.9 10.6 %collective-permute-done.6 = bf16[256,1536]{1,0:T(8,128)(2,1)S(1)} collective-permute-done((bf16[256,1536]{1,0:T(8,128)(2,1)S(1)}, bf16[256,1536]{1,0:T(8,128)(2,1)S(1)}, u32[]{:S(2)}, u32[]{:S(2)}) %collective-permute-start.6) | collective-permute-done | bytes 786464 | tf_op jit(solution)/shard_map/ppermute | solution.py:139
  57.6 11.4 %collective-permute-done.7.refs_6_ = bf16[512,640]{1,0:T(8,128)(2,1)S(1)} collective-permute-done((bf16[512,640]{1,0:T(8,128)(2,1)S(1)}, bf16[512,640]{1,0:T(8,128)(2,1)S(1)}, u32[]{:S(2)}, u32[]{:S(2)}) %collective-permute-start.7) | collective-permute-done | bytes 655392 | tf_op jit(solution)/shard_map/ppermute | solution.py:61
  69.0 7.1 %all-gather.5.cloned.1.call-done.refs_7_.refs_8_ = bf16[2048,2048]{1,0:T(8,128)(2,1)} async-done(((bf16[256,2048]{1,0:T(8,128)(2,1)}), bf16[2048,2048]{1,0:T(8,128)(2,1)}) %all-gather.5.cloned.1.call-update) | async-done | bytes 8388624 | tf_op jit(solution)/shard_map/all_gather | solution.py:798
  76.4 4.3 collective-permute-start.9
  83.5 23.1 %attn_forward.1 = (bf16[2048,2048]{1,0:T(8,128)(2,1)}, bf16[2048,256]{1,0:T(8,128)(2,1)}, bf16[2048,256]{1,0:T(8,128)(2,1)}, bf16[2048,128]{1,0:T(8,128)(2,1)}, ...) custom-call(s32[1]{0:T(128)} %bitcast.refs_0_, bf16[512,640]{1,0:T(8,128)(2,1)} %copy-done.16, ...), custom_call_target="tpu_custom_call" | custom-call | flops 1 | bytes 1 | tf_op jit(solution)/shard_map/attn_forward/pallas_call | solution.py:411
  106.6 5.0 collective-permute-done.11
  112.2 2.8 collective-permute-done.9.refs_5_
  115.1 3.0 collective-permute-start.12
  119.8 12.8 %collective-permute-done.14 = bf16[256,2048]{1,0:T(8,128)(2,1)S(1)} collective-permute-done((bf16[256,2048]{1,0:T(8,128)(2,1)}, bf16[256,2048]{1,0:T(8,128)(2,1)S(1)}, u32[]{:S(2)}, u32[]{:S(2)}) %collective-permute-start.14) | collective-permute-done | bytes 1048608 | tf_op jit(solution)/shard_map/ppermute | solution.py:764
  132.5 14.5 %collective-permute-done.15 = bf16[256,2048]{1,0:T(8,128)(2,1)} collective-permute-done((bf16[256,2048]{1,0:T(8,128)(2,1)S(1)}, bf16[256,2048]{1,0:T(8,128)(2,1)}, u32[]{:S(2)}, u32[]{:S(2)}) %collective-permute-start.15) | collective-permute-done | bytes 1048608 | tf_op jit(solution)/shard_map/ppermute | solution.py:764
  147.0 5.1 collective-permute-done.12.refs_3_
  156.8 2.9 collective-permute-start.16
  167.1 3.6 broadcast_select_fusion.1
  170.7 6.4 pad_maximum_fusion
  177.1 8.3 %copy.80 = bf16[4,2,256,2048]{3,2,1,0:T(8,128)(2,1)} copy(bf16[4,2,256,2048]{3,2,0,1:T(8,128)(2,1)} %pad_maximum_fusion) | data formatting | bytes 16777216 | tf_op jit(solution)/shard_map/concatenate | solution.py:45
  185.4 13.1 %collective-permute-done.18.refs_5_ = bf16[512,1536]{1,0:T(8,128)(2,1)} collective-permute-done((bf16[512,1536]{1,0:T(8,128)(2,1)}, bf16[512,1536]{1,0:T(8,128)(2,1)}, u32[]{:S(2)}, u32[]{:S(2)}) %collective-permute-start.18) | collective-permute-done | bytes 1572896 | tf_op jit(solution)/shard_map/ppermute | solution.py:891
  205.3 48.8 %collective-permute-done.20.refs_7_ = bf16[256,1536]{1,0:T(8,128)(2,1)S(1)} collective-permute-done((bf16[256,1536]{1,0:T(8,128)(2,1)S(1)}, bf16[256,1536]{1,0:T(8,128)(2,1)S(1)}, u32[]{:S(2)}, u32[]{:S(2)}) %collective-permute-start.20) | collective-permute-done | bytes 786464 | tf_op jit(solution)/shard_map/ppermute | solution.py:61
  254.2 2.4 collective-permute-start.21
  256.7 30.3 %ffn_main.2 = (bf16[2048,2048]{1,0:T(8,128)(2,1)}, bf16[2048,512]{1,0:T(8,128)(2,1)}, bf16[2048,1024]{1,0:T(8,128)(2,1)}, bf16[512,2048]{1,0:T(8,128)(2,1)}) custom-call(s32[1]{0:T(128)} %bitcast.refs_0_, bf16[512,1536]{1,0:T(8,128)(2,1)} %pad_maximum_fusion.5.refs_1_, bf16[512,1536]{1,0:T(8,128)(2,1)} %collective-permute-done.8.refs_2_, ...), custom_call_target="tpu_custom_call" | custom-call | flops 1 | bytes 1 | tf_op jit(solution)/shard_map/ffn_main/pallas_call | solution.py:599
  287.1 2.9 collective-permute-done.21.refs_3_
  290.2 3.4 collective-permute-start.23
  293.6 8.8 %ffn_weights.3 = bf16[512,1536]{1,0:T(8,128)(2,1)} custom-call(bf16[2048,2048]{1,0:T(8,128)(2,1)} %all-gather.7.cloned.1.call-done.refs_8_.x_ref.refs_7_, bf16[2048,2048]{1,0:T(8,128)(2,1)} %bitcast.55, bf16[2048,512]{1,0:T(8,128)(2,1)} %get-tuple-element.211.act_ref.act_1, bf16[2048,1024]{1,0:T(8,128)(2,1)} %get-tuple-element.213.both_ref), custom_call_target="tpu_custom_call" | custom-call | flops 1 | bytes 1 | tf_op jit(solution)/shard_map/ffn_weights/pallas_call | solution.py:662
  304.2 15.8 %ffn_weights.4 = bf16[1536,1536]{1,0:T(8,128)(2,1)} custom-call(bf16[2048,2048]{1,0:T(8,128)(2,1)} %all-gather.7.cloned.1.call-done.refs_8_.x_ref.refs_7_, bf16[2048,2048]{1,0:T(8,128)(2,1)} %bitcast.56, bf16[2048,512]{1,0:T(8,128)(2,1)} %get-tuple-element.211.act_ref.act_1, bf16[2048,1024]{1,0:T(8,128)(2,1)} %get-tuple-element.213.both_ref), custom_call_target="tpu_custom_call" | custom-call | flops 1 | bytes 1 | tf_op jit(solution)/shard_map/ffn_weights/pallas_call | solution.py:662
  319.9 3.2 collective-permute-done.23.refs_6_
  323.1 31.6 %ffn_main.3 = (bf16[2048,2048]{1,0:T(8,128)(2,1)}, bf16[2048,512]{1,0:T(8,128)(2,1)}, bf16[2048,1024]{1,0:T(8,128)(2,1)}, bf16[512,2048]{1,0:T(8,128)(2,1)}) custom-call(s32[1]{0:T(128)} %bitcast.refs_0_, bf16[512,1536]{1,0:T(8,128)(2,1)} %pad_maximum_fusion.6.refs_1_, bf16[512,1536]{1,0:T(8,128)(2,1)} %collective-permute-done.19.refs_2_, ...), custom_call_target="tpu_custom_call" | custom-call | flops 1 | bytes 1 | tf_op jit(solution)/shard_map/ffn_main/pallas_call | solution.py:599
  354.8 3.5 add_convert_fusion.5
  358.3 3.3 collective-permute-start.25
  362.0 19.7 %ffn_weights.5 = bf16[2048,1536]{1,0:T(8,128)(2,1)} custom-call(bf16[2048,2048]{1,0:T(8,128)(2,1)} %all-gather.7.cloned.1.call-done.refs_8_.x_ref.refs_7_, bf16[2048,2048]{1,0:T(8,128)(2,1)} %bitcast.58, bf16[2048,512]{1,0:T(8,128)(2,1)} %get-tuple-element.226.act_ref.act_2, bf16[2048,1024]{1,0:T(8,128)(2,1)} %get-tuple-element.223.both_ref), custom_call_target="tpu_custom_call" | custom-call | flops 1 | bytes 1 | tf_op jit(solution)/shard_map/ffn_weights/pallas_call | solution.py:662
  381.7 10.5 %collective-permute-done.25 = bf16[512,1536]{1,0:T(8,128)(2,1)} collective-permute-done((bf16[512,1536]{1,0:T(8,128)(2,1)}, bf16[512,1536]{1,0:T(8,128)(2,1)}, u32[]{:S(2)}, u32[]{:S(2)}) %collective-permute-start.25) | collective-permute-done | bytes 1572896 | tf_op jit(solution)/shard_map/ppermute | solution.py:86
  393.4 2.7 slice.464
  396.7 16.3 %ffn_out.1 = (bf16[2048,2048]{1,0:T(8,128)(2,1)}, f32[1,2048]{1,0:T(1,128)}) custom-call(bf16[2048,512]{1,0:T(8,128)(2,1)} %get-tuple-element.211.act_ref.act_1, bf16[2048,512]{1,0:T(8,128)(2,1)} %get-tuple-element.226.act_ref.act_2, bf16[512,2048]{1,0:T(8,128)(2,1)} %get-tuple-element.227.down_1, bf16[512,2048]{1,0:T(8,128)(2,1)} %get-tuple-element.228.down_2, ...), custom_call_target="tpu_custom_call" | custom-call | flops 1 | bytes 1 | tf_op jit(solution)/shard_map/ffn_out/pallas_call | solution.py:688
  412.9 14.1 %collective-permute-done.27 = bf16[512,1536]{1,0:T(8,128)(2,1)} collective-permute-done((bf16[512,1536]{1,0:T(8,128)(2,1)}, bf16[512,1536]{1,0:T(8,128)(2,1)}, u32[]{:S(2)}, u32[]{:S(2)}) %collective-permute-start.27) | collective-permute-done | bytes 1572896 | tf_op jit(solution)/shard_map/ppermute | solution.py:81
  427.0 3.7 reduce-scatter.6.cloned.1.call-done.back_ref
  430.7 5.1 select_bitcast_fusion
  435.8 2.6 collective-permute-start.28
  438.4 3.0 add_convert_fusion.3
  443.8 3.5 add_convert_fusion.4
  448.1 8.9 %residual_backward.1 = (f32[256,2048]{1,0:T(8,128)}, bf16[256,2048]{1,0:T(8,128)(2,1)}, bf16[256,2048]{1,0:T(8,128)(2,1)}) custom-call(bf16[256,2048]{1,0:T(8,128)(2,1)} %reduce-scatter.6.cloned.1.call-done.back_ref, f32[256,2048]{1,0:T(8,128)} %get-tuple-element.344.residual_ref, f32[256,1]{1,0:T(8,128)} %copy.81.scale_ref, f32[1,2048]{1,0:T(1,128)} %bitcast.68, ...), custom_call_target="tpu_custom_call" | custom-call | flops 1 | bytes 1 | tf_op jit(solution)/shard_map/residual_backward/pallas_call | solution.py:540
  459.2 4.4 all-to-all-start
  463.6 5.9 fusion
  473.0 6.7 collective-permute-done.30
  479.7 3.7 collective-permute-done.29
  484.7 3.5 add_convert_fusion.2
  488.2 3.1 collective-permute-start.31
  491.4 33.4 %attn_backward.1 = (bf16[2048,2048]{1,0:T(8,128)(2,1)}, f32[1,2048]{1,0:T(1,128)}, bf16[512,384]{1,0:T(8,128)(2,1)}, bf16[512,384]{1,0:T(8,128)(2,1)}, bf16[512,...) custom-call(s32[1]{0:T(128)} %bitcast.refs_0_, bf16[512,640]{1,0:T(8,128)(2,1)} %copy-done.16, bf16[512,640]{1,0:T(8,128)(2,1)} %copy-done.25, ...), custom_call_target="tpu_custom_call" | custom-call | flops 1 | bytes 1 | tf_op jit(solution)/shard_map/attn_backward/pallas_call | solution.py:450
  541.3 5.0 all-gather.11.cloned.1.call-done.res_ref
  546.3 3.9 add_convert_fusion
  550.3 3.4 collective-permute-start.40
  553.8 3.4 convert_add_fusion.3
  558.6 3.2 fusion.11
  562.6 3.4 out_weights.1
  565.9 20.2 %collective-permute-done.39 = bf16[512,1536]{1,0:T(8,128)(2,1)S(1)} collective-permute-done((bf16[512,1536]{1,0:T(8,128)(2,1)S(1)}, bf16[512,1536]{1,0:T(8,128)(2,1)S(1)}, u32[]{:S(2)}, u32[]{:S(2)}) %collective-permute-start.39) | collective-permute-done | bytes 1572896 | tf_op jit(solution)/shard_map/ppermute | solution.py:94
  588.3 2.5 convert_add_fusion.2
  591.2 2.4 collective-permute-start.42
  596.5 19.6 %collective-permute-done.46 = bf16[256,2048]{1,0:T(8,128)(2,1)} collective-permute-done((bf16[256,2048]{1,0:T(8,128)(2,1)}, bf16[256,2048]{1,0:T(8,128)(2,1)}, u32[]{:S(2)}, u32[]{:S(2)}) %collective-permute-start.46) | collective-permute-done | bytes 1048608 | tf_op jit(solution)/shard_map/ppermute | solution.py:767
  617.0 4.0 collective-permute-done.42
  621.1 28.1 %collective-permute-done.43 = bf16[512,640]{1,0:T(8,128)(2,1)S(1)} collective-permute-done((bf16[512,640]{1,0:T(8,128)(2,1)S(1)}, bf16[512,640]{1,0:T(8,128)(2,1)S(1)}, u32[]{:S(2)}, u32[]{:S(2)}) %collective-permute-start.43) | collective-permute-done | bytes 655392 | tf_op jit(solution)/shard_map/ppermute | solution.py:103
  660.4 3.4 fusion.9
  669.5 4.1 multiply_subtract_fusion
  673.6 11.5 %multiply_subtract_fusion.1 = (f32[256,2048]{1,0:T(8,128)}, f32[256,2048]{1,0:T(8,128)}, f32[256,2048]{1,0:T(8,128)}, f32[256,2048]{1,0:T(8,128)}, f32[256,2048]...) fusion(f32[256,2048]{1,0:T(8,128)S(1)} %copy-done.8, f32[256,2048]{1,0:T(8,128)} %param.47, ...), kind=kLoop, calls=%fused_computation.50 | loop fusion | flops 20971520 | bytes 33554432 | tf_op jit(solution)/shard_map/sub | solution.py:727
  (364 shorter events, 113.1 us)
Async XLA Ops:
  7.2 68.9 %all-gather.5.cloned.1.call-start = ((), (), s32[]{:S(2)}) async-start(), calls=%async_computation.4 | async-start | bytes 9437184 | tf_op jit(solution)/shard_map/all_gather | solution.py:798
  11.7 186.8 %reduce-scatter.4.cloned.1.call-start = ((), (), s32[]{:S(2)}) async-start(), calls=%async_computation.5 | async-start | bytes 9437184 | tf_op jit(solution)/shard_map/reduce_scatter | solution.py:882
  12.3 8.9 %collective-permute-start = (bf16[256,640]{1,0:T(8,128)(2,1)S(1)}, bf16[256,640]{1,0:T(8,128)(2,1)S(1)}, u32[]{:S(2)}, u32[]{:S(2)}) collective-permute-start(bf16[256,640]{1,0:T(8,128)(2,1)S(1)} %pad_maximum_fusion.16), channel_id=1, source_target_pairs={{0,4},{4,0},{1,5},{5,1},{2,6},{6,2},{3,7},{7,3},{8,12},{12,8},{9,1... | collective-permute-start | bytes 983048 | tf_op jit(solution)/shard_map/ppermute | solution.py:139
  13.6 7.5 %collective-permute-start.1 = (s32[2,1024]{1,0:T(2,128)S(1)}, s32[2,1024]{1,0:T(2,128)S(1)}, u32[]{:S(2)}, u32[]{:S(2)}) collective-permute-start(s32[2,1024]{1,0:T(2,128)S(1)} %pad_add_fusion.1), channel_id=1, source_target_pairs={{0,4},{4,0},{1,5},{5,1},{2,6},{6,2},{3,7},{7,3},{8,12},{12,8},{9,1... | collective-permute-start | bytes 24584 | tf_op jit(solution)/shard_map/ppermute | solution.py:801
  21.2 61.0 %copy-start.55 = (s32[1,2048]{1,0:T(1,128)}, s32[1,2048]{1,0:T(1,128)S(1)}, u32[]{:S(2)}) copy-start(s32[1,2048]{1,0:T(1,128)S(1)} %get-tuple-element.440) | copy-start | bytes 24580
  21.5 14.7 %collective-permute-start.2 = (bf16[512,640]{1,0:T(8,128)(2,1)S(1)}, bf16[512,640]{1,0:T(8,128)(2,1)S(1)}, u32[]{:S(2)}, u32[]{:S(2)}) collective-permute-start(bf16[512,640]{1,0:T(8,128)(2,1)S(1)} %pad_maximum_fusion.13.refs_1_), channel_id=1, source_target_pairs={{0,8},{8,0},{16,24},{24,16},{1,9},{9,1},{17,25},{25,17},{2,10},{10... | collective-permute-start | bytes 1966088 | tf_op jit(solution)/shard_map/ppermute | solution.py:53
  21.8 17.5 %collective-permute-start.3 = (bf16[512,640]{1,0:T(8,128)(2,1)S(1)}, bf16[512,640]{1,0:T(8,128)(2,1)S(1)}, u32[]{:S(2)}, u32[]{:S(2)}) collective-permute-start(bf16[512,640]{1,0:T(8,128)(2,1)S(1)} %pad_maximum_fusion.13.refs_1_), channel_id=1, source_target_pairs={{8,16},{16,8},{9,17},{17,9},{10,18},{18,10},{11,19},{19,11},{12,20... | collective-permute-start | bytes 1966088 | tf_op jit(solution)/shard_map/ppermute | solution.py:53
  31.6 21.8 %collective-permute-start.6 = (bf16[256,1536]{1,0:T(8,128)(2,1)S(1)}, bf16[256,1536]{1,0:T(8,128)(2,1)S(1)}, u32[]{:S(2)}, u32[]{:S(2)}) collective-permute-start(bf16[256,1536]{1,0:T(8,128)(2,1)S(1)} %pad_maximum_fusion.10), channel_id=1, source_target_pairs={{0,4},{4,0},{1,5},{5,1},{2,6},{6,2},{3,7},{7,3},{8,12},{12,8},{9,1... | collective-permute-start | bytes 2359304 | tf_op jit(solution)/shard_map/ppermute | solution.py:139
  39.3 15.7 %collective-permute-start.4 = (bf16[512,640]{1,0:T(8,128)(2,1)S(1)}, bf16[512,640]{1,0:T(8,128)(2,1)S(1)}, u32[]{:S(2)}, u32[]{:S(2)}) collective-permute-start(bf16[512,640]{1,0:T(8,128)(2,1)S(1)} %collective-permute-done.2.refs_2_), channel_id=1, source_target_pairs={{8,16},{16,8},{9,17},{17,9},{10,18},{18,10},{11,19},{19,11},{12,20... | collective-permute-start | bytes 1966088 | tf_op jit(solution)/shard_map/ppermute | solution.py:57
  42.3 13.4 %collective-permute-start.5 = (bf16[512,640]{1,0:T(8,128)(2,1)S(1)}, bf16[512,640]{1,0:T(8,128)(2,1)S(1)}, u32[]{:S(2)}, u32[]{:S(2)}) collective-permute-start(bf16[512,640]{1,0:T(8,128)(2,1)S(1)} %collective-permute-done.3.refs_5_), channel_id=1, source_target_pairs={{0,8},{8,0},{16,24},{24,16},{1,9},{9,1},{17,25},{25,17},{2,10},{10... | collective-permute-start | bytes 1966088 | tf_op jit(solution)/shard_map/ppermute | solution.py:57
  42.9 109.8 %copy-start.6 = (bf16[256,2048]{1,0:T(8,128)(2,1)}, bf16[256,2048]{1,0:T(8,128)(2,1)S(1)}, u32[]{:S(2)}) copy-start(bf16[256,2048]{1,0:T(8,128)(2,1)S(1)} %maximum_select_fusion.7.grad_ref) | copy-start | bytes 3145732
  55.7 13.3 %collective-permute-start.7 = (bf16[512,640]{1,0:T(8,128)(2,1)S(1)}, bf16[512,640]{1,0:T(8,128)(2,1)S(1)}, u32[]{:S(2)}, u32[]{:S(2)}) collective-permute-start(bf16[512,640]{1,0:T(8,128)(2,1)S(1)} %collective-permute-done.4.refs_3_), channel_id=1, source_target_pairs={{0,8},{8,0},{16,24},{24,16},{1,9},{9,1},{17,25},{25,17},{2,10},{10... | collective-permute-start | bytes 1966088 | tf_op jit(solution)/shard_map/ppermute | solution.py:61
  76.1 36.0 %collective-permute-start.8 = (bf16[512,1536]{1,0:T(8,128)(2,1)}, bf16[512,1536]{1,0:T(8,128)(2,1)}, u32[]{:S(2)}, u32[]{:S(2)}) collective-permute-start(bf16[512,1536]{1,0:T(8,128)(2,1)} %pad_maximum_fusion.5.refs_1_), channel_id=1, source_target_pairs={{0,8},{8,0},{16,24},{24,16},{1,9},{9,1},{17,25},{25,17},{2,10},{10... | collective-permute-start | bytes 4718600 | tf_op jit(solution)/shard_map/ppermute | solution.py:53
  76.4 38.6 %collective-permute-start.9 = (bf16[512,1536]{1,0:T(8,128)(2,1)}, bf16[512,1536]{1,0:T(8,128)(2,1)}, u32[]{:S(2)}, u32[]{:S(2)}) collective-permute-start(bf16[512,1536]{1,0:T(8,128)(2,1)} %pad_maximum_fusion.5.refs_1_), channel_id=1, source_target_pairs={{8,16},{16,8},{9,17},{17,9},{10,18},{18,10},{11,19},{19,11},{12,20... | collective-permute-start | bytes 4718600 | tf_op jit(solution)/shard_map/ppermute | solution.py:53
  80.6 31.0 %collective-permute-start.10 = (bf16[256,2048]{1,0:T(8,128)(2,1)S(1)}, bf16[256,2048]{1,0:T(8,128)(2,1)}, u32[]{:S(2)}, u32[]{:S(2)}) collective-permute-start(bf16[256,2048]{1,0:T(8,128)(2,1)S(1)} %maximum_select_fusion.7.grad_ref), channel_id=1, source_target_pairs={{0,2},{1,5},{2,0},{3,7},{4,6},{5,1},{6,4},{7,3},{8,10},{9,13},{10,... | collective-permute-start | bytes 3145736 | tf_op jit(solution)/shard_map/ppermute | solution.py:767
  81.0 30.6 %collective-permute-start.11 = (bf16[256,1536]{1,0:T(8,128)(2,1)}, bf16[256,1536]{1,0:T(8,128)(2,1)S(1)}, u32[]{:S(2)}, u32[]{:S(2)}) collective-permute-start(bf16[256,1536]{1,0:T(8,128)(2,1)} %pad_maximum_fusion.12), channel_id=1, source_target_pairs={{0,4},{4,0},{1,5},{5,1},{2,6},{6,2},{3,7},{7,3},{8,12},{12,8},{9,1... | collective-permute-start | bytes 2359304 | tf_op jit(solution)/shard_map/ppermute | solution.py:139
  115.0 141.7 %all-gather.7.cloned.1.call-start = ((), (), s32[]{:S(2)}) async-start(), calls=%async_computation.6 | async-start | bytes 9437184 | tf_op jit(solution)/shard_map/all_gather | solution.py:909
  115.1 37.0 %collective-permute-start.12 = (bf16[512,1536]{1,0:T(8,128)(2,1)}, bf16[512,1536]{1,0:T(8,128)(2,1)}, u32[]{:S(2)}, u32[]{:S(2)}) collective-permute-start(bf16[512,1536]{1,0:T(8,128)(2,1)} %collective-permute-done.8.refs_2_), channel_id=1, source_target_pairs={{8,16},{16,8},{9,17},{17,9},{10,18},{18,10},{11,19},{19,11},{12,20... | collective-permute-start | bytes 4718600 | tf_op jit(solution)/shard_map/ppermute | solution.py:57
  118.1 34.6 %collective-permute-start.13 = (bf16[512,1536]{1,0:T(8,128)(2,1)}, bf16[512,1536]{1,0:T(8,128)(2,1)}, u32[]{:S(2)}, u32[]{:S(2)}) collective-permute-start(bf16[512,1536]{1,0:T(8,128)(2,1)} %collective-permute-done.9.refs_5_), channel_id=1, source_target_pairs={{0,8},{8,0},{16,24},{24,16},{1,9},{9,1},{17,25},{25,17},{2,10},{10... | collective-permute-start | bytes 4718600 | tf_op jit(solution)/shard_map/ppermute | solution.py:57
  118.2 14.3 %collective-permute-start.14 = (bf16[256,2048]{1,0:T(8,128)(2,1)}, bf16[256,2048]{1,0:T(8,128)(2,1)S(1)}, u32[]{:S(2)}, u32[]{:S(2)}) collective-permute-start(bf16[256,2048]{1,0:T(8,128)(2,1)} %collective-permute-done.10), channel_id=1, source_target_pairs={{0,4},{1,3},{2,6},{3,1},{4,0},{5,7},{6,2},{7,5},{8,12},{9,11},{10,... | collective-permute-start | bytes 3145736 | tf_op jit(solution)/shard_map/ppermute | solution.py:764
  119.5 27.6 %collective-permute-start.15 = (bf16[256,2048]{1,0:T(8,128)(2,1)S(1)}, bf16[256,2048]{1,0:T(8,128)(2,1)}, u32[]{:S(2)}, u32[]{:S(2)}) collective-permute-start(bf16[256,2048]{1,0:T(8,128)(2,1)S(1)} %maximum_select_fusion.7.grad_ref), channel_id=1, source_target_pairs={{0,4},{1,3},{2,6},{3,1},{4,0},{5,7},{6,2},{7,5},{8,12},{9,11},{10,... | collective-permute-start | bytes 3145736 | tf_op jit(solution)/shard_map/ppermute | solution.py:764
  156.8 10.3 %collective-permute-start.16 = (bf16[1024,2048]{1,0:T(8,128)(2,1)S(1)}, bf16[1024,2048]{1,0:T(8,128)(2,1)S(1)}, u32[]{:S(2)}, u32[]{:S(2)}) collective-permute-start(bf16[1024,2048]{1,0:T(8,128)(2,1)S(1)} %pad_maximum_fusion.1), channel_id=1, source_target_pairs={{0,1},{1,0},{2,3},{3,2},{4,5},{5,4},{6,7},{7,6},{8,9},{9,8},{10,11... | collective-permute-start | bytes 12582920 | tf_op jit(solution)/shard_map/ppermute | solution.py:770
  161.1 37.5 %collective-permute-start.18 = (bf16[512,1536]{1,0:T(8,128)(2,1)}, bf16[512,1536]{1,0:T(8,128)(2,1)}, u32[]{:S(2)}, u32[]{:S(2)}) collective-permute-start(bf16[512,1536]{1,0:T(8,128)(2,1)} %pad_maximum_fusion.6.refs_1_), channel_id=1, source_target_pairs={{8,16},{16,8},{9,17},{17,9},{10,18},{18,10},{11,19},{19,11},{12,20... | collective-permute-start | bytes 4718600 | tf_op jit(solution)/shard_map/ppermute | solution.py:891
  163.2 37.1 %copy-start.60 = (f32[2048]{0:T(1024)}, f32[2048]{0:T(1024)S(1)}, u32[]{:S(2)}) copy-start(f32[2048]{0:T(1024)S(1)} %maximum_select_fusion.18) | copy-start | bytes 24580
  165.3 20.1 %collective-permute-start.17 = (bf16[256,1536]{1,0:T(8,128)(2,1)}, bf16[256,1536]{1,0:T(8,128)(2,1)S(1)}, u32[]{:S(2)}, u32[]{:S(2)}) collective-permute-start(bf16[256,1536]{1,0:T(8,128)(2,1)} %slice.455), channel_id=1, source_target_pairs={{0,8},{8,0},{16,24},{24,16},{1,9},{9,1},{17,25},{25,17},{2,10},{10... | collective-permute-start | bytes 2359304 | tf_op jit(solution)/shard_map/ppermute | solution.py:61
  185.4 17.0 %copy-start.37 = (bf16[256,1536]{1,0:T(8,128)(2,1)}, bf16[256,1536]{1,0:T(8,128)(2,1)S(1)}, u32[]{:S(2)}) copy-start(bf16[256,1536]{1,0:T(8,128)(2,1)S(1)} %collective-permute-done.17.refs_6_) | copy-start | bytes 2359300
  202.5 152.3 %all-gather.9.cloned.1.call-start = ((), (), s32[]{:S(2)}) async-start(), calls=%async_computation.7 | async-start | bytes 9437184 | tf_op jit(solution)/shard_map/all_gather | solution.py:919
  202.5 51.6 %collective-permute-start.19 = (bf16[512,1536]{1,0:T(8,128)(2,1)}, bf16[512,1536]{1,0:T(8,128)(2,1)}, u32[]{:S(2)}, u32[]{:S(2)}) collective-permute-start(bf16[512,1536]{1,0:T(8,128)(2,1)} %pad_maximum_fusion.6.refs_1_), channel_id=1, source_target_pairs={{0,8},{8,0},{16,24},{24,16},{1,9},{9,1},{17,25},{25,17},{2,10},{10... | collective-permute-start | bytes 4718600 | tf_op jit(solution)/shard_map/ppermute | solution.py:914
  203.8 50.3 %collective-permute-start.20 = (bf16[256,1536]{1,0:T(8,128)(2,1)S(1)}, bf16[256,1536]{1,0:T(8,128)(2,1)S(1)}, u32[]{:S(2)}, u32[]{:S(2)}) collective-permute-start(bf16[256,1536]{1,0:T(8,128)(2,1)S(1)} %slice.462), channel_id=1, source_target_pairs={{0,8},{8,0},{16,24},{24,16},{1,9},{9,1},{17,25},{25,17},{2,10},{10... | collective-permute-start | bytes 2359304 | tf_op jit(solution)/shard_map/ppermute | solution.py:61
  254.1 176.6 %reduce-scatter.6.cloned.1.call-start = ((), (), s32[]{:S(2)}) async-start(), calls=%async_computation.8 | async-start | bytes 9437184 | tf_op jit(solution)/shard_map/reduce_scatter | solution.py:942
  254.2 35.7 %collective-permute-start.21 = (bf16[512,1536]{1,0:T(8,128)(2,1)}, bf16[512,1536]{1,0:T(8,128)(2,1)}, u32[]{:S(2)}, u32[]{:S(2)}) collective-permute-start(bf16[512,1536]{1,0:T(8,128)(2,1)} %collective-permute-done.19.refs_2_), channel_id=1, source_target_pairs={{8,16},{16,8},{9,17},{17,9},{10,18},{18,10},{11,19},{19,11},{12,20... | collective-permute-start | bytes 4718600 | tf_op jit(solution)/shard_map/ppermute | solution.py:57
  256.6 33.6 %collective-permute-start.22 = (bf16[512,1536]{1,0:T(8,128)(2,1)}, bf16[512,1536]{1,0:T(8,128)(2,1)}, u32[]{:S(2)}, u32[]{:S(2)}) collective-permute-start(bf16[512,1536]{1,0:T(8,128)(2,1)} %collective-permute-done.18.refs_5_), channel_id=1, source_target_pairs={{0,8},{8,0},{16,24},{24,16},{1,9},{9,1},{17,25},{25,17},{2,10},{10... | collective-permute-start | bytes 4718600 | tf_op jit(solution)/shard_map/ppermute | solution.py:57
  290.2 32.9 %collective-permute-start.23 = (bf16[512,1536]{1,0:T(8,128)(2,1)}, bf16[512,1536]{1,0:T(8,128)(2,1)}, u32[]{:S(2)}, u32[]{:S(2)}) collective-permute-start(bf16[512,1536]{1,0:T(8,128)(2,1)} %collective-permute-done.21.refs_3_), channel_id=1, source_target_pairs={{8,0},{16,24},{9,1},{17,25},{10,2},{18,26},{11,3},{19,27},{12,4},{... | collective-permute-start | bytes 4718600 | tf_op jit(solution)/shard_map/ppermute | solution.py:61
  302.4 52.4 %collective-permute-start.24 = (bf16[512,1536]{1,0:T(8,128)(2,1)}, bf16[512,1536]{1,0:T(8,128)(2,1)}, u32[]{:S(2)}, u32[]{:S(2)}) collective-permute-start(bf16[512,1536]{1,0:T(8,128)(2,1)} %ffn_weights.3), channel_id=1, source_target_pairs={{0,8},{24,16},{1,9},{25,17},{2,10},{26,18},{3,11},{27,19},{4,12},{... | collective-permute-start | bytes 4718600 | tf_op jit(solution)/shard_map/ppermute | solution.py:81
  358.3 33.9 %collective-permute-start.25 = (bf16[512,1536]{1,0:T(8,128)(2,1)}, bf16[512,1536]{1,0:T(8,128)(2,1)}, u32[]{:S(2)}, u32[]{:S(2)}) collective-permute-start(bf16[512,1536]{1,0:T(8,128)(2,1)} %add_convert_fusion.5), channel_id=1, source_target_pairs={{8,16},{16,8},{9,17},{17,9},{10,18},{18,10},{11,19},{19,11},{12,20... | collective-permute-start | bytes 4718600 | tf_op jit(solution)/shard_map/ppermute | solution.py:86
  361.6 31.8 %collective-permute-start.26 = (bf16[512,1536]{1,0:T(8,128)(2,1)}, bf16[512,1536]{1,0:T(8,128)(2,1)}, u32[]{:S(2)}, u32[]{:S(2)}) collective-permute-start(bf16[512,1536]{1,0:T(8,128)(2,1)} %add_convert_fusion.5), channel_id=1, source_target_pairs={{0,8},{8,0},{16,24},{24,16},{1,9},{9,1},{17,25},{25,17},{2,10},{10... | collective-permute-start | bytes 4718600 | tf_op jit(solution)/shard_map/ppermute | solution.py:86
  396.2 30.9 %collective-permute-start.27 = (bf16[512,1536]{1,0:T(8,128)(2,1)}, bf16[512,1536]{1,0:T(8,128)(2,1)}, u32[]{:S(2)}, u32[]{:S(2)}) collective-permute-start(bf16[512,1536]{1,0:T(8,128)(2,1)} %slice.464), channel_id=1, source_target_pairs={{0,8},{8,0},{16,24},{24,16},{1,9},{9,1},{17,25},{25,17},{2,10},{10... | collective-permute-start | bytes 4718600 | tf_op jit(solution)/shard_map/ppermute | solution.py:81
  435.8 27.8 %collective-permute-start.28 = (bf16[4,256,2048]{2,1,0:T(8,128)(2,1)}, bf16[4,256,2048]{2,1,0:T(8,128)(2,1)}, u32[]{:S(2)}, u32[]{:S(2)}) collective-permute-start(bf16[4,256,2048]{2,1,0:T(8,128)(2,1)} %select_bitcast_fusion), channel_id=1, source_target_pairs={{0,1},{1,0},{2,3},{3,2},{4,5},{5,4},{6,7},{7,6},{8,9},{9,8},{10,11... | collective-permute-start | bytes 12582920 | tf_op jit(solution)/shard_map/ppermute | solution.py:770
  441.4 38.2 %collective-permute-start.30 = (bf16[512,1536]{1,0:T(8,128)(2,1)}, bf16[512,1536]{1,0:T(8,128)(2,1)}, u32[]{:S(2)}, u32[]{:S(2)}) collective-permute-start(bf16[512,1536]{1,0:T(8,128)(2,1)} %add_convert_fusion.3), channel_id=1, source_target_pairs={{8,16},{16,8},{9,17},{17,9},{10,18},{18,10},{11,19},{19,11},{12,20... | collective-permute-start | bytes 4718600 | tf_op jit(solution)/shard_map/ppermute | solution.py:94
  447.3 36.0 %collective-permute-start.29 = (bf16[512,1536]{1,0:T(8,128)(2,1)}, bf16[512,1536]{1,0:T(8,128)(2,1)}, u32[]{:S(2)}, u32[]{:S(2)}) collective-permute-start(bf16[512,1536]{1,0:T(8,128)(2,1)} %add_convert_fusion.4), channel_id=1, source_target_pairs={{0,8},{8,0},{16,24},{24,16},{1,9},{9,1},{17,25},{25,17},{2,10},{10... | collective-permute-start | bytes 4718600 | tf_op jit(solution)/shard_map/ppermute | solution.py:94
  459.2 24.1 %all-to-all-start = ((bf16[256,8,256]{2,0,1:T(8,128)(2,1)}), bf16[256,8,256]{2,0,1:T(8,128)(2,1)}, u32[]{:S(2)}, u32[]{:S(2)}) async-start(bf16[256,8,256]{2,0,1:T(8,128)(2,1)} %bitcast.63), calls=%async_computation.2 | async-start | bytes 2097152 | tf_op jit(solution)/shard_map/all_to_all | solution.py:956
  463.6 82.7 %all-gather.11.cloned.1.call-start = ((), (), s32[]{:S(2)}) async-start(), calls=%async_computation.9 | async-start | bytes 9437184 | tf_op jit(solution)/shard_map/all_gather | solution.py:973
  483.4 166.6 %reduce-scatter.8.cloned.1.call-start = ((), (), s32[]{:S(2)}) async-start(), calls=%async_computation.10 | async-start | bytes 9437184 | tf_op jit(solution)/shard_map/reduce_scatter | solution.py:986
  483.4 57.9 %collective-permute-start.38 = (bf16[2,256,2048]{2,1,0:T(8,128)(2,1)}, bf16[2,256,2048]{2,1,0:T(8,128)(2,1)}, u32[]{:S(2)}, u32[]{:S(2)}) collective-permute-start(bf16[2,256,2048]{2,1,0:T(8,128)(2,1)} %pad_maximum_fusion.4), channel_id=1, source_target_pairs={{0,4},{1,3},{2,6},{3,1},{4,0},{5,7},{6,2},{7,5},{8,12},{9,11},{10,... | collective-permute-start | bytes 6291464 | tf_op jit(solution)/shard_map/ppermute | solution.py:764
  488.2 53.2 %collective-permute-start.31 = (bf16[512,1536]{1,0:T(8,128)(2,1)}, bf16[512,1536]{1,0:T(8,128)(2,1)}, u32[]{:S(2)}, u32[]{:S(2)}) collective-permute-start(bf16[512,1536]{1,0:T(8,128)(2,1)} %add_convert_fusion.2), channel_id=1, source_target_pairs={{8,16},{16,8},{9,17},{17,9},{10,18},{18,10},{11,19},{19,11},{12,20... | collective-permute-start | bytes 4718600 | tf_op jit(solution)/shard_map/ppermute | solution.py:86
  491.3 50.1 %collective-permute-start.32 = (bf16[512,1536]{1,0:T(8,128)(2,1)}, bf16[512,1536]{1,0:T(8,128)(2,1)}, u32[]{:S(2)}, u32[]{:S(2)}) collective-permute-start(bf16[512,1536]{1,0:T(8,128)(2,1)} %add_convert_fusion.2), channel_id=1, source_target_pairs={{0,8},{8,0},{16,24},{24,16},{1,9},{9,1},{17,25},{25,17},{2,10},{10... | collective-permute-start | bytes 4718600 | tf_op jit(solution)/shard_map/ppermute | solution.py:86
  525.6 1.7 collective-permute-start.33
  527.3 3.4 collective-permute-start.34
  530.7 3.4 collective-permute-start.35
  534.0 3.1 collective-permute-start.36
  537.1 3.6 collective-permute-start.37
  550.2 35.9 %collective-permute-start.39 = (bf16[512,1536]{1,0:T(8,128)(2,1)S(1)}, bf16[512,1536]{1,0:T(8,128)(2,1)S(1)}, u32[]{:S(2)}, u32[]{:S(2)}) collective-permute-start(bf16[512,1536]{1,0:T(8,128)(2,1)S(1)} %get-tuple-element.327), channel_id=1, source_target_pairs={{0,8},{8,0},{16,24},{24,16},{1,9},{9,1},{17,25},{25,17},{2,10},{10... | collective-permute-start | bytes 4718600 | tf_op jit(solution)/shard_map/ppermute | solution.py:94
  550.3 38.0 %collective-permute-start.40 = (bf16[512,1536]{1,0:T(8,128)(2,1)S(1)}, bf16[512,1536]{1,0:T(8,128)(2,1)}, u32[]{:S(2)}, u32[]{:S(2)}) collective-permute-start(bf16[512,1536]{1,0:T(8,128)(2,1)S(1)} %get-tuple-element.326), channel_id=1, source_target_pairs={{8,16},{16,8},{9,17},{17,9},{10,18},{18,10},{11,19},{19,11},{12,20... | collective-permute-start | bytes 4718600 | tf_op jit(solution)/shard_map/ppermute | solution.py:94
  557.4 36.2 %collective-permute-start.44 = (bf16[256,1536]{1,0:T(8,128)(2,1)S(1)}, bf16[256,1536]{1,0:T(8,128)(2,1)}, u32[]{:S(2)}, u32[]{:S(2)}) collective-permute-start(bf16[256,1536]{1,0:T(8,128)(2,1)S(1)} %select_convert_fusion.1), channel_id=1, source_target_pairs={{0,4},{4,0},{1,5},{5,1},{2,6},{6,2},{3,7},{7,3},{8,12},{12,8},{9,1... | collective-permute-start | bytes 2359304 | tf_op jit(solution)/shard_map/ppermute | solution.py:167
  561.8 54.3 %collective-permute-start.46 = (bf16[256,2048]{1,0:T(8,128)(2,1)}, bf16[256,2048]{1,0:T(8,128)(2,1)}, u32[]{:S(2)}, u32[]{:S(2)}) collective-permute-start(bf16[256,2048]{1,0:T(8,128)(2,1)} %fusion.11), channel_id=1, source_target_pairs={{0,2},{1,5},{2,0},{3,7},{4,6},{5,1},{6,4},{7,3},{8,10},{9,13},{10,... | collective-permute-start | bytes 3145736 | tf_op jit(solution)/shard_map/ppermute | solution.py:767
  591.0 59.0 %collective-permute-start.45 = (bf16[256,1536]{1,0:T(8,128)(2,1)S(1)}, bf16[256,1536]{1,0:T(8,128)(2,1)}, u32[]{:S(2)}, u32[]{:S(2)}) collective-permute-start(bf16[256,1536]{1,0:T(8,128)(2,1)S(1)} %select_convert_fusion), channel_id=1, source_target_pairs={{0,4},{4,0},{1,5},{5,1},{2,6},{6,2},{3,7},{7,3},{8,12},{12,8},{9,1... | collective-permute-start | bytes 2359304 | tf_op jit(solution)/shard_map/ppermute | solution.py:167
  591.1 25.9 %collective-permute-start.41 = (bf16[512,640]{1,0:T(8,128)(2,1)S(1)}, bf16[512,640]{1,0:T(8,128)(2,1)S(1)}, u32[]{:S(2)}, u32[]{:S(2)}) collective-permute-start(bf16[512,640]{1,0:T(8,128)(2,1)S(1)} %get-tuple-element.266), channel_id=1, source_target_pairs={{0,8},{8,0},{16,24},{24,16},{1,9},{9,1},{17,25},{25,17},{2,10},{10... | collective-permute-start | bytes 1966088 | tf_op jit(solution)/shard_map/ppermute | solution.py:103
  591.2 29.9 %collective-permute-start.42 = (bf16[512,640]{1,0:T(8,128)(2,1)S(1)}, bf16[512,640]{1,0:T(8,128)(2,1)S(1)}, u32[]{:S(2)}, u32[]{:S(2)}) collective-permute-start(bf16[512,640]{1,0:T(8,128)(2,1)S(1)} %get-tuple-element.267), channel_id=1, source_target_pairs={{0,16},{8,24},{16,0},{24,8},{1,17},{9,25},{17,1},{25,9},{2,18},{10... | collective-permute-start | bytes 1966088 | tf_op jit(solution)/shard_map/ppermute | solution.py:103
  593.6 55.6 %collective-permute-start.43 = (bf16[512,640]{1,0:T(8,128)(2,1)S(1)}, bf16[512,640]{1,0:T(8,128)(2,1)S(1)}, u32[]{:S(2)}, u32[]{:S(2)}) collective-permute-start(bf16[512,640]{1,0:T(8,128)(2,1)S(1)} %get-tuple-element.268), channel_id=1, source_target_pairs={{0,24},{8,16},{16,8},{24,0},{1,25},{9,17},{17,9},{25,1},{2,26},{10... | collective-permute-start | bytes 1966088 | tf_op jit(solution)/shard_map/ppermute | solution.py:103
  617.0 32.1 %copy-start.41 = (bf16[512,640]{1,0:T(8,128)(2,1)}, bf16[512,640]{1,0:T(8,128)(2,1)S(1)}, u32[]{:S(2)}) copy-start(bf16[512,640]{1,0:T(8,128)(2,1)S(1)} %collective-permute-done.41) | copy-start | bytes 1966084
  621.1 28.1 %copy-start.43 = (bf16[512,640]{1,0:T(8,128)(2,1)}, bf16[512,640]{1,0:T(8,128)(2,1)S(1)}, u32[]{:S(2)}) copy-start(bf16[512,640]{1,0:T(8,128)(2,1)S(1)} %collective-permute-done.42) | copy-start | bytes 1966084
  655.3 29.8 %copy-start.67 = (f32[1,2048]{1,0:T(1,128)}, f32[1,2048]{1,0:T(1,128)S(1)}, u32[]{:S(2)}) copy-start(f32[1,2048]{1,0:T(1,128)S(1)} %get-tuple-element.432) | copy-start | bytes 24580
  655.3 29.9 %copy-start.68 = (f32[1,2048]{1,0:T(1,128)}, f32[1,2048]{1,0:T(1,128)S(1)}, u32[]{:S(2)}) copy-start(f32[1,2048]{1,0:T(1,128)S(1)} %get-tuple-element.433) | copy-start | bytes 24580
  658.4 27.5 %collective-permute-start.47 = (bf16[256,640]{1,0:T(8,128)(2,1)}, bf16[256,640]{1,0:T(8,128)(2,1)}, u32[]{:S(2)}, u32[]{:S(2)}) collective-permute-start(bf16[256,640]{1,0:T(8,128)(2,1)} %select_convert_fusion.2), channel_id=1, source_target_pairs={{0,4},{4,0},{1,5},{5,1},{2,6},{6,2},{3,7},{7,3},{8,12},{12,8},{9,1... | collective-permute-start | bytes 983048 | tf_op jit(solution)/shard_map/ppermute | solution.py:167
  (73 other events, 315.9 us)
Sparse Core Ops, SparseCore 0:
  11.8 64.2 all-gather.4
  115.1 73.6 reduce-scatter.3
  202.6 53.8 all-gather.6
  258.9 54.3 all-gather.8
  355.0 75.7 reduce-scatter.5
  483.5 62.7 all-gather.10
  549.7 90.3 reduce-scatter.7

commit v6 on v5

--- a/solution.py
+++ b/solution.py
@@ -77,12 +77,8 @@
     return add(part, jnp.where(is_inner(), arrived, jnp.zeros_like(arrived)))
 
 
-def sum_far(part, perm=NEAR):
-    return lax.ppermute(part, "do", perm)
-
-
 def sum_middle(parts, far):
-    second = add_inner(parts[2], far).astype(LOW)
+    second = add_inner(parts[2], cat(far, 0)).astype(LOW)
     return lax.ppermute(second, "do", MIDDLE), lax.ppermute(second, "do", NEAR)
 
 
@@ -630,41 +626,60 @@
     if not plan.line:
         out_refs[0][...], out_refs[1][...] = row, col
         return
-    rows, wide, out = plan.rows, row.shape[1], out_refs[0]
-    out[:, :wide] = row
-    for i in range(0, col.shape[0], rows):
-        for x in range(2):
-            out[x * rows : (x + 1) * rows, wide + i : wide + i + rows] = col[
-                i : i + rows, x * rows : (x + 1) * rows
-            ]
-
-
-def ffn_weights(plan, tokens, grads, act, both_grad, first, count):
+    rows, wide = plan.rows, row.shape[1]
+
+    def pack(halves):
+        for x, (out, at) in enumerate(halves):
+            out[at : at + rows, :wide] = row[x * rows : (x + 1) * rows]
+            for i in range(0, col.shape[0], rows):
+                out[at : at + rows, wide + i : wide + i + rows] = col[
+                    i : i + rows, x * rows : (x + 1) * rows
+                ]
+
+    if len(out_refs) == 1:
+        pack([(out_refs[0], 0), (out_refs[0], rows)])
+        return
+
+    @pl.when(pl.program_id(0) == 0)
+    def _():
+        pack([(out_refs[0], 0), (out_refs[1], 0)])
+
+    @pl.when(pl.program_id(0) > 0)
+    def _():
+        pack([(out_refs[2], 0), (out_refs[2], rows)])
+
+
+def ffn_weights(plan, tokens, grads, act, both_grad, order):
     rows, width = tokens.shape
     block = width // 4
     wide, hidden = both_grad.shape[1], act.shape[1]
-
-    def columns(shift):
-        return pl.BlockSpec((rows, block), lambda i: (0, i + shift))
-
-    if plan.line:
+    count, begin = len(order), order[0]
+    step = order[1] - order[0] if begin < 3 else (order[1] - 3) % 4
+    assert all(order[i] == (begin + step * i) % 4 for i in range(count))
+
+    def columns():
+        return pl.BlockSpec((rows, block), lambda i: (0, (begin + step * i) % 4))
+
+    if not plan.line:
+        out_specs = [
+            pl.BlockSpec((block, wide), lambda i: ((begin + step * i) % 4, 0)),
+            pl.BlockSpec((hidden, block), lambda i: (0, (begin + step * i) % 4)),
+        ]
+        shapes = [(count * block, wide), (hidden, count * block)]
+    elif begin == 3:
+        out_specs = [once((plan.rows, wide + hidden))] * 2 + [
+            pl.BlockSpec((block, wide + hidden), lambda i: (jnp.maximum(i - 1, 0), 0))
+        ]
+        shapes = [(plan.rows, wide + hidden)] * 2 + [((count - 1) * block, wide + hidden)]
+    else:
         out_specs = [pl.BlockSpec((block, wide + hidden), lambda i: (i, 0))]
-        out_shape = [jax.ShapeDtypeStruct((count * block, wide + hidden), LOW)]
-    else:
-        out_specs = [
-            pl.BlockSpec((block, wide), lambda i: (i, 0)),
-            pl.BlockSpec((hidden, block), lambda i: (0, i)),
-        ]
-        out_shape = [
-            jax.ShapeDtypeStruct((count * block, wide), LOW),
-            jax.ShapeDtypeStruct((hidden, count * block), LOW),
-        ]
+        shapes = [(count * block, wide + hidden)]
     return pl.pallas_call(
         functools.partial(ffn_weights_kernel, plan),
         grid=(count,),
-        in_specs=[columns(first), columns(first), once(act.shape), once(both_grad.shape)],
+        in_specs=[columns(), columns(), once(act.shape), once(both_grad.shape)],
         out_specs=out_specs,
-        out_shape=out_shape,
+        out_shape=[jax.ShapeDtypeStruct(shape, LOW) for shape in shapes],
         compiler_params=pltpu.CompilerParams(vmem_limit_bytes=60 * MIB),
         cost_estimate=SMALL,
         name="ffn_weights",
@@ -737,6 +752,129 @@
             values = values + lax.ppermute(values, axis, [(i, i ^ step) for i in range(size)])
             step *= 2
     return values
+
+
+def adamw_write(refs, grad, master, first, second):
+    refs[0][...] = grad
+    refs[1][...], refs[2][...], refs[3][...] = adamw_update(
+        master[...], grad, first[...], second[...], WEIGHT_DECAY, LEARN_RATE
+    )
+
+
+def adamw_ffn_kernel(x_ref, mine_1, theirs_1, mine_2, theirs_2, *refs):
+    step = pl.program_id(0)
+    low_is_own = x_ref[0] == 0
+    states, outs = refs[:9], refs[9:]
+    rows = states[0].shape[0]
+    hidden = states[0].shape[1] // 4
+    here = pl.ds(pl.multiple_of(step * rows, rows), rows)
+    for i in range(2):
+        lanes = slice(i * hidden, (i + 1) * hidden)
+        own = cat([mine_1[here, lanes], mine_2[here, lanes]], 1)
+        other = cat([theirs_1[here, lanes], theirs_2[here, lanes]], 1).astype(F32)
+        low = jnp.where(low_is_own, own, other)
+        high = jnp.where(low_is_own, other, own)
+        adamw_write(outs[4 * i : 4 * i + 4], cat([low, high], 1), *states[3 * i : 3 * i + 3])
+    lanes = slice(2 * hidden, 3 * hidden)
+    first = step % 2 == 0
+    own = jnp.where(first, mine_1[:, lanes], mine_2[:, lanes])
+    other = jnp.where(first, theirs_1[:, lanes], theirs_2[:, lanes]).astype(F32)
+    grad = jnp.where(step // 2 == x_ref[0], own, other)
+    width = states[6].shape[1]
+    grad = cat([grad[:, j : j + width] for j in range(0, hidden, width)], 0)
+    adamw_write(outs[8:], grad, *states[6:])
+
+
+def adamw_ffn(x, pair_1, pair_2, states):
+    steps = 4
+
+    def cut(array):
+        return pl.BlockSpec((array.shape[0] // steps, array.shape[1]), lambda i: (i, 0))
+
+    packs = [*pair_1, *pair_2]
+    flat = [array for triple in states for array in triple]
+    outs = [triple[0] for triple in states for _ in range(4)]
+    result = pl.pallas_call(
+        adamw_ffn_kernel,
+        grid=(steps,),
+        in_specs=[pl.BlockSpec(memory_space=pltpu.SMEM)]
+        + [once(pack.shape) for pack in packs]
+        + [cut(array) for array in flat],
+        out_specs=[cut(array) for array in outs],
+        out_shape=[jax.ShapeDtypeStruct(array.shape, F32) for array in outs],
+        compiler_params=pltpu.CompilerParams(vmem_limit_bytes=60 * MIB),
+        cost_estimate=SMALL,
+        name="adamw_ffn",
+    )(x.astype(jnp.int32).reshape(1), *packs, *flat)
+    return [result[4 * i : 4 * i + 4] for i in range(3)]
+
+
+def adamw_attn_kernel(x_ref, mine_ref, theirs_ref, *refs):
+    low_is_own = x_ref[0] == 0
+    states, outs = refs[:12], refs[12:]
+    own, other = mine_ref[...], theirs_ref[...].astype(F32)
+    low = jnp.where(low_is_own, own, other)
+    high = jnp.where(low_is_own, other, own)
+    wide = states[0].shape[1] // 2
+    adamw_write(outs[:4], cat([low[:, :wide], high[:, :wide]], 1), *states[:3])
+    low_kv, high_kv = low[:, wide : wide + 128], high[:, wide : wide + 128]
+    is_key = lanes_of(low_kv.shape) < HD
+    key = jnp.where(is_key, low_kv, pltpu.roll(high_kv, HD, 1))
+    adamw_write(outs[4:8], key, *states[3:6])
+    value = jnp.where(is_key, pltpu.roll(low_kv, HD, 1), high_kv)
+    adamw_write(outs[8:12], value, *states[6:9])
+    adamw_write(outs[12:], cat([low[:, wide + 128 :], high[:, wide + 128 :]], 0), *states[9:])
+
+
+def adamw_attn(x, pair, states):
+    flat = [array for triple in states for array in triple]
+    outs = [triple[0] for triple in states for _ in range(4)]
+    result = pl.pallas_call(
+        adamw_attn_kernel,
+        grid=(1,),
+        in_specs=[pl.BlockSpec(memory_space=pltpu.SMEM)]
+        + [once(array.shape) for array in [*pair, *flat]],
+        out_specs=[once(array.shape) for array in outs],
+        out_shape=[jax.ShapeDtypeStruct(array.shape, F32) for array in outs],
+        compiler_params=pltpu.CompilerParams(vmem_limit_bytes=60 * MIB),
+        cost_estimate=SMALL,
+        name="adamw_attn",
+    )(x.astype(jnp.int32).reshape(1), *pair, *flat)
+    return [result[4 * i : 4 * i + 4] for i in range(4)]
+
+
+def finish_kernel(
+    place_ref, back_ref, inputs_ref, scale_ref, gain_ref, res_grad_ref, residual_ref, stays_ref,
+    first_ref, second_ref, out_ref, in_grad_ref,
+):
+    back = norm_back(
+        back_ref[...].astype(F32), inputs_ref[...].astype(F32), scale_ref[...], gain_ref[...]
+    )
+    in_grad = res_grad_ref[...] + back
+    summed = add(stays_ref[...], first_ref[0], second_ref[...])
+    out = (residual_ref[...] + summed).astype(LOW)
+    quarter = out.shape[1] // 4
+    for k in range(4):
+        there = pl.ds(pl.multiple_of((place_ref[0] ^ k) * quarter, quarter), quarter)
+        out_ref[:, there] = out[:, k * quarter : (k + 1) * quarter]
+        in_grad_ref[:, there] = in_grad[:, k * quarter : (k + 1) * quarter]
+
+
+def finish(place, back, inputs, scale, gain, res_grad, residual, stays, first, second):
+    arrays = [back, inputs, scale, gain[None, :], res_grad, residual, stays, first, second]
+    return pl.pallas_call(
+        finish_kernel,
+        grid=(1,),
+        in_specs=[pl.BlockSpec(memory_space=pltpu.SMEM)] + [once(a.shape) for a in arrays],
+        out_specs=[once(inputs.shape)] * 2,
+        out_shape=[
+            jax.ShapeDtypeStruct(inputs.shape, LOW),
+            jax.ShapeDtypeStruct(inputs.shape, F32),
+        ],
+        compiler_params=pltpu.CompilerParams(vmem_limit_bytes=60 * MIB),
+        cost_estimate=SMALL,
+        name="finish",
+    )(place.astype(jnp.int32).reshape(1), *arrays)
 
 
 def pick(index, low, high):
@@ -792,7 +930,8 @@
     plane_sizes = (("tp", sizes["tp"]), ("di", sizes["di"]))
 
     gain_one, gain_two = plan.reorder(gain_attn), plan.reorder(gain_ffn)
-    inputs_f = plan.reorder(layer_input).astype(F32)
+    inputs_low = plan.reorder(layer_input)
+    inputs_f = inputs_low.astype(F32)
     grad_low = plan.reorder(out_grad)
     normed, scale_one = norm_rows(inputs_f, gain_one)
     normed_all = lax.all_gather(normed.astype(LOW), axes, axis=0, tiled=True)
@@ -886,9 +1025,7 @@
             across_near_1, out_1, grad_xy, theirs_2, grad_first
         )
         block_2 = plan.join(own_2, theirs_2)
-        half = plan.rows
-        out_near_low = line_last(across_near_1[:half])
-        across_2 = lax.ppermute(block_2, "do", MIDDLE)
+        out_near_1 = line_last(across_near_1)
     grad_x = pick(core, grad_first, grad_second)
     grad_y = pick(core, grad_second, grad_first)
     over_y = cat([pick(plane.y, grad_low, grad_y), pick(plane.y, grad_y, grad_low)], 0)
@@ -900,60 +1037,75 @@
     grad_all = cat([pick(core, mine, theirs), pick(core, theirs, mine)], 1).reshape(rows, width)
 
     if plan.line:
-        attn_sum, grad_all, out_near_low, across_2 = fence(
-            attn_sum, grad_all, out_near_low, across_2
-        )
+        attn_sum, grad_all, out_near_1 = fence(attn_sum, grad_all, out_near_1)
     residual = inputs_f + attn_sum.astype(F32)
     normed_two, scale_two = norm_rows(residual, gain_two)
     two_low = normed_two.astype(LOW)
     two_all = lax.all_gather(two_low, axes, axis=0, tiled=True)
 
     if plan.line:
-        across_near_1, across_2, block_2, _ = fence(across_near_1, across_2, block_2, two_low)
-        out_near_high = line_last(across_near_1[half:])
-        near_2 = lax.ppermute(block_2, "do", NEAR)
-        near_2, across_2, wout, out_near_high = fence(near_2, across_2, wout, out_near_high)
+        first_weights = (block_1, near_1, across_near_1, out_1, across_1, (out_near_1,))
+        block_2, _ = fence(block_2, two_low)
+        near_2, across_2 = line_near(block_2)
+        near_2, across_2, wout = fence(near_2, across_2, wout)
         across_near_2, out_2 = line_far(near_2, across_2)
-        out_near_1 = (out_near_low, out_near_high)
-        first_weights = (block_1, near_1, across_near_1, out_1, across_1, out_near_1)
     wout_all = lax.all_gather(wout, axes, axis=0, tiled=True)
+    if plan.line:
+        two_all, across_near_2, out_2 = fence(two_all, across_near_2, out_2)
+        out_near_2 = line_last(across_near_2)
     first = Loader(plan, first_weights, *ffn_shapes)
     back_1, act_1, both_1, down_1 = ffn_main(first, two_all, grad_all, None)
     if plan.line:
-        back_1, act_1, both_1, across_near_2, out_2 = fence(
-            back_1, act_1, both_1, across_near_2, out_2
-        )
-        out_near_2 = line_last(across_near_2, OUTWARD)
-        (last_1,) = ffn_weights(plan, two_all, grad_all, act_1, both_1, 3, 1)
-        last_1, both_1 = fence(last_1, both_1)
-        far_1 = sum_far(last_1, INWARD)
-        (rest_1,) = ffn_weights(plan, two_all, grad_all, act_1, both_1, 0, 3)
-        back_1, rest_1, out_near_2 = fence(back_1, rest_1, out_near_2)
+        *last_1, third_1 = ffn_weights(plan, two_all, grad_all, act_1, both_1, (3, 2))
+        back_1, last_1, out_near_2 = fence(back_1, last_1, out_near_2)
+        far_1 = [lax.ppermute(part, "do", NEAR) for part in last_1]
         second_weights = (block_2, near_2, across_near_2, out_2, across_2, (out_near_2,))
     else:
-        grads_1 = ffn_weights(plan, two_all, grad_all, act_1, both_1, 0, 4)
+        grads_1 = ffn_weights(plan, two_all, grad_all, act_1, both_1, (0, 1, 2, 3))
     second = Loader(plan, second_weights, *ffn_shapes)
     back_2, act_2, both_2, down_2 = ffn_main(second, two_all, grad_all, back_1)
     if plan.line:
-        back_2, act_2, both_2, far_1, wout_all = fence(back_2, act_2, both_2, far_1, wout_all)
+        back_2, act_2, both_2, far_1, wout_all, act_1 = fence(
+            back_2, act_2, both_2, far_1, wout_all, act_1
+        )
         block = plan.block
-        grads_1 = [rest_1[:block], rest_1[block : 2 * block], rest_1[2 * block :], last_1]
-        crossed_1, inward_1 = sum_middle(grads_1, far_1)
+        crossed_1, inward_1 = sum_middle([None, None, third_1], far_1)
     back_sum = lax.psum_scatter(back_2, axes, scatter_dimension=0, tiled=True)
-    grads_2 = ffn_weights(plan, two_all, grad_all, act_2, both_2, 0, 4)
-    if plan.line:
-        grads_2, act_2, crossed_1, inward_1 = fence(grads_2, act_2, crossed_1, inward_1)
-        (grads_2,) = grads_2
-        grads_2 = [grads_2[k * block : (k + 1) * block] for k in range(4)]
-        far_2 = sum_far(grads_2[3])
+    order = (3, 0, 1, 2) if plan.line else (0, 1, 2, 3)
+    grads_2 = ffn_weights(plan, two_all, grad_all, act_2, both_2, order)
+    if plan.line:
+        *last_2, rest_2 = grads_2
+        act_1, rest_2 = fence(act_1, rest_2)
+        (rest_1,) = ffn_weights(plan, two_all, grad_all, act_1, both_1, (0, 1))
+        act_2, rest_1, crossed_1, inward_1, last_2 = fence(
+            act_2, rest_1, crossed_1, inward_1, last_2
+        )
+        grads_1 = [rest_1[:block], rest_1[block:], third_1, cat(last_1, 0)]
+        grads_2 = [rest_2[:block], rest_2[block : 2 * block], rest_2[2 * block :], cat(last_2, 0)]
+        far_low = lax.ppermute(last_2[0], "do", NEAR)
     out_part, gain_two_part = ffn_out(act_1, act_2, down_1, down_2, back_2, two_all)
     if plan.line:
-        back_sum, out_part, far_2 = fence(back_sum, out_part, far_2)
+        out_part, far_low, last_high = fence(out_part, far_low, last_2[1])
+        far_high = lax.ppermute(last_high, "do", NEAR)
+
+    if plan.line:
+        back_sum, out_part = fence(back_sum, out_part)
 
     residual_grad, res_low, ctx_grad = residual_backward(
         back_sum, residual, scale_two, gain_two, grad_low, wout_all
     )
+    if plan.line:
+        ctx_grad, res_low, far_high = fence(ctx_grad, res_low, far_high)
+        second = add_inner(grads_2[2], cat([far_low, far_high], 0)).astype(LOW)
+        first_1, third_1 = sum_near_parts(grads_1, crossed_1, inward_1)
+        ctx_grad, near_both, across_both = fence(
+            ctx_grad, cat([second, first_1], 0), cat([second, third_1], 0)
+        )
+        near_both = lax.ppermute(near_both, "do", NEAR)
+        across_both = lax.ppermute(across_both, "do", MIDDLE)
     ctx_grad = lax.all_to_all(ctx_grad, axes, split_axis=1, concat_axis=0, tiled=True)
+    if plan.line:
+        ctx_grad, res_low, out_part = fence(ctx_grad, res_low, out_part)
 
     out_shape = (rows // own_rows // 2, 2, own_rows, width)
     parts = out_part.reshape(out_shape)
@@ -962,13 +1114,8 @@
     step = plane.first_step()
     goes = jnp.stack([plane.at(summed, step), plane.at(summed, 3)])
     goes_on, stays = plane.at(summed, 3 - step), plane.at(summed, 0)
-
-    if plan.line:
-        crossed_2, inward_2 = sum_middle(grads_2, far_2)
-        near_sum_1, across_sum_1 = sum_near_send(*sum_near_parts(grads_1, crossed_1, inward_1))
-        ctx_grad, res_low, goes, goes_on, stays, near_sum_1, across_sum_1 = fence(
-            ctx_grad, res_low, goes, goes_on, stays, near_sum_1, across_sum_1
-        )
+    if plan.line:
+        ctx_grad, goes, goes_on, stays = fence(ctx_grad, goes, goes_on, stays)
     arrives = plane.swap_first(goes)
     res_all = lax.all_gather(res_low, axes, axis=0, tiled=True)
     back_one_part, gain_one_part, *grads_qkv = attn_backward(
@@ -976,16 +1123,19 @@
     )
     if plan.line:
         gain_parts = jnp.stack([gain_one_part[0] / gain_one, gain_two_part[0] / gain_two])
-        gain_parts = sum_over(plan.reorder(gain_parts), plane_sizes + (("do", sizes["do"]),))
-        back_one_part, grads_qkv, res_all, crossed_2, inward_2, gain_parts, arrives = fence(
-            back_one_part, grads_qkv, res_all, crossed_2, inward_2, gain_parts, arrives
+        gain_sums = sum_over(plan.reorder(gain_parts), plane_sizes + (("do", sizes["do"]),))
+        back_one_part, grads_qkv, res_all, gain_sums, arrives, near_both, across_both = fence(
+            back_one_part, grads_qkv, res_all, gain_sums, arrives, near_both, across_both
         )
+        crossed_2, inward_2 = across_both[:block], near_both[:block]
+        near_sum_1, across_sum_1 = near_both[block:], across_both[block:]
     else:
         gain_parts = jnp.stack([gain_one_part[0] / gain_one, gain_two_part[0] / gain_two])
-        gain_parts = sum_over(gain_parts, plane_sizes)
+        gain_sums = sum_over(gain_parts, (("do", sizes["do"]),) + plane_sizes)
     back_one = lax.psum_scatter(back_one_part, axes, scatter_dimension=0, tiled=True)
     grads_attn = out_weights(plan, ctx, res_all, grads_qkv)
     if plan.line:
+        half = plan.rows
 
         def trade(total):
             return plan.trade(total[:half], total[half:])
@@ -995,69 +1145,73 @@
         near_sum_2, across_sum_2, grads_attn = fence(near_sum_2, across_sum_2, grads_attn)
         direct = send_direct(grads_attn)
         ffn_pair_2 = trade(sum_own(grads_2, near_sum_2, across_sum_2))
-    summed = add(stays, arrives[0])
-    arrives = plane.swap_second(add(goes_on, arrives[1]).astype(LOW))
-    if plan.line:
-        direct, ffn_pair_1, ffn_pair_2, arrives, back_one, gain_parts = fence(
-            direct, ffn_pair_1, ffn_pair_2, arrives, back_one, gain_parts
-        )
+    second = plane.swap_second(add(goes_on, arrives[1]).astype(LOW))
+    place = lax.axis_index("do") if plan.line else jnp.zeros((), jnp.int32)
+    states = {
+        "attn": [
+            (w_query, m_query, v_query), (w_key, m_key, v_key),
+            (w_value, m_value, v_value), (w_out, m_out, v_out),
+        ],
+        "ffn": [(w_gate, m_gate, v_gate), (w_up, m_up, v_up), (w_down, m_down, v_down)],
+    }
+    if plan.line:
+        ffn_updated = adamw_ffn(lax.axis_index("di"), ffn_pair_1, ffn_pair_2, states["ffn"])
+        direct, ffn_updated, second, back_one = fence(direct, ffn_updated, second, back_one)
         attn_pair = trade(add(grads_attn[0], *direct))
-        gain_sums = gain_parts
-        qkv_pair, out_pair = plan.unpack(attn_pair, attn_shapes[0][1])
-        ffn_grads = [plan.unpack(pair, 2 * hidden) for pair in (ffn_pair_1, ffn_pair_2)]
+        attn_updated = adamw_attn(lax.axis_index("di"), attn_pair, states["attn"])
     else:
+
+        def join(pair, axis):
+            own, other = pair[0], pair[1].astype(F32)
+            return by_x(cat([own, other], axis), cat([other, own], axis))
+
+        def from_chunks(pairs, axis):
+            return join([cat([pair[i] for pair in pairs], axis) for i in range(2)], axis)
+
+        def cut(pair, start, stop):
+            return tuple(part[:, start:stop] for part in pair)
+
+        def update(grad, state):
+            return (grad, *adamw_update(state[0], grad, *state[1:], WEIGHT_DECAY, LEARN_RATE))
+
         qkv_pair = plan.plain_sum_row(grads_qkv[0])
         out_pair = plan.plain_sum_col(grads_attn[0])
-        ffn_grads = [
+        ffn_pairs = [
             (plan.plain_sum_row(row), plan.plain_sum_col(col)) for row, col in (grads_1, grads_2)
         ]
-        gain_sums = sum_over(gain_parts, (("do", sizes["do"]),))
-    in_grad = residual_grad + norm_back(back_one.astype(F32), inputs_f, scale_one, gain_one)
-    out_value = residual + add(summed, arrives)
+        at_k = halves_q[0].shape[1]
+        at_v = at_k + halves_k[0].shape[1]
+        end = at_v + halves_v[0].shape[1]
+        attn_grads = [
+            join(cut(qkv_pair, 0, at_k), 1),
+            join(cut(qkv_pair, at_k, at_v), 1),
+            join(cut(qkv_pair, at_v, end), 1),
+            join(out_pair, 0),
+        ]
+        ffn_grads = [
+            from_chunks([cut(row, 0, hidden) for row, _ in ffn_pairs], 1),
+            from_chunks([cut(row, hidden, 2 * hidden) for row, _ in ffn_pairs], 1),
+            from_chunks([col for _, col in ffn_pairs], 0),
+        ]
+        attn_updated = [update(g, s) for g, s in zip(attn_grads, states["attn"])]
+        ffn_updated = [update(g, s) for g, s in zip(ffn_grads, states["ffn"])]
+    out_value, in_grad = finish(
+        place, back_one, inputs_low, scale_one, gain_one, residual_grad, residual, stays, arrives,
+        second,
+    )
     grad_gain_attn, grad_gain_ffn = gain_sums[0], gain_sums[1]
-
-    def join(pair, axis):
-        own, other = pair[0], pair[1].astype(F32)
-        return by_x(cat([own, other], axis), cat([other, own], axis))
-
-    def from_chunks(pairs, axis):
-        own = cat([pair[0] for pair in pairs], axis)
-        other = cat([pair[1] for pair in pairs], axis)
-        return join((own, other), axis)
-
-    def cut(pair, start, stop):
-        return tuple(part[:, start:stop] for part in pair)
-
-    at_k = halves_q[0].shape[1]
-    at_v = at_k + halves_k[0].shape[1]
-    end = at_v + halves_v[0].shape[1]
-    grad_query = join(cut(qkv_pair, 0, at_k), 1)
-    grad_key = join(cut(qkv_pair, at_k, at_v), 1)
-    grad_value = join(cut(qkv_pair, at_v, end), 1)
-    grad_out = join(out_pair, 0)
-    grad_gate = from_chunks([cut(gu, 0, hidden) for gu, _ in ffn_grads], 1)
-    grad_up = from_chunks([cut(gu, hidden, 2 * hidden) for gu, _ in ffn_grads], 1)
-    grad_down = from_chunks([down for _, down in ffn_grads], 0)
-
-    grads = (grad_query, grad_key, grad_value, grad_out, grad_gate, grad_up, grad_down)
-    masters = (w_query, w_key, w_value, w_out, w_gate, w_up, w_down)
-    firsts = (m_query, m_key, m_value, m_out, m_gate, m_up, m_down)
-    seconds = (v_query, v_key, v_value, v_out, v_gate, v_up, v_down)
-    updated = [
-        adamw_update(w, g, m, v, WEIGHT_DECAY, LEARN_RATE)
-        for w, g, m, v in zip(masters, grads, firsts, seconds)
-    ]
+    updated = attn_updated + ffn_updated
     gain_updated = [
         adamw_update(gain_attn, grad_gain_attn, m_gain_attn, v_gain_attn, 0.0, GAIN_RATE),
         adamw_update(gain_ffn, grad_gain_ffn, m_gain_ffn, v_gain_ffn, 0.0, GAIN_RATE),
     ]
     return (
-        plan.reorder(out_value.astype(LOW)),
-        plan.reorder(in_grad),
-        *grads,
+        out_value,
+        in_grad,
         *[u[0] for u in updated],
         *[u[1] for u in updated],
         *[u[2] for u in updated],
+        *[u[3] for u in updated],
         grad_gain_attn,
         grad_gain_ffn,
         *[u[0] for u in gain_updated],

time: 711 us -> 692 us (0.973)
  Pallas kernels: 191 us -> 223 us
  other arithmetic: 110 us -> 78.7 us
  waiting for transfers between devices: 276 us -> 255 us
  blocking collectives: 0 us -> 17.6 us
    ppermute x3, waiting for transfers between devices: 0.01 us -> 42.6 us  [trade(): theirs = lax.ppermute(self.by_x(high, low).astype(LOW), 'di', PAIR)]
    ppermute x4 -> x3, waiting for transfers between devices: 63.4 us -> 21 us  [line_last(): return lax.ppermute(across_near, 'do', perm)]
    ppermute x4 -> x6, waiting for transfers between devices: 7.94 us -> 42.8 us  [line_near(): return (lax.ppermute(own, 'do', NEAR), lax.ppermute(own, 'do', MIDDLE))]
    ppermute x3, waiting for transfers between devices: 33 us -> 0.01 us  [send_direct(): lax.ppermute(part, 'do', perm)]
    pallas_call x0 -> x3, Pallas kernels: none -> 30.6 us  [the longest x1 17.6 us: adamw_ffn(): pl.pallas_call(adamw_ffn_kernel, grid=(steps,), in_specs=[pl.BlockSpec(me...]
    ppermute x6, waiting for transfers between devices: 11.1 us -> 41.6 us  [line_far(): return (lax.ppermute(near, 'do', MIDDLE), lax.ppermute(across, 'do', NEAR))]
    ppermute x4 -> x6, waiting for transfers between devices: 27.2 us -> 0.02 us  [the longest x2 0.01 us: on_device(): far_1 = [lax.ppermute(part, 'do', NEAR) for part in last_1]]
    ppermute x2, waiting for transfers between devices: 19.6 us -> 0.01 us  [swap_second(): return lax.ppermute(value, self.axes, self.pairs(False))]
  transfers between devices with their start and end apart: 56 -> 54, of which waited for: 38 -> 31; matrix products, arithmetic and copies ran while one was open for 16% -> 12% of each run, Pallas kernels for 27% -> 32%
where the time goes in v6:
time: 692 us; the launch traced here: 683 us
  waiting for transfers between devices  255 us (37%)
  Pallas kernels  223 us (32%)
  other arithmetic  78.7 us (11%)
  starting transfers between devices  64.6 us (9%)
  local copies, waits for them, and re-layouts  28.1 us (4%)
  blocking collectives  17.6 us (3%)
  between operations  15.8 us (2%)
    pallas_call x2, Pallas kernels, ffn_main(): pl.pallas_call(functools.partial(ffn_main_kernel, loader, len(more)), gri...  61.9 us
    pallas_call x3, Pallas kernels, ffn_weights(): pl.pallas_call(functools.partial(ffn_weights_kernel, plan), grid=(count,)...  45.8 us
    ppermute x6, waiting for transfers between devices, line_near(): return (lax.ppermute(own, 'do', NEAR), lax.ppermute(own, 'do', MIDDLE))  42.8 us
    ppermute x3, waiting for transfers between devices, trade(): theirs = lax.ppermute(self.by_x(high, low).astype(LOW), 'di', PAIR)  42.6 us
    ppermute x6, waiting for transfers between devices, line_far(): return (lax.ppermute(near, 'do', MIDDLE), lax.ppermute(across, 'do', NEAR))  41.6 us
    pallas_call x1, Pallas kernels, attn_backward(): pl.pallas_call(functools.partial(attn_backward_kernel, heads // 128, load...  33 us
    ppermute x3, waiting for transfers between devices, swap_first(): return lax.ppermute(value, self.axes, self.pairs(True))  27.3 us
    pallas_call x1, Pallas kernels, attn_forward(): pl.pallas_call(functools.partial(attn_forward_kernel, heads // 128, loade...  23.2 us
  transfers between devices with their start and end apart: 54, of which 31 were waited for; matrix products, arithmetic and copies ran while one was open for 12% of the time, Pallas kernels for 32%

profile of v6, /device:TPU:9, one launch (start us, length us, event | category | flops | bytes accessed | tf_op | source)
XLA Modules:
  0.0 683.2 jit_solution(17487283696497132024)
XLA Ops:
  18.2 2.8 collective-permute-done.1
  21.6 4.2 collective-permute-start.3
  25.9 3.7 fusion.5
  36.1 3.0 collective-permute-done.3.refs_5_
  39.1 3.1 collective-permute-start.4
  42.7 10.1 %collective-permute-done.6 = bf16[256,1536]{1,0:T(8,128)(2,1)S(1)} collective-permute-done((bf16[256,1536]{1,0:T(8,128)(2,1)S(1)}, bf16[256,1536]{1,0:T(8,128)(2,1)S(1)}, u32[]{:S(2)}, u32[]{:S(2)}) %collective-permute-start.6) | collective-permute-done | bytes 786464 | tf_op jit(solution)/shard_map/ppermute | solution.py:135
  57.5 11.4 %collective-permute-done.7.refs_6_ = bf16[512,640]{1,0:T(8,128)(2,1)} collective-permute-done((bf16[512,640]{1,0:T(8,128)(2,1)S(1)}, bf16[512,640]{1,0:T(8,128)(2,1)}, u32[]{:S(2)}, u32[]{:S(2)}) %collective-permute-start.7) | collective-permute-done | bytes 655392 | tf_op jit(solution)/shard_map/ppermute | solution.py:61
  68.8 6.9 %all-gather.5.cloned.1.call-done.refs_7_.refs_8_ = bf16[2048,2048]{1,0:T(8,128)(2,1)} async-done(((bf16[256,2048]{1,0:T(8,128)(2,1)}), bf16[2048,2048]{1,0:T(8,128)(2,1)}) %all-gather.5.cloned.1.call-update) | async-done | bytes 8388624 | tf_op jit(solution)/shard_map/all_gather | solution.py:937
  76.0 4.3 collective-permute-start.9
  83.1 23.2 %attn_forward.1 = (bf16[2048,2048]{1,0:T(8,128)(2,1)}, bf16[2048,256]{1,0:T(8,128)(2,1)}, bf16[2048,256]{1,0:T(8,128)(2,1)}, bf16[2048,128]{1,0:T(8,128)(2,1)}, ...) custom-call(s32[1]{0:T(128)} %bitcast.1.refs_0_, bf16[512,640]{1,0:T(8,128)(2,1)} %copy-done.15, ...), custom_call_target="tpu_custom_call" | custom-call | flops 1 | bytes 1 | tf_op jit(solution)/shard_map/attn_forward/pallas_call | solution.py:407
  106.3 4.9 collective-permute-done.11
  111.8 2.8 collective-permute-done.9.refs_5_
  114.7 3.0 collective-permute-start.12
  119.3 12.8 %collective-permute-done.14 = bf16[256,2048]{1,0:T(8,128)(2,1)} collective-permute-done((bf16[256,2048]{1,0:T(8,128)(2,1)}, bf16[256,2048]{1,0:T(8,128)(2,1)}, u32[]{:S(2)}, u32[]{:S(2)}) %collective-permute-start.14) | collective-permute-done | bytes 1048608 | tf_op jit(solution)/shard_map/ppermute | solution.py:902
  132.1 14.5 %collective-permute-done.15 = bf16[256,2048]{1,0:T(8,128)(2,1)} collective-permute-done((bf16[256,2048]{1,0:T(8,128)(2,1)S(1)}, bf16[256,2048]{1,0:T(8,128)(2,1)}, u32[]{:S(2)}, u32[]{:S(2)}) %collective-permute-start.15) | collective-permute-done | bytes 1048608 | tf_op jit(solution)/shard_map/ppermute | solution.py:902
  146.6 5.1 collective-permute-done.12.refs_3_
  152.3 2.1 broadcast_select_fusion.9
  156.6 2.9 collective-permute-start.16
  161.7 4.6 collective-permute-done.16
  166.3 4.6 broadcast_select_fusion.1
  170.9 7.5 %pad_maximum_fusion = bf16[4,2,256,2048]{3,2,0,1:T(8,128)(2,1)} fusion(bf16[4,1,256,2048]{3,2,0,1:T(8,128)(2,1)} %bitcast.61, bf16[4,1,256,2048]{3,2,0,1:T(8,128)(2,1)} %bitcast.60), kind=kLoop, calls=%fused_computation | loop fusion | flops 4194304 | bytes 16777216 | tf_op jit(solution)/shard_map/concatenate | solution.py:45
  178.4 8.5 %copy.81 = bf16[4,2,256,2048]{3,2,1,0:T(8,128)(2,1)} copy(bf16[4,2,256,2048]{3,2,0,1:T(8,128)(2,1)} %pad_maximum_fusion) | data formatting | bytes 16777216 | tf_op jit(solution)/shard_map/concatenate | solution.py:45
  187.0 9.6 %collective-permute-done.17.refs_6_ = bf16[512,1536]{1,0:T(8,128)(2,1)S(1)} collective-permute-done((bf16[512,1536]{1,0:T(8,128)(2,1)}, bf16[512,1536]{1,0:T(8,128)(2,1)S(1)}, u32[]{:S(2)}, u32[]{:S(2)}) %collective-permute-start.17) | collective-permute-done | bytes 1572896 | tf_op jit(solution)/shard_map/ppermute | solution.py:61
  196.6 2.2 multiply_reduce_fusion
  198.9 2.2 convert_add_fusion.3
  205.8 32.3 %collective-permute-done.18.refs_2_ = bf16[512,1536]{1,0:T(8,128)(2,1)S(1)} collective-permute-done((bf16[512,1536]{1,0:T(8,128)(2,1)S(1)}, bf16[512,1536]{1,0:T(8,128)(2,1)S(1)}, u32[]{:S(2)}, u32[]{:S(2)}) %collective-permute-start.18) | collective-permute-done | bytes 1572896 | tf_op jit(solution)/shard_map/ppermute | solution.py:53
  238.0 2.6 collective-permute-done.19.refs_5_
  241.8 2.6 collective-permute-start.20
  244.6 33.2 %collective-permute-done.20.refs_3_ = bf16[512,1536]{1,0:T(8,128)(2,1)S(1)} collective-permute-done((bf16[512,1536]{1,0:T(8,128)(2,1)S(1)}, bf16[512,1536]{1,0:T(8,128)(2,1)S(1)}, u32[]{:S(2)}, u32[]{:S(2)}) %collective-permute-start.20) | collective-permute-done | bytes 1572896 | tf_op jit(solution)/shard_map/ppermute | solution.py:57
  279.1 30.4 %ffn_main.2 = (bf16[2048,2048]{1,0:T(8,128)(2,1)}, bf16[2048,512]{1,0:T(8,128)(2,1)}, bf16[2048,1024]{1,0:T(8,128)(2,1)}, bf16[512,2048]{1,0:T(8,128)(2,1)}) custom-call(s32[1]{0:T(128)} %bitcast.1.refs_0_, bf16[512,1536]{1,0:T(8,128)(2,1)} %pad_maximum_fusion.7.refs_1_, bf16[512,1536]{1,0:T(8,128)(2,1)} %collective-permute-done.8.refs_2_, ...), custom_call_target="tpu_custom_call" | custom-call | flops 1 | bytes 1 | tf_op jit(solution)/shard_map/ffn_main/pallas_call | solution.py:595
  309.6 13.1 %ffn_weights.3 = (bf16[256,1536]{1,0:T(8,128)(2,1)}, bf16[256,1536]{1,0:T(8,128)(2,1)}, bf16[512,1536]{1,0:T(8,128)(2,1)}) custom-call(bf16[2048,2048]{1,0:T(8,128)(2,1)} %all-gather.7.cloned.1.call-done.refs_7_.x_ref, bf16[2048,2048]{1,0:T(8,128)(2,1)} %bitcast.54, bf16[2048,512]{1,0:T(8,128)(2,1)} %get-tuple-element.273.act_ref.act_1, ...), custom_call_target="tpu_custom_call" | custom-call | flops 1 | bytes 1 | tf_op jit(solution)/shard_map/ffn_weights/pallas_call | solution.py:677
  322.6 2.3 collective-permute-start.23
  325.0 31.5 %ffn_main.3 = (bf16[2048,2048]{1,0:T(8,128)(2,1)}, bf16[2048,512]{1,0:T(8,128)(2,1)}, bf16[2048,1024]{1,0:T(8,128)(2,1)}, bf16[512,2048]{1,0:T(8,128)(2,1)}) custom-call(s32[1]{0:T(128)} %bitcast.1.refs_0_, bf16[512,1536]{1,0:T(8,128)(2,1)} %copy-done.12, bf16[512,1536]{1,0:T(8,128)(2,1)} %copy-done.26, bf16[512,1536]{1,0:T(8,128)(2,1)} %copy-done.28, ...), custom_call_target="tpu_custom_call" | custom-call | flops 1 | bytes 1 | tf_op jit(solution)/shard_map/ffn_main/pallas_call | solution.py:595
  361.8 20.3 %ffn_weights.4 = (bf16[256,1536]{1,0:T(8,128)(2,1)}, bf16[256,1536]{1,0:T(8,128)(2,1)}, bf16[1536,1536]{1,0:T(8,128)(2,1)}) custom-call(bf16[2048,2048]{1,0:T(8,128)(2,1)} %all-gather.7.cloned.1.call-done.refs_7_.x_ref, bf16[2048,2048]{1,0:T(8,128)(2,1)} %bitcast.56, bf16[2048,512]{1,0:T(8,128)(2,1)} %get-tuple-element.279.act_ref.act_2, ...), custom_call_target="tpu_custom_call" | custom-call | flops 1 | bytes 1 | tf_op jit(solution)/shard_map/ffn_weights/pallas_call | solution.py:677
  382.1 12.4 %ffn_weights.5 = bf16[1024,1536]{1,0:T(8,128)(2,1)} custom-call(bf16[2048,2048]{1,0:T(8,128)(2,1)} %all-gather.7.cloned.1.call-done.refs_7_.x_ref, bf16[2048,2048]{1,0:T(8,128)(2,1)} %bitcast.57, bf16[2048,512]{1,0:T(8,128)(2,1)} %get-tuple-element.273.act_ref.act_1, bf16[2048,1024]{1,0:T(8,128)(2,1)} %get-tuple-element.256.both_ref), custom_call_target="tpu_custom_call" | custom-call | flops 1 | bytes 1 | tf_op jit(solution)/shard_map/ffn_weights/pallas_call | solution.py:677
  394.5 2.5 collective-permute-start.27
  397.0 16.5 %ffn_out.1 = (bf16[2048,2048]{1,0:T(8,128)(2,1)}, f32[1,2048]{1,0:T(1,128)}) custom-call(bf16[2048,512]{1,0:T(8,128)(2,1)} %get-tuple-element.273.act_ref.act_1, bf16[2048,512]{1,0:T(8,128)(2,1)} %get-tuple-element.279.act_ref.act_2, bf16[512,2048]{1,0:T(8,128)(2,1)} %get-tuple-element.280.down_1, bf16[512,2048]{1,0:T(8,128)(2,1)} %get-tuple-element.281.down_2, ...), custom_call_target="tpu_custom_call" | custom-call | flops 1 | bytes 1 | tf_op jit(solution)/shard_map/ffn_out/pallas_call | solution.py:703
  415.8 5.6 add_convert_fusion.2
  421.5 10.0 %reduce-scatter.6.cloned.1.call-done.back_ref = bf16[256,2048]{1,0:T(8,128)(2,1)} async-done(((bf16[2048,2048]{1,0:T(8,128)(2,1)}), bf16[256,2048]{1,0:T(8,128)(2,1)}) %reduce-scatter.6.cloned.1.call-update) | async-done | bytes 1048592 | tf_op jit(solution)/shard_map/reduce_scatter | solution.py:1073
  431.4 8.8 %residual_backward.1 = (f32[256,2048]{1,0:T(8,128)}, bf16[256,2048]{1,0:T(8,128)(2,1)}, bf16[256,2048]{1,0:T(8,128)(2,1)}) custom-call(bf16[256,2048]{1,0:T(8,128)(2,1)} %reduce-scatter.6.cloned.1.call-done.back_ref, f32[256,2048]{1,0:T(8,128)} %get-tuple-element.411.residual_ref, f32[256,1]{1,0:T(8,128)} %copy.82.scale_ref, f32[1,2048]{1,0:T(1,128)} %bitcast.69, ...), custom_call_target="tpu_custom_call" | custom-call | flops 1 | bytes 1 | tf_op jit(solution)/shard_map/residual_backward/pallas_call | solution.py:536
  440.3 2.5 add_convert_fusion.4
  443.1 2.9 pad_maximum_fusion.2
  446.1 17.6 %all_to_all.19 = bf16[256,8,256]{2,0,1:T(8,128)(2,1)} all-to-all(bf16[256,8,256]{2,0,1:T(8,128)(2,1)S(1)} %bitcast.63), channel_id=1, replica_groups=mesh['do'=4,'di'=2,'tp'=4] {'di','tp'}, dimensions={1} | all-to-all | bytes 2097152 | tf_op jit(solution)/shard_map/all_to_all | solution.py:1106
  463.8 5.1 select_bitcast_fusion
  469.9 4.3 collective-permute-start.37
  474.2 2.6 collective-permute-done.29
  476.8 5.9 fusion
  487.3 33.0 %attn_backward.1 = (bf16[2048,2048]{1,0:T(8,128)(2,1)}, f32[1,2048]{1,0:T(1,128)}, bf16[512,384]{1,0:T(8,128)(2,1)}, bf16[512,384]{1,0:T(8,128)(2,1)}, bf16[512,...) custom-call(s32[1]{0:T(128)} %bitcast.1.refs_0_, bf16[512,640]{1,0:T(8,128)(2,1)} %copy-done.15, bf16[512,640]{1,0:T(8,128)(2,1)} %copy-done.20, ...), custom_call_target="tpu_custom_call" | custom-call | flops 1 | bytes 1 | tf_op jit(solution)/shard_map/attn_backward/pallas_call | solution.py:446
  523.1 11.3 %collective-permute-done.31 = f32[2,2048]{1,0:T(2,128)S(1)} collective-permute-done((f32[2,2048]{1,0:T(2,128)S(1)}, f32[2,2048]{1,0:T(2,128)S(1)}, u32[]{:S(2)}, u32[]{:S(2)}) %collective-permute-start.31) | collective-permute-done | bytes 16416 | tf_op jit(solution)/shard_map/ppermute | solution.py:752
  537.8 2.7 collective-permute-done.33
  545.7 4.5 convert_add_fusion.2
  550.4 4.4 collective-permute-start.39
  554.8 2.8 fusion.4
  559.2 4.2 copy-done
  563.4 3.3 out_weights.1
  568.1 17.0 %collective-permute-done.38 = bf16[512,1536]{1,0:T(8,128)(2,1)S(1)} collective-permute-done((bf16[512,1536]{1,0:T(8,128)(2,1)S(1)}, bf16[512,1536]{1,0:T(8,128)(2,1)S(1)}, u32[]{:S(2)}, u32[]{:S(2)}) %collective-permute-start.38) | collective-permute-done | bytes 1572896 | tf_op jit(solution)/shard_map/ppermute | solution.py:90
  585.1 2.2 collective-permute-done.39
  590.8 2.3 collective-permute-start.41
  593.2 23.4 %collective-permute-done.43.theirs_1 = bf16[256,1536]{1,0:T(8,128)(2,1)S(1)} collective-permute-done((bf16[256,1536]{1,0:T(8,128)(2,1)S(1)}, bf16[256,1536]{1,0:T(8,128)(2,1)S(1)}, u32[]{:S(2)}, u32[]{:S(2)}) %collective-permute-start.43) | collective-permute-done | bytes 786464 | tf_op jit(solution)/shard_map/ppermute | solution.py:163
  618.6 19.2 %collective-permute-done.44.theirs_2 = bf16[256,1536]{1,0:T(8,128)(2,1)S(1)} collective-permute-done((bf16[256,1536]{1,0:T(8,128)(2,1)S(1)}, bf16[256,1536]{1,0:T(8,128)(2,1)S(1)}, u32[]{:S(2)}, u32[]{:S(2)}) %collective-permute-start.44) | collective-permute-done | bytes 786464 | tf_op jit(solution)/shard_map/ppermute | solution.py:163
  638.7 17.6 %adamw_ffn.1 = (f32[256,2048]{1,0:T(8,128)}, f32[256,2048]{1,0:T(8,128)}, f32[256,2048]{1,0:T(8,128)}, f32[256,2048]{1,0:T(8,128)}, f32[256,2048]{1,0:T(8,128)},...) custom-call(s32[1]{0:T(128)} %bitcast.23.x_ref, ...), custom_call_target="tpu_custom_call" | custom-call | flops 1 | bytes 1 | tf_op jit(solution)/shard_map/adamw_ffn/pallas_call | solution.py:797
  658.3 2.3 collective-permute-start.46
  661.3 7.5 %finish.1 = (bf16[256,2048]{1,0:T(8,128)(2,1)}, f32[256,2048]{1,0:T(8,128)}) custom-call(s32[1]{0:T(128)} %bitcast.place_ref, bf16[256,2048]{1,0:T(8,128)(2,1)} %reduce-scatter.8.cloned.1.call-done.back_ref, bf16[256,2048]{1,0:T(8,128)(2,1)} %copy-done.6, f32[256,1]{1,0:T(8,128)} %copy.87.scale_ref, f32[1,2048]{1,0:T(1,128)} %bitcast.68, ...), custom_call_target="tpu_custom_call" | custom-call | flops 1 | bytes 1 | tf_op jit(solution)/shard_map/finish/pallas_call | solution.py:865
  670.4 5.5 adamw_attn.1
  (286 shorter events, 78.8 us)
Async XLA Ops:
  7.2 68.5 %all-gather.5.cloned.1.call-start = ((), (), s32[]{:S(2)}) async-start(), calls=%async_computation.4 | async-start | bytes 9437184 | tf_op jit(solution)/shard_map/all_gather | solution.py:937
  9.7 189.2 %copy-start.6 = (bf16[256,2048]{1,0:T(8,128)(2,1)}, bf16[256,2048]{1,0:T(8,128)(2,1)S(1)}, u32[]{:S(2)}) copy-start(bf16[256,2048]{1,0:T(8,128)(2,1)S(1)} %get-tuple-element.395.inputs_ref) | copy-start | bytes 3145732
  9.9 510.4 %copy-start.40 = (f32[2048]{0:T(1024)}, f32[2048]{0:T(1024)S(1)}, u32[]{:S(2)}) copy-start(f32[2048]{0:T(1024)S(1)} %maximum_select_fusion.8) | copy-start | bytes 24580
  11.3 185.3 %reduce-scatter.4.cloned.1.call-start = ((), (), s32[]{:S(2)}) async-start(), calls=%async_computation.5 | async-start | bytes 9437184 | tf_op jit(solution)/shard_map/reduce_scatter | solution.py:1021
  12.1 8.9 %collective-permute-start = (bf16[256,640]{1,0:T(8,128)(2,1)S(1)}, bf16[256,640]{1,0:T(8,128)(2,1)S(1)}, u32[]{:S(2)}, u32[]{:S(2)}) collective-permute-start(bf16[256,640]{1,0:T(8,128)(2,1)S(1)} %pad_maximum_fusion.17), channel_id=1, source_target_pairs={{0,4},{4,0},{1,5},{5,1},{2,6},{6,2},{3,7},{7,3},{8,12},{12,8},{9,1... | collective-permute-start | bytes 983048 | tf_op jit(solution)/shard_map/ppermute | solution.py:135
  13.4 7.5 %collective-permute-start.1 = (s32[2,1024]{1,0:T(2,128)S(1)}, s32[2,1024]{1,0:T(2,128)S(1)}, u32[]{:S(2)}, u32[]{:S(2)}) collective-permute-start(s32[2,1024]{1,0:T(2,128)S(1)} %pad_add_fusion.1), channel_id=1, source_target_pairs={{0,4},{4,0},{1,5},{5,1},{2,6},{6,2},{3,7},{7,3},{8,12},{12,8},{9,1... | collective-permute-start | bytes 24584 | tf_op jit(solution)/shard_map/ppermute | solution.py:940
  21.0 60.8 %copy-start.39 = (s32[1,2048]{1,0:T(1,128)}, s32[1,2048]{1,0:T(1,128)S(1)}, u32[]{:S(2)}) copy-start(s32[1,2048]{1,0:T(1,128)S(1)} %get-tuple-element.473) | copy-start | bytes 24580
  21.3 14.7 %collective-permute-start.2 = (bf16[512,640]{1,0:T(8,128)(2,1)S(1)}, bf16[512,640]{1,0:T(8,128)(2,1)S(1)}, u32[]{:S(2)}, u32[]{:S(2)}) collective-permute-start(bf16[512,640]{1,0:T(8,128)(2,1)S(1)} %pad_maximum_fusion.15.refs_1_), channel_id=1, source_target_pairs={{0,8},{8,0},{16,24},{24,16},{1,9},{9,1},{17,25},{25,17},{2,10},{10... | collective-permute-start | bytes 1966088 | tf_op jit(solution)/shard_map/ppermute | solution.py:53
  21.6 17.5 %collective-permute-start.3 = (bf16[512,640]{1,0:T(8,128)(2,1)S(1)}, bf16[512,640]{1,0:T(8,128)(2,1)S(1)}, u32[]{:S(2)}, u32[]{:S(2)}) collective-permute-start(bf16[512,640]{1,0:T(8,128)(2,1)S(1)} %pad_maximum_fusion.15.refs_1_), channel_id=1, source_target_pairs={{8,16},{16,8},{9,17},{17,9},{10,18},{18,10},{11,19},{19,11},{12,20... | collective-permute-start | bytes 1966088 | tf_op jit(solution)/shard_map/ppermute | solution.py:53
  31.5 21.4 %collective-permute-start.6 = (bf16[256,1536]{1,0:T(8,128)(2,1)S(1)}, bf16[256,1536]{1,0:T(8,128)(2,1)S(1)}, u32[]{:S(2)}, u32[]{:S(2)}) collective-permute-start(bf16[256,1536]{1,0:T(8,128)(2,1)S(1)} %pad_maximum_fusion.12), channel_id=1, source_target_pairs={{0,4},{4,0},{1,5},{5,1},{2,6},{6,2},{3,7},{7,3},{8,12},{12,8},{9,1... | collective-permute-start | bytes 2359304 | tf_op jit(solution)/shard_map/ppermute | solution.py:135
  39.1 15.7 %collective-permute-start.4 = (bf16[512,640]{1,0:T(8,128)(2,1)S(1)}, bf16[512,640]{1,0:T(8,128)(2,1)S(1)}, u32[]{:S(2)}, u32[]{:S(2)}) collective-permute-start(bf16[512,640]{1,0:T(8,128)(2,1)S(1)} %collective-permute-done.2.refs_2_), channel_id=1, source_target_pairs={{8,16},{16,8},{9,17},{17,9},{10,18},{18,10},{11,19},{19,11},{12,20... | collective-permute-start | bytes 1966088 | tf_op jit(solution)/shard_map/ppermute | solution.py:57
  42.2 13.4 %collective-permute-start.5 = (bf16[512,640]{1,0:T(8,128)(2,1)S(1)}, bf16[512,640]{1,0:T(8,128)(2,1)S(1)}, u32[]{:S(2)}, u32[]{:S(2)}) collective-permute-start(bf16[512,640]{1,0:T(8,128)(2,1)S(1)} %collective-permute-done.3.refs_5_), channel_id=1, source_target_pairs={{0,8},{8,0},{16,24},{24,16},{1,9},{9,1},{17,25},{25,17},{2,10},{10... | collective-permute-start | bytes 1966088 | tf_op jit(solution)/shard_map/ppermute | solution.py:57
  42.7 109.6 %copy-start.8 = (bf16[256,2048]{1,0:T(8,128)(2,1)}, bf16[256,2048]{1,0:T(8,128)(2,1)S(1)}, u32[]{:S(2)}) copy-start(bf16[256,2048]{1,0:T(8,128)(2,1)S(1)} %maximum_select_fusion.5.grad_ref) | copy-start | bytes 3145732
  55.5 13.3 %collective-permute-start.7 = (bf16[512,640]{1,0:T(8,128)(2,1)S(1)}, bf16[512,640]{1,0:T(8,128)(2,1)}, u32[]{:S(2)}, u32[]{:S(2)}) collective-permute-start(bf16[512,640]{1,0:T(8,128)(2,1)S(1)} %collective-permute-done.4.refs_3_), channel_id=1, source_target_pairs={{0,8},{8,0},{16,24},{24,16},{1,9},{9,1},{17,25},{25,17},{2,10},{10... | collective-permute-start | bytes 1966088 | tf_op jit(solution)/shard_map/ppermute | solution.py:61
  75.7 36.0 %collective-permute-start.8 = (bf16[512,1536]{1,0:T(8,128)(2,1)}, bf16[512,1536]{1,0:T(8,128)(2,1)}, u32[]{:S(2)}, u32[]{:S(2)}) collective-permute-start(bf16[512,1536]{1,0:T(8,128)(2,1)} %pad_maximum_fusion.7.refs_1_), channel_id=1, source_target_pairs={{0,8},{8,0},{16,24},{24,16},{1,9},{9,1},{17,25},{25,17},{2,10},{10... | collective-permute-start | bytes 4718600 | tf_op jit(solution)/shard_map/ppermute | solution.py:53
  76.0 38.6 %collective-permute-start.9 = (bf16[512,1536]{1,0:T(8,128)(2,1)}, bf16[512,1536]{1,0:T(8,128)(2,1)}, u32[]{:S(2)}, u32[]{:S(2)}) collective-permute-start(bf16[512,1536]{1,0:T(8,128)(2,1)} %pad_maximum_fusion.7.refs_1_), channel_id=1, source_target_pairs={{8,16},{16,8},{9,17},{17,9},{10,18},{18,10},{11,19},{19,11},{12,20... | collective-permute-start | bytes 4718600 | tf_op jit(solution)/shard_map/ppermute | solution.py:53
  80.2 31.0 %collective-permute-start.10 = (bf16[256,2048]{1,0:T(8,128)(2,1)S(1)}, bf16[256,2048]{1,0:T(8,128)(2,1)}, u32[]{:S(2)}, u32[]{:S(2)}) collective-permute-start(bf16[256,2048]{1,0:T(8,128)(2,1)S(1)} %maximum_select_fusion.5.grad_ref), channel_id=1, source_target_pairs={{0,2},{1,5},{2,0},{3,7},{4,6},{5,1},{6,4},{7,3},{8,10},{9,13},{10,... | collective-permute-start | bytes 3145736 | tf_op jit(solution)/shard_map/ppermute | solution.py:905
  80.6 30.6 %collective-permute-start.11 = (bf16[256,1536]{1,0:T(8,128)(2,1)}, bf16[256,1536]{1,0:T(8,128)(2,1)}, u32[]{:S(2)}, u32[]{:S(2)}) collective-permute-start(bf16[256,1536]{1,0:T(8,128)(2,1)} %pad_maximum_fusion.14), channel_id=1, source_target_pairs={{0,4},{4,0},{1,5},{5,1},{2,6},{6,2},{3,7},{7,3},{8,12},{12,8},{9,1... | collective-permute-start | bytes 2359304 | tf_op jit(solution)/shard_map/ppermute | solution.py:135
  114.6 164.3 %all-gather.7.cloned.1.call-start = ((), (), s32[]{:S(2)}) async-start(), calls=%async_computation.6 | async-start | bytes 9437184 | tf_op jit(solution)/shard_map/all_gather | solution.py:1044
  114.7 37.0 %collective-permute-start.12 = (bf16[512,1536]{1,0:T(8,128)(2,1)}, bf16[512,1536]{1,0:T(8,128)(2,1)}, u32[]{:S(2)}, u32[]{:S(2)}) collective-permute-start(bf16[512,1536]{1,0:T(8,128)(2,1)} %collective-permute-done.8.refs_2_), channel_id=1, source_target_pairs={{8,16},{16,8},{9,17},{17,9},{10,18},{18,10},{11,19},{19,11},{12,20... | collective-permute-start | bytes 4718600 | tf_op jit(solution)/shard_map/ppermute | solution.py:57
  117.7 34.6 %collective-permute-start.13 = (bf16[512,1536]{1,0:T(8,128)(2,1)}, bf16[512,1536]{1,0:T(8,128)(2,1)}, u32[]{:S(2)}, u32[]{:S(2)}) collective-permute-start(bf16[512,1536]{1,0:T(8,128)(2,1)} %collective-permute-done.9.refs_5_), channel_id=1, source_target_pairs={{0,8},{8,0},{16,24},{24,16},{1,9},{9,1},{17,25},{25,17},{2,10},{10... | collective-permute-start | bytes 4718600 | tf_op jit(solution)/shard_map/ppermute | solution.py:57
  117.8 14.3 %collective-permute-start.14 = (bf16[256,2048]{1,0:T(8,128)(2,1)}, bf16[256,2048]{1,0:T(8,128)(2,1)}, u32[]{:S(2)}, u32[]{:S(2)}) collective-permute-start(bf16[256,2048]{1,0:T(8,128)(2,1)} %collective-permute-done.10), channel_id=1, source_target_pairs={{0,4},{1,3},{2,6},{3,1},{4,0},{5,7},{6,2},{7,5},{8,12},{9,11},{10,... | collective-permute-start | bytes 3145736 | tf_op jit(solution)/shard_map/ppermute | solution.py:902
  119.1 27.5 %collective-permute-start.15 = (bf16[256,2048]{1,0:T(8,128)(2,1)S(1)}, bf16[256,2048]{1,0:T(8,128)(2,1)}, u32[]{:S(2)}, u32[]{:S(2)}) collective-permute-start(bf16[256,2048]{1,0:T(8,128)(2,1)S(1)} %maximum_select_fusion.5.grad_ref), channel_id=1, source_target_pairs={{0,4},{1,3},{2,6},{3,1},{4,0},{5,7},{6,2},{7,5},{8,12},{9,11},{10,... | collective-permute-start | bytes 3145736 | tf_op jit(solution)/shard_map/ppermute | solution.py:902
  156.6 9.7 %collective-permute-start.16 = (bf16[1024,2048]{1,0:T(8,128)(2,1)S(1)}, bf16[1024,2048]{1,0:T(8,128)(2,1)S(1)}, u32[]{:S(2)}, u32[]{:S(2)}) collective-permute-start(bf16[1024,2048]{1,0:T(8,128)(2,1)S(1)} %pad_maximum_fusion.1), channel_id=1, source_target_pairs={{0,1},{1,0},{2,3},{3,2},{4,5},{5,4},{6,7},{7,6},{8,9},{9,8},{10,11... | collective-permute-start | bytes 12582920 | tf_op jit(solution)/shard_map/ppermute | solution.py:908
  159.5 37.1 %collective-permute-start.17 = (bf16[512,1536]{1,0:T(8,128)(2,1)}, bf16[512,1536]{1,0:T(8,128)(2,1)S(1)}, u32[]{:S(2)}, u32[]{:S(2)}) collective-permute-start(bf16[512,1536]{1,0:T(8,128)(2,1)} %collective-permute-done.12.refs_3_), channel_id=1, source_target_pairs={{0,8},{8,0},{16,24},{24,16},{1,9},{9,1},{17,25},{25,17},{2,10},{10... | collective-permute-start | bytes 4718600 | tf_op jit(solution)/shard_map/ppermute | solution.py:61
  161.7 37.2 %copy-start.41 = (f32[2048]{0:T(1024)}, f32[2048]{0:T(1024)S(1)}, u32[]{:S(2)}) copy-start(f32[2048]{0:T(1024)S(1)} %maximum_select_fusion.10) | copy-start | bytes 24580
  201.1 155.4 %all-gather.9.cloned.1.call-start = ((), (), s32[]{:S(2)}) async-start(), calls=%async_computation.7 | async-start | bytes 9437184 | tf_op jit(solution)/shard_map/all_gather | solution.py:1052
  202.5 107.0 %copy-start.12 = (bf16[512,1536]{1,0:T(8,128)(2,1)}, bf16[512,1536]{1,0:T(8,128)(2,1)S(1)}, u32[]{:S(2)}) copy-start(bf16[512,1536]{1,0:T(8,128)(2,1)S(1)} %pad_maximum_fusion.8.refs_1_) | copy-start | bytes 4718596
  202.5 35.5 %collective-permute-start.18 = (bf16[512,1536]{1,0:T(8,128)(2,1)S(1)}, bf16[512,1536]{1,0:T(8,128)(2,1)S(1)}, u32[]{:S(2)}, u32[]{:S(2)}) collective-permute-start(bf16[512,1536]{1,0:T(8,128)(2,1)S(1)} %pad_maximum_fusion.8.refs_1_), channel_id=1, source_target_pairs={{0,8},{8,0},{16,24},{24,16},{1,9},{9,1},{17,25},{25,17},{2,10},{10... | collective-permute-start | bytes 4718600 | tf_op jit(solution)/shard_map/ppermute | solution.py:53
  203.8 36.8 %collective-permute-start.19 = (bf16[512,1536]{1,0:T(8,128)(2,1)S(1)}, bf16[512,1536]{1,0:T(8,128)(2,1)S(1)}, u32[]{:S(2)}, u32[]{:S(2)}) collective-permute-start(bf16[512,1536]{1,0:T(8,128)(2,1)S(1)} %pad_maximum_fusion.8.refs_1_), channel_id=1, source_target_pairs={{8,16},{16,8},{9,17},{17,9},{10,18},{18,10},{11,19},{19,11},{12,20... | collective-permute-start | bytes 4718600 | tf_op jit(solution)/shard_map/ppermute | solution.py:53
  238.0 71.5 %copy-start.26 = (bf16[512,1536]{1,0:T(8,128)(2,1)}, bf16[512,1536]{1,0:T(8,128)(2,1)S(1)}, u32[]{:S(2)}) copy-start(bf16[512,1536]{1,0:T(8,128)(2,1)S(1)} %collective-permute-done.18.refs_2_) | copy-start | bytes 4718596
  241.8 189.6 %reduce-scatter.6.cloned.1.call-start = ((), (), s32[]{:S(2)}) async-start(), calls=%async_computation.8 | async-start | bytes 9437184 | tf_op jit(solution)/shard_map/reduce_scatter | solution.py:1073
  241.8 36.0 %collective-permute-start.20 = (bf16[512,1536]{1,0:T(8,128)(2,1)S(1)}, bf16[512,1536]{1,0:T(8,128)(2,1)S(1)}, u32[]{:S(2)}, u32[]{:S(2)}) collective-permute-start(bf16[512,1536]{1,0:T(8,128)(2,1)S(1)} %collective-permute-done.18.refs_2_), channel_id=1, source_target_pairs={{8,16},{16,8},{9,17},{17,9},{10,18},{18,10},{11,19},{19,11},{12,20... | collective-permute-start | bytes 4718600 | tf_op jit(solution)/shard_map/ppermute | solution.py:57
  244.5 34.5 %collective-permute-start.21 = (bf16[512,1536]{1,0:T(8,128)(2,1)}, bf16[512,1536]{1,0:T(8,128)(2,1)}, u32[]{:S(2)}, u32[]{:S(2)}) collective-permute-start(bf16[512,1536]{1,0:T(8,128)(2,1)} %copy-done.27), channel_id=1, source_target_pairs={{0,8},{8,0},{16,24},{24,16},{1,9},{9,1},{17,25},{25,17},{2,10},{10... | collective-permute-start | bytes 4718600 | tf_op jit(solution)/shard_map/ppermute | solution.py:57
  279.0 43.7 %collective-permute-start.22 = (bf16[512,1536]{1,0:T(8,128)(2,1)}, bf16[512,1536]{1,0:T(8,128)(2,1)}, u32[]{:S(2)}, u32[]{:S(2)}) collective-permute-start(bf16[512,1536]{1,0:T(8,128)(2,1)} %copy-done.28), channel_id=1, source_target_pairs={{0,8},{8,0},{16,24},{24,16},{1,9},{9,1},{17,25},{25,17},{2,10},{10... | collective-permute-start | bytes 4718600 | tf_op jit(solution)/shard_map/ppermute | solution.py:61
  322.6 33.9 %collective-permute-start.23 = (bf16[256,1536]{1,0:T(8,128)(2,1)}, bf16[256,1536]{1,0:T(8,128)(2,1)S(1)}, u32[]{:S(2)}, u32[]{:S(2)}) collective-permute-start(bf16[256,1536]{1,0:T(8,128)(2,1)} %get-tuple-element.264), channel_id=1, source_target_pairs={{0,8},{8,0},{16,24},{24,16},{1,9},{9,1},{17,25},{25,17},{2,10},{10... | collective-permute-start | bytes 2359304 | tf_op jit(solution)/shard_map/ppermute | solution.py:1061
  324.9 31.6 %collective-permute-start.24 = (bf16[256,1536]{1,0:T(8,128)(2,1)}, bf16[256,1536]{1,0:T(8,128)(2,1)S(1)}, u32[]{:S(2)}, u32[]{:S(2)}) collective-permute-start(bf16[256,1536]{1,0:T(8,128)(2,1)} %get-tuple-element.265), channel_id=1, source_target_pairs={{0,8},{8,0},{16,24},{24,16},{1,9},{9,1},{17,25},{25,17},{2,10},{10... | collective-permute-start | bytes 2359304 | tf_op jit(solution)/shard_map/ppermute | solution.py:1061
  356.6 187.6 %all-gather.11.cloned.1.call-start = ((), (), s32[]{:S(2)}) async-start(), calls=%async_computation.9 | async-start | bytes 9437184 | tf_op jit(solution)/shard_map/all_gather | solution.py:1120
  359.6 34.9 %collective-permute-start.25 = (bf16[512,1536]{1,0:T(8,128)(2,1)}, bf16[512,1536]{1,0:T(8,128)(2,1)S(1)}, u32[]{:S(2)}, u32[]{:S(2)}) collective-permute-start(bf16[512,1536]{1,0:T(8,128)(2,1)} %add_convert_fusion.5), channel_id=1, source_target_pairs={{8,16},{16,8},{9,17},{17,9},{10,18},{18,10},{11,19},{19,11},{12,20... | collective-permute-start | bytes 4718600 | tf_op jit(solution)/shard_map/ppermute | solution.py:82
  361.5 33.0 %collective-permute-start.26 = (bf16[512,1536]{1,0:T(8,128)(2,1)}, bf16[512,1536]{1,0:T(8,128)(2,1)S(1)}, u32[]{:S(2)}, u32[]{:S(2)}) collective-permute-start(bf16[512,1536]{1,0:T(8,128)(2,1)} %add_convert_fusion.5), channel_id=1, source_target_pairs={{0,8},{8,0},{16,24},{24,16},{1,9},{9,1},{17,25},{25,17},{2,10},{10... | collective-permute-start | bytes 4718600 | tf_op jit(solution)/shard_map/ppermute | solution.py:82
  394.5 19.0 %collective-permute-start.27 = (bf16[256,1536]{1,0:T(8,128)(2,1)}, bf16[256,1536]{1,0:T(8,128)(2,1)}, u32[]{:S(2)}, u32[]{:S(2)}) collective-permute-start(bf16[256,1536]{1,0:T(8,128)(2,1)} %get-tuple-element.283), channel_id=1, source_target_pairs={{0,8},{8,0},{16,24},{24,16},{1,9},{9,1},{17,25},{25,17},{2,10},{10... | collective-permute-start | bytes 2359304 | tf_op jit(solution)/shard_map/ppermute | solution.py:1085
  413.5 26.7 %collective-permute-start.28 = (bf16[256,1536]{1,0:T(8,128)(2,1)}, bf16[256,1536]{1,0:T(8,128)(2,1)}, u32[]{:S(2)}, u32[]{:S(2)}) collective-permute-start(bf16[256,1536]{1,0:T(8,128)(2,1)} %get-tuple-element.290), channel_id=1, source_target_pairs={{0,8},{8,0},{16,24},{24,16},{1,9},{9,1},{17,25},{25,17},{2,10},{10... | collective-permute-start | bytes 2359304 | tf_op jit(solution)/shard_map/ppermute | solution.py:1089
  463.8 192.7 %reduce-scatter.8.cloned.1.call-start = ((), (), s32[]{:S(2)}) async-start(), calls=%async_computation.10 | async-start | bytes 9437184 | tf_op jit(solution)/shard_map/reduce_scatter | solution.py:1135
  468.9 7.9 %collective-permute-start.29 = (bf16[4,256,2048]{2,1,0:T(8,128)(2,1)}, bf16[4,256,2048]{2,1,0:T(8,128)(2,1)}, u32[]{:S(2)}, u32[]{:S(2)}) collective-permute-start(bf16[4,256,2048]{2,1,0:T(8,128)(2,1)} %select_bitcast_fusion), channel_id=1, source_target_pairs={{0,1},{1,0},{2,3},{3,2},{4,5},{5,4},{6,7},{7,6},{8,9},{9,8},{10,11... | collective-permute-start | bytes 12582920 | tf_op jit(solution)/shard_map/ppermute | solution.py:908
  469.7 74.5 %collective-permute-start.36 = (bf16[1024,1536]{1,0:T(8,128)(2,1)}, bf16[1024,1536]{1,0:T(8,128)(2,1)}, u32[]{:S(2)}, u32[]{:S(2)}) collective-permute-start(bf16[1024,1536]{1,0:T(8,128)(2,1)} %get-tuple-element.315), channel_id=1, source_target_pairs={{0,8},{8,0},{16,24},{24,16},{1,9},{9,1},{17,25},{25,17},{2,10},{10... | collective-permute-start | bytes 9437192 | tf_op jit(solution)/shard_map/ppermute | solution.py:1104
  469.9 74.2 %collective-permute-start.37 = (bf16[1024,1536]{1,0:T(8,128)(2,1)}, bf16[1024,1536]{1,0:T(8,128)(2,1)}, u32[]{:S(2)}, u32[]{:S(2)}) collective-permute-start(bf16[1024,1536]{1,0:T(8,128)(2,1)} %get-tuple-element.316), channel_id=1, source_target_pairs={{8,16},{16,8},{9,17},{17,9},{10,18},{18,10},{11,19},{19,11},{12,20... | collective-permute-start | bytes 9437192 | tf_op jit(solution)/shard_map/ppermute | solution.py:1105
  486.1 58.1 %collective-permute-start.35 = (bf16[2,256,2048]{2,1,0:T(8,128)(2,1)}, bf16[2,256,2048]{2,1,0:T(8,128)(2,1)}, u32[]{:S(2)}, u32[]{:S(2)}) collective-permute-start(bf16[2,256,2048]{2,1,0:T(8,128)(2,1)} %pad_maximum_fusion.6), channel_id=1, source_target_pairs={{0,4},{1,3},{2,6},{3,1},{4,0},{5,7},{6,2},{7,5},{8,12},{9,11},{10,... | collective-permute-start | bytes 6291464 | tf_op jit(solution)/shard_map/ppermute | solution.py:902
  521.1 1.4 collective-permute-start.30
  522.6 11.8 %collective-permute-start.31 = (f32[2,2048]{1,0:T(2,128)S(1)}, f32[2,2048]{1,0:T(2,128)S(1)}, u32[]{:S(2)}, u32[]{:S(2)}) collective-permute-start(f32[2,2048]{1,0:T(2,128)S(1)} %add.163), channel_id=1, source_target_pairs={{0,2},{1,3},{2,0},{3,1},{4,6},{5,7},{6,4},{7,5},{8,10},{9,11},{10,... | collective-permute-start | bytes 49160 | tf_op jit(solution)/shard_map/ppermute | solution.py:752
  534.4 3.1 collective-permute-start.32
  537.5 3.1 collective-permute-start.33
  540.6 3.6 collective-permute-start.34
  550.2 34.9 %collective-permute-start.38 = (bf16[512,1536]{1,0:T(8,128)(2,1)S(1)}, bf16[512,1536]{1,0:T(8,128)(2,1)S(1)}, u32[]{:S(2)}, u32[]{:S(2)}) collective-permute-start(bf16[512,1536]{1,0:T(8,128)(2,1)S(1)} %get-tuple-element.405), channel_id=1, source_target_pairs={{0,8},{8,0},{16,24},{24,16},{1,9},{9,1},{17,25},{25,17},{2,10},{10... | collective-permute-start | bytes 4718600 | tf_op jit(solution)/shard_map/ppermute | solution.py:90
  550.4 37.0 %collective-permute-start.39 = (bf16[512,1536]{1,0:T(8,128)(2,1)S(1)}, bf16[512,1536]{1,0:T(8,128)(2,1)S(1)}, u32[]{:S(2)}, u32[]{:S(2)}) collective-permute-start(bf16[512,1536]{1,0:T(8,128)(2,1)S(1)} %get-tuple-element.406), channel_id=1, source_target_pairs={{8,16},{16,8},{9,17},{17,9},{10,18},{18,10},{11,19},{19,11},{12,20... | collective-permute-start | bytes 4718600 | tf_op jit(solution)/shard_map/ppermute | solution.py:90
  557.5 98.8 %collective-permute-start.45 = (bf16[256,2048]{1,0:T(8,128)(2,1)}, bf16[256,2048]{1,0:T(8,128)(2,1)}, u32[]{:S(2)}, u32[]{:S(2)}) collective-permute-start(bf16[256,2048]{1,0:T(8,128)(2,1)} %fusion.4), channel_id=1, source_target_pairs={{0,2},{1,5},{2,0},{3,7},{4,6},{5,1},{6,4},{7,3},{8,10},{9,13},{10,... | collective-permute-start | bytes 3145736 | tf_op jit(solution)/shard_map/ppermute | solution.py:905
  558.8 57.7 %collective-permute-start.43 = (bf16[256,1536]{1,0:T(8,128)(2,1)S(1)}, bf16[256,1536]{1,0:T(8,128)(2,1)S(1)}, u32[]{:S(2)}, u32[]{:S(2)}) collective-permute-start(bf16[256,1536]{1,0:T(8,128)(2,1)S(1)} %select_convert_fusion.1), channel_id=1, source_target_pairs={{0,4},{4,0},{1,5},{5,1},{2,6},{6,2},{3,7},{7,3},{8,12},{12,8},{9,1... | collective-permute-start | bytes 2359304 | tf_op jit(solution)/shard_map/ppermute | solution.py:163
  589.4 27.2 %copy-start.44 = (f32[2048]{0:T(1024)S(1)}, f32[2048]{0:T(1024)}, u32[]{:S(2)}) copy-start(f32[2048]{0:T(1024)} %param.57) | copy-start | bytes 24580
  589.6 48.3 %collective-permute-start.44 = (bf16[256,1536]{1,0:T(8,128)(2,1)S(1)}, bf16[256,1536]{1,0:T(8,128)(2,1)S(1)}, u32[]{:S(2)}, u32[]{:S(2)}) collective-permute-start(bf16[256,1536]{1,0:T(8,128)(2,1)S(1)} %select_convert_fusion), channel_id=1, source_target_pairs={{0,4},{4,0},{1,5},{5,1},{2,6},{6,2},{3,7},{7,3},{8,12},{12,8},{9,1... | collective-permute-start | bytes 2359304 | tf_op jit(solution)/shard_map/ppermute | solution.py:163
  590.7 27.9 %copy-start.47 = (f32[1,2048]{1,0:T(1,128)}, f32[1,2048]{1,0:T(1,128)S(1)}, u32[]{:S(2)}) copy-start(f32[1,2048]{1,0:T(1,128)S(1)} %get-tuple-element.465) | copy-start | bytes 24580
  590.7 69.9 %copy-start.48 = (f32[1,2048]{1,0:T(1,128)}, f32[1,2048]{1,0:T(1,128)S(1)}, u32[]{:S(2)}) copy-start(f32[1,2048]{1,0:T(1,128)S(1)} %get-tuple-element.466) | copy-start | bytes 24580
  590.7 65.7 %collective-permute-start.40 = (bf16[512,640]{1,0:T(8,128)(2,1)S(1)}, bf16[512,640]{1,0:T(8,128)(2,1)}, u32[]{:S(2)}, u32[]{:S(2)}) collective-permute-start(bf16[512,640]{1,0:T(8,128)(2,1)S(1)} %get-tuple-element.329), channel_id=1, source_target_pairs={{0,8},{8,0},{16,24},{24,16},{1,9},{9,1},{17,25},{25,17},{2,10},{10... | collective-permute-start | bytes 1966088 | tf_op jit(solution)/shard_map/ppermute | solution.py:99
  590.8 65.6 %collective-permute-start.41 = (bf16[512,640]{1,0:T(8,128)(2,1)S(1)}, bf16[512,640]{1,0:T(8,128)(2,1)}, u32[]{:S(2)}, u32[]{:S(2)}) collective-permute-start(bf16[512,640]{1,0:T(8,128)(2,1)S(1)} %get-tuple-element.330), channel_id=1, source_target_pairs={{0,16},{8,24},{16,0},{24,8},{1,17},{9,25},{17,1},{25,9},{2,18},{10... | collective-permute-start | bytes 1966088 | tf_op jit(solution)/shard_map/ppermute | solution.py:99
  616.5 39.9 %collective-permute-start.42 = (bf16[512,640]{1,0:T(8,128)(2,1)S(1)}, bf16[512,640]{1,0:T(8,128)(2,1)}, u32[]{:S(2)}, u32[]{:S(2)}) collective-permute-start(bf16[512,640]{1,0:T(8,128)(2,1)S(1)} %get-tuple-element.331), channel_id=1, source_target_pairs={{0,24},{8,16},{16,8},{24,0},{1,25},{9,17},{17,9},{25,1},{2,26},{10... | collective-permute-start | bytes 1966088 | tf_op jit(solution)/shard_map/ppermute | solution.py:99
  658.3 11.3 %collective-permute-start.46 = (bf16[256,640]{1,0:T(8,128)(2,1)S(1)}, bf16[256,640]{1,0:T(8,128)(2,1)S(1)}, u32[]{:S(2)}, u32[]{:S(2)}) collective-permute-start(bf16[256,640]{1,0:T(8,128)(2,1)S(1)} %select_convert_fusion.2), channel_id=1, source_target_pairs={{0,4},{4,0},{1,5},{5,1},{2,6},{6,2},{3,7},{7,3},{8,12},{12,8},{9,1... | collective-permute-start | bytes 983048 | tf_op jit(solution)/shard_map/ppermute | solution.py:163
  (50 other events, 248.4 us)
Sparse Core Ops, SparseCore 0:
  11.4 64.2 all-gather.4
  114.7 73.6 reduce-scatter.3
  201.2 53.1 all-gather.6
  256.4 54.3 all-gather.8
  356.7 74.6 reduce-scatter.5
  463.9 66.3 all-gather.10
  544.3 96.1 reduce-scatter.7

commit v7 on v6

--- a/solution.py
+++ b/solution.py
@@ -54,7 +54,8 @@
 
 
 def line_far(near, across):
-    return lax.ppermute(near, "do", MIDDLE), lax.ppermute(across, "do", NEAR)
+    out = lax.ppermute(across, "do", NEAR)
+    return lax.ppermute(near, "do", MIDDLE), out
 
 
 def line_last(across_near, perm=NEAR):
@@ -79,7 +80,8 @@
 
 def sum_middle(parts, far):
     second = add_inner(parts[2], cat(far, 0)).astype(LOW)
-    return lax.ppermute(second, "do", MIDDLE), lax.ppermute(second, "do", NEAR)
+    inward = lax.ppermute(second, "do", NEAR)
+    return lax.ppermute(second, "do", MIDDLE), inward
 
 
 def sum_near_parts(parts, crossed, inward):
@@ -313,23 +315,30 @@
     keys, values = split_kv(both)
     allowed = allowed_pairs(col_ref[...], row_ref[0])
     lane = lanes_of((both.shape[0], 128))
-    log_sums = jnp.zeros((both.shape[0], 128), F32)
+    log_sums = [jnp.zeros((both.shape[0] // 2, 128), F32)] * 2
     contexts = []
+    half = both.shape[0] // 2
     for pair in range(pairs):
-        heads = queries[:, pair * 128 : (pair + 1) * 128]
-        context = None
-        for side in range(2):
-            scores = dot(heads, keys[side], 1, 1) * HD**-0.5
-            masked = jnp.where(allowed, scores, -1e30)
-            top = jnp.max(masked, axis=1, keepdims=True)
-            weights = jnp.exp(masked - top)
-            totals = jnp.sum(weights, axis=1, keepdims=True)
-            probs = (weights * (1.0 / totals)).astype(LOW)
-            piece = dot(probs, values[side], 1, 0)
-            context = piece if context is None else context + piece
-            log_sums = jnp.where(lane == 2 * pair + side, top + jnp.log(totals), log_sums)
-        contexts.append(context.astype(LOW))
-    lse_ref[...] = log_sums
+        bands = []
+        for low, high in ((0, half), (half, 2 * half)):
+            heads = queries[low:high, pair * 128 : (pair + 1) * 128]
+            context = None
+            for side in range(2):
+                scores = dot(heads, keys[side][:high], 1, 1) * HD**-0.5
+                masked = jnp.where(allowed[low:high, :high], scores, -1e30)
+                top = jnp.max(masked, axis=1, keepdims=True)
+                weights = jnp.exp(masked - top)
+                totals = jnp.sum(weights, axis=1, keepdims=True)
+                probs = (weights * (1.0 / totals)).astype(LOW)
+                piece = dot(probs, values[side][:high], 1, 0)
+                context = piece if context is None else context + piece
+                at = 2 * pair + side
+                log_sums[low // half] = jnp.where(
+                    lane[:half] == at, top + jnp.log(totals), log_sums[low // half]
+                )
+            bands.append(context.astype(LOW))
+        contexts.append(cat(bands, 0))
+    lse_ref[...] = cat(log_sums, 0)
     context_low = cat(contexts, 1)
     ctx_ref[...] = context_low
     part_ref[...] = dot(context_low, wout_ref[...], 1, 0).astype(LOW)
@@ -993,11 +1002,11 @@
             near, across, cosine, sine, own_2, other_2
         )
         across_near, out = line_far(near, across)
-        across_near, out, theirs_1 = fence(across_near, out, theirs_1)
+        out, across_near, theirs_1 = fence(out, across_near, theirs_1)
         out_near = line_last(across_near)
         block_1 = plan.join(own_1, theirs_1)
-        out_near, normed_all, block_1, grad_low, other_2, seg_col, seg_row = fence(
-            out_near, normed_all, block_1, grad_low, other_2, seg_col, seg_row
+        out_near, block_1, grad_low, other_2, seg_col, seg_row = fence(
+            out_near, block_1, grad_low, other_2, seg_col, seg_row
         )
         attn_weights = (attn_block, near, across_near, out, across, (out_near,))
         near_1, across_1 = line_near(block_1)
@@ -1021,8 +1030,8 @@
     attn_sum = lax.psum_scatter(attn_part, axes, scatter_dimension=0, tiled=True)
     grad_xy = plane.swap_first(grad_second)
     if plan.line:
-        across_near_1, out_1, grad_xy, theirs_2, grad_first = fence(
-            across_near_1, out_1, grad_xy, theirs_2, grad_first
+        out_1, across_near_1, grad_xy, theirs_2, grad_first = fence(
+            out_1, across_near_1, grad_xy, theirs_2, grad_first
         )
         block_2 = plan.join(own_2, theirs_2)
         out_near_1 = line_last(across_near_1)
@@ -1031,13 +1040,14 @@
     over_y = cat([pick(plane.y, grad_low, grad_y), pick(plane.y, grad_y, grad_low)], 0)
     over_xy = cat([pick(plane.y, grad_x, grad_xy), pick(plane.y, grad_xy, grad_x)], 0)
     grad_core = cat([by_x(over_y, over_xy), by_x(over_xy, over_y)], 0)
+    if plan.line:
+        attn_sum, out_near_1, grad_core, block_2 = fence(
+            attn_sum, out_near_1, grad_core, block_2
+        )
     grad_other = plane.swap_core(grad_core)
     groups = (rows // own_rows // 2, 1, own_rows, width)
     mine, theirs = grad_core.reshape(groups), grad_other.reshape(groups)
     grad_all = cat([pick(core, mine, theirs), pick(core, theirs, mine)], 1).reshape(rows, width)
-
-    if plan.line:
-        attn_sum, grad_all, out_near_1 = fence(attn_sum, grad_all, out_near_1)
     residual = inputs_f + attn_sum.astype(F32)
     normed_two, scale_two = norm_rows(residual, gain_two)
     two_low = normed_two.astype(LOW)
@@ -1047,18 +1057,21 @@
         first_weights = (block_1, near_1, across_near_1, out_1, across_1, (out_near_1,))
         block_2, _ = fence(block_2, two_low)
         near_2, across_2 = line_near(block_2)
-        near_2, across_2, wout = fence(near_2, across_2, wout)
+        near_2, across_2, wout, grad_all = fence(near_2, across_2, wout, grad_all)
         across_near_2, out_2 = line_far(near_2, across_2)
     wout_all = lax.all_gather(wout, axes, axis=0, tiled=True)
-    if plan.line:
-        two_all, across_near_2, out_2 = fence(two_all, across_near_2, out_2)
-        out_near_2 = line_last(across_near_2)
     first = Loader(plan, first_weights, *ffn_shapes)
     back_1, act_1, both_1, down_1 = ffn_main(first, two_all, grad_all, None)
     if plan.line:
+        back_1, act_1, both_1, out_2, across_near_2 = fence(
+            back_1, act_1, both_1, out_2, across_near_2
+        )
+        out_near_2 = line_last(across_near_2, OUTWARD)
         *last_1, third_1 = ffn_weights(plan, two_all, grad_all, act_1, both_1, (3, 2))
-        back_1, last_1, out_near_2 = fence(back_1, last_1, out_near_2)
-        far_1 = [lax.ppermute(part, "do", NEAR) for part in last_1]
+        last_1, both_1 = fence(last_1, both_1)
+        far_1 = [lax.ppermute(part, "do", INWARD) for part in last_1]
+        (rest_1,) = ffn_weights(plan, two_all, grad_all, act_1, both_1, (0, 1))
+        back_1, rest_1, out_near_2 = fence(back_1, rest_1, out_near_2)
         second_weights = (block_2, near_2, across_near_2, out_2, across_2, (out_near_2,))
     else:
         grads_1 = ffn_weights(plan, two_all, grad_all, act_1, both_1, (0, 1, 2, 3))
@@ -1075,10 +1088,8 @@
     grads_2 = ffn_weights(plan, two_all, grad_all, act_2, both_2, order)
     if plan.line:
         *last_2, rest_2 = grads_2
-        act_1, rest_2 = fence(act_1, rest_2)
-        (rest_1,) = ffn_weights(plan, two_all, grad_all, act_1, both_1, (0, 1))
-        act_2, rest_1, crossed_1, inward_1, last_2 = fence(
-            act_2, rest_1, crossed_1, inward_1, last_2
+        act_2, rest_2, inward_1, crossed_1, last_2 = fence(
+            act_2, rest_2, inward_1, crossed_1, last_2
         )
         grads_1 = [rest_1[:block], rest_1[block:], third_1, cat(last_1, 0)]
         grads_2 = [rest_2[:block], rest_2[block : 2 * block], rest_2[2 * block :], cat(last_2, 0)]

time: 692 us -> 673 us (0.973)
  waiting for transfers between devices: 255 us -> 229 us
    ppermute x6, waiting for transfers between devices: 42.8 us -> 17.7 us  [line_near(): return (lax.ppermute(own, 'do', NEAR), lax.ppermute(own, 'do', MIDDLE))]
    ppermute x10, waiting for transfers between devices: 41.6 us -> 17.9 us  [the longest x1 7.33 us: sum_middle(): inward = lax.ppermute(second, 'do', NEAR)]
    reduce_scatter x1, waiting for transfers between devices: 0.01 us -> 14.5 us  [on_device(): lax.psum_scatter(attn_part, axes, scatter_dimension=0, tiled=True)]
    ppermute x3, waiting for transfers between devices: 21 us -> 32.9 us  [line_last(): return lax.ppermute(across_near, 'do', perm)]
    all_gather x1, waiting for transfers between devices: 0.01 us -> 11.8 us  [on_device(): two_all = lax.all_gather(two_low, axes, axis=0, tiled=True)]
  transfers between devices with their start and end apart: 54 -> 54, of which waited for: 31 -> 33; matrix products, arithmetic and copies ran while one was open for 12% -> 12% of each run, Pallas kernels for 32% -> 33%
where the time goes in v7:
time: 673 us; the launch traced here: 664 us
  waiting for transfers between devices  229 us (34%)
  Pallas kernels  224 us (33%)
  other arithmetic  80.6 us (12%)
  starting transfers between devices  69.8 us (10%)
  local copies, waits for them, and re-layouts  26.9 us (4%)
  blocking collectives  17.6 us (3%)
  between operations  15.9 us (2%)
    pallas_call x2, Pallas kernels, ffn_main(): pl.pallas_call(functools.partial(ffn_main_kernel, loader, len(more)), gri...  62.3 us
    pallas_call x3, Pallas kernels, ffn_weights(): pl.pallas_call(functools.partial(ffn_weights_kernel, plan), grid=(count,)...  47.7 us
    ppermute x3, waiting for transfers between devices, trade(): theirs = lax.ppermute(self.by_x(high, low).astype(LOW), 'di', PAIR)  42.6 us
    pallas_call x1, Pallas kernels, attn_backward(): pl.pallas_call(functools.partial(attn_backward_kernel, heads // 128, load...  33 us
    ppermute x3, waiting for transfers between devices, line_last(): return lax.ppermute(across_near, 'do', perm)  32.9 us
    ppermute x3, waiting for transfers between devices, swap_first(): return lax.ppermute(value, self.axes, self.pairs(True))  24 us
    pallas_call x1, Pallas kernels, attn_forward(): pl.pallas_call(functools.partial(attn_forward_kernel, heads // 128, loade...  22.4 us
    concatenate x15, other arithmetic, cat(): return jnp.concatenate(parts, axis)  19.4 us
  transfers between devices with their start and end apart: 54, of which 33 were waited for; matrix products, arithmetic and copies ran while one was open for 12% of the time, Pallas kernels for 33%

profile of v7, /device:TPU:9, one launch (start us, length us, event | category | flops | bytes accessed | tf_op | source)
XLA Modules:
  0.0 664.5 jit_solution(8606930572639915649)
XLA Ops:
  18.2 2.8 collective-permute-done.1
  21.6 4.2 collective-permute-start.3
  25.9 3.7 fusion.5
  36.1 3.0 collective-permute-done.3.refs_5_
  39.1 3.1 collective-permute-start.5
  42.7 10.2 %collective-permute-done.6 = bf16[256,1536]{1,0:T(8,128)(2,1)S(1)} collective-permute-done((bf16[256,1536]{1,0:T(8,128)(2,1)S(1)}, bf16[256,1536]{1,0:T(8,128)(2,1)S(1)}, u32[]{:S(2)}, u32[]{:S(2)}) %collective-permute-start.6) | collective-permute-done | bytes 786464 | tf_op jit(solution)/shard_map/ppermute | solution.py:137
  57.5 9.2 %collective-permute-done.7.refs_6_ = bf16[512,640]{1,0:T(8,128)(2,1)S(1)} collective-permute-done((bf16[512,640]{1,0:T(8,128)(2,1)S(1)}, bf16[512,640]{1,0:T(8,128)(2,1)S(1)}, u32[]{:S(2)}, u32[]{:S(2)}) %collective-permute-start.7) | collective-permute-done | bytes 655392 | tf_op jit(solution)/shard_map/ppermute | solution.py:62
  69.0 5.2 collective-permute-start.9
  77.0 22.4 %attn_forward.1 = (bf16[2048,2048]{1,0:T(8,128)(2,1)}, bf16[2048,256]{1,0:T(8,128)(2,1)}, bf16[2048,256]{1,0:T(8,128)(2,1)}, bf16[2048,128]{1,0:T(8,128)(2,1)}, ...) custom-call(s32[1]{0:T(128)} %bitcast.1.refs_0_, bf16[512,640]{1,0:T(8,128)(2,1)} %copy-done.15, ...), custom_call_target="tpu_custom_call" | custom-call | flops 1 | bytes 1 | tf_op jit(solution)/shard_map/attn_forward/pallas_call | solution.py:416
  99.4 5.7 collective-permute-done.11
  105.3 3.2 collective-permute-start.13
  110.1 12.7 %collective-permute-done.14 = bf16[256,2048]{1,0:T(8,128)(2,1)} collective-permute-done((bf16[256,2048]{1,0:T(8,128)(2,1)}, bf16[256,2048]{1,0:T(8,128)(2,1)}, u32[]{:S(2)}, u32[]{:S(2)}) %collective-permute-start.14) | collective-permute-done | bytes 1048608 | tf_op jit(solution)/shard_map/ppermute | solution.py:911
  122.8 11.2 %collective-permute-done.15 = bf16[256,2048]{1,0:T(8,128)(2,1)} collective-permute-done((bf16[256,2048]{1,0:T(8,128)(2,1)S(1)}, bf16[256,2048]{1,0:T(8,128)(2,1)}, u32[]{:S(2)}, u32[]{:S(2)}) %collective-permute-start.15) | collective-permute-done | bytes 1048608 | tf_op jit(solution)/shard_map/ppermute | solution.py:911
  134.1 2.9 collective-permute-done.12.refs_4_
  145.2 2.6 pad_maximum_fusion.1
  147.8 19.7 %collective-permute-done.16.refs_6_ = bf16[512,1536]{1,0:T(8,128)(2,1)} collective-permute-done((bf16[512,1536]{1,0:T(8,128)(2,1)}, bf16[512,1536]{1,0:T(8,128)(2,1)}, u32[]{:S(2)}, u32[]{:S(2)}) %collective-permute-start.16) | collective-permute-done | bytes 1572896 | tf_op jit(solution)/shard_map/ppermute | solution.py:62
  167.5 14.5 %reduce-scatter.4.cloned.1.call-done = bf16[256,2048]{1,0:T(8,128)(2,1)} async-done(((bf16[2048,2048]{1,0:T(8,128)(2,1)}), bf16[256,2048]{1,0:T(8,128)(2,1)}) %reduce-scatter.4.cloned.1.call-update) | async-done | bytes 1048592 | tf_op jit(solution)/shard_map/reduce_scatter | solution.py:1030
  187.0 4.0 collective-permute-start.18
  191.1 2.7 collective-permute-done.19
  193.7 4.2 broadcast_select_fusion.1
  197.9 6.3 pad_maximum_fusion
  204.2 8.3 %copy.81 = bf16[4,2,256,2048]{3,2,1,0:T(8,128)(2,1)} copy(bf16[4,2,256,2048]{3,2,0,1:T(8,128)(2,1)} %pad_maximum_fusion) | data formatting | bytes 16777216 | tf_op jit(solution)/shard_map/concatenate | solution.py:45
  212.6 10.3 %collective-permute-done.17.refs_2_ = bf16[512,1536]{1,0:T(8,128)(2,1)} collective-permute-done((bf16[512,1536]{1,0:T(8,128)(2,1)S(1)}, bf16[512,1536]{1,0:T(8,128)(2,1)}, u32[]{:S(2)}, u32[]{:S(2)}) %collective-permute-start.17) | collective-permute-done | bytes 1572896 | tf_op jit(solution)/shard_map/ppermute | solution.py:53
  222.8 2.8 collective-permute-done.18.refs_5_
  225.8 3.3 collective-permute-start.21
  229.1 11.8 %all-gather.7.cloned.1.call-done.refs_7_.x_ref = bf16[2048,2048]{1,0:T(8,128)(2,1)} async-done(((bf16[256,2048]{1,0:T(8,128)(2,1)}), bf16[2048,2048]{1,0:T(8,128)(2,1)}) %all-gather.7.cloned.1.call-update) | async-done | bytes 8388624 | tf_op jit(solution)/shard_map/all_gather | solution.py:1054
  240.9 30.3 %ffn_main.2 = (bf16[2048,2048]{1,0:T(8,128)(2,1)}, bf16[2048,512]{1,0:T(8,128)(2,1)}, bf16[2048,1024]{1,0:T(8,128)(2,1)}, bf16[512,2048]{1,0:T(8,128)(2,1)}) custom-call(s32[1]{0:T(128)} %bitcast.1.refs_0_, bf16[512,1536]{1,0:T(8,128)(2,1)} %pad_maximum_fusion.7.refs_1_, bf16[512,1536]{1,0:T(8,128)(2,1)} %collective-permute-done.8.refs_2_, ...), custom_call_target="tpu_custom_call" | custom-call | flops 1 | bytes 1 | tf_op jit(solution)/shard_map/ffn_main/pallas_call | solution.py:604
  271.3 3.3 collective-permute-start.22
  274.6 13.1 %ffn_weights.3 = (bf16[256,1536]{1,0:T(8,128)(2,1)}, bf16[256,1536]{1,0:T(8,128)(2,1)}, bf16[512,1536]{1,0:T(8,128)(2,1)}) custom-call(bf16[2048,2048]{1,0:T(8,128)(2,1)} %all-gather.7.cloned.1.call-done.refs_7_.x_ref, bf16[2048,2048]{1,0:T(8,128)(2,1)} %bitcast.54, bf16[2048,512]{1,0:T(8,128)(2,1)} %get-tuple-element.284.act_ref.act_1, ...), custom_call_target="tpu_custom_call" | custom-call | flops 1 | bytes 1 | tf_op jit(solution)/shard_map/ffn_weights/pallas_call | solution.py:686
  290.7 12.2 %ffn_weights.4 = bf16[1024,1536]{1,0:T(8,128)(2,1)} custom-call(bf16[2048,2048]{1,0:T(8,128)(2,1)} %all-gather.7.cloned.1.call-done.refs_7_.x_ref, bf16[2048,2048]{1,0:T(8,128)(2,1)} %bitcast.55, bf16[2048,512]{1,0:T(8,128)(2,1)} %get-tuple-element.284.act_ref.act_1, bf16[2048,1024]{1,0:T(8,128)(2,1)} %get-tuple-element.265.both_ref), custom_call_target="tpu_custom_call" | custom-call | flops 1 | bytes 1 | tf_op jit(solution)/shard_map/ffn_weights/pallas_call | solution.py:686
  303.0 4.0 collective-permute-done.22.refs_6_
  307.0 32.0 %ffn_main.3 = (bf16[2048,2048]{1,0:T(8,128)(2,1)}, bf16[2048,512]{1,0:T(8,128)(2,1)}, bf16[2048,1024]{1,0:T(8,128)(2,1)}, bf16[512,2048]{1,0:T(8,128)(2,1)}) custom-call(s32[1]{0:T(128)} %bitcast.1.refs_0_, bf16[512,1536]{1,0:T(8,128)(2,1)} %pad_maximum_fusion.8.refs_1_, bf16[512,1536]{1,0:T(8,128)(2,1)} %collective-permute-done.17.refs_2_, ...), custom_call_target="tpu_custom_call" | custom-call | flops 1 | bytes 1 | tf_op jit(solution)/shard_map/ffn_main/pallas_call | solution.py:604
  340.4 3.0 add_convert_fusion.5
  345.4 4.2 collective-permute-start.26
  349.6 22.4 %ffn_weights.5 = (bf16[256,1536]{1,0:T(8,128)(2,1)}, bf16[256,1536]{1,0:T(8,128)(2,1)}, bf16[1536,1536]{1,0:T(8,128)(2,1)}) custom-call(bf16[2048,2048]{1,0:T(8,128)(2,1)} %all-gather.7.cloned.1.call-done.refs_7_.x_ref, bf16[2048,2048]{1,0:T(8,128)(2,1)} %bitcast.57, bf16[2048,512]{1,0:T(8,128)(2,1)} %get-tuple-element.285.act_ref.act_2, ...), custom_call_target="tpu_custom_call" | custom-call | flops 1 | bytes 1 | tf_op jit(solution)/shard_map/ffn_weights/pallas_call | solution.py:686
  372.0 7.3 %collective-permute-done.25 = bf16[512,1536]{1,0:T(8,128)(2,1)S(1)} collective-permute-done((bf16[512,1536]{1,0:T(8,128)(2,1)}, bf16[512,1536]{1,0:T(8,128)(2,1)S(1)}, u32[]{:S(2)}, u32[]{:S(2)}) %collective-permute-start.25) | collective-permute-done | bytes 1572896 | tf_op jit(solution)/shard_map/ppermute | solution.py:83
  379.4 3.7 collective-permute-done.26
  384.2 16.1 %ffn_out.1 = (bf16[2048,2048]{1,0:T(8,128)(2,1)}, f32[1,2048]{1,0:T(1,128)}) custom-call(bf16[2048,512]{1,0:T(8,128)(2,1)} %get-tuple-element.284.act_ref.act_1, bf16[2048,512]{1,0:T(8,128)(2,1)} %get-tuple-element.285.act_ref.act_2, bf16[512,2048]{1,0:T(8,128)(2,1)} %get-tuple-element.286.down_1, bf16[512,2048]{1,0:T(8,128)(2,1)} %get-tuple-element.287.down_2, ...), custom_call_target="tpu_custom_call" | custom-call | flops 1 | bytes 1 | tf_op jit(solution)/shard_map/ffn_out/pallas_call | solution.py:712
  401.6 4.9 add_convert_fusion.2
  406.6 6.0 reduce-scatter.6.cloned.1.call-done.back_ref
  412.6 8.8 %residual_backward.1 = (f32[256,2048]{1,0:T(8,128)}, bf16[256,2048]{1,0:T(8,128)(2,1)}, bf16[256,2048]{1,0:T(8,128)(2,1)}) custom-call(bf16[256,2048]{1,0:T(8,128)(2,1)} %reduce-scatter.6.cloned.1.call-done.back_ref, f32[256,2048]{1,0:T(8,128)} %get-tuple-element.417.residual_ref, f32[256,1]{1,0:T(8,128)} %copy.82.scale_ref, f32[1,2048]{1,0:T(1,128)} %bitcast.69, ...), custom_call_target="tpu_custom_call" | custom-call | flops 1 | bytes 1 | tf_op jit(solution)/shard_map/residual_backward/pallas_call | solution.py:545
  421.5 2.5 add_convert_fusion.4
  424.3 3.0 pad_maximum_fusion.2
  427.3 17.6 %all_to_all.19 = bf16[256,8,256]{2,0,1:T(8,128)(2,1)} all-to-all(bf16[256,8,256]{2,0,1:T(8,128)(2,1)S(1)} %bitcast.63), channel_id=1, replica_groups=mesh['do'=4,'di'=2,'tp'=4] {'di','tp'}, dimensions={1} | all-to-all | bytes 2097152 | tf_op jit(solution)/shard_map/all_to_all | solution.py:1117
  445.0 5.1 select_bitcast_fusion
  451.1 4.3 collective-permute-start.37
  455.4 2.6 collective-permute-done.29
  458.0 5.9 fusion
  468.5 33.0 %attn_backward.1 = (bf16[2048,2048]{1,0:T(8,128)(2,1)}, f32[1,2048]{1,0:T(1,128)}, bf16[512,384]{1,0:T(8,128)(2,1)}, bf16[512,384]{1,0:T(8,128)(2,1)}, bf16[512,...) custom-call(s32[1]{0:T(128)} %bitcast.1.refs_0_, bf16[512,640]{1,0:T(8,128)(2,1)} %copy-done.15, bf16[512,640]{1,0:T(8,128)(2,1)} %copy-done.20, ...), custom_call_target="tpu_custom_call" | custom-call | flops 1 | bytes 1 | tf_op jit(solution)/shard_map/attn_backward/pallas_call | solution.py:455
  504.3 11.3 %collective-permute-done.31 = f32[2,2048]{1,0:T(2,128)S(1)} collective-permute-done((f32[2,2048]{1,0:T(2,128)S(1)}, f32[2,2048]{1,0:T(2,128)S(1)}, u32[]{:S(2)}, u32[]{:S(2)}) %collective-permute-start.31) | collective-permute-done | bytes 16416 | tf_op jit(solution)/shard_map/ppermute | solution.py:761
  519.0 2.7 collective-permute-done.33
  526.9 4.5 convert_add_fusion.2
  531.6 4.4 collective-permute-start.39
  536.0 2.8 fusion.4
  540.5 4.1 copy-done
  544.6 3.3 out_weights.1
  549.3 17.0 %collective-permute-done.38 = bf16[512,1536]{1,0:T(8,128)(2,1)S(1)} collective-permute-done((bf16[512,1536]{1,0:T(8,128)(2,1)S(1)}, bf16[512,1536]{1,0:T(8,128)(2,1)S(1)}, u32[]{:S(2)}, u32[]{:S(2)}) %collective-permute-start.38) | collective-permute-done | bytes 1572896 | tf_op jit(solution)/shard_map/ppermute | solution.py:92
  572.0 2.3 collective-permute-start.41
  574.4 23.4 %collective-permute-done.43.theirs_1 = bf16[256,1536]{1,0:T(8,128)(2,1)S(1)} collective-permute-done((bf16[256,1536]{1,0:T(8,128)(2,1)S(1)}, bf16[256,1536]{1,0:T(8,128)(2,1)S(1)}, u32[]{:S(2)}, u32[]{:S(2)}) %collective-permute-start.43) | collective-permute-done | bytes 786464 | tf_op jit(solution)/shard_map/ppermute | solution.py:165
  599.9 19.2 %collective-permute-done.44.theirs_2 = bf16[256,1536]{1,0:T(8,128)(2,1)S(1)} collective-permute-done((bf16[256,1536]{1,0:T(8,128)(2,1)S(1)}, bf16[256,1536]{1,0:T(8,128)(2,1)S(1)}, u32[]{:S(2)}, u32[]{:S(2)}) %collective-permute-start.44) | collective-permute-done | bytes 786464 | tf_op jit(solution)/shard_map/ppermute | solution.py:165
  620.0 17.6 %adamw_ffn.1 = (f32[256,2048]{1,0:T(8,128)}, f32[256,2048]{1,0:T(8,128)}, f32[256,2048]{1,0:T(8,128)}, f32[256,2048]{1,0:T(8,128)}, f32[256,2048]{1,0:T(8,128)},...) custom-call(s32[1]{0:T(128)} %bitcast.23.x_ref, ...), custom_call_target="tpu_custom_call" | custom-call | flops 1 | bytes 1 | tf_op jit(solution)/shard_map/adamw_ffn/pallas_call | solution.py:806
  639.6 2.3 collective-permute-start.46
  642.6 7.5 %finish.1 = (bf16[256,2048]{1,0:T(8,128)(2,1)}, f32[256,2048]{1,0:T(8,128)}) custom-call(s32[1]{0:T(128)} %bitcast.place_ref, bf16[256,2048]{1,0:T(8,128)(2,1)} %reduce-scatter.8.cloned.1.call-done.back_ref, bf16[256,2048]{1,0:T(8,128)(2,1)} %copy-done.6, f32[256,1]{1,0:T(8,128)} %copy.87.scale_ref, f32[1,2048]{1,0:T(1,128)} %bitcast.68, ...), custom_call_target="tpu_custom_call" | custom-call | flops 1 | bytes 1 | tf_op jit(solution)/shard_map/finish/pallas_call | solution.py:874
  651.7 5.5 adamw_attn.1
  (280 shorter events, 84.9 us)
Async XLA Ops:
  7.2 69.8 %all-gather.5.cloned.1.call-start = ((), (), s32[]{:S(2)}) async-start(), calls=%async_computation.4 | async-start | bytes 9437184 | tf_op jit(solution)/shard_map/all_gather | solution.py:946
  9.7 174.0 %copy-start.6 = (bf16[256,2048]{1,0:T(8,128)(2,1)}, bf16[256,2048]{1,0:T(8,128)(2,1)S(1)}, u32[]{:S(2)}) copy-start(bf16[256,2048]{1,0:T(8,128)(2,1)S(1)} %get-tuple-element.401.inputs_ref) | copy-start | bytes 3145732
  9.9 491.6 %copy-start.39 = (f32[2048]{0:T(1024)}, f32[2048]{0:T(1024)S(1)}, u32[]{:S(2)}) copy-start(f32[2048]{0:T(1024)S(1)} %maximum_select_fusion.8) | copy-start | bytes 24580
  11.3 170.7 %reduce-scatter.4.cloned.1.call-start = ((), (), s32[]{:S(2)}) async-start(), calls=%async_computation.5 | async-start | bytes 9437184 | tf_op jit(solution)/shard_map/reduce_scatter | solution.py:1030
  12.1 8.9 %collective-permute-start = (bf16[256,640]{1,0:T(8,128)(2,1)S(1)}, bf16[256,640]{1,0:T(8,128)(2,1)S(1)}, u32[]{:S(2)}, u32[]{:S(2)}) collective-permute-start(bf16[256,640]{1,0:T(8,128)(2,1)S(1)} %pad_maximum_fusion.17), channel_id=1, source_target_pairs={{0,4},{4,0},{1,5},{5,1},{2,6},{6,2},{3,7},{7,3},{8,12},{12,8},{9,1... | collective-permute-start | bytes 983048 | tf_op jit(solution)/shard_map/ppermute | solution.py:137
  13.4 7.5 %collective-permute-start.1 = (s32[2,1024]{1,0:T(2,128)S(1)}, s32[2,1024]{1,0:T(2,128)S(1)}, u32[]{:S(2)}, u32[]{:S(2)}) collective-permute-start(s32[2,1024]{1,0:T(2,128)S(1)} %pad_add_fusion.1), channel_id=1, source_target_pairs={{0,4},{4,0},{1,5},{5,1},{2,6},{6,2},{3,7},{7,3},{8,12},{12,8},{9,1... | collective-permute-start | bytes 24584 | tf_op jit(solution)/shard_map/ppermute | solution.py:949
  21.0 54.7 %copy-start.38 = (s32[1,2048]{1,0:T(1,128)}, s32[1,2048]{1,0:T(1,128)S(1)}, u32[]{:S(2)}) copy-start(s32[1,2048]{1,0:T(1,128)S(1)} %get-tuple-element.479) | copy-start | bytes 24580
  21.3 14.7 %collective-permute-start.2 = (bf16[512,640]{1,0:T(8,128)(2,1)S(1)}, bf16[512,640]{1,0:T(8,128)(2,1)S(1)}, u32[]{:S(2)}, u32[]{:S(2)}) collective-permute-start(bf16[512,640]{1,0:T(8,128)(2,1)S(1)} %pad_maximum_fusion.15.refs_1_), channel_id=1, source_target_pairs={{0,8},{8,0},{16,24},{24,16},{1,9},{9,1},{17,25},{25,17},{2,10},{10... | collective-permute-start | bytes 1966088 | tf_op jit(solution)/shard_map/ppermute | solution.py:53
  21.6 17.5 %collective-permute-start.3 = (bf16[512,640]{1,0:T(8,128)(2,1)S(1)}, bf16[512,640]{1,0:T(8,128)(2,1)S(1)}, u32[]{:S(2)}, u32[]{:S(2)}) collective-permute-start(bf16[512,640]{1,0:T(8,128)(2,1)S(1)} %pad_maximum_fusion.15.refs_1_), channel_id=1, source_target_pairs={{8,16},{16,8},{9,17},{17,9},{10,18},{18,10},{11,19},{19,11},{12,20... | collective-permute-start | bytes 1966088 | tf_op jit(solution)/shard_map/ppermute | solution.py:53
  31.5 21.4 %collective-permute-start.6 = (bf16[256,1536]{1,0:T(8,128)(2,1)S(1)}, bf16[256,1536]{1,0:T(8,128)(2,1)S(1)}, u32[]{:S(2)}, u32[]{:S(2)}) collective-permute-start(bf16[256,1536]{1,0:T(8,128)(2,1)S(1)} %pad_maximum_fusion.12), channel_id=1, source_target_pairs={{0,4},{4,0},{1,5},{5,1},{2,6},{6,2},{3,7},{7,3},{8,12},{12,8},{9,1... | collective-permute-start | bytes 2359304 | tf_op jit(solution)/shard_map/ppermute | solution.py:137
  39.1 13.9 %collective-permute-start.4 = (bf16[512,640]{1,0:T(8,128)(2,1)S(1)}, bf16[512,640]{1,0:T(8,128)(2,1)S(1)}, u32[]{:S(2)}, u32[]{:S(2)}) collective-permute-start(bf16[512,640]{1,0:T(8,128)(2,1)S(1)} %collective-permute-done.3.refs_5_), channel_id=1, source_target_pairs={{0,8},{8,0},{16,24},{24,16},{1,9},{9,1},{17,25},{25,17},{2,10},{10... | collective-permute-start | bytes 1966088 | tf_op jit(solution)/shard_map/ppermute | solution.py:57
  39.1 15.7 %collective-permute-start.5 = (bf16[512,640]{1,0:T(8,128)(2,1)S(1)}, bf16[512,640]{1,0:T(8,128)(2,1)S(1)}, u32[]{:S(2)}, u32[]{:S(2)}) collective-permute-start(bf16[512,640]{1,0:T(8,128)(2,1)S(1)} %collective-permute-done.2.refs_2_), channel_id=1, source_target_pairs={{8,16},{16,8},{9,17},{17,9},{10,18},{18,10},{11,19},{19,11},{12,20... | collective-permute-start | bytes 1966088 | tf_op jit(solution)/shard_map/ppermute | solution.py:58
  42.7 98.8 %copy-start.8 = (bf16[256,2048]{1,0:T(8,128)(2,1)}, bf16[256,2048]{1,0:T(8,128)(2,1)S(1)}, u32[]{:S(2)}) copy-start(bf16[256,2048]{1,0:T(8,128)(2,1)S(1)} %maximum_select_fusion.3.grad_ref) | copy-start | bytes 3145732
  54.8 11.8 %collective-permute-start.7 = (bf16[512,640]{1,0:T(8,128)(2,1)S(1)}, bf16[512,640]{1,0:T(8,128)(2,1)S(1)}, u32[]{:S(2)}, u32[]{:S(2)}) collective-permute-start(bf16[512,640]{1,0:T(8,128)(2,1)S(1)} %collective-permute-done.5.refs_3_), channel_id=1, source_target_pairs={{0,8},{8,0},{16,24},{24,16},{1,9},{9,1},{17,25},{25,17},{2,10},{10... | collective-permute-start | bytes 1966088 | tf_op jit(solution)/shard_map/ppermute | solution.py:62
  66.6 38.5 %collective-permute-start.8 = (bf16[512,1536]{1,0:T(8,128)(2,1)}, bf16[512,1536]{1,0:T(8,128)(2,1)}, u32[]{:S(2)}, u32[]{:S(2)}) collective-permute-start(bf16[512,1536]{1,0:T(8,128)(2,1)} %pad_maximum_fusion.7.refs_1_), channel_id=1, source_target_pairs={{0,8},{8,0},{16,24},{24,16},{1,9},{9,1},{17,25},{25,17},{2,10},{10... | collective-permute-start | bytes 4718600 | tf_op jit(solution)/shard_map/ppermute | solution.py:53
  69.0 36.2 %collective-permute-start.9 = (bf16[512,1536]{1,0:T(8,128)(2,1)}, bf16[512,1536]{1,0:T(8,128)(2,1)}, u32[]{:S(2)}, u32[]{:S(2)}) collective-permute-start(bf16[512,1536]{1,0:T(8,128)(2,1)} %pad_maximum_fusion.7.refs_1_), channel_id=1, source_target_pairs={{8,16},{16,8},{9,17},{17,9},{10,18},{18,10},{11,19},{19,11},{12,20... | collective-permute-start | bytes 4718600 | tf_op jit(solution)/shard_map/ppermute | solution.py:53
  74.1 31.0 %collective-permute-start.10 = (bf16[256,2048]{1,0:T(8,128)(2,1)S(1)}, bf16[256,2048]{1,0:T(8,128)(2,1)}, u32[]{:S(2)}, u32[]{:S(2)}) collective-permute-start(bf16[256,2048]{1,0:T(8,128)(2,1)S(1)} %maximum_select_fusion.3.grad_ref), channel_id=1, source_target_pairs={{0,2},{1,5},{2,0},{3,7},{4,6},{5,1},{6,4},{7,3},{8,10},{9,13},{10,... | collective-permute-start | bytes 3145736 | tf_op jit(solution)/shard_map/ppermute | solution.py:914
  74.5 30.6 %collective-permute-start.11 = (bf16[256,1536]{1,0:T(8,128)(2,1)}, bf16[256,1536]{1,0:T(8,128)(2,1)}, u32[]{:S(2)}, u32[]{:S(2)}) collective-permute-start(bf16[256,1536]{1,0:T(8,128)(2,1)} %pad_maximum_fusion.14), channel_id=1, source_target_pairs={{0,4},{4,0},{1,5},{5,1},{2,6},{6,2},{3,7},{7,3},{8,12},{12,8},{9,1... | collective-permute-start | bytes 2359304 | tf_op jit(solution)/shard_map/ppermute | solution.py:137
  105.2 135.7 %all-gather.7.cloned.1.call-start = ((), (), s32[]{:S(2)}) async-start(), calls=%async_computation.6 | async-start | bytes 9437184 | tf_op jit(solution)/shard_map/all_gather | solution.py:1054
  105.2 31.8 %collective-permute-start.12 = (bf16[512,1536]{1,0:T(8,128)(2,1)}, bf16[512,1536]{1,0:T(8,128)(2,1)}, u32[]{:S(2)}, u32[]{:S(2)}) collective-permute-start(bf16[512,1536]{1,0:T(8,128)(2,1)} %collective-permute-done.9.refs_5_), channel_id=1, source_target_pairs={{0,8},{8,0},{16,24},{24,16},{1,9},{9,1},{17,25},{25,17},{2,10},{10... | collective-permute-start | bytes 4718600 | tf_op jit(solution)/shard_map/ppermute | solution.py:57
  105.3 33.6 %collective-permute-start.13 = (bf16[512,1536]{1,0:T(8,128)(2,1)}, bf16[512,1536]{1,0:T(8,128)(2,1)}, u32[]{:S(2)}, u32[]{:S(2)}) collective-permute-start(bf16[512,1536]{1,0:T(8,128)(2,1)} %collective-permute-done.8.refs_2_), channel_id=1, source_target_pairs={{8,16},{16,8},{9,17},{17,9},{10,18},{18,10},{11,19},{19,11},{12,20... | collective-permute-start | bytes 4718600 | tf_op jit(solution)/shard_map/ppermute | solution.py:58
  108.5 14.3 %collective-permute-start.14 = (bf16[256,2048]{1,0:T(8,128)(2,1)}, bf16[256,2048]{1,0:T(8,128)(2,1)}, u32[]{:S(2)}, u32[]{:S(2)}) collective-permute-start(bf16[256,2048]{1,0:T(8,128)(2,1)} %collective-permute-done.10), channel_id=1, source_target_pairs={{0,4},{1,3},{2,6},{3,1},{4,0},{5,7},{6,2},{7,5},{8,12},{9,11},{10,... | collective-permute-start | bytes 3145736 | tf_op jit(solution)/shard_map/ppermute | solution.py:911
  109.8 24.3 %collective-permute-start.15 = (bf16[256,2048]{1,0:T(8,128)(2,1)S(1)}, bf16[256,2048]{1,0:T(8,128)(2,1)}, u32[]{:S(2)}, u32[]{:S(2)}) collective-permute-start(bf16[256,2048]{1,0:T(8,128)(2,1)S(1)} %maximum_select_fusion.3.grad_ref), channel_id=1, source_target_pairs={{0,4},{1,3},{2,6},{3,1},{4,0},{5,7},{6,2},{7,5},{8,12},{9,11},{10,... | collective-permute-start | bytes 3145736 | tf_op jit(solution)/shard_map/ppermute | solution.py:911
  110.1 73.6 %copy-start.40 = (f32[2048]{0:T(1024)}, f32[2048]{0:T(1024)S(1)}, u32[]{:S(2)}) copy-start(f32[2048]{0:T(1024)S(1)} %maximum_select_fusion.10) | copy-start | bytes 24580
  138.9 28.6 %collective-permute-start.16 = (bf16[512,1536]{1,0:T(8,128)(2,1)}, bf16[512,1536]{1,0:T(8,128)(2,1)}, u32[]{:S(2)}, u32[]{:S(2)}) collective-permute-start(bf16[512,1536]{1,0:T(8,128)(2,1)} %collective-permute-done.13.refs_3_), channel_id=1, source_target_pairs={{0,8},{8,0},{16,24},{24,16},{1,9},{9,1},{17,25},{25,17},{2,10},{10... | collective-permute-start | bytes 4718600 | tf_op jit(solution)/shard_map/ppermute | solution.py:62
  185.9 153.0 %all-gather.9.cloned.1.call-start = ((), (), s32[]{:S(2)}) async-start(), calls=%async_computation.7 | async-start | bytes 9437184 | tf_op jit(solution)/shard_map/all_gather | solution.py:1062
  186.0 7.8 %collective-permute-start.19 = (bf16[1024,2048]{1,0:T(8,128)(2,1)}, bf16[1024,2048]{1,0:T(8,128)(2,1)S(1)}, u32[]{:S(2)}, u32[]{:S(2)}) collective-permute-start(bf16[1024,2048]{1,0:T(8,128)(2,1)} %pad_maximum_fusion.1), channel_id=1, source_target_pairs={{0,1},{1,0},{2,3},{3,2},{4,5},{5,4},{6,7},{7,6},{8,9},{9,8},{10,11... | collective-permute-start | bytes 12582920 | tf_op jit(solution)/shard_map/ppermute | solution.py:917
  186.7 36.1 %collective-permute-start.17 = (bf16[512,1536]{1,0:T(8,128)(2,1)S(1)}, bf16[512,1536]{1,0:T(8,128)(2,1)}, u32[]{:S(2)}, u32[]{:S(2)}) collective-permute-start(bf16[512,1536]{1,0:T(8,128)(2,1)S(1)} %copy-done.12), channel_id=1, source_target_pairs={{0,8},{8,0},{16,24},{24,16},{1,9},{9,1},{17,25},{25,17},{2,10},{10... | collective-permute-start | bytes 4718600 | tf_op jit(solution)/shard_map/ppermute | solution.py:53
  187.0 38.6 %collective-permute-start.18 = (bf16[512,1536]{1,0:T(8,128)(2,1)S(1)}, bf16[512,1536]{1,0:T(8,128)(2,1)}, u32[]{:S(2)}, u32[]{:S(2)}) collective-permute-start(bf16[512,1536]{1,0:T(8,128)(2,1)S(1)} %copy-done.12), channel_id=1, source_target_pairs={{8,16},{16,8},{9,17},{17,9},{10,18},{18,10},{11,19},{19,11},{12,20... | collective-permute-start | bytes 4718600 | tf_op jit(solution)/shard_map/ppermute | solution.py:53
  225.7 186.9 %reduce-scatter.6.cloned.1.call-start = ((), (), s32[]{:S(2)}) async-start(), calls=%async_computation.8 | async-start | bytes 9437184 | tf_op jit(solution)/shard_map/reduce_scatter | solution.py:1086
  225.7 45.5 %collective-permute-start.20 = (bf16[512,1536]{1,0:T(8,128)(2,1)}, bf16[512,1536]{1,0:T(8,128)(2,1)S(1)}, u32[]{:S(2)}, u32[]{:S(2)}) collective-permute-start(bf16[512,1536]{1,0:T(8,128)(2,1)} %collective-permute-done.18.refs_5_), channel_id=1, source_target_pairs={{0,8},{8,0},{16,24},{24,16},{1,9},{9,1},{17,25},{25,17},{2,10},{10... | collective-permute-start | bytes 4718600 | tf_op jit(solution)/shard_map/ppermute | solution.py:57
  225.8 45.4 %collective-permute-start.21 = (bf16[512,1536]{1,0:T(8,128)(2,1)}, bf16[512,1536]{1,0:T(8,128)(2,1)S(1)}, u32[]{:S(2)}, u32[]{:S(2)}) collective-permute-start(bf16[512,1536]{1,0:T(8,128)(2,1)} %collective-permute-done.17.refs_2_), channel_id=1, source_target_pairs={{8,16},{16,8},{9,17},{17,9},{10,18},{18,10},{11,19},{19,11},{12,20... | collective-permute-start | bytes 4718600 | tf_op jit(solution)/shard_map/ppermute | solution.py:58
  271.3 35.7 %collective-permute-start.22 = (bf16[512,1536]{1,0:T(8,128)(2,1)S(1)}, bf16[512,1536]{1,0:T(8,128)(2,1)}, u32[]{:S(2)}, u32[]{:S(2)}) collective-permute-start(bf16[512,1536]{1,0:T(8,128)(2,1)S(1)} %collective-permute-done.21.refs_3_), channel_id=1, source_target_pairs={{8,0},{16,24},{9,1},{17,25},{10,2},{18,26},{11,3},{19,27},{12,4},{... | collective-permute-start | bytes 4718600 | tf_op jit(solution)/shard_map/ppermute | solution.py:62
  287.7 51.3 %collective-permute-start.23 = (bf16[256,1536]{1,0:T(8,128)(2,1)}, bf16[256,1536]{1,0:T(8,128)(2,1)}, u32[]{:S(2)}, u32[]{:S(2)}) collective-permute-start(bf16[256,1536]{1,0:T(8,128)(2,1)} %get-tuple-element.271), channel_id=1, source_target_pairs={{0,8},{24,16},{1,9},{25,17},{2,10},{26,18},{3,11},{27,19},{4,12},{... | collective-permute-start | bytes 2359304 | tf_op jit(solution)/shard_map/ppermute | solution.py:1072
  289.0 50.0 %collective-permute-start.24 = (bf16[256,1536]{1,0:T(8,128)(2,1)}, bf16[256,1536]{1,0:T(8,128)(2,1)}, u32[]{:S(2)}, u32[]{:S(2)}) collective-permute-start(bf16[256,1536]{1,0:T(8,128)(2,1)} %get-tuple-element.272), channel_id=1, source_target_pairs={{0,8},{24,16},{1,9},{25,17},{2,10},{26,18},{3,11},{27,19},{4,12},{... | collective-permute-start | bytes 2359304 | tf_op jit(solution)/shard_map/ppermute | solution.py:1072
  339.0 186.4 %all-gather.11.cloned.1.call-start = ((), (), s32[]{:S(2)}) async-start(), calls=%async_computation.9 | async-start | bytes 9437184 | tf_op jit(solution)/shard_map/all_gather | solution.py:1131
  343.4 36.0 %collective-permute-start.25 = (bf16[512,1536]{1,0:T(8,128)(2,1)}, bf16[512,1536]{1,0:T(8,128)(2,1)S(1)}, u32[]{:S(2)}, u32[]{:S(2)}) collective-permute-start(bf16[512,1536]{1,0:T(8,128)(2,1)} %add_convert_fusion.5), channel_id=1, source_target_pairs={{0,8},{8,0},{16,24},{24,16},{1,9},{9,1},{17,25},{25,17},{2,10},{10... | collective-permute-start | bytes 4718600 | tf_op jit(solution)/shard_map/ppermute | solution.py:83
  345.4 37.7 %collective-permute-start.26 = (bf16[512,1536]{1,0:T(8,128)(2,1)}, bf16[512,1536]{1,0:T(8,128)(2,1)S(1)}, u32[]{:S(2)}, u32[]{:S(2)}) collective-permute-start(bf16[512,1536]{1,0:T(8,128)(2,1)} %add_convert_fusion.5), channel_id=1, source_target_pairs={{8,16},{16,8},{9,17},{17,9},{10,18},{18,10},{11,19},{19,11},{12,20... | collective-permute-start | bytes 4718600 | tf_op jit(solution)/shard_map/ppermute | solution.py:84
  383.1 17.5 %collective-permute-start.27 = (bf16[256,1536]{1,0:T(8,128)(2,1)}, bf16[256,1536]{1,0:T(8,128)(2,1)}, u32[]{:S(2)}, u32[]{:S(2)}) collective-permute-start(bf16[256,1536]{1,0:T(8,128)(2,1)} %get-tuple-element.289), channel_id=1, source_target_pairs={{0,8},{8,0},{16,24},{24,16},{1,9},{9,1},{17,25},{25,17},{2,10},{10... | collective-permute-start | bytes 2359304 | tf_op jit(solution)/shard_map/ppermute | solution.py:1096
  400.5 20.9 %collective-permute-start.28 = (bf16[256,1536]{1,0:T(8,128)(2,1)}, bf16[256,1536]{1,0:T(8,128)(2,1)}, u32[]{:S(2)}, u32[]{:S(2)}) collective-permute-start(bf16[256,1536]{1,0:T(8,128)(2,1)} %get-tuple-element.296), channel_id=1, source_target_pairs={{0,8},{8,0},{16,24},{24,16},{1,9},{9,1},{17,25},{25,17},{2,10},{10... | collective-permute-start | bytes 2359304 | tf_op jit(solution)/shard_map/ppermute | solution.py:1100
  445.0 192.7 %reduce-scatter.8.cloned.1.call-start = ((), (), s32[]{:S(2)}) async-start(), calls=%async_computation.10 | async-start | bytes 9437184 | tf_op jit(solution)/shard_map/reduce_scatter | solution.py:1146
  450.1 7.9 %collective-permute-start.29 = (bf16[4,256,2048]{2,1,0:T(8,128)(2,1)}, bf16[4,256,2048]{2,1,0:T(8,128)(2,1)}, u32[]{:S(2)}, u32[]{:S(2)}) collective-permute-start(bf16[4,256,2048]{2,1,0:T(8,128)(2,1)} %select_bitcast_fusion), channel_id=1, source_target_pairs={{0,1},{1,0},{2,3},{3,2},{4,5},{5,4},{6,7},{7,6},{8,9},{9,8},{10,11... | collective-permute-start | bytes 12582920 | tf_op jit(solution)/shard_map/ppermute | solution.py:917
  450.9 74.5 %collective-permute-start.36 = (bf16[1024,1536]{1,0:T(8,128)(2,1)}, bf16[1024,1536]{1,0:T(8,128)(2,1)}, u32[]{:S(2)}, u32[]{:S(2)}) collective-permute-start(bf16[1024,1536]{1,0:T(8,128)(2,1)} %get-tuple-element.321), channel_id=1, source_target_pairs={{0,8},{8,0},{16,24},{24,16},{1,9},{9,1},{17,25},{25,17},{2,10},{10... | collective-permute-start | bytes 9437192 | tf_op jit(solution)/shard_map/ppermute | solution.py:1115
  451.1 74.2 %collective-permute-start.37 = (bf16[1024,1536]{1,0:T(8,128)(2,1)}, bf16[1024,1536]{1,0:T(8,128)(2,1)}, u32[]{:S(2)}, u32[]{:S(2)}) collective-permute-start(bf16[1024,1536]{1,0:T(8,128)(2,1)} %get-tuple-element.322), channel_id=1, source_target_pairs={{8,16},{16,8},{9,17},{17,9},{10,18},{18,10},{11,19},{19,11},{12,20... | collective-permute-start | bytes 9437192 | tf_op jit(solution)/shard_map/ppermute | solution.py:1116
  467.3 58.1 %collective-permute-start.35 = (bf16[2,256,2048]{2,1,0:T(8,128)(2,1)}, bf16[2,256,2048]{2,1,0:T(8,128)(2,1)}, u32[]{:S(2)}, u32[]{:S(2)}) collective-permute-start(bf16[2,256,2048]{2,1,0:T(8,128)(2,1)} %pad_maximum_fusion.6), channel_id=1, source_target_pairs={{0,4},{1,3},{2,6},{3,1},{4,0},{5,7},{6,2},{7,5},{8,12},{9,11},{10,... | collective-permute-start | bytes 6291464 | tf_op jit(solution)/shard_map/ppermute | solution.py:911
  502.4 1.4 collective-permute-start.30
  503.8 11.8 %collective-permute-start.31 = (f32[2,2048]{1,0:T(2,128)S(1)}, f32[2,2048]{1,0:T(2,128)S(1)}, u32[]{:S(2)}, u32[]{:S(2)}) collective-permute-start(f32[2,2048]{1,0:T(2,128)S(1)} %add.163), channel_id=1, source_target_pairs={{0,2},{1,3},{2,0},{3,1},{4,6},{5,7},{6,4},{7,5},{8,10},{9,11},{10,... | collective-permute-start | bytes 49160 | tf_op jit(solution)/shard_map/ppermute | solution.py:761
  515.6 3.1 collective-permute-start.32
  518.7 3.1 collective-permute-start.33
  521.8 3.6 collective-permute-start.34
  531.4 34.9 %collective-permute-start.38 = (bf16[512,1536]{1,0:T(8,128)(2,1)S(1)}, bf16[512,1536]{1,0:T(8,128)(2,1)S(1)}, u32[]{:S(2)}, u32[]{:S(2)}) collective-permute-start(bf16[512,1536]{1,0:T(8,128)(2,1)S(1)} %get-tuple-element.411), channel_id=1, source_target_pairs={{0,8},{8,0},{16,24},{24,16},{1,9},{9,1},{17,25},{25,17},{2,10},{10... | collective-permute-start | bytes 4718600 | tf_op jit(solution)/shard_map/ppermute | solution.py:92
  531.6 37.0 %collective-permute-start.39 = (bf16[512,1536]{1,0:T(8,128)(2,1)S(1)}, bf16[512,1536]{1,0:T(8,128)(2,1)S(1)}, u32[]{:S(2)}, u32[]{:S(2)}) collective-permute-start(bf16[512,1536]{1,0:T(8,128)(2,1)S(1)} %get-tuple-element.412), channel_id=1, source_target_pairs={{8,16},{16,8},{9,17},{17,9},{10,18},{18,10},{11,19},{19,11},{12,20... | collective-permute-start | bytes 4718600 | tf_op jit(solution)/shard_map/ppermute | solution.py:92
  538.8 98.9 %collective-permute-start.45 = (bf16[256,2048]{1,0:T(8,128)(2,1)}, bf16[256,2048]{1,0:T(8,128)(2,1)}, u32[]{:S(2)}, u32[]{:S(2)}) collective-permute-start(bf16[256,2048]{1,0:T(8,128)(2,1)} %fusion.4), channel_id=1, source_target_pairs={{0,2},{1,5},{2,0},{3,7},{4,6},{5,1},{6,4},{7,3},{8,10},{9,13},{10,... | collective-permute-start | bytes 3145736 | tf_op jit(solution)/shard_map/ppermute | solution.py:914
  540.0 57.8 %collective-permute-start.43 = (bf16[256,1536]{1,0:T(8,128)(2,1)S(1)}, bf16[256,1536]{1,0:T(8,128)(2,1)S(1)}, u32[]{:S(2)}, u32[]{:S(2)}) collective-permute-start(bf16[256,1536]{1,0:T(8,128)(2,1)S(1)} %select_convert_fusion.1), channel_id=1, source_target_pairs={{0,4},{4,0},{1,5},{5,1},{2,6},{6,2},{3,7},{7,3},{8,12},{12,8},{9,1... | collective-permute-start | bytes 2359304 | tf_op jit(solution)/shard_map/ppermute | solution.py:165
  570.6 27.2 %copy-start.43 = (f32[2048]{0:T(1024)S(1)}, f32[2048]{0:T(1024)}, u32[]{:S(2)}) copy-start(f32[2048]{0:T(1024)} %param.57) | copy-start | bytes 24580
  570.6 27.2 %copy-start.52 = (f32[2048]{0:T(1024)S(1)}, f32[2048]{0:T(1024)}, u32[]{:S(2)}) copy-start(f32[2048]{0:T(1024)} %param.59) | copy-start | bytes 24580
  570.6 27.2 %copy-start.53 = (f32[2048]{0:T(1024)S(1)}, f32[2048]{0:T(1024)}, u32[]{:S(2)}) copy-start(f32[2048]{0:T(1024)} %param.61) | copy-start | bytes 24580
  570.8 48.3 %collective-permute-start.44 = (bf16[256,1536]{1,0:T(8,128)(2,1)S(1)}, bf16[256,1536]{1,0:T(8,128)(2,1)S(1)}, u32[]{:S(2)}, u32[]{:S(2)}) collective-permute-start(bf16[256,1536]{1,0:T(8,128)(2,1)S(1)} %select_convert_fusion), channel_id=1, source_target_pairs={{0,4},{4,0},{1,5},{5,1},{2,6},{6,2},{3,7},{7,3},{8,12},{12,8},{9,1... | collective-permute-start | bytes 2359304 | tf_op jit(solution)/shard_map/ppermute | solution.py:165
  571.9 28.0 %copy-start.46 = (f32[1,2048]{1,0:T(1,128)}, f32[1,2048]{1,0:T(1,128)S(1)}, u32[]{:S(2)}) copy-start(f32[1,2048]{1,0:T(1,128)S(1)} %get-tuple-element.471) | copy-start | bytes 24580
  572.0 70.0 %copy-start.47 = (f32[1,2048]{1,0:T(1,128)}, f32[1,2048]{1,0:T(1,128)S(1)}, u32[]{:S(2)}) copy-start(f32[1,2048]{1,0:T(1,128)S(1)} %get-tuple-element.472) | copy-start | bytes 24580
  572.0 65.7 %collective-permute-start.40 = (bf16[512,640]{1,0:T(8,128)(2,1)S(1)}, bf16[512,640]{1,0:T(8,128)(2,1)}, u32[]{:S(2)}, u32[]{:S(2)}) collective-permute-start(bf16[512,640]{1,0:T(8,128)(2,1)S(1)} %get-tuple-element.335), channel_id=1, source_target_pairs={{0,8},{8,0},{16,24},{24,16},{1,9},{9,1},{17,25},{25,17},{2,10},{10... | collective-permute-start | bytes 1966088 | tf_op jit(solution)/shard_map/ppermute | solution.py:101
  572.0 65.6 %collective-permute-start.41 = (bf16[512,640]{1,0:T(8,128)(2,1)S(1)}, bf16[512,640]{1,0:T(8,128)(2,1)}, u32[]{:S(2)}, u32[]{:S(2)}) collective-permute-start(bf16[512,640]{1,0:T(8,128)(2,1)S(1)} %get-tuple-element.336), channel_id=1, source_target_pairs={{0,16},{8,24},{16,0},{24,8},{1,17},{9,25},{17,1},{25,9},{2,18},{10... | collective-permute-start | bytes 1966088 | tf_op jit(solution)/shard_map/ppermute | solution.py:101
  597.8 39.9 %collective-permute-start.42 = (bf16[512,640]{1,0:T(8,128)(2,1)S(1)}, bf16[512,640]{1,0:T(8,128)(2,1)}, u32[]{:S(2)}, u32[]{:S(2)}) collective-permute-start(bf16[512,640]{1,0:T(8,128)(2,1)S(1)} %get-tuple-element.337), channel_id=1, source_target_pairs={{0,24},{8,16},{16,8},{24,0},{1,25},{9,17},{17,9},{25,1},{2,26},{10... | collective-permute-start | bytes 1966088 | tf_op jit(solution)/shard_map/ppermute | solution.py:101
  639.6 11.4 %collective-permute-start.46 = (bf16[256,640]{1,0:T(8,128)(2,1)S(1)}, bf16[256,640]{1,0:T(8,128)(2,1)S(1)}, u32[]{:S(2)}, u32[]{:S(2)}) collective-permute-start(bf16[256,640]{1,0:T(8,128)(2,1)S(1)} %select_convert_fusion.2), channel_id=1, source_target_pairs={{0,4},{4,0},{1,5},{5,1},{2,6},{6,2},{3,7},{7,3},{8,12},{12,8},{9,1... | collective-permute-start | bytes 983048 | tf_op jit(solution)/shard_map/ppermute | solution.py:165
  (47 other events, 207.3 us)
Sparse Core Ops, SparseCore 0:
  11.4 64.2 all-gather.4
  105.3 76.6 reduce-scatter.3
  186.1 54.7 all-gather.6
  242.8 54.3 all-gather.8
  339.1 73.4 reduce-scatter.5
  445.1 66.3 all-gather.10
  525.6 96.1 reduce-scatter.7

commit v8 on v7

--- a/solution.py
+++ b/solution.py
@@ -94,12 +94,6 @@
 
 def sum_own(parts, from_near, from_across):
     return add_inner(parts[0], from_across) + from_near.astype(F32)
-
-
-def send_direct(parts):
-    return [
-        lax.ppermute(part, "do", perm) for part, perm in zip(parts[1:], (NEAR, CROSS, MIRROR))
-    ]
 
 
 class Plan:
@@ -480,9 +474,18 @@
     )(*loader.operands, ctx_grad, normed, queries, both, lse, cosine, sine, seg_col, seg_row)
 
 
+PACKS = (
+    ((0, 0), (0, 1)),
+    ((1, 0), (1, 1), (2, 1)),
+    ((2, 0),),
+    ((3, 0),),
+    ((3, 1),),
+)
+
+
 def out_weights_kernel(plan, ctx_ref, res_ref, *refs):
-    count = plan.cuts
-    qkv_refs, grad_refs, acc = refs[:-1][: count * plan.line], refs[-1 - count : -1], refs[-1]
+    count = plan.cuts * plan.line
+    qkv_refs, grad_refs, acc = refs[:count], refs[count:-1], refs[-1]
     step = pl.program_id(0)
 
     @pl.when(step == 0)
@@ -497,25 +500,27 @@
             grad_refs[0][...] = acc[...].astype(LOW)
             return
         rows = plan.rows
-        for k, (qkv, out) in enumerate(zip(qkv_refs, grad_refs)):
-            wide = qkv.shape[1]
-            out[:, :wide] = qkv[...]
-            for x in range(2):
-                at = k * plan.block + x * rows
-                out[x * rows : (x + 1) * rows, wide:] = acc[:, at : at + rows].astype(LOW)
+        for out, halves in zip(grad_refs, PACKS):
+            for i, (k, x) in enumerate(halves):
+                wide = qkv_refs[k].shape[1]
+                here, at = slice(i * rows, (i + 1) * rows), k * plan.block + x * rows
+                out[here, :wide] = qkv_refs[k][x * rows : (x + 1) * rows, :]
+                out[here, wide:] = acc[:, at : at + rows].astype(LOW)
 
 
 def out_weights(plan, ctx, res_all, grads_qkv):
     rows, width = res_all.shape
     heads = ctx.shape[1]
     extra = list(grads_qkv) if plan.line else []
-    shape = (plan.block, extra[0].shape[1] + heads) if plan.line else (heads, width)
+    shapes = [(heads, width)]
+    if plan.line:
+        shapes = [(len(halves) * plan.rows, extra[0].shape[1] + heads) for halves in PACKS]
     return pl.pallas_call(
         functools.partial(out_weights_kernel, plan),
         grid=(rows // LEN,),
         in_specs=[per_seq((LEN, heads)), per_seq((LEN, width))] + [once(g.shape) for g in extra],
-        out_specs=[once(shape)] * plan.cuts,
-        out_shape=[jax.ShapeDtypeStruct(shape, LOW)] * plan.cuts,
+        out_specs=[once(shape) for shape in shapes],
+        out_shape=[jax.ShapeDtypeStruct(shape, LOW) for shape in shapes],
         scratch_shapes=[pltpu.VMEM((heads, width), F32)],
         compiler_params=pltpu.CompilerParams(vmem_limit_bytes=40 * MIB),
         cost_estimate=SMALL,
@@ -1154,7 +1159,9 @@
         near_sum_2, across_sum_2 = sum_near_send(*sum_near_parts(grads_2, crossed_2, inward_2))
         ffn_pair_1 = trade(sum_own(grads_1, near_sum_1, across_sum_1))
         near_sum_2, across_sum_2, grads_attn = fence(near_sum_2, across_sum_2, grads_attn)
-        direct = send_direct(grads_attn)
+        own_attn, to_near, to_cross, to_mirror, kept = grads_attn
+        from_near = lax.ppermute(to_near, "do", NEAR)
+        direct = [lax.ppermute(to_cross, "do", CROSS), lax.ppermute(to_mirror, "do", MIRROR)]
         ffn_pair_2 = trade(sum_own(grads_2, near_sum_2, across_sum_2))
     second = plane.swap_second(add(goes_on, arrives[1]).astype(LOW))
     place = lax.axis_index("do") if plan.line else jnp.zeros((), jnp.int32)
@@ -1166,9 +1173,14 @@
         "ffn": [(w_gate, m_gate, v_gate), (w_up, m_up, v_up), (w_down, m_down, v_down)],
     }
     if plan.line:
+        from_near, ffn_pair_1, ffn_pair_2 = fence(from_near, ffn_pair_1, ffn_pair_2)
+        passed = add(kept, from_near[2 * half :]).astype(LOW)
+        direct.append(lax.ppermute(passed, "do", MIRROR))
         ffn_updated = adamw_ffn(lax.axis_index("di"), ffn_pair_1, ffn_pair_2, states["ffn"])
         direct, ffn_updated, second, back_one = fence(direct, ffn_updated, second, back_one)
-        attn_pair = trade(add(grads_attn[0], *direct))
+        low = add(own_attn[:half], from_near[:half], direct[0], direct[1])
+        high = add(own_attn[half:], from_near[half : 2 * half], direct[2])
+        attn_pair = plan.trade(low, high)
         attn_updated = adamw_attn(lax.axis_index("di"), attn_pair, states["attn"])
     else:
 

time: 673 us -> 665 us (0.988)
  waiting for transfers between devices: 229 us -> 213 us
    ppermute x3, waiting for transfers between devices: 42.6 us -> 19.5 us  [trade(): theirs = lax.ppermute(self.by_x(high, low).astype(LOW), 'di', PAIR)]
  transfers between devices with their start and end apart: 54 -> 55, of which waited for: 33 -> 34; matrix products, arithmetic and copies ran while one was open for 12% -> 13% of each run, Pallas kernels for 33% -> 34%
where the time goes in v8:
time: 665 us; the launch traced here: 652 us
  Pallas kernels  225 us (34%)
  waiting for transfers between devices  213 us (32%)
  other arithmetic  84.1 us (13%)
  starting transfers between devices  69.3 us (10%)
  local copies, waits for them, and re-layouts  27 us (4%)
  blocking collectives  17.6 us (3%)
  between operations  15.8 us (2%)
    pallas_call x2, Pallas kernels, ffn_main(): pl.pallas_call(functools.partial(ffn_main_kernel, loader, len(more)), gri...  62.4 us
    pallas_call x3, Pallas kernels, ffn_weights(): pl.pallas_call(functools.partial(ffn_weights_kernel, plan), grid=(count,)...  47.7 us
    pallas_call x1, Pallas kernels, attn_backward(): pl.pallas_call(functools.partial(attn_backward_kernel, heads // 128, load...  33 us
    ppermute x3, waiting for transfers between devices, line_last(): return lax.ppermute(across_near, 'do', perm)  32.9 us
    ppermute x3, waiting for transfers between devices, swap_first(): return lax.ppermute(value, self.axes, self.pairs(True))  24 us
    pallas_call x1, Pallas kernels, attn_forward(): pl.pallas_call(functools.partial(attn_forward_kernel, heads // 128, loade...  22.4 us
    ppermute x3, waiting for transfers between devices, trade(): theirs = lax.ppermute(self.by_x(high, low).astype(LOW), 'di', PAIR)  19.5 us
    ppermute x2, waiting for transfers between devices, sum_near_send(): return (lax.ppermute(first, 'do', NEAR), lax.ppermute(third, 'do', MIDDLE))  19.1 us
  transfers between devices with their start and end apart: 55, of which 34 were waited for; matrix products, arithmetic and copies ran while one was open for 13% of the time, Pallas kernels for 34%

profile of v8, /device:TPU:9, one launch (start us, length us, event | category | flops | bytes accessed | tf_op | source)
XLA Modules:
  0.0 651.9 jit_solution(8037379975283262279)
XLA Ops:
  18.2 2.8 collective-permute-done.1
  21.6 4.2 collective-permute-start.3
  25.9 3.7 fusion.6
  36.1 3.0 collective-permute-done.3.refs_5_
  39.1 3.1 collective-permute-start.5
  42.7 10.2 %collective-permute-done.6 = bf16[256,1536]{1,0:T(8,128)(2,1)S(1)} collective-permute-done((bf16[256,1536]{1,0:T(8,128)(2,1)S(1)}, bf16[256,1536]{1,0:T(8,128)(2,1)S(1)}, u32[]{:S(2)}, u32[]{:S(2)}) %collective-permute-start.6) | collective-permute-done | bytes 786464 | tf_op jit(solution)/shard_map/ppermute | solution.py:131
  57.5 9.2 %collective-permute-done.7.refs_6_ = bf16[512,640]{1,0:T(8,128)(2,1)S(1)} collective-permute-done((bf16[512,640]{1,0:T(8,128)(2,1)S(1)}, bf16[512,640]{1,0:T(8,128)(2,1)S(1)}, u32[]{:S(2)}, u32[]{:S(2)}) %collective-permute-start.7) | collective-permute-done | bytes 655392 | tf_op jit(solution)/shard_map/ppermute | solution.py:62
  66.6 2.3 collective-permute-start.8
  69.0 5.2 collective-permute-start.9
  77.0 22.4 %attn_forward.1 = (bf16[2048,2048]{1,0:T(8,128)(2,1)}, bf16[2048,256]{1,0:T(8,128)(2,1)}, bf16[2048,256]{1,0:T(8,128)(2,1)}, bf16[2048,128]{1,0:T(8,128)(2,1)}, ...) custom-call(s32[1]{0:T(128)} %bitcast.1.refs_0_, bf16[512,640]{1,0:T(8,128)(2,1)} %copy-done.16, ...), custom_call_target="tpu_custom_call" | custom-call | flops 1 | bytes 1 | tf_op jit(solution)/shard_map/attn_forward/pallas_call | solution.py:410
  99.4 5.7 collective-permute-done.11
  105.3 3.2 collective-permute-start.13
  110.1 12.7 %collective-permute-done.14 = bf16[256,2048]{1,0:T(8,128)(2,1)} collective-permute-done((bf16[256,2048]{1,0:T(8,128)(2,1)}, bf16[256,2048]{1,0:T(8,128)(2,1)}, u32[]{:S(2)}, u32[]{:S(2)}) %collective-permute-start.14) | collective-permute-done | bytes 1048608 | tf_op jit(solution)/shard_map/ppermute | solution.py:916
  122.8 11.2 %collective-permute-done.15 = bf16[256,2048]{1,0:T(8,128)(2,1)} collective-permute-done((bf16[256,2048]{1,0:T(8,128)(2,1)S(1)}, bf16[256,2048]{1,0:T(8,128)(2,1)}, u32[]{:S(2)}, u32[]{:S(2)}) %collective-permute-start.15) | collective-permute-done | bytes 1048608 | tf_op jit(solution)/shard_map/ppermute | solution.py:916
  134.1 2.9 collective-permute-done.12.refs_4_
  145.2 2.7 pad_maximum_fusion.1
  147.8 19.7 %collective-permute-done.16.refs_6_ = bf16[512,1536]{1,0:T(8,128)(2,1)} collective-permute-done((bf16[512,1536]{1,0:T(8,128)(2,1)}, bf16[512,1536]{1,0:T(8,128)(2,1)}, u32[]{:S(2)}, u32[]{:S(2)}) %collective-permute-start.16) | collective-permute-done | bytes 1572896 | tf_op jit(solution)/shard_map/ppermute | solution.py:62
  167.5 14.4 %reduce-scatter.4.cloned.1.call-done = bf16[256,2048]{1,0:T(8,128)(2,1)} async-done(((bf16[2048,2048]{1,0:T(8,128)(2,1)}), bf16[256,2048]{1,0:T(8,128)(2,1)}) %reduce-scatter.4.cloned.1.call-update) | async-done | bytes 1048592 | tf_op jit(solution)/shard_map/reduce_scatter | solution.py:1035
  187.0 4.1 collective-permute-start.18
  191.1 2.7 collective-permute-done.19
  193.8 4.2 broadcast_select_fusion.1
  198.0 6.4 pad_maximum_fusion
  204.3 8.4 %copy.81 = bf16[4,2,256,2048]{3,2,1,0:T(8,128)(2,1)} copy(bf16[4,2,256,2048]{3,2,0,1:T(8,128)(2,1)} %pad_maximum_fusion) | data formatting | bytes 16777216 | tf_op jit(solution)/shard_map/concatenate | solution.py:45
  212.7 10.2 %collective-permute-done.17.refs_2_ = bf16[512,1536]{1,0:T(8,128)(2,1)} collective-permute-done((bf16[512,1536]{1,0:T(8,128)(2,1)S(1)}, bf16[512,1536]{1,0:T(8,128)(2,1)}, u32[]{:S(2)}, u32[]{:S(2)}) %collective-permute-start.17) | collective-permute-done | bytes 1572896 | tf_op jit(solution)/shard_map/ppermute | solution.py:53
  222.8 2.8 collective-permute-done.18.refs_5_
  225.8 3.3 collective-permute-start.21
  229.1 11.8 %all-gather.7.cloned.1.call-done.refs_7_.x_ref = bf16[2048,2048]{1,0:T(8,128)(2,1)} async-done(((bf16[256,2048]{1,0:T(8,128)(2,1)}), bf16[2048,2048]{1,0:T(8,128)(2,1)}) %all-gather.7.cloned.1.call-update) | async-done | bytes 8388624 | tf_op jit(solution)/shard_map/all_gather | solution.py:1059
  240.9 30.3 %ffn_main.2 = (bf16[2048,2048]{1,0:T(8,128)(2,1)}, bf16[2048,512]{1,0:T(8,128)(2,1)}, bf16[2048,1024]{1,0:T(8,128)(2,1)}, bf16[512,2048]{1,0:T(8,128)(2,1)}) custom-call(s32[1]{0:T(128)} %bitcast.1.refs_0_, bf16[512,1536]{1,0:T(8,128)(2,1)} %pad_maximum_fusion.7.refs_1_, bf16[512,1536]{1,0:T(8,128)(2,1)} %collective-permute-done.8.refs_2_, ...), custom_call_target="tpu_custom_call" | custom-call | flops 1 | bytes 1 | tf_op jit(solution)/shard_map/ffn_main/pallas_call | solution.py:609
  271.3 3.5 collective-permute-start.22
  274.7 13.1 %ffn_weights.3 = (bf16[256,1536]{1,0:T(8,128)(2,1)}, bf16[256,1536]{1,0:T(8,128)(2,1)}, bf16[512,1536]{1,0:T(8,128)(2,1)}) custom-call(bf16[2048,2048]{1,0:T(8,128)(2,1)} %all-gather.7.cloned.1.call-done.refs_7_.x_ref, bf16[2048,2048]{1,0:T(8,128)(2,1)} %bitcast.54, bf16[2048,512]{1,0:T(8,128)(2,1)} %get-tuple-element.291.act_ref.act_1, ...), custom_call_target="tpu_custom_call" | custom-call | flops 1 | bytes 1 | tf_op jit(solution)/shard_map/ffn_weights/pallas_call | solution.py:691
  290.9 12.2 %ffn_weights.4 = bf16[1024,1536]{1,0:T(8,128)(2,1)} custom-call(bf16[2048,2048]{1,0:T(8,128)(2,1)} %all-gather.7.cloned.1.call-done.refs_7_.x_ref, bf16[2048,2048]{1,0:T(8,128)(2,1)} %bitcast.55, bf16[2048,512]{1,0:T(8,128)(2,1)} %get-tuple-element.291.act_ref.act_1, bf16[2048,1024]{1,0:T(8,128)(2,1)} %get-tuple-element.272.both_ref), custom_call_target="tpu_custom_call" | custom-call | flops 1 | bytes 1 | tf_op jit(solution)/shard_map/ffn_weights/pallas_call | solution.py:691
  303.1 4.0 collective-permute-done.22.refs_6_
  307.1 32.1 %ffn_main.3 = (bf16[2048,2048]{1,0:T(8,128)(2,1)}, bf16[2048,512]{1,0:T(8,128)(2,1)}, bf16[2048,1024]{1,0:T(8,128)(2,1)}, bf16[512,2048]{1,0:T(8,128)(2,1)}) custom-call(s32[1]{0:T(128)} %bitcast.1.refs_0_, bf16[512,1536]{1,0:T(8,128)(2,1)} %pad_maximum_fusion.8.refs_1_, bf16[512,1536]{1,0:T(8,128)(2,1)} %collective-permute-done.17.refs_2_, ...), custom_call_target="tpu_custom_call" | custom-call | flops 1 | bytes 1 | tf_op jit(solution)/shard_map/ffn_main/pallas_call | solution.py:609
  340.6 3.0 add_convert_fusion.5
  345.6 4.3 collective-permute-start.26
  349.8 22.4 %ffn_weights.5 = (bf16[256,1536]{1,0:T(8,128)(2,1)}, bf16[256,1536]{1,0:T(8,128)(2,1)}, bf16[1536,1536]{1,0:T(8,128)(2,1)}) custom-call(bf16[2048,2048]{1,0:T(8,128)(2,1)} %all-gather.7.cloned.1.call-done.refs_7_.x_ref, bf16[2048,2048]{1,0:T(8,128)(2,1)} %bitcast.57, bf16[2048,512]{1,0:T(8,128)(2,1)} %get-tuple-element.292.act_ref.act_2, ...), custom_call_target="tpu_custom_call" | custom-call | flops 1 | bytes 1 | tf_op jit(solution)/shard_map/ffn_weights/pallas_call | solution.py:691
  372.2 7.3 %collective-permute-done.25 = bf16[512,1536]{1,0:T(8,128)(2,1)S(1)} collective-permute-done((bf16[512,1536]{1,0:T(8,128)(2,1)}, bf16[512,1536]{1,0:T(8,128)(2,1)S(1)}, u32[]{:S(2)}, u32[]{:S(2)}) %collective-permute-start.25) | collective-permute-done | bytes 1572896 | tf_op jit(solution)/shard_map/ppermute | solution.py:83
  379.5 3.8 collective-permute-done.26
  384.5 16.1 %ffn_out.1 = (bf16[2048,2048]{1,0:T(8,128)(2,1)}, f32[1,2048]{1,0:T(1,128)}) custom-call(bf16[2048,512]{1,0:T(8,128)(2,1)} %get-tuple-element.291.act_ref.act_1, bf16[2048,512]{1,0:T(8,128)(2,1)} %get-tuple-element.292.act_ref.act_2, bf16[512,2048]{1,0:T(8,128)(2,1)} %get-tuple-element.293.down_1, bf16[512,2048]{1,0:T(8,128)(2,1)} %get-tuple-element.294.down_2, ...), custom_call_target="tpu_custom_call" | custom-call | flops 1 | bytes 1 | tf_op jit(solution)/shard_map/ffn_out/pallas_call | solution.py:717
  401.9 4.9 add_convert_fusion.2
  406.8 6.0 reduce-scatter.6.cloned.1.call-done.back_ref
  412.8 8.8 %residual_backward.1 = (f32[256,2048]{1,0:T(8,128)}, bf16[256,2048]{1,0:T(8,128)(2,1)}, bf16[256,2048]{1,0:T(8,128)(2,1)}) custom-call(bf16[256,2048]{1,0:T(8,128)(2,1)} %reduce-scatter.6.cloned.1.call-done.back_ref, f32[256,2048]{1,0:T(8,128)} %get-tuple-element.433.residual_ref, f32[256,1]{1,0:T(8,128)} %copy.82.scale_ref, f32[1,2048]{1,0:T(1,128)} %bitcast.69, ...), custom_call_target="tpu_custom_call" | custom-call | flops 1 | bytes 1 | tf_op jit(solution)/shard_map/residual_backward/pallas_call | solution.py:550
  421.7 2.5 add_convert_fusion.4
  426.5 17.6 %all_to_all.19 = bf16[256,8,256]{2,0,1:T(8,128)(2,1)} all-to-all(bf16[256,8,256]{2,0,1:T(8,128)(2,1)S(1)} %bitcast.63), channel_id=1, replica_groups=mesh['do'=4,'di'=2,'tp'=4] {'di','tp'}, dimensions={1} | all-to-all | bytes 2097152 | tf_op jit(solution)/shard_map/all_to_all | solution.py:1122
  444.2 5.1 select_bitcast_fusion
  450.3 4.3 collective-permute-start.37
  454.6 2.6 collective-permute-done.29
  457.2 6.1 fusion
  467.8 33.0 %attn_backward.1 = (bf16[2048,2048]{1,0:T(8,128)(2,1)}, f32[1,2048]{1,0:T(1,128)}, bf16[512,384]{1,0:T(8,128)(2,1)}, bf16[512,384]{1,0:T(8,128)(2,1)}, bf16[512,...) custom-call(s32[1]{0:T(128)} %bitcast.1.refs_0_, bf16[512,640]{1,0:T(8,128)(2,1)} %copy-done.16, bf16[512,640]{1,0:T(8,128)(2,1)} %copy-done.21, ...), custom_call_target="tpu_custom_call" | custom-call | flops 1 | bytes 1 | tf_op jit(solution)/shard_map/attn_backward/pallas_call | solution.py:449
  503.6 11.3 %collective-permute-done.31 = f32[2,2048]{1,0:T(2,128)S(1)} collective-permute-done((f32[2,2048]{1,0:T(2,128)S(1)}, f32[2,2048]{1,0:T(2,128)S(1)}, u32[]{:S(2)}, u32[]{:S(2)}) %collective-permute-start.31) | collective-permute-done | bytes 16416 | tf_op jit(solution)/shard_map/ppermute | solution.py:766
  518.3 2.8 collective-permute-done.33
  526.1 6.2 convert_add_fusion.2
  532.4 4.1 collective-permute-start.39
  537.3 2.6 select_convert_fusion.1
  541.1 3.7 copy-done
  544.8 4.1 out_weights.1
  550.3 17.3 %collective-permute-done.38 = bf16[512,1536]{1,0:T(8,128)(2,1)} collective-permute-done((bf16[512,1536]{1,0:T(8,128)(2,1)}, bf16[512,1536]{1,0:T(8,128)(2,1)}, u32[]{:S(2)}, u32[]{:S(2)}) %collective-permute-start.38) | collective-permute-done | bytes 1572896 | tf_op jit(solution)/shard_map/ppermute | solution.py:92
  569.4 3.0 convert_add_fusion.1
  579.8 19.4 %collective-permute-done.44.theirs_2 = bf16[256,1536]{1,0:T(8,128)(2,1)S(1)} collective-permute-done((bf16[256,1536]{1,0:T(8,128)(2,1)S(1)}, bf16[256,1536]{1,0:T(8,128)(2,1)S(1)}, u32[]{:S(2)}, u32[]{:S(2)}) %collective-permute-start.44) | collective-permute-done | bytes 786464 | tf_op jit(solution)/shard_map/ppermute | solution.py:159
  602.2 17.7 %adamw_ffn.1 = (f32[256,2048]{1,0:T(8,128)}, f32[256,2048]{1,0:T(8,128)}, f32[256,2048]{1,0:T(8,128)}, f32[256,2048]{1,0:T(8,128)}, f32[256,2048]{1,0:T(8,128)},...) custom-call(s32[1]{0:T(128)} %bitcast.23.x_ref, ...), custom_call_target="tpu_custom_call" | custom-call | flops 1 | bytes 1 | tf_op jit(solution)/shard_map/adamw_ffn/pallas_call | solution.py:811
  621.4 5.2 collective-permute-done.45
  626.7 2.5 select_convert_fusion.2
  630.9 7.5 %finish.1 = (bf16[256,2048]{1,0:T(8,128)(2,1)}, f32[256,2048]{1,0:T(8,128)}) custom-call(s32[1]{0:T(128)} %bitcast.place_ref, bf16[256,2048]{1,0:T(8,128)(2,1)} %reduce-scatter.8.cloned.1.call-done.back_ref, bf16[256,2048]{1,0:T(8,128)(2,1)} %copy-done.6, f32[256,1]{1,0:T(8,128)} %copy.87.scale_ref, f32[1,2048]{1,0:T(1,128)} %bitcast.68, ...), custom_call_target="tpu_custom_call" | custom-call | flops 1 | bytes 1 | tf_op jit(solution)/shard_map/finish/pallas_call | solution.py:879
  639.1 5.5 adamw_attn.1
  (291 shorter events, 87.8 us)
Async XLA Ops:
  7.2 69.8 %all-gather.5.cloned.1.call-start = ((), (), s32[]{:S(2)}) async-start(), calls=%async_computation.4 | async-start | bytes 9437184 | tf_op jit(solution)/shard_map/all_gather | solution.py:951
  9.7 174.0 %copy-start.6 = (bf16[256,2048]{1,0:T(8,128)(2,1)}, bf16[256,2048]{1,0:T(8,128)(2,1)S(1)}, u32[]{:S(2)}) copy-start(bf16[256,2048]{1,0:T(8,128)(2,1)S(1)} %get-tuple-element.415.inputs_ref) | copy-start | bytes 3145732
  9.9 490.9 %copy-start.44 = (f32[2048]{0:T(1024)}, f32[2048]{0:T(1024)S(1)}, u32[]{:S(2)}) copy-start(f32[2048]{0:T(1024)S(1)} %maximum_select_fusion.8) | copy-start | bytes 24580
  11.3 170.7 %reduce-scatter.4.cloned.1.call-start = ((), (), s32[]{:S(2)}) async-start(), calls=%async_computation.5 | async-start | bytes 9437184 | tf_op jit(solution)/shard_map/reduce_scatter | solution.py:1035
  12.1 8.9 %collective-permute-start = (bf16[256,640]{1,0:T(8,128)(2,1)S(1)}, bf16[256,640]{1,0:T(8,128)(2,1)S(1)}, u32[]{:S(2)}, u32[]{:S(2)}) collective-permute-start(bf16[256,640]{1,0:T(8,128)(2,1)S(1)} %pad_maximum_fusion.17), channel_id=1, source_target_pairs={{0,4},{4,0},{1,5},{5,1},{2,6},{6,2},{3,7},{7,3},{8,12},{12,8},{9,1... | collective-permute-start | bytes 983048 | tf_op jit(solution)/shard_map/ppermute | solution.py:131
  13.4 7.5 %collective-permute-start.1 = (s32[2,1024]{1,0:T(2,128)S(1)}, s32[2,1024]{1,0:T(2,128)S(1)}, u32[]{:S(2)}, u32[]{:S(2)}) collective-permute-start(s32[2,1024]{1,0:T(2,128)S(1)} %pad_add_fusion.1), channel_id=1, source_target_pairs={{0,4},{4,0},{1,5},{5,1},{2,6},{6,2},{3,7},{7,3},{8,12},{12,8},{9,1... | collective-permute-start | bytes 24584 | tf_op jit(solution)/shard_map/ppermute | solution.py:954
  21.0 54.7 %copy-start.43 = (s32[1,2048]{1,0:T(1,128)}, s32[1,2048]{1,0:T(1,128)S(1)}, u32[]{:S(2)}) copy-start(s32[1,2048]{1,0:T(1,128)S(1)} %get-tuple-element.495) | copy-start | bytes 24580
  21.3 14.7 %collective-permute-start.2 = (bf16[512,640]{1,0:T(8,128)(2,1)S(1)}, bf16[512,640]{1,0:T(8,128)(2,1)S(1)}, u32[]{:S(2)}, u32[]{:S(2)}) collective-permute-start(bf16[512,640]{1,0:T(8,128)(2,1)S(1)} %pad_maximum_fusion.15.refs_1_), channel_id=1, source_target_pairs={{0,8},{8,0},{16,24},{24,16},{1,9},{9,1},{17,25},{25,17},{2,10},{10... | collective-permute-start | bytes 1966088 | tf_op jit(solution)/shard_map/ppermute | solution.py:53
  21.6 17.5 %collective-permute-start.3 = (bf16[512,640]{1,0:T(8,128)(2,1)S(1)}, bf16[512,640]{1,0:T(8,128)(2,1)S(1)}, u32[]{:S(2)}, u32[]{:S(2)}) collective-permute-start(bf16[512,640]{1,0:T(8,128)(2,1)S(1)} %pad_maximum_fusion.15.refs_1_), channel_id=1, source_target_pairs={{8,16},{16,8},{9,17},{17,9},{10,18},{18,10},{11,19},{19,11},{12,20... | collective-permute-start | bytes 1966088 | tf_op jit(solution)/shard_map/ppermute | solution.py:53
  31.5 21.4 %collective-permute-start.6 = (bf16[256,1536]{1,0:T(8,128)(2,1)S(1)}, bf16[256,1536]{1,0:T(8,128)(2,1)S(1)}, u32[]{:S(2)}, u32[]{:S(2)}) collective-permute-start(bf16[256,1536]{1,0:T(8,128)(2,1)S(1)} %pad_maximum_fusion.12), channel_id=1, source_target_pairs={{0,4},{4,0},{1,5},{5,1},{2,6},{6,2},{3,7},{7,3},{8,12},{12,8},{9,1... | collective-permute-start | bytes 2359304 | tf_op jit(solution)/shard_map/ppermute | solution.py:131
  39.1 13.9 %collective-permute-start.4 = (bf16[512,640]{1,0:T(8,128)(2,1)S(1)}, bf16[512,640]{1,0:T(8,128)(2,1)S(1)}, u32[]{:S(2)}, u32[]{:S(2)}) collective-permute-start(bf16[512,640]{1,0:T(8,128)(2,1)S(1)} %collective-permute-done.3.refs_5_), channel_id=1, source_target_pairs={{0,8},{8,0},{16,24},{24,16},{1,9},{9,1},{17,25},{25,17},{2,10},{10... | collective-permute-start | bytes 1966088 | tf_op jit(solution)/shard_map/ppermute | solution.py:57
  39.1 15.7 %collective-permute-start.5 = (bf16[512,640]{1,0:T(8,128)(2,1)S(1)}, bf16[512,640]{1,0:T(8,128)(2,1)S(1)}, u32[]{:S(2)}, u32[]{:S(2)}) collective-permute-start(bf16[512,640]{1,0:T(8,128)(2,1)S(1)} %collective-permute-done.2.refs_2_), channel_id=1, source_target_pairs={{8,16},{16,8},{9,17},{17,9},{10,18},{18,10},{11,19},{19,11},{12,20... | collective-permute-start | bytes 1966088 | tf_op jit(solution)/shard_map/ppermute | solution.py:58
  42.7 98.8 %copy-start.9 = (bf16[256,2048]{1,0:T(8,128)(2,1)}, bf16[256,2048]{1,0:T(8,128)(2,1)S(1)}, u32[]{:S(2)}) copy-start(bf16[256,2048]{1,0:T(8,128)(2,1)S(1)} %maximum_select_fusion.3.grad_ref) | copy-start | bytes 3145732
  54.8 11.8 %collective-permute-start.7 = (bf16[512,640]{1,0:T(8,128)(2,1)S(1)}, bf16[512,640]{1,0:T(8,128)(2,1)S(1)}, u32[]{:S(2)}, u32[]{:S(2)}) collective-permute-start(bf16[512,640]{1,0:T(8,128)(2,1)S(1)} %collective-permute-done.5.refs_3_), channel_id=1, source_target_pairs={{0,8},{8,0},{16,24},{24,16},{1,9},{9,1},{17,25},{25,17},{2,10},{10... | collective-permute-start | bytes 1966088 | tf_op jit(solution)/shard_map/ppermute | solution.py:62
  66.6 38.5 %collective-permute-start.8 = (bf16[512,1536]{1,0:T(8,128)(2,1)}, bf16[512,1536]{1,0:T(8,128)(2,1)}, u32[]{:S(2)}, u32[]{:S(2)}) collective-permute-start(bf16[512,1536]{1,0:T(8,128)(2,1)} %pad_maximum_fusion.7.refs_1_), channel_id=1, source_target_pairs={{0,8},{8,0},{16,24},{24,16},{1,9},{9,1},{17,25},{25,17},{2,10},{10... | collective-permute-start | bytes 4718600 | tf_op jit(solution)/shard_map/ppermute | solution.py:53
  69.0 36.2 %collective-permute-start.9 = (bf16[512,1536]{1,0:T(8,128)(2,1)}, bf16[512,1536]{1,0:T(8,128)(2,1)}, u32[]{:S(2)}, u32[]{:S(2)}) collective-permute-start(bf16[512,1536]{1,0:T(8,128)(2,1)} %pad_maximum_fusion.7.refs_1_), channel_id=1, source_target_pairs={{8,16},{16,8},{9,17},{17,9},{10,18},{18,10},{11,19},{19,11},{12,20... | collective-permute-start | bytes 4718600 | tf_op jit(solution)/shard_map/ppermute | solution.py:53
  74.1 31.0 %collective-permute-start.10 = (bf16[256,2048]{1,0:T(8,128)(2,1)S(1)}, bf16[256,2048]{1,0:T(8,128)(2,1)}, u32[]{:S(2)}, u32[]{:S(2)}) collective-permute-start(bf16[256,2048]{1,0:T(8,128)(2,1)S(1)} %maximum_select_fusion.3.grad_ref), channel_id=1, source_target_pairs={{0,2},{1,5},{2,0},{3,7},{4,6},{5,1},{6,4},{7,3},{8,10},{9,13},{10,... | collective-permute-start | bytes 3145736 | tf_op jit(solution)/shard_map/ppermute | solution.py:919
  74.5 30.6 %collective-permute-start.11 = (bf16[256,1536]{1,0:T(8,128)(2,1)}, bf16[256,1536]{1,0:T(8,128)(2,1)}, u32[]{:S(2)}, u32[]{:S(2)}) collective-permute-start(bf16[256,1536]{1,0:T(8,128)(2,1)} %pad_maximum_fusion.14), channel_id=1, source_target_pairs={{0,4},{4,0},{1,5},{5,1},{2,6},{6,2},{3,7},{7,3},{8,12},{12,8},{9,1... | collective-permute-start | bytes 2359304 | tf_op jit(solution)/shard_map/ppermute | solution.py:131
  105.2 135.8 %all-gather.7.cloned.1.call-start = ((), (), s32[]{:S(2)}) async-start(), calls=%async_computation.6 | async-start | bytes 9437184 | tf_op jit(solution)/shard_map/all_gather | solution.py:1059
  105.2 31.8 %collective-permute-start.12 = (bf16[512,1536]{1,0:T(8,128)(2,1)}, bf16[512,1536]{1,0:T(8,128)(2,1)}, u32[]{:S(2)}, u32[]{:S(2)}) collective-permute-start(bf16[512,1536]{1,0:T(8,128)(2,1)} %collective-permute-done.9.refs_5_), channel_id=1, source_target_pairs={{0,8},{8,0},{16,24},{24,16},{1,9},{9,1},{17,25},{25,17},{2,10},{10... | collective-permute-start | bytes 4718600 | tf_op jit(solution)/shard_map/ppermute | solution.py:57
  105.3 33.6 %collective-permute-start.13 = (bf16[512,1536]{1,0:T(8,128)(2,1)}, bf16[512,1536]{1,0:T(8,128)(2,1)}, u32[]{:S(2)}, u32[]{:S(2)}) collective-permute-start(bf16[512,1536]{1,0:T(8,128)(2,1)} %collective-permute-done.8.refs_2_), channel_id=1, source_target_pairs={{8,16},{16,8},{9,17},{17,9},{10,18},{18,10},{11,19},{19,11},{12,20... | collective-permute-start | bytes 4718600 | tf_op jit(solution)/shard_map/ppermute | solution.py:58
  108.5 14.3 %collective-permute-start.14 = (bf16[256,2048]{1,0:T(8,128)(2,1)}, bf16[256,2048]{1,0:T(8,128)(2,1)}, u32[]{:S(2)}, u32[]{:S(2)}) collective-permute-start(bf16[256,2048]{1,0:T(8,128)(2,1)} %collective-permute-done.10), channel_id=1, source_target_pairs={{0,4},{1,3},{2,6},{3,1},{4,0},{5,7},{6,2},{7,5},{8,12},{9,11},{10,... | collective-permute-start | bytes 3145736 | tf_op jit(solution)/shard_map/ppermute | solution.py:916
  109.8 24.3 %collective-permute-start.15 = (bf16[256,2048]{1,0:T(8,128)(2,1)S(1)}, bf16[256,2048]{1,0:T(8,128)(2,1)}, u32[]{:S(2)}, u32[]{:S(2)}) collective-permute-start(bf16[256,2048]{1,0:T(8,128)(2,1)S(1)} %maximum_select_fusion.3.grad_ref), channel_id=1, source_target_pairs={{0,4},{1,3},{2,6},{3,1},{4,0},{5,7},{6,2},{7,5},{8,12},{9,11},{10,... | collective-permute-start | bytes 3145736 | tf_op jit(solution)/shard_map/ppermute | solution.py:916
  110.1 73.7 %copy-start.45 = (f32[2048]{0:T(1024)}, f32[2048]{0:T(1024)S(1)}, u32[]{:S(2)}) copy-start(f32[2048]{0:T(1024)S(1)} %maximum_select_fusion.10) | copy-start | bytes 24580
  138.9 28.6 %collective-permute-start.16 = (bf16[512,1536]{1,0:T(8,128)(2,1)}, bf16[512,1536]{1,0:T(8,128)(2,1)}, u32[]{:S(2)}, u32[]{:S(2)}) collective-permute-start(bf16[512,1536]{1,0:T(8,128)(2,1)} %collective-permute-done.13.refs_3_), channel_id=1, source_target_pairs={{0,8},{8,0},{16,24},{24,16},{1,9},{9,1},{17,25},{25,17},{2,10},{10... | collective-permute-start | bytes 4718600 | tf_op jit(solution)/shard_map/ppermute | solution.py:62
  186.0 153.3 %all-gather.9.cloned.1.call-start = ((), (), s32[]{:S(2)}) async-start(), calls=%async_computation.7 | async-start | bytes 9437184 | tf_op jit(solution)/shard_map/all_gather | solution.py:1067
  186.0 7.8 %collective-permute-start.19 = (bf16[1024,2048]{1,0:T(8,128)(2,1)}, bf16[1024,2048]{1,0:T(8,128)(2,1)S(1)}, u32[]{:S(2)}, u32[]{:S(2)}) collective-permute-start(bf16[1024,2048]{1,0:T(8,128)(2,1)} %pad_maximum_fusion.1), channel_id=1, source_target_pairs={{0,1},{1,0},{2,3},{3,2},{4,5},{5,4},{6,7},{7,6},{8,9},{9,8},{10,11... | collective-permute-start | bytes 12582920 | tf_op jit(solution)/shard_map/ppermute | solution.py:922
  186.8 36.1 %collective-permute-start.17 = (bf16[512,1536]{1,0:T(8,128)(2,1)S(1)}, bf16[512,1536]{1,0:T(8,128)(2,1)}, u32[]{:S(2)}, u32[]{:S(2)}) collective-permute-start(bf16[512,1536]{1,0:T(8,128)(2,1)S(1)} %copy-done.13), channel_id=1, source_target_pairs={{0,8},{8,0},{16,24},{24,16},{1,9},{9,1},{17,25},{25,17},{2,10},{10... | collective-permute-start | bytes 4718600 | tf_op jit(solution)/shard_map/ppermute | solution.py:53
  187.0 38.6 %collective-permute-start.18 = (bf16[512,1536]{1,0:T(8,128)(2,1)S(1)}, bf16[512,1536]{1,0:T(8,128)(2,1)}, u32[]{:S(2)}, u32[]{:S(2)}) collective-permute-start(bf16[512,1536]{1,0:T(8,128)(2,1)S(1)} %copy-done.13), channel_id=1, source_target_pairs={{8,16},{16,8},{9,17},{17,9},{10,18},{18,10},{11,19},{19,11},{12,20... | collective-permute-start | bytes 4718600 | tf_op jit(solution)/shard_map/ppermute | solution.py:53
  225.7 187.1 %reduce-scatter.6.cloned.1.call-start = ((), (), s32[]{:S(2)}) async-start(), calls=%async_computation.8 | async-start | bytes 9437184 | tf_op jit(solution)/shard_map/reduce_scatter | solution.py:1091
  225.8 45.5 %collective-permute-start.20 = (bf16[512,1536]{1,0:T(8,128)(2,1)}, bf16[512,1536]{1,0:T(8,128)(2,1)S(1)}, u32[]{:S(2)}, u32[]{:S(2)}) collective-permute-start(bf16[512,1536]{1,0:T(8,128)(2,1)} %collective-permute-done.18.refs_5_), channel_id=1, source_target_pairs={{0,8},{8,0},{16,24},{24,16},{1,9},{9,1},{17,25},{25,17},{2,10},{10... | collective-permute-start | bytes 4718600 | tf_op jit(solution)/shard_map/ppermute | solution.py:57
  225.8 45.4 %collective-permute-start.21 = (bf16[512,1536]{1,0:T(8,128)(2,1)}, bf16[512,1536]{1,0:T(8,128)(2,1)S(1)}, u32[]{:S(2)}, u32[]{:S(2)}) collective-permute-start(bf16[512,1536]{1,0:T(8,128)(2,1)} %collective-permute-done.17.refs_2_), channel_id=1, source_target_pairs={{8,16},{16,8},{9,17},{17,9},{10,18},{18,10},{11,19},{19,11},{12,20... | collective-permute-start | bytes 4718600 | tf_op jit(solution)/shard_map/ppermute | solution.py:58
  271.2 16.6 %copy-start.28 = (bf16[512,1536]{1,0:T(8,128)(2,1)}, bf16[512,1536]{1,0:T(8,128)(2,1)S(1)}, u32[]{:S(2)}) copy-start(bf16[512,1536]{1,0:T(8,128)(2,1)S(1)} %collective-permute-done.20.refs_4_) | copy-start | bytes 4718596
  271.3 16.5 %copy-start.29 = (bf16[512,1536]{1,0:T(8,128)(2,1)}, bf16[512,1536]{1,0:T(8,128)(2,1)S(1)}, u32[]{:S(2)}) copy-start(bf16[512,1536]{1,0:T(8,128)(2,1)S(1)} %collective-permute-done.21.refs_3_) | copy-start | bytes 4718596
  271.3 35.8 %collective-permute-start.22 = (bf16[512,1536]{1,0:T(8,128)(2,1)S(1)}, bf16[512,1536]{1,0:T(8,128)(2,1)}, u32[]{:S(2)}, u32[]{:S(2)}) collective-permute-start(bf16[512,1536]{1,0:T(8,128)(2,1)S(1)} %collective-permute-done.21.refs_3_), channel_id=1, source_target_pairs={{8,0},{16,24},{9,1},{17,25},{10,2},{18,26},{11,3},{19,27},{12,4},{... | collective-permute-start | bytes 4718600 | tf_op jit(solution)/shard_map/ppermute | solution.py:62
  287.8 51.4 %collective-permute-start.23 = (bf16[256,1536]{1,0:T(8,128)(2,1)}, bf16[256,1536]{1,0:T(8,128)(2,1)}, u32[]{:S(2)}, u32[]{:S(2)}) collective-permute-start(bf16[256,1536]{1,0:T(8,128)(2,1)} %get-tuple-element.278), channel_id=1, source_target_pairs={{0,8},{24,16},{1,9},{25,17},{2,10},{26,18},{3,11},{27,19},{4,12},{... | collective-permute-start | bytes 2359304 | tf_op jit(solution)/shard_map/ppermute | solution.py:1077
  289.1 50.1 %collective-permute-start.24 = (bf16[256,1536]{1,0:T(8,128)(2,1)}, bf16[256,1536]{1,0:T(8,128)(2,1)}, u32[]{:S(2)}, u32[]{:S(2)}) collective-permute-start(bf16[256,1536]{1,0:T(8,128)(2,1)} %get-tuple-element.279), channel_id=1, source_target_pairs={{0,8},{24,16},{1,9},{25,17},{2,10},{26,18},{3,11},{27,19},{4,12},{... | collective-permute-start | bytes 2359304 | tf_op jit(solution)/shard_map/ppermute | solution.py:1077
  339.3 185.4 %all-gather.11.cloned.1.call-start = ((), (), s32[]{:S(2)}) async-start(), calls=%async_computation.9 | async-start | bytes 9437184 | tf_op jit(solution)/shard_map/all_gather | solution.py:1136
  343.6 35.9 %collective-permute-start.25 = (bf16[512,1536]{1,0:T(8,128)(2,1)}, bf16[512,1536]{1,0:T(8,128)(2,1)S(1)}, u32[]{:S(2)}, u32[]{:S(2)}) collective-permute-start(bf16[512,1536]{1,0:T(8,128)(2,1)} %add_convert_fusion.5), channel_id=1, source_target_pairs={{0,8},{8,0},{16,24},{24,16},{1,9},{9,1},{17,25},{25,17},{2,10},{10... | collective-permute-start | bytes 4718600 | tf_op jit(solution)/shard_map/ppermute | solution.py:83
  345.6 37.7 %collective-permute-start.26 = (bf16[512,1536]{1,0:T(8,128)(2,1)}, bf16[512,1536]{1,0:T(8,128)(2,1)S(1)}, u32[]{:S(2)}, u32[]{:S(2)}) collective-permute-start(bf16[512,1536]{1,0:T(8,128)(2,1)} %add_convert_fusion.5), channel_id=1, source_target_pairs={{8,16},{16,8},{9,17},{17,9},{10,18},{18,10},{11,19},{19,11},{12,20... | collective-permute-start | bytes 4718600 | tf_op jit(solution)/shard_map/ppermute | solution.py:84
  383.3 17.5 %collective-permute-start.27 = (bf16[256,1536]{1,0:T(8,128)(2,1)}, bf16[256,1536]{1,0:T(8,128)(2,1)}, u32[]{:S(2)}, u32[]{:S(2)}) collective-permute-start(bf16[256,1536]{1,0:T(8,128)(2,1)} %get-tuple-element.296), channel_id=1, source_target_pairs={{0,8},{8,0},{16,24},{24,16},{1,9},{9,1},{17,25},{25,17},{2,10},{10... | collective-permute-start | bytes 2359304 | tf_op jit(solution)/shard_map/ppermute | solution.py:1101
  384.5 17.4 %copy-start.8 = (bf16[1024,1536]{1,0:T(8,128)(2,1)S(1)}, bf16[1024,1536]{1,0:T(8,128)(2,1)}, u32[]{:S(2)}) copy-start(bf16[1024,1536]{1,0:T(8,128)(2,1)} %ffn_weights.4) | copy-start | bytes 9437188
  400.8 20.9 %collective-permute-start.28 = (bf16[256,1536]{1,0:T(8,128)(2,1)}, bf16[256,1536]{1,0:T(8,128)(2,1)}, u32[]{:S(2)}, u32[]{:S(2)}) collective-permute-start(bf16[256,1536]{1,0:T(8,128)(2,1)} %get-tuple-element.303), channel_id=1, source_target_pairs={{0,8},{8,0},{16,24},{24,16},{1,9},{9,1},{17,25},{25,17},{2,10},{10... | collective-permute-start | bytes 2359304 | tf_op jit(solution)/shard_map/ppermute | solution.py:1105
  444.1 182.5 %reduce-scatter.8.cloned.1.call-start = ((), (), s32[]{:S(2)}) async-start(), calls=%async_computation.10 | async-start | bytes 9437184 | tf_op jit(solution)/shard_map/reduce_scatter | solution.py:1151
  449.3 7.9 %collective-permute-start.29 = (bf16[4,256,2048]{2,1,0:T(8,128)(2,1)}, bf16[4,256,2048]{2,1,0:T(8,128)(2,1)}, u32[]{:S(2)}, u32[]{:S(2)}) collective-permute-start(bf16[4,256,2048]{2,1,0:T(8,128)(2,1)} %select_bitcast_fusion), channel_id=1, source_target_pairs={{0,1},{1,0},{2,3},{3,2},{4,5},{5,4},{6,7},{7,6},{8,9},{9,8},{10,11... | collective-permute-start | bytes 12582920 | tf_op jit(solution)/shard_map/ppermute | solution.py:922
  450.0 74.6 %collective-permute-start.36 = (bf16[1024,1536]{1,0:T(8,128)(2,1)}, bf16[1024,1536]{1,0:T(8,128)(2,1)}, u32[]{:S(2)}, u32[]{:S(2)}) collective-permute-start(bf16[1024,1536]{1,0:T(8,128)(2,1)} %get-tuple-element.328), channel_id=1, source_target_pairs={{0,8},{8,0},{16,24},{24,16},{1,9},{9,1},{17,25},{25,17},{2,10},{10... | collective-permute-start | bytes 9437192 | tf_op jit(solution)/shard_map/ppermute | solution.py:1120
  450.3 74.4 %collective-permute-start.37 = (bf16[1024,1536]{1,0:T(8,128)(2,1)S(1)}, bf16[1024,1536]{1,0:T(8,128)(2,1)}, u32[]{:S(2)}, u32[]{:S(2)}) collective-permute-start(bf16[1024,1536]{1,0:T(8,128)(2,1)S(1)} %get-tuple-element.329), channel_id=1, source_target_pairs={{8,16},{16,8},{9,17},{17,9},{10,18},{18,10},{11,19},{19,11},{12,20... | collective-permute-start | bytes 9437192 | tf_op jit(solution)/shard_map/ppermute | solution.py:1121
  466.6 58.1 %collective-permute-start.35 = (bf16[2,256,2048]{2,1,0:T(8,128)(2,1)}, bf16[2,256,2048]{2,1,0:T(8,128)(2,1)}, u32[]{:S(2)}, u32[]{:S(2)}) collective-permute-start(bf16[2,256,2048]{2,1,0:T(8,128)(2,1)} %pad_maximum_fusion.6), channel_id=1, source_target_pairs={{0,4},{1,3},{2,6},{3,1},{4,0},{5,7},{6,2},{7,5},{8,12},{9,11},{10,... | collective-permute-start | bytes 6291464 | tf_op jit(solution)/shard_map/ppermute | solution.py:916
  501.6 1.4 collective-permute-start.30
  503.1 11.8 %collective-permute-start.31 = (f32[2,2048]{1,0:T(2,128)S(1)}, f32[2,2048]{1,0:T(2,128)S(1)}, u32[]{:S(2)}, u32[]{:S(2)}) collective-permute-start(f32[2,2048]{1,0:T(2,128)S(1)} %add.172), channel_id=1, source_target_pairs={{0,2},{1,3},{2,0},{3,1},{4,6},{5,7},{6,4},{7,5},{8,10},{9,11},{10,... | collective-permute-start | bytes 49160 | tf_op jit(solution)/shard_map/ppermute | solution.py:766
  514.9 3.1 collective-permute-start.32
  518.0 3.1 collective-permute-start.33
  521.1 3.6 collective-permute-start.34
  532.3 35.2 %collective-permute-start.38 = (bf16[512,1536]{1,0:T(8,128)(2,1)}, bf16[512,1536]{1,0:T(8,128)(2,1)}, u32[]{:S(2)}, u32[]{:S(2)}) collective-permute-start(bf16[512,1536]{1,0:T(8,128)(2,1)} %get-tuple-element.425), channel_id=1, source_target_pairs={{0,8},{8,0},{16,24},{24,16},{1,9},{9,1},{17,25},{25,17},{2,10},{10... | collective-permute-start | bytes 4718600 | tf_op jit(solution)/shard_map/ppermute | solution.py:92
  532.4 37.0 %collective-permute-start.39 = (bf16[512,1536]{1,0:T(8,128)(2,1)}, bf16[512,1536]{1,0:T(8,128)(2,1)}, u32[]{:S(2)}, u32[]{:S(2)}) collective-permute-start(bf16[512,1536]{1,0:T(8,128)(2,1)} %get-tuple-element.426), channel_id=1, source_target_pairs={{8,16},{16,8},{9,17},{17,9},{10,18},{18,10},{11,19},{19,11},{12,20... | collective-permute-start | bytes 4718600 | tf_op jit(solution)/shard_map/ppermute | solution.py:92
  539.9 39.8 %collective-permute-start.43 = (bf16[256,1536]{1,0:T(8,128)(2,1)S(1)}, bf16[256,1536]{1,0:T(8,128)(2,1)S(1)}, u32[]{:S(2)}, u32[]{:S(2)}) collective-permute-start(bf16[256,1536]{1,0:T(8,128)(2,1)S(1)} %select_convert_fusion.1), channel_id=1, source_target_pairs={{0,4},{4,0},{1,5},{5,1},{2,6},{6,2},{3,7},{7,3},{8,12},{12,8},{9,1... | collective-permute-start | bytes 2359304 | tf_op jit(solution)/shard_map/ppermute | solution.py:159
  572.5 26.7 %collective-permute-start.44 = (bf16[256,1536]{1,0:T(8,128)(2,1)S(1)}, bf16[256,1536]{1,0:T(8,128)(2,1)S(1)}, u32[]{:S(2)}, u32[]{:S(2)}) collective-permute-start(bf16[256,1536]{1,0:T(8,128)(2,1)S(1)} %select_convert_fusion), channel_id=1, source_target_pairs={{0,4},{4,0},{1,5},{5,1},{2,6},{6,2},{3,7},{7,3},{8,12},{12,8},{9,1... | collective-permute-start | bytes 2359304 | tf_op jit(solution)/shard_map/ppermute | solution.py:159
  573.6 25.6 %collective-permute-start.42 = (bf16[768,640]{1,0:T(8,128)(2,1)S(1)}, bf16[768,640]{1,0:T(8,128)(2,1)S(1)}, u32[]{:S(2)}, u32[]{:S(2)}) collective-permute-start(bf16[768,640]{1,0:T(8,128)(2,1)S(1)} %get-tuple-element.346), channel_id=1, source_target_pairs={{0,8},{8,0},{16,24},{24,16},{1,9},{9,1},{17,25},{25,17},{2,10},{10... | collective-permute-start | bytes 2949128 | tf_op jit(solution)/shard_map/ppermute | solution.py:1163
  575.3 46.2 %collective-permute-start.46 = (bf16[256,2048]{1,0:T(8,128)(2,1)S(1)}, bf16[256,2048]{1,0:T(8,128)(2,1)S(1)}, u32[]{:S(2)}, u32[]{:S(2)}) collective-permute-start(bf16[256,2048]{1,0:T(8,128)(2,1)S(1)} %fusion.4), channel_id=1, source_target_pairs={{0,2},{1,5},{2,0},{3,7},{4,6},{5,1},{6,4},{7,3},{8,10},{9,13},{10,... | collective-permute-start | bytes 3145736 | tf_op jit(solution)/shard_map/ppermute | solution.py:919
  576.4 45.1 %collective-permute-start.40 = (bf16[256,640]{1,0:T(8,128)(2,1)}, bf16[256,640]{1,0:T(8,128)(2,1)}, u32[]{:S(2)}, u32[]{:S(2)}) collective-permute-start(bf16[256,640]{1,0:T(8,128)(2,1)} %get-tuple-element.343), channel_id=1, source_target_pairs={{0,16},{8,24},{16,0},{24,8},{1,17},{9,25},{17,1},{25,9},{2,18},{10... | collective-permute-start | bytes 983048 | tf_op jit(solution)/shard_map/ppermute | solution.py:1164
  579.7 21.8 %copy-start.38 = (bf16[256,1536]{1,0:T(8,128)(2,1)}, bf16[256,1536]{1,0:T(8,128)(2,1)S(1)}, u32[]{:S(2)}) copy-start(bf16[256,1536]{1,0:T(8,128)(2,1)S(1)} %collective-permute-done.43.theirs_1) | copy-start | bytes 2359300
  579.7 41.7 %collective-permute-start.41 = (bf16[256,640]{1,0:T(8,128)(2,1)S(1)}, bf16[256,640]{1,0:T(8,128)(2,1)}, u32[]{:S(2)}, u32[]{:S(2)}) collective-permute-start(bf16[256,640]{1,0:T(8,128)(2,1)S(1)} %get-tuple-element.344), channel_id=1, source_target_pairs={{0,24},{8,16},{16,8},{24,0},{1,25},{9,17},{17,9},{25,1},{2,26},{10... | collective-permute-start | bytes 983048 | tf_op jit(solution)/shard_map/ppermute | solution.py:1164
  600.3 26.4 %collective-permute-start.45 = (bf16[256,640]{1,0:T(8,128)(2,1)}, bf16[256,640]{1,0:T(8,128)(2,1)}, u32[]{:S(2)}, u32[]{:S(2)}) collective-permute-start(bf16[256,640]{1,0:T(8,128)(2,1)} %add_convert_fusion.6), channel_id=1, source_target_pairs={{0,24},{8,16},{16,8},{24,0},{1,25},{9,17},{17,9},{25,1},{2,26},{10... | collective-permute-start | bytes 983048 | tf_op jit(solution)/shard_map/ppermute | solution.py:1178
  629.2 9.2 %collective-permute-start.47 = (bf16[256,640]{1,0:T(8,128)(2,1)S(1)}, bf16[256,640]{1,0:T(8,128)(2,1)S(1)}, u32[]{:S(2)}, u32[]{:S(2)}) collective-permute-start(bf16[256,640]{1,0:T(8,128)(2,1)S(1)} %get-tuple-element.431), channel_id=1, source_target_pairs={{0,4},{4,0},{1,5},{5,1},{2,6},{6,2},{3,7},{7,3},{8,12},{12,8},{9,1... | collective-permute-start | bytes 983048 | tf_op jit(solution)/shard_map/ppermute | solution.py:159
  (53 other events, 247.2 us)
Sparse Core Ops, SparseCore 0:
  11.4 64.2 all-gather.4
  105.3 76.6 reduce-scatter.3
  186.1 54.7 all-gather.6
  242.8 54.3 all-gather.8
  339.4 73.4 reduce-scatter.5
  444.3 66.3 all-gather.10
  524.9 91.5 reduce-scatter.7

commit v9 on v8

--- a/solution.py
+++ b/solution.py
@@ -824,31 +824,40 @@
 
 
 def adamw_attn_kernel(x_ref, mine_ref, theirs_ref, *refs):
+    step = pl.program_id(0)
     low_is_own = x_ref[0] == 0
     states, outs = refs[:12], refs[12:]
-    own, other = mine_ref[...], theirs_ref[...].astype(F32)
+    rows, wide = states[0].shape[0], states[0].shape[1] // 2
+    here = pl.ds(pl.multiple_of(step * rows, rows), rows)
+    end = wide + 128
+    own, other = mine_ref[here, :end], theirs_ref[here, :end].astype(F32)
     low = jnp.where(low_is_own, own, other)
     high = jnp.where(low_is_own, other, own)
-    wide = states[0].shape[1] // 2
     adamw_write(outs[:4], cat([low[:, :wide], high[:, :wide]], 1), *states[:3])
-    low_kv, high_kv = low[:, wide : wide + 128], high[:, wide : wide + 128]
+    low_kv, high_kv = low[:, wide:], high[:, wide:]
     is_key = lanes_of(low_kv.shape) < HD
     key = jnp.where(is_key, low_kv, pltpu.roll(high_kv, HD, 1))
     adamw_write(outs[4:8], key, *states[3:6])
     value = jnp.where(is_key, pltpu.roll(low_kv, HD, 1), high_kv)
     adamw_write(outs[8:12], value, *states[6:9])
-    adamw_write(outs[12:], cat([low[:, wide + 128 :], high[:, wide + 128 :]], 0), *states[9:])
+    grad = jnp.where(step == x_ref[0], mine_ref[:, end:], theirs_ref[:, end:].astype(F32))
+    adamw_write(outs[12:], grad, *states[9:])
 
 
 def adamw_attn(x, pair, states):
     flat = [array for triple in states for array in triple]
     outs = [triple[0] for triple in states for _ in range(4)]
+
+    def cut(array):
+        return per_seq((array.shape[0] // 2, array.shape[1]))
+
     result = pl.pallas_call(
         adamw_attn_kernel,
-        grid=(1,),
+        grid=(2,),
         in_specs=[pl.BlockSpec(memory_space=pltpu.SMEM)]
-        + [once(array.shape) for array in [*pair, *flat]],
-        out_specs=[once(array.shape) for array in outs],
+        + [once(array.shape) for array in pair]
+        + [cut(array) for array in flat],
+        out_specs=[cut(array) for array in outs],
         out_shape=[jax.ShapeDtypeStruct(array.shape, F32) for array in outs],
         compiler_params=pltpu.CompilerParams(vmem_limit_bytes=60 * MIB),
         cost_estimate=SMALL,
@@ -876,11 +885,15 @@
 
 def finish(place, back, inputs, scale, gain, res_grad, residual, stays, first, second):
     arrays = [back, inputs, scale, gain[None, :], res_grad, residual, stays, first, second]
+    rows, width = inputs.shape
+    cut = per_seq((rows // 4, width))
+    specs = [cut, cut, per_seq((rows // 4, 1)), once((1, width)), cut, cut, cut]
+    specs += [pl.BlockSpec((1, rows // 4, width), lambda i: (0, i, 0)), cut]
     return pl.pallas_call(
         finish_kernel,
-        grid=(1,),
-        in_specs=[pl.BlockSpec(memory_space=pltpu.SMEM)] + [once(a.shape) for a in arrays],
-        out_specs=[once(inputs.shape)] * 2,
+        grid=(4,),
+        in_specs=[pl.BlockSpec(memory_space=pltpu.SMEM)] + specs,
+        out_specs=[cut] * 2,
         out_shape=[
             jax.ShapeDtypeStruct(inputs.shape, LOW),
             jax.ShapeDtypeStruct(inputs.shape, F32),

time: 665 us -> 664 us (level)
  transfers between devices with their start and end apart: 55 -> 55, of which waited for: 34 -> 35; matrix products, arithmetic and copies ran while one was open for 13% -> 13% of each run, Pallas kernels for 34% -> 34%
where the time goes in v9:
time: 664 us; the launch traced here: 651 us
  Pallas kernels  224 us (34%)
  waiting for transfers between devices  213 us (32%)
  other arithmetic  84.1 us (13%)
  starting transfers between devices  69.3 us (10%)
  local copies, waits for them, and re-layouts  27 us (4%)
  blocking collectives  17.6 us (3%)
  between operations  15.8 us (2%)
    pallas_call x2, Pallas kernels, ffn_main(): pl.pallas_call(functools.partial(ffn_main_kernel, loader, len(more)), gri...  62.4 us
    pallas_call x3, Pallas kernels, ffn_weights(): pl.pallas_call(functools.partial(ffn_weights_kernel, plan), grid=(count,)...  47.7 us
    pallas_call x1, Pallas kernels, attn_backward(): pl.pallas_call(functools.partial(attn_backward_kernel, heads // 128, load...  33 us
    ppermute x3, waiting for transfers between devices, line_last(): return lax.ppermute(across_near, 'do', perm)  32.9 us
    ppermute x3, waiting for transfers between devices, swap_first(): return lax.ppermute(value, self.axes, self.pairs(True))  24 us
    pallas_call x1, Pallas kernels, attn_forward(): pl.pallas_call(functools.partial(attn_forward_kernel, heads // 128, loade...  22.4 us
    ppermute x3, waiting for transfers between devices, trade(): theirs = lax.ppermute(self.by_x(high, low).astype(LOW), 'di', PAIR)  20.1 us
    ppermute x2, waiting for transfers between devices, sum_near_send(): return (lax.ppermute(first, 'do', NEAR), lax.ppermute(third, 'do', MIDDLE))  19.1 us
  transfers between devices with their start and end apart: 55, of which 35 were waited for; matrix products, arithmetic and copies ran while one was open for 13% of the time, Pallas kernels for 34%

profile of v9, /device:TPU:9, one launch (start us, length us, event | category | flops | bytes accessed | tf_op | source)
XLA Modules:
  0.0 651.2 jit_solution(17120490092244466592)
XLA Ops:
  18.2 2.8 collective-permute-done.1
  21.6 4.2 collective-permute-start.3
  25.9 3.7 fusion.6
  36.1 3.0 collective-permute-done.3.refs_5_
  39.1 3.1 collective-permute-start.5
  42.7 10.2 %collective-permute-done.6 = bf16[256,1536]{1,0:T(8,128)(2,1)S(1)} collective-permute-done((bf16[256,1536]{1,0:T(8,128)(2,1)S(1)}, bf16[256,1536]{1,0:T(8,128)(2,1)S(1)}, u32[]{:S(2)}, u32[]{:S(2)}) %collective-permute-start.6) | collective-permute-done | bytes 786464 | tf_op jit(solution)/shard_map/ppermute | solution.py:131
  57.5 9.2 %collective-permute-done.7.refs_6_ = bf16[512,640]{1,0:T(8,128)(2,1)S(1)} collective-permute-done((bf16[512,640]{1,0:T(8,128)(2,1)S(1)}, bf16[512,640]{1,0:T(8,128)(2,1)S(1)}, u32[]{:S(2)}, u32[]{:S(2)}) %collective-permute-start.7) | collective-permute-done | bytes 655392 | tf_op jit(solution)/shard_map/ppermute | solution.py:62
  66.6 2.3 collective-permute-start.8
  69.0 5.2 collective-permute-start.9
  77.0 22.4 %attn_forward.1 = (bf16[2048,2048]{1,0:T(8,128)(2,1)}, bf16[2048,256]{1,0:T(8,128)(2,1)}, bf16[2048,256]{1,0:T(8,128)(2,1)}, bf16[2048,128]{1,0:T(8,128)(2,1)}, ...) custom-call(s32[1]{0:T(128)} %bitcast.1.refs_0_, bf16[512,640]{1,0:T(8,128)(2,1)} %copy-done.16, ...), custom_call_target="tpu_custom_call" | custom-call | flops 1 | bytes 1 | tf_op jit(solution)/shard_map/attn_forward/pallas_call | solution.py:410
  99.4 5.7 collective-permute-done.11
  105.3 3.2 collective-permute-start.13
  110.1 12.7 %collective-permute-done.14 = bf16[256,2048]{1,0:T(8,128)(2,1)} collective-permute-done((bf16[256,2048]{1,0:T(8,128)(2,1)}, bf16[256,2048]{1,0:T(8,128)(2,1)}, u32[]{:S(2)}, u32[]{:S(2)}) %collective-permute-start.14) | collective-permute-done | bytes 1048608 | tf_op jit(solution)/shard_map/ppermute | solution.py:929
  122.8 11.2 %collective-permute-done.15 = bf16[256,2048]{1,0:T(8,128)(2,1)} collective-permute-done((bf16[256,2048]{1,0:T(8,128)(2,1)S(1)}, bf16[256,2048]{1,0:T(8,128)(2,1)}, u32[]{:S(2)}, u32[]{:S(2)}) %collective-permute-start.15) | collective-permute-done | bytes 1048608 | tf_op jit(solution)/shard_map/ppermute | solution.py:929
  134.1 2.9 collective-permute-done.12.refs_4_
  145.2 2.7 pad_maximum_fusion.1
  147.8 19.7 %collective-permute-done.16.refs_6_ = bf16[512,1536]{1,0:T(8,128)(2,1)} collective-permute-done((bf16[512,1536]{1,0:T(8,128)(2,1)}, bf16[512,1536]{1,0:T(8,128)(2,1)}, u32[]{:S(2)}, u32[]{:S(2)}) %collective-permute-start.16) | collective-permute-done | bytes 1572896 | tf_op jit(solution)/shard_map/ppermute | solution.py:62
  167.5 14.4 %reduce-scatter.4.cloned.1.call-done = bf16[256,2048]{1,0:T(8,128)(2,1)} async-done(((bf16[2048,2048]{1,0:T(8,128)(2,1)}), bf16[256,2048]{1,0:T(8,128)(2,1)}) %reduce-scatter.4.cloned.1.call-update) | async-done | bytes 1048592 | tf_op jit(solution)/shard_map/reduce_scatter | solution.py:1048
  187.0 4.1 collective-permute-start.18
  191.1 2.7 collective-permute-done.19
  193.8 4.2 broadcast_select_fusion.1
  198.0 6.4 pad_maximum_fusion
  204.3 8.4 %copy.81 = bf16[4,2,256,2048]{3,2,1,0:T(8,128)(2,1)} copy(bf16[4,2,256,2048]{3,2,0,1:T(8,128)(2,1)} %pad_maximum_fusion) | data formatting | bytes 16777216 | tf_op jit(solution)/shard_map/concatenate | solution.py:45
  212.7 10.2 %collective-permute-done.17.refs_2_ = bf16[512,1536]{1,0:T(8,128)(2,1)} collective-permute-done((bf16[512,1536]{1,0:T(8,128)(2,1)S(1)}, bf16[512,1536]{1,0:T(8,128)(2,1)}, u32[]{:S(2)}, u32[]{:S(2)}) %collective-permute-start.17) | collective-permute-done | bytes 1572896 | tf_op jit(solution)/shard_map/ppermute | solution.py:53
  222.8 2.8 collective-permute-done.18.refs_5_
  225.8 3.3 collective-permute-start.21
  229.1 11.8 %all-gather.7.cloned.1.call-done.refs_7_.x_ref = bf16[2048,2048]{1,0:T(8,128)(2,1)} async-done(((bf16[256,2048]{1,0:T(8,128)(2,1)}), bf16[2048,2048]{1,0:T(8,128)(2,1)}) %all-gather.7.cloned.1.call-update) | async-done | bytes 8388624 | tf_op jit(solution)/shard_map/all_gather | solution.py:1072
  240.9 30.3 %ffn_main.2 = (bf16[2048,2048]{1,0:T(8,128)(2,1)}, bf16[2048,512]{1,0:T(8,128)(2,1)}, bf16[2048,1024]{1,0:T(8,128)(2,1)}, bf16[512,2048]{1,0:T(8,128)(2,1)}) custom-call(s32[1]{0:T(128)} %bitcast.1.refs_0_, bf16[512,1536]{1,0:T(8,128)(2,1)} %pad_maximum_fusion.7.refs_1_, bf16[512,1536]{1,0:T(8,128)(2,1)} %collective-permute-done.8.refs_2_, ...), custom_call_target="tpu_custom_call" | custom-call | flops 1 | bytes 1 | tf_op jit(solution)/shard_map/ffn_main/pallas_call | solution.py:609
  271.3 3.5 collective-permute-start.22
  274.7 13.1 %ffn_weights.3 = (bf16[256,1536]{1,0:T(8,128)(2,1)}, bf16[256,1536]{1,0:T(8,128)(2,1)}, bf16[512,1536]{1,0:T(8,128)(2,1)}) custom-call(bf16[2048,2048]{1,0:T(8,128)(2,1)} %all-gather.7.cloned.1.call-done.refs_7_.x_ref, bf16[2048,2048]{1,0:T(8,128)(2,1)} %bitcast.54, bf16[2048,512]{1,0:T(8,128)(2,1)} %get-tuple-element.291.act_ref.act_1, ...), custom_call_target="tpu_custom_call" | custom-call | flops 1 | bytes 1 | tf_op jit(solution)/shard_map/ffn_weights/pallas_call | solution.py:691
  290.9 12.2 %ffn_weights.4 = bf16[1024,1536]{1,0:T(8,128)(2,1)} custom-call(bf16[2048,2048]{1,0:T(8,128)(2,1)} %all-gather.7.cloned.1.call-done.refs_7_.x_ref, bf16[2048,2048]{1,0:T(8,128)(2,1)} %bitcast.55, bf16[2048,512]{1,0:T(8,128)(2,1)} %get-tuple-element.291.act_ref.act_1, bf16[2048,1024]{1,0:T(8,128)(2,1)} %get-tuple-element.272.both_ref), custom_call_target="tpu_custom_call" | custom-call | flops 1 | bytes 1 | tf_op jit(solution)/shard_map/ffn_weights/pallas_call | solution.py:691
  303.1 4.0 collective-permute-done.22.refs_6_
  307.1 32.1 %ffn_main.3 = (bf16[2048,2048]{1,0:T(8,128)(2,1)}, bf16[2048,512]{1,0:T(8,128)(2,1)}, bf16[2048,1024]{1,0:T(8,128)(2,1)}, bf16[512,2048]{1,0:T(8,128)(2,1)}) custom-call(s32[1]{0:T(128)} %bitcast.1.refs_0_, bf16[512,1536]{1,0:T(8,128)(2,1)} %pad_maximum_fusion.8.refs_1_, bf16[512,1536]{1,0:T(8,128)(2,1)} %collective-permute-done.17.refs_2_, ...), custom_call_target="tpu_custom_call" | custom-call | flops 1 | bytes 1 | tf_op jit(solution)/shard_map/ffn_main/pallas_call | solution.py:609
  340.6 3.0 add_convert_fusion.5
  345.6 4.3 collective-permute-start.26
  349.8 22.4 %ffn_weights.5 = (bf16[256,1536]{1,0:T(8,128)(2,1)}, bf16[256,1536]{1,0:T(8,128)(2,1)}, bf16[1536,1536]{1,0:T(8,128)(2,1)}) custom-call(bf16[2048,2048]{1,0:T(8,128)(2,1)} %all-gather.7.cloned.1.call-done.refs_7_.x_ref, bf16[2048,2048]{1,0:T(8,128)(2,1)} %bitcast.57, bf16[2048,512]{1,0:T(8,128)(2,1)} %get-tuple-element.292.act_ref.act_2, ...), custom_call_target="tpu_custom_call" | custom-call | flops 1 | bytes 1 | tf_op jit(solution)/shard_map/ffn_weights/pallas_call | solution.py:691
  372.2 7.3 %collective-permute-done.25 = bf16[512,1536]{1,0:T(8,128)(2,1)S(1)} collective-permute-done((bf16[512,1536]{1,0:T(8,128)(2,1)}, bf16[512,1536]{1,0:T(8,128)(2,1)S(1)}, u32[]{:S(2)}, u32[]{:S(2)}) %collective-permute-start.25) | collective-permute-done | bytes 1572896 | tf_op jit(solution)/shard_map/ppermute | solution.py:83
  379.5 3.8 collective-permute-done.26
  384.5 16.1 %ffn_out.1 = (bf16[2048,2048]{1,0:T(8,128)(2,1)}, f32[1,2048]{1,0:T(1,128)}) custom-call(bf16[2048,512]{1,0:T(8,128)(2,1)} %get-tuple-element.291.act_ref.act_1, bf16[2048,512]{1,0:T(8,128)(2,1)} %get-tuple-element.292.act_ref.act_2, bf16[512,2048]{1,0:T(8,128)(2,1)} %get-tuple-element.293.down_1, bf16[512,2048]{1,0:T(8,128)(2,1)} %get-tuple-element.294.down_2, ...), custom_call_target="tpu_custom_call" | custom-call | flops 1 | bytes 1 | tf_op jit(solution)/shard_map/ffn_out/pallas_call | solution.py:717
  401.9 4.9 add_convert_fusion.2
  406.8 6.0 reduce-scatter.6.cloned.1.call-done.back_ref
  412.8 8.8 %residual_backward.1 = (f32[256,2048]{1,0:T(8,128)}, bf16[256,2048]{1,0:T(8,128)(2,1)}, bf16[256,2048]{1,0:T(8,128)(2,1)}) custom-call(bf16[256,2048]{1,0:T(8,128)(2,1)} %reduce-scatter.6.cloned.1.call-done.back_ref, f32[256,2048]{1,0:T(8,128)} %get-tuple-element.433.residual_ref, f32[256,1]{1,0:T(8,128)} %copy.82.scale_ref, f32[1,2048]{1,0:T(1,128)} %bitcast.69, ...), custom_call_target="tpu_custom_call" | custom-call | flops 1 | bytes 1 | tf_op jit(solution)/shard_map/residual_backward/pallas_call | solution.py:550
  421.7 2.5 add_convert_fusion.4
  426.5 17.6 %all_to_all.19 = bf16[256,8,256]{2,0,1:T(8,128)(2,1)} all-to-all(bf16[256,8,256]{2,0,1:T(8,128)(2,1)S(1)} %bitcast.63), channel_id=1, replica_groups=mesh['do'=4,'di'=2,'tp'=4] {'di','tp'}, dimensions={1} | all-to-all | bytes 2097152 | tf_op jit(solution)/shard_map/all_to_all | solution.py:1135
  444.2 5.1 select_bitcast_fusion
  450.3 4.3 collective-permute-start.37
  454.6 2.6 collective-permute-done.29
  457.2 6.1 fusion
  467.8 33.0 %attn_backward.1 = (bf16[2048,2048]{1,0:T(8,128)(2,1)}, f32[1,2048]{1,0:T(1,128)}, bf16[512,384]{1,0:T(8,128)(2,1)}, bf16[512,384]{1,0:T(8,128)(2,1)}, bf16[512,...) custom-call(s32[1]{0:T(128)} %bitcast.1.refs_0_, bf16[512,640]{1,0:T(8,128)(2,1)} %copy-done.16, bf16[512,640]{1,0:T(8,128)(2,1)} %copy-done.21, ...), custom_call_target="tpu_custom_call" | custom-call | flops 1 | bytes 1 | tf_op jit(solution)/shard_map/attn_backward/pallas_call | solution.py:449
  503.6 11.3 %collective-permute-done.31 = f32[2,2048]{1,0:T(2,128)S(1)} collective-permute-done((f32[2,2048]{1,0:T(2,128)S(1)}, f32[2,2048]{1,0:T(2,128)S(1)}, u32[]{:S(2)}, u32[]{:S(2)}) %collective-permute-start.31) | collective-permute-done | bytes 16416 | tf_op jit(solution)/shard_map/ppermute | solution.py:766
  518.3 2.8 collective-permute-done.33
  526.1 6.2 convert_add_fusion.2
  532.4 4.1 collective-permute-start.39
  537.3 2.6 select_convert_fusion.1
  541.1 3.7 copy-done
  544.8 4.1 out_weights.1
  550.3 17.3 %collective-permute-done.38 = bf16[512,1536]{1,0:T(8,128)(2,1)} collective-permute-done((bf16[512,1536]{1,0:T(8,128)(2,1)}, bf16[512,1536]{1,0:T(8,128)(2,1)}, u32[]{:S(2)}, u32[]{:S(2)}) %collective-permute-start.38) | collective-permute-done | bytes 1572896 | tf_op jit(solution)/shard_map/ppermute | solution.py:92
  569.4 3.0 convert_add_fusion.1
  579.8 19.4 %collective-permute-done.44.theirs_2 = bf16[256,1536]{1,0:T(8,128)(2,1)S(1)} collective-permute-done((bf16[256,1536]{1,0:T(8,128)(2,1)S(1)}, bf16[256,1536]{1,0:T(8,128)(2,1)S(1)}, u32[]{:S(2)}, u32[]{:S(2)}) %collective-permute-start.44) | collective-permute-done | bytes 786464 | tf_op jit(solution)/shard_map/ppermute | solution.py:159
  602.2 17.7 %adamw_ffn.1 = (f32[256,2048]{1,0:T(8,128)}, f32[256,2048]{1,0:T(8,128)}, f32[256,2048]{1,0:T(8,128)}, f32[256,2048]{1,0:T(8,128)}, f32[256,2048]{1,0:T(8,128)},...) custom-call(s32[1]{0:T(128)} %bitcast.23.x_ref, ...), custom_call_target="tpu_custom_call" | custom-call | flops 1 | bytes 1 | tf_op jit(solution)/shard_map/adamw_ffn/pallas_call | solution.py:811
  621.4 5.2 collective-permute-done.45
  626.7 2.5 select_convert_fusion.2
  630.9 6.4 finish.1
  638.7 5.2 adamw_attn.1
  (291 shorter events, 88.5 us)
Async XLA Ops:
  7.2 69.8 %all-gather.5.cloned.1.call-start = ((), (), s32[]{:S(2)}) async-start(), calls=%async_computation.4 | async-start | bytes 9437184 | tf_op jit(solution)/shard_map/all_gather | solution.py:964
  9.7 174.0 %copy-start.6 = (bf16[256,2048]{1,0:T(8,128)(2,1)}, bf16[256,2048]{1,0:T(8,128)(2,1)S(1)}, u32[]{:S(2)}) copy-start(bf16[256,2048]{1,0:T(8,128)(2,1)S(1)} %get-tuple-element.415.inputs_ref) | copy-start | bytes 3145732
  9.9 490.9 %copy-start.44 = (f32[2048]{0:T(1024)}, f32[2048]{0:T(1024)S(1)}, u32[]{:S(2)}) copy-start(f32[2048]{0:T(1024)S(1)} %maximum_select_fusion.8) | copy-start | bytes 24580
  11.3 170.7 %reduce-scatter.4.cloned.1.call-start = ((), (), s32[]{:S(2)}) async-start(), calls=%async_computation.5 | async-start | bytes 9437184 | tf_op jit(solution)/shard_map/reduce_scatter | solution.py:1048
  12.1 8.9 %collective-permute-start = (bf16[256,640]{1,0:T(8,128)(2,1)S(1)}, bf16[256,640]{1,0:T(8,128)(2,1)S(1)}, u32[]{:S(2)}, u32[]{:S(2)}) collective-permute-start(bf16[256,640]{1,0:T(8,128)(2,1)S(1)} %pad_maximum_fusion.17), channel_id=1, source_target_pairs={{0,4},{4,0},{1,5},{5,1},{2,6},{6,2},{3,7},{7,3},{8,12},{12,8},{9,1... | collective-permute-start | bytes 983048 | tf_op jit(solution)/shard_map/ppermute | solution.py:131
  13.4 7.5 %collective-permute-start.1 = (s32[2,1024]{1,0:T(2,128)S(1)}, s32[2,1024]{1,0:T(2,128)S(1)}, u32[]{:S(2)}, u32[]{:S(2)}) collective-permute-start(s32[2,1024]{1,0:T(2,128)S(1)} %pad_add_fusion.1), channel_id=1, source_target_pairs={{0,4},{4,0},{1,5},{5,1},{2,6},{6,2},{3,7},{7,3},{8,12},{12,8},{9,1... | collective-permute-start | bytes 24584 | tf_op jit(solution)/shard_map/ppermute | solution.py:967
  21.0 54.7 %copy-start.43 = (s32[1,2048]{1,0:T(1,128)}, s32[1,2048]{1,0:T(1,128)S(1)}, u32[]{:S(2)}) copy-start(s32[1,2048]{1,0:T(1,128)S(1)} %get-tuple-element.495) | copy-start | bytes 24580
  21.3 14.7 %collective-permute-start.2 = (bf16[512,640]{1,0:T(8,128)(2,1)S(1)}, bf16[512,640]{1,0:T(8,128)(2,1)S(1)}, u32[]{:S(2)}, u32[]{:S(2)}) collective-permute-start(bf16[512,640]{1,0:T(8,128)(2,1)S(1)} %pad_maximum_fusion.15.refs_1_), channel_id=1, source_target_pairs={{0,8},{8,0},{16,24},{24,16},{1,9},{9,1},{17,25},{25,17},{2,10},{10... | collective-permute-start | bytes 1966088 | tf_op jit(solution)/shard_map/ppermute | solution.py:53
  21.6 17.5 %collective-permute-start.3 = (bf16[512,640]{1,0:T(8,128)(2,1)S(1)}, bf16[512,640]{1,0:T(8,128)(2,1)S(1)}, u32[]{:S(2)}, u32[]{:S(2)}) collective-permute-start(bf16[512,640]{1,0:T(8,128)(2,1)S(1)} %pad_maximum_fusion.15.refs_1_), channel_id=1, source_target_pairs={{8,16},{16,8},{9,17},{17,9},{10,18},{18,10},{11,19},{19,11},{12,20... | collective-permute-start | bytes 1966088 | tf_op jit(solution)/shard_map/ppermute | solution.py:53
  31.5 21.4 %collective-permute-start.6 = (bf16[256,1536]{1,0:T(8,128)(2,1)S(1)}, bf16[256,1536]{1,0:T(8,128)(2,1)S(1)}, u32[]{:S(2)}, u32[]{:S(2)}) collective-permute-start(bf16[256,1536]{1,0:T(8,128)(2,1)S(1)} %pad_maximum_fusion.12), channel_id=1, source_target_pairs={{0,4},{4,0},{1,5},{5,1},{2,6},{6,2},{3,7},{7,3},{8,12},{12,8},{9,1... | collective-permute-start | bytes 2359304 | tf_op jit(solution)/shard_map/ppermute | solution.py:131
  39.1 13.9 %collective-permute-start.4 = (bf16[512,640]{1,0:T(8,128)(2,1)S(1)}, bf16[512,640]{1,0:T(8,128)(2,1)S(1)}, u32[]{:S(2)}, u32[]{:S(2)}) collective-permute-start(bf16[512,640]{1,0:T(8,128)(2,1)S(1)} %collective-permute-done.3.refs_5_), channel_id=1, source_target_pairs={{0,8},{8,0},{16,24},{24,16},{1,9},{9,1},{17,25},{25,17},{2,10},{10... | collective-permute-start | bytes 1966088 | tf_op jit(solution)/shard_map/ppermute | solution.py:57
  39.1 15.7 %collective-permute-start.5 = (bf16[512,640]{1,0:T(8,128)(2,1)S(1)}, bf16[512,640]{1,0:T(8,128)(2,1)S(1)}, u32[]{:S(2)}, u32[]{:S(2)}) collective-permute-start(bf16[512,640]{1,0:T(8,128)(2,1)S(1)} %collective-permute-done.2.refs_2_), channel_id=1, source_target_pairs={{8,16},{16,8},{9,17},{17,9},{10,18},{18,10},{11,19},{19,11},{12,20... | collective-permute-start | bytes 1966088 | tf_op jit(solution)/shard_map/ppermute | solution.py:58
  42.7 98.8 %copy-start.9 = (bf16[256,2048]{1,0:T(8,128)(2,1)}, bf16[256,2048]{1,0:T(8,128)(2,1)S(1)}, u32[]{:S(2)}) copy-start(bf16[256,2048]{1,0:T(8,128)(2,1)S(1)} %maximum_select_fusion.3.grad_ref) | copy-start | bytes 3145732
  54.8 11.8 %collective-permute-start.7 = (bf16[512,640]{1,0:T(8,128)(2,1)S(1)}, bf16[512,640]{1,0:T(8,128)(2,1)S(1)}, u32[]{:S(2)}, u32[]{:S(2)}) collective-permute-start(bf16[512,640]{1,0:T(8,128)(2,1)S(1)} %collective-permute-done.5.refs_3_), channel_id=1, source_target_pairs={{0,8},{8,0},{16,24},{24,16},{1,9},{9,1},{17,25},{25,17},{2,10},{10... | collective-permute-start | bytes 1966088 | tf_op jit(solution)/shard_map/ppermute | solution.py:62
  66.6 38.5 %collective-permute-start.8 = (bf16[512,1536]{1,0:T(8,128)(2,1)}, bf16[512,1536]{1,0:T(8,128)(2,1)}, u32[]{:S(2)}, u32[]{:S(2)}) collective-permute-start(bf16[512,1536]{1,0:T(8,128)(2,1)} %pad_maximum_fusion.7.refs_1_), channel_id=1, source_target_pairs={{0,8},{8,0},{16,24},{24,16},{1,9},{9,1},{17,25},{25,17},{2,10},{10... | collective-permute-start | bytes 4718600 | tf_op jit(solution)/shard_map/ppermute | solution.py:53
  69.0 36.2 %collective-permute-start.9 = (bf16[512,1536]{1,0:T(8,128)(2,1)}, bf16[512,1536]{1,0:T(8,128)(2,1)}, u32[]{:S(2)}, u32[]{:S(2)}) collective-permute-start(bf16[512,1536]{1,0:T(8,128)(2,1)} %pad_maximum_fusion.7.refs_1_), channel_id=1, source_target_pairs={{8,16},{16,8},{9,17},{17,9},{10,18},{18,10},{11,19},{19,11},{12,20... | collective-permute-start | bytes 4718600 | tf_op jit(solution)/shard_map/ppermute | solution.py:53
  74.1 31.0 %collective-permute-start.10 = (bf16[256,2048]{1,0:T(8,128)(2,1)S(1)}, bf16[256,2048]{1,0:T(8,128)(2,1)}, u32[]{:S(2)}, u32[]{:S(2)}) collective-permute-start(bf16[256,2048]{1,0:T(8,128)(2,1)S(1)} %maximum_select_fusion.3.grad_ref), channel_id=1, source_target_pairs={{0,2},{1,5},{2,0},{3,7},{4,6},{5,1},{6,4},{7,3},{8,10},{9,13},{10,... | collective-permute-start | bytes 3145736 | tf_op jit(solution)/shard_map/ppermute | solution.py:932
  74.5 30.6 %collective-permute-start.11 = (bf16[256,1536]{1,0:T(8,128)(2,1)}, bf16[256,1536]{1,0:T(8,128)(2,1)}, u32[]{:S(2)}, u32[]{:S(2)}) collective-permute-start(bf16[256,1536]{1,0:T(8,128)(2,1)} %pad_maximum_fusion.14), channel_id=1, source_target_pairs={{0,4},{4,0},{1,5},{5,1},{2,6},{6,2},{3,7},{7,3},{8,12},{12,8},{9,1... | collective-permute-start | bytes 2359304 | tf_op jit(solution)/shard_map/ppermute | solution.py:131
  105.2 135.8 %all-gather.7.cloned.1.call-start = ((), (), s32[]{:S(2)}) async-start(), calls=%async_computation.6 | async-start | bytes 9437184 | tf_op jit(solution)/shard_map/all_gather | solution.py:1072
  105.2 31.8 %collective-permute-start.12 = (bf16[512,1536]{1,0:T(8,128)(2,1)}, bf16[512,1536]{1,0:T(8,128)(2,1)}, u32[]{:S(2)}, u32[]{:S(2)}) collective-permute-start(bf16[512,1536]{1,0:T(8,128)(2,1)} %collective-permute-done.9.refs_5_), channel_id=1, source_target_pairs={{0,8},{8,0},{16,24},{24,16},{1,9},{9,1},{17,25},{25,17},{2,10},{10... | collective-permute-start | bytes 4718600 | tf_op jit(solution)/shard_map/ppermute | solution.py:57
  105.3 33.6 %collective-permute-start.13 = (bf16[512,1536]{1,0:T(8,128)(2,1)}, bf16[512,1536]{1,0:T(8,128)(2,1)}, u32[]{:S(2)}, u32[]{:S(2)}) collective-permute-start(bf16[512,1536]{1,0:T(8,128)(2,1)} %collective-permute-done.8.refs_2_), channel_id=1, source_target_pairs={{8,16},{16,8},{9,17},{17,9},{10,18},{18,10},{11,19},{19,11},{12,20... | collective-permute-start | bytes 4718600 | tf_op jit(solution)/shard_map/ppermute | solution.py:58
  108.5 14.3 %collective-permute-start.14 = (bf16[256,2048]{1,0:T(8,128)(2,1)}, bf16[256,2048]{1,0:T(8,128)(2,1)}, u32[]{:S(2)}, u32[]{:S(2)}) collective-permute-start(bf16[256,2048]{1,0:T(8,128)(2,1)} %collective-permute-done.10), channel_id=1, source_target_pairs={{0,4},{1,3},{2,6},{3,1},{4,0},{5,7},{6,2},{7,5},{8,12},{9,11},{10,... | collective-permute-start | bytes 3145736 | tf_op jit(solution)/shard_map/ppermute | solution.py:929
  109.8 24.3 %collective-permute-start.15 = (bf16[256,2048]{1,0:T(8,128)(2,1)S(1)}, bf16[256,2048]{1,0:T(8,128)(2,1)}, u32[]{:S(2)}, u32[]{:S(2)}) collective-permute-start(bf16[256,2048]{1,0:T(8,128)(2,1)S(1)} %maximum_select_fusion.3.grad_ref), channel_id=1, source_target_pairs={{0,4},{1,3},{2,6},{3,1},{4,0},{5,7},{6,2},{7,5},{8,12},{9,11},{10,... | collective-permute-start | bytes 3145736 | tf_op jit(solution)/shard_map/ppermute | solution.py:929
  110.1 73.7 %copy-start.45 = (f32[2048]{0:T(1024)}, f32[2048]{0:T(1024)S(1)}, u32[]{:S(2)}) copy-start(f32[2048]{0:T(1024)S(1)} %maximum_select_fusion.10) | copy-start | bytes 24580
  138.9 28.6 %collective-permute-start.16 = (bf16[512,1536]{1,0:T(8,128)(2,1)}, bf16[512,1536]{1,0:T(8,128)(2,1)}, u32[]{:S(2)}, u32[]{:S(2)}) collective-permute-start(bf16[512,1536]{1,0:T(8,128)(2,1)} %collective-permute-done.13.refs_3_), channel_id=1, source_target_pairs={{0,8},{8,0},{16,24},{24,16},{1,9},{9,1},{17,25},{25,17},{2,10},{10... | collective-permute-start | bytes 4718600 | tf_op jit(solution)/shard_map/ppermute | solution.py:62
  186.0 153.3 %all-gather.9.cloned.1.call-start = ((), (), s32[]{:S(2)}) async-start(), calls=%async_computation.7 | async-start | bytes 9437184 | tf_op jit(solution)/shard_map/all_gather | solution.py:1080
  186.0 7.8 %collective-permute-start.19 = (bf16[1024,2048]{1,0:T(8,128)(2,1)}, bf16[1024,2048]{1,0:T(8,128)(2,1)S(1)}, u32[]{:S(2)}, u32[]{:S(2)}) collective-permute-start(bf16[1024,2048]{1,0:T(8,128)(2,1)} %pad_maximum_fusion.1), channel_id=1, source_target_pairs={{0,1},{1,0},{2,3},{3,2},{4,5},{5,4},{6,7},{7,6},{8,9},{9,8},{10,11... | collective-permute-start | bytes 12582920 | tf_op jit(solution)/shard_map/ppermute | solution.py:935
  186.8 36.1 %collective-permute-start.17 = (bf16[512,1536]{1,0:T(8,128)(2,1)S(1)}, bf16[512,1536]{1,0:T(8,128)(2,1)}, u32[]{:S(2)}, u32[]{:S(2)}) collective-permute-start(bf16[512,1536]{1,0:T(8,128)(2,1)S(1)} %copy-done.13), channel_id=1, source_target_pairs={{0,8},{8,0},{16,24},{24,16},{1,9},{9,1},{17,25},{25,17},{2,10},{10... | collective-permute-start | bytes 4718600 | tf_op jit(solution)/shard_map/ppermute | solution.py:53
  187.0 38.6 %collective-permute-start.18 = (bf16[512,1536]{1,0:T(8,128)(2,1)S(1)}, bf16[512,1536]{1,0:T(8,128)(2,1)}, u32[]{:S(2)}, u32[]{:S(2)}) collective-permute-start(bf16[512,1536]{1,0:T(8,128)(2,1)S(1)} %copy-done.13), channel_id=1, source_target_pairs={{8,16},{16,8},{9,17},{17,9},{10,18},{18,10},{11,19},{19,11},{12,20... | collective-permute-start | bytes 4718600 | tf_op jit(solution)/shard_map/ppermute | solution.py:53
  225.7 187.1 %reduce-scatter.6.cloned.1.call-start = ((), (), s32[]{:S(2)}) async-start(), calls=%async_computation.8 | async-start | bytes 9437184 | tf_op jit(solution)/shard_map/reduce_scatter | solution.py:1104
  225.8 45.5 %collective-permute-start.20 = (bf16[512,1536]{1,0:T(8,128)(2,1)}, bf16[512,1536]{1,0:T(8,128)(2,1)S(1)}, u32[]{:S(2)}, u32[]{:S(2)}) collective-permute-start(bf16[512,1536]{1,0:T(8,128)(2,1)} %collective-permute-done.18.refs_5_), channel_id=1, source_target_pairs={{0,8},{8,0},{16,24},{24,16},{1,9},{9,1},{17,25},{25,17},{2,10},{10... | collective-permute-start | bytes 4718600 | tf_op jit(solution)/shard_map/ppermute | solution.py:57
  225.8 45.4 %collective-permute-start.21 = (bf16[512,1536]{1,0:T(8,128)(2,1)}, bf16[512,1536]{1,0:T(8,128)(2,1)S(1)}, u32[]{:S(2)}, u32[]{:S(2)}) collective-permute-start(bf16[512,1536]{1,0:T(8,128)(2,1)} %collective-permute-done.17.refs_2_), channel_id=1, source_target_pairs={{8,16},{16,8},{9,17},{17,9},{10,18},{18,10},{11,19},{19,11},{12,20... | collective-permute-start | bytes 4718600 | tf_op jit(solution)/shard_map/ppermute | solution.py:58
  271.2 16.6 %copy-start.28 = (bf16[512,1536]{1,0:T(8,128)(2,1)}, bf16[512,1536]{1,0:T(8,128)(2,1)S(1)}, u32[]{:S(2)}) copy-start(bf16[512,1536]{1,0:T(8,128)(2,1)S(1)} %collective-permute-done.20.refs_4_) | copy-start | bytes 4718596
  271.3 16.5 %copy-start.29 = (bf16[512,1536]{1,0:T(8,128)(2,1)}, bf16[512,1536]{1,0:T(8,128)(2,1)S(1)}, u32[]{:S(2)}) copy-start(bf16[512,1536]{1,0:T(8,128)(2,1)S(1)} %collective-permute-done.21.refs_3_) | copy-start | bytes 4718596
  271.3 35.8 %collective-permute-start.22 = (bf16[512,1536]{1,0:T(8,128)(2,1)S(1)}, bf16[512,1536]{1,0:T(8,128)(2,1)}, u32[]{:S(2)}, u32[]{:S(2)}) collective-permute-start(bf16[512,1536]{1,0:T(8,128)(2,1)S(1)} %collective-permute-done.21.refs_3_), channel_id=1, source_target_pairs={{8,0},{16,24},{9,1},{17,25},{10,2},{18,26},{11,3},{19,27},{12,4},{... | collective-permute-start | bytes 4718600 | tf_op jit(solution)/shard_map/ppermute | solution.py:62
  287.8 51.4 %collective-permute-start.23 = (bf16[256,1536]{1,0:T(8,128)(2,1)}, bf16[256,1536]{1,0:T(8,128)(2,1)}, u32[]{:S(2)}, u32[]{:S(2)}) collective-permute-start(bf16[256,1536]{1,0:T(8,128)(2,1)} %get-tuple-element.278), channel_id=1, source_target_pairs={{0,8},{24,16},{1,9},{25,17},{2,10},{26,18},{3,11},{27,19},{4,12},{... | collective-permute-start | bytes 2359304 | tf_op jit(solution)/shard_map/ppermute | solution.py:1090
  289.1 50.1 %collective-permute-start.24 = (bf16[256,1536]{1,0:T(8,128)(2,1)}, bf16[256,1536]{1,0:T(8,128)(2,1)}, u32[]{:S(2)}, u32[]{:S(2)}) collective-permute-start(bf16[256,1536]{1,0:T(8,128)(2,1)} %get-tuple-element.279), channel_id=1, source_target_pairs={{0,8},{24,16},{1,9},{25,17},{2,10},{26,18},{3,11},{27,19},{4,12},{... | collective-permute-start | bytes 2359304 | tf_op jit(solution)/shard_map/ppermute | solution.py:1090
  339.3 185.4 %all-gather.11.cloned.1.call-start = ((), (), s32[]{:S(2)}) async-start(), calls=%async_computation.9 | async-start | bytes 9437184 | tf_op jit(solution)/shard_map/all_gather | solution.py:1149
  343.6 35.9 %collective-permute-start.25 = (bf16[512,1536]{1,0:T(8,128)(2,1)}, bf16[512,1536]{1,0:T(8,128)(2,1)S(1)}, u32[]{:S(2)}, u32[]{:S(2)}) collective-permute-start(bf16[512,1536]{1,0:T(8,128)(2,1)} %add_convert_fusion.5), channel_id=1, source_target_pairs={{0,8},{8,0},{16,24},{24,16},{1,9},{9,1},{17,25},{25,17},{2,10},{10... | collective-permute-start | bytes 4718600 | tf_op jit(solution)/shard_map/ppermute | solution.py:83
  345.6 37.7 %collective-permute-start.26 = (bf16[512,1536]{1,0:T(8,128)(2,1)}, bf16[512,1536]{1,0:T(8,128)(2,1)S(1)}, u32[]{:S(2)}, u32[]{:S(2)}) collective-permute-start(bf16[512,1536]{1,0:T(8,128)(2,1)} %add_convert_fusion.5), channel_id=1, source_target_pairs={{8,16},{16,8},{9,17},{17,9},{10,18},{18,10},{11,19},{19,11},{12,20... | collective-permute-start | bytes 4718600 | tf_op jit(solution)/shard_map/ppermute | solution.py:84
  383.3 17.5 %collective-permute-start.27 = (bf16[256,1536]{1,0:T(8,128)(2,1)}, bf16[256,1536]{1,0:T(8,128)(2,1)}, u32[]{:S(2)}, u32[]{:S(2)}) collective-permute-start(bf16[256,1536]{1,0:T(8,128)(2,1)} %get-tuple-element.296), channel_id=1, source_target_pairs={{0,8},{8,0},{16,24},{24,16},{1,9},{9,1},{17,25},{25,17},{2,10},{10... | collective-permute-start | bytes 2359304 | tf_op jit(solution)/shard_map/ppermute | solution.py:1114
  384.5 17.4 %copy-start.8 = (bf16[1024,1536]{1,0:T(8,128)(2,1)S(1)}, bf16[1024,1536]{1,0:T(8,128)(2,1)}, u32[]{:S(2)}) copy-start(bf16[1024,1536]{1,0:T(8,128)(2,1)} %ffn_weights.4) | copy-start | bytes 9437188
  400.8 20.9 %collective-permute-start.28 = (bf16[256,1536]{1,0:T(8,128)(2,1)}, bf16[256,1536]{1,0:T(8,128)(2,1)}, u32[]{:S(2)}, u32[]{:S(2)}) collective-permute-start(bf16[256,1536]{1,0:T(8,128)(2,1)} %get-tuple-element.303), channel_id=1, source_target_pairs={{0,8},{8,0},{16,24},{24,16},{1,9},{9,1},{17,25},{25,17},{2,10},{10... | collective-permute-start | bytes 2359304 | tf_op jit(solution)/shard_map/ppermute | solution.py:1118
  444.1 182.5 %reduce-scatter.8.cloned.1.call-start = ((), (), s32[]{:S(2)}) async-start(), calls=%async_computation.10 | async-start | bytes 9437184 | tf_op jit(solution)/shard_map/reduce_scatter | solution.py:1164
  449.3 7.9 %collective-permute-start.29 = (bf16[4,256,2048]{2,1,0:T(8,128)(2,1)}, bf16[4,256,2048]{2,1,0:T(8,128)(2,1)}, u32[]{:S(2)}, u32[]{:S(2)}) collective-permute-start(bf16[4,256,2048]{2,1,0:T(8,128)(2,1)} %select_bitcast_fusion), channel_id=1, source_target_pairs={{0,1},{1,0},{2,3},{3,2},{4,5},{5,4},{6,7},{7,6},{8,9},{9,8},{10,11... | collective-permute-start | bytes 12582920 | tf_op jit(solution)/shard_map/ppermute | solution.py:935
  450.0 74.6 %collective-permute-start.36 = (bf16[1024,1536]{1,0:T(8,128)(2,1)}, bf16[1024,1536]{1,0:T(8,128)(2,1)}, u32[]{:S(2)}, u32[]{:S(2)}) collective-permute-start(bf16[1024,1536]{1,0:T(8,128)(2,1)} %get-tuple-element.328), channel_id=1, source_target_pairs={{0,8},{8,0},{16,24},{24,16},{1,9},{9,1},{17,25},{25,17},{2,10},{10... | collective-permute-start | bytes 9437192 | tf_op jit(solution)/shard_map/ppermute | solution.py:1133
  450.3 74.4 %collective-permute-start.37 = (bf16[1024,1536]{1,0:T(8,128)(2,1)S(1)}, bf16[1024,1536]{1,0:T(8,128)(2,1)}, u32[]{:S(2)}, u32[]{:S(2)}) collective-permute-start(bf16[1024,1536]{1,0:T(8,128)(2,1)S(1)} %get-tuple-element.329), channel_id=1, source_target_pairs={{8,16},{16,8},{9,17},{17,9},{10,18},{18,10},{11,19},{19,11},{12,20... | collective-permute-start | bytes 9437192 | tf_op jit(solution)/shard_map/ppermute | solution.py:1134
  466.6 58.1 %collective-permute-start.35 = (bf16[2,256,2048]{2,1,0:T(8,128)(2,1)}, bf16[2,256,2048]{2,1,0:T(8,128)(2,1)}, u32[]{:S(2)}, u32[]{:S(2)}) collective-permute-start(bf16[2,256,2048]{2,1,0:T(8,128)(2,1)} %pad_maximum_fusion.6), channel_id=1, source_target_pairs={{0,4},{1,3},{2,6},{3,1},{4,0},{5,7},{6,2},{7,5},{8,12},{9,11},{10,... | collective-permute-start | bytes 6291464 | tf_op jit(solution)/shard_map/ppermute | solution.py:929
  501.6 1.4 collective-permute-start.30
  503.1 11.8 %collective-permute-start.31 = (f32[2,2048]{1,0:T(2,128)S(1)}, f32[2,2048]{1,0:T(2,128)S(1)}, u32[]{:S(2)}, u32[]{:S(2)}) collective-permute-start(f32[2,2048]{1,0:T(2,128)S(1)} %add.172), channel_id=1, source_target_pairs={{0,2},{1,3},{2,0},{3,1},{4,6},{5,7},{6,4},{7,5},{8,10},{9,11},{10,... | collective-permute-start | bytes 49160 | tf_op jit(solution)/shard_map/ppermute | solution.py:766
  514.9 3.1 collective-permute-start.32
  518.0 3.1 collective-permute-start.33
  521.1 3.6 collective-permute-start.34
  532.3 35.2 %collective-permute-start.38 = (bf16[512,1536]{1,0:T(8,128)(2,1)}, bf16[512,1536]{1,0:T(8,128)(2,1)}, u32[]{:S(2)}, u32[]{:S(2)}) collective-permute-start(bf16[512,1536]{1,0:T(8,128)(2,1)} %get-tuple-element.425), channel_id=1, source_target_pairs={{0,8},{8,0},{16,24},{24,16},{1,9},{9,1},{17,25},{25,17},{2,10},{10... | collective-permute-start | bytes 4718600 | tf_op jit(solution)/shard_map/ppermute | solution.py:92
  532.4 37.0 %collective-permute-start.39 = (bf16[512,1536]{1,0:T(8,128)(2,1)}, bf16[512,1536]{1,0:T(8,128)(2,1)}, u32[]{:S(2)}, u32[]{:S(2)}) collective-permute-start(bf16[512,1536]{1,0:T(8,128)(2,1)} %get-tuple-element.426), channel_id=1, source_target_pairs={{8,16},{16,8},{9,17},{17,9},{10,18},{18,10},{11,19},{19,11},{12,20... | collective-permute-start | bytes 4718600 | tf_op jit(solution)/shard_map/ppermute | solution.py:92
  539.9 39.8 %collective-permute-start.43 = (bf16[256,1536]{1,0:T(8,128)(2,1)S(1)}, bf16[256,1536]{1,0:T(8,128)(2,1)S(1)}, u32[]{:S(2)}, u32[]{:S(2)}) collective-permute-start(bf16[256,1536]{1,0:T(8,128)(2,1)S(1)} %select_convert_fusion.1), channel_id=1, source_target_pairs={{0,4},{4,0},{1,5},{5,1},{2,6},{6,2},{3,7},{7,3},{8,12},{12,8},{9,1... | collective-permute-start | bytes 2359304 | tf_op jit(solution)/shard_map/ppermute | solution.py:159
  572.5 26.7 %collective-permute-start.44 = (bf16[256,1536]{1,0:T(8,128)(2,1)S(1)}, bf16[256,1536]{1,0:T(8,128)(2,1)S(1)}, u32[]{:S(2)}, u32[]{:S(2)}) collective-permute-start(bf16[256,1536]{1,0:T(8,128)(2,1)S(1)} %select_convert_fusion), channel_id=1, source_target_pairs={{0,4},{4,0},{1,5},{5,1},{2,6},{6,2},{3,7},{7,3},{8,12},{12,8},{9,1... | collective-permute-start | bytes 2359304 | tf_op jit(solution)/shard_map/ppermute | solution.py:159
  573.6 25.6 %collective-permute-start.42 = (bf16[768,640]{1,0:T(8,128)(2,1)S(1)}, bf16[768,640]{1,0:T(8,128)(2,1)S(1)}, u32[]{:S(2)}, u32[]{:S(2)}) collective-permute-start(bf16[768,640]{1,0:T(8,128)(2,1)S(1)} %get-tuple-element.346), channel_id=1, source_target_pairs={{0,8},{8,0},{16,24},{24,16},{1,9},{9,1},{17,25},{25,17},{2,10},{10... | collective-permute-start | bytes 2949128 | tf_op jit(solution)/shard_map/ppermute | solution.py:1176
  575.3 46.2 %collective-permute-start.46 = (bf16[256,2048]{1,0:T(8,128)(2,1)S(1)}, bf16[256,2048]{1,0:T(8,128)(2,1)S(1)}, u32[]{:S(2)}, u32[]{:S(2)}) collective-permute-start(bf16[256,2048]{1,0:T(8,128)(2,1)S(1)} %fusion.4), channel_id=1, source_target_pairs={{0,2},{1,5},{2,0},{3,7},{4,6},{5,1},{6,4},{7,3},{8,10},{9,13},{10,... | collective-permute-start | bytes 3145736 | tf_op jit(solution)/shard_map/ppermute | solution.py:932
  576.4 45.1 %collective-permute-start.40 = (bf16[256,640]{1,0:T(8,128)(2,1)}, bf16[256,640]{1,0:T(8,128)(2,1)}, u32[]{:S(2)}, u32[]{:S(2)}) collective-permute-start(bf16[256,640]{1,0:T(8,128)(2,1)} %get-tuple-element.343), channel_id=1, source_target_pairs={{0,16},{8,24},{16,0},{24,8},{1,17},{9,25},{17,1},{25,9},{2,18},{10... | collective-permute-start | bytes 983048 | tf_op jit(solution)/shard_map/ppermute | solution.py:1177
  579.7 21.8 %copy-start.38 = (bf16[256,1536]{1,0:T(8,128)(2,1)}, bf16[256,1536]{1,0:T(8,128)(2,1)S(1)}, u32[]{:S(2)}) copy-start(bf16[256,1536]{1,0:T(8,128)(2,1)S(1)} %collective-permute-done.43.theirs_1) | copy-start | bytes 2359300
  579.7 41.7 %collective-permute-start.41 = (bf16[256,640]{1,0:T(8,128)(2,1)S(1)}, bf16[256,640]{1,0:T(8,128)(2,1)}, u32[]{:S(2)}, u32[]{:S(2)}) collective-permute-start(bf16[256,640]{1,0:T(8,128)(2,1)S(1)} %get-tuple-element.344), channel_id=1, source_target_pairs={{0,24},{8,16},{16,8},{24,0},{1,25},{9,17},{17,9},{25,1},{2,26},{10... | collective-permute-start | bytes 983048 | tf_op jit(solution)/shard_map/ppermute | solution.py:1177
  600.3 26.4 %collective-permute-start.45 = (bf16[256,640]{1,0:T(8,128)(2,1)}, bf16[256,640]{1,0:T(8,128)(2,1)}, u32[]{:S(2)}, u32[]{:S(2)}) collective-permute-start(bf16[256,640]{1,0:T(8,128)(2,1)} %add_convert_fusion.6), channel_id=1, source_target_pairs={{0,24},{8,16},{16,8},{24,0},{1,25},{9,17},{17,9},{25,1},{2,26},{10... | collective-permute-start | bytes 983048 | tf_op jit(solution)/shard_map/ppermute | solution.py:1191
  629.2 8.8 %collective-permute-start.47 = (bf16[256,640]{1,0:T(8,128)(2,1)S(1)}, bf16[256,640]{1,0:T(8,128)(2,1)S(1)}, u32[]{:S(2)}, u32[]{:S(2)}) collective-permute-start(bf16[256,640]{1,0:T(8,128)(2,1)S(1)} %get-tuple-element.431), channel_id=1, source_target_pairs={{0,4},{4,0},{1,5},{5,1},{2,6},{6,2},{3,7},{7,3},{8,12},{12,8},{9,1... | collective-permute-start | bytes 983048 | tf_op jit(solution)/shard_map/ppermute | solution.py:159
  (53 other events, 247.2 us)
Sparse Core Ops, SparseCore 0:
  11.4 64.2 all-gather.4
  105.3 76.6 reduce-scatter.3
  186.1 54.7 all-gather.6
  242.8 54.3 all-gather.8
  339.4 73.4 reduce-scatter.5
  444.3 66.3 all-gather.10
  524.9 91.5 reduce-scatter.7
